TPU v7x, 32 devices: a whole 2x2x4 slice. The times are simulated.
32 devices in a mesh: heads: 4 (over y, x), blk: 8 (over z, core).
Axes of the slice: x: 2, y: 2, z: 4, core: 2. Of those that a mesh axis runs over, the one named last changes fastest.
Arguments:
- inputs: bfloat16 [16384, 2048], P(('blk', 'heads')), may hold values from -6 to 6
- positions: int32 [16384], P('blk'), may hold values from 0 to 1999, as said below
- attn_gain: bfloat16 [2048], P(('heads', 'blk')), may hold values from 0.25 to 1.75
- qkv_weight: bfloat16 [2048, 1536], P(('heads', 'blk')), may hold values from -0.125 to 0.125
- q_gain: bfloat16 [64], replicated, may hold values from 0.796875 to 1.796875
- k_gain: bfloat16 [64], replicated, may hold values from 0.796875 to 1.796875
- out_weight: bfloat16 [1024, 2048], P(('heads', 'blk')), may hold values from -1.5 to 1.5
- ffn_gain: bfloat16 [2048], P(('heads', 'blk')), may hold values from 0.25 to 1.75
- ffn_in_weight: bfloat16 [2048, 10240], P(('heads', 'blk')), may hold values from -0.125 to 0.125
- ffn_out_weight: bfloat16 [5120, 2048], P(('heads', 'blk')), may hold values from -0.078125 to 0.078125
- cotangent: bfloat16 [16384, 2048], P(('blk', 'heads')), may hold values from -6 to 6
Outputs:
- layer_out: bfloat16 [16384, 2048], P(('blk', 'heads'))
- input_grad: float32 [16384, 2048], P(('blk', 'heads'))
- attn_gain_grad: float32 [2048], P(('heads', 'blk'))
- qkv_grad: float32 [2048, 1536], P(('heads', 'blk'))
- q_gain_grad: float32 [64], replicated
- k_gain_grad: float32 [64], replicated
- out_grad: float32 [1024, 2048], P(('heads', 'blk'))
- ffn_gain_grad: float32 [2048], P(('heads', 'blk'))
- ffn_in_grad: float32 [2048, 10240], P(('heads', 'blk'))
- ffn_out_grad: float32 [5120, 2048], P(('heads', 'blk'))
Inputs may be any that keep to these rules, and one draw needn't show every extreme that they name: `positions`: positions count up by one along a document and start at 0 where a new one begins; a document begins at every multiple of 8192 tokens; no document has more than 2000 tokens and the first of the stream has exactly 2000; a document that a sequence's end does not cut has at least 200 tokens.
All inputs are finite; a program needn't handle non-finite values.
Results may differ from a plain program's by a relative error of at most 0.015.
Values may be sent and summed in bfloat16 or wider, within the bound.
A program may use at most 320 MiB of HBM per device.

v0:
```python
import jax
import jax.numpy as jnp
from jax import lax
from jax.sharding import PartitionSpec as P

HEADS = 16
KV_HEADS = 4
DOC_MAX = 2000


EPS = 1e-06
ROPE_BASE = 10000.0
NEG = -1e30


def from_behind(block, axis, distance):
    devices = range(lax.axis_size(axis))
    route = [(i - distance, i) for i in devices if i - distance in devices]
    return lax.ppermute(block, axis, route)


def rms_scale(values, scaling):
    return values * lax.rsqrt(jnp.mean(values * values, axis=-1, keepdims=True) + EPS) * scaling


def norm_back(values, scaling, gradient):
    inverse = lax.rsqrt(jnp.mean(values * values, axis=-1, keepdims=True) + EPS)
    scaled = gradient * scaling
    moment = jnp.mean(scaled * values, axis=-1, keepdims=True)
    return (
        inverse * scaled - values * inverse * inverse * inverse * moment,
        gradient * values * inverse,
    )


def rotation(positions, head_dim):
    half_width = head_dim // 2
    frequency = ROPE_BASE ** (-2.0 * jnp.arange(half_width, dtype=jnp.float32) / head_dim)
    angles = positions.astype(jnp.float32)[:, None] * frequency[None, :]
    return (jnp.cos(angles)[:, None, :], jnp.sin(angles)[:, None, :])


def rotate(values, cosine, sine):
    half_width = values.shape[-1] // 2
    front_half = values[..., :half_width]
    second = values[..., half_width:]
    return jnp.concatenate(
        [front_half * cosine - second * sine, second * cosine + front_half * sine], axis=-1
    )


def swiglu_forward(normed_rows, in_matrix, unit_count):
    gate_up = jnp.dot(normed_rows, in_matrix, preferred_element_type=jnp.float32)
    gate = gate_up[:, :unit_count]
    upward = gate_up[:, unit_count:]
    sigmoid = jax.nn.sigmoid(gate)
    activated = gate * sigmoid
    hidden = (activated * upward).astype(jnp.bfloat16)
    return (gate, upward, sigmoid, activated, hidden)


def swiglu_back(hidden_grad, gate, upward, sigmoid, activated):
    gate_grad = hidden_grad * upward * sigmoid * (1.0 + gate * (1.0 - sigmoid))
    upward_grad = hidden_grad * activated
    return jnp.concatenate([gate_grad, upward_grad], axis=-1).astype(jnp.bfloat16)


def local(
    inputs,
    positions,
    attn_gain,
    qkv_weight,
    q_gain,
    k_gain,
    out_weight,
    ffn_gain,
    ffn_in_weight,
    ffn_out_weight,
    cotangent,
):
    token_count = inputs.shape[0]
    head_dim = q_gain.shape[0]
    group_size = HEADS // KV_HEADS
    score_scale = head_dim ** (-0.5)
    query_width = HEADS * head_dim
    key_width = KV_HEADS * head_dim
    own_positions = lax.dynamic_slice_in_dim(
        positions, lax.axis_index("heads") * token_count, token_count, 0
    )
    cosine, sine = rotation(own_positions, head_dim)
    hidden_in = inputs.astype(jnp.float32)
    attn_norm_gain, ffn_norm_gain, qkv_full, out_full = (
        lax.all_gather(attn_gain, ("heads", "blk"), axis=0, tiled=True),
        lax.all_gather(ffn_gain, ("heads", "blk"), axis=0, tiled=True),
        lax.all_gather(qkv_weight, ("heads", "blk"), axis=0, tiled=True),
        lax.all_gather(out_weight, ("heads", "blk"), axis=0, tiled=True),
    )
    ffn_scaling = ffn_norm_gain.astype(jnp.float32)
    normed = rms_scale(hidden_in, attn_norm_gain.astype(jnp.float32)).astype(jnp.bfloat16)
    projected = jnp.dot(normed, qkv_full, preferred_element_type=jnp.float32)
    query_raw = projected[:, :query_width].reshape(token_count, HEADS, head_dim)
    key_raw = projected[:, query_width : query_width + key_width].reshape(
        token_count, KV_HEADS, head_dim
    )
    value_raw = projected[:, query_width + key_width :].reshape(token_count, KV_HEADS, head_dim)
    query_scaling = q_gain.astype(jnp.float32)
    key_scaling = k_gain.astype(jnp.float32)
    query_low = rotate(rms_scale(query_raw, query_scaling), cosine, sine).astype(jnp.bfloat16)
    key_low = rotate(rms_scale(key_raw, key_scaling), cosine, sine).astype(jnp.bfloat16)
    pair_low = jnp.concatenate([key_low, value_raw.astype(jnp.bfloat16)], axis=-1)
    query_blk, pair_blk = (
        lax.all_to_all(
            query_low.reshape(token_count, KV_HEADS, group_size * head_dim),
            "heads",
            split_axis=1,
            concat_axis=0,
            tiled=True,
        ),
        lax.all_to_all(pair_low, "heads", split_axis=1, concat_axis=0, tiled=True),
    )
    block_len = query_blk.shape[0]
    local_groups = query_blk.shape[1]
    prior_pair = from_behind(pair_blk, "blk", 1)
    pair_all = jnp.concatenate([prior_pair, pair_blk], axis=0)
    query_rows = min(512, block_len)
    window = min(block_len, -(-DOC_MAX // 128) * 128)
    key_span = window + query_rows
    queries = query_blk.reshape(block_len, local_groups, group_size, head_dim)
    starts = jnp.arange(block_len // query_rows, dtype=jnp.int32) * query_rows

    def scores_at(row_start):
        query_part = lax.dynamic_slice_in_dim(queries, row_start, query_rows, 0)
        window_start = row_start + block_len - window
        pair_part = lax.dynamic_slice_in_dim(pair_all, window_start, key_span, 0)
        key_part = pair_part[..., :head_dim]
        value_part = pair_part[..., head_dim:]
        position_part = lax.dynamic_slice_in_dim(positions, row_start, query_rows, 0)
        query_index = row_start + block_len + jnp.arange(query_rows, dtype=jnp.int32)
        key_index = window_start + jnp.arange(key_span, dtype=jnp.int32)
        allowed = (key_index[None, :] <= query_index[:, None]) & (
            key_index[None, :] >= (query_index - position_part)[:, None]
        )
        scores = (
            jnp.einsum("qcgd,kcd->cgqk", query_part, key_part, preferred_element_type=jnp.float32)
            * score_scale
        )
        return (query_part, key_part, value_part, window_start, jnp.where(allowed, scores, NEG))

    def attend(row_start):
        query_part, key_part, value_part, window_start, scores = scores_at(row_start)
        top = jnp.max(scores, axis=-1, keepdims=True)
        expo = jnp.exp(scores - top)
        total = jnp.sum(expo, axis=-1, keepdims=True)
        probs = (expo / total).astype(jnp.bfloat16)
        mixed = jnp.einsum("cgqk,kcd->qcgd", probs, value_part, preferred_element_type=jnp.float32)
        return (mixed.astype(jnp.bfloat16), top + jnp.log(total))

    attended, log_sums = lax.map(attend, starts)
    attended_blk = attended.reshape(block_len, local_groups, group_size * head_dim)
    attended_tok = lax.all_to_all(
        attended_blk, "heads", split_axis=0, concat_axis=1, tiled=True
    ).reshape(token_count, query_width)
    residual = hidden_in + jnp.dot(attended_tok, out_full, preferred_element_type=jnp.float32)
    ffn_normed = rms_scale(residual, ffn_scaling).astype(jnp.bfloat16)
    outer_grad = cotangent.astype(jnp.float32)
    ffn_up_full, ffn_down_full = (
        lax.all_gather(ffn_in_weight, ("heads", "blk"), axis=0, tiled=True),
        lax.all_gather(ffn_out_weight, ("heads", "blk"), axis=0, tiled=True),
    )
    hidden_units = ffn_down_full.shape[0]
    gate, upward, sigmoid, activated, hidden = swiglu_forward(ffn_normed, ffn_up_full, hidden_units)
    output = residual + jnp.dot(hidden, ffn_down_full, preferred_element_type=jnp.float32)
    layer_out = output.astype(jnp.bfloat16)
    held = lax.optimization_barrier((ffn_in_weight, ffn_out_weight, output))
    ffn_up_full, ffn_down_full = (
        lax.all_gather(held[0], ("heads", "blk"), axis=0, tiled=True),
        lax.all_gather(held[1], ("heads", "blk"), axis=0, tiled=True),
    )
    hidden_grad = jnp.dot(cotangent, ffn_down_full.T, preferred_element_type=jnp.float32)
    down_grad = jnp.dot(hidden.T, cotangent, preferred_element_type=jnp.float32)
    gate_up_grad = swiglu_back(hidden_grad, gate, upward, sigmoid, activated)
    up_proj_grad = jnp.dot(ffn_normed.T, gate_up_grad, preferred_element_type=jnp.float32)
    ffn_normed_grad = jnp.dot(gate_up_grad, ffn_up_full.T, preferred_element_type=jnp.float32)
    ffn_in_grad, ffn_out_grad = (
        lax.psum_scatter(up_proj_grad, ("heads", "blk"), scatter_dimension=0, tiled=True),
        lax.psum_scatter(down_grad, ("heads", "blk"), scatter_dimension=0, tiled=True),
    )
    residual_norm_grad, ffn_gain_terms = norm_back(residual, ffn_scaling, ffn_normed_grad)
    residual_grad = outer_grad + residual_norm_grad
    held = lax.optimization_barrier((attn_gain, qkv_weight, out_weight, residual_grad))
    attn_norm_gain, qkv_full, out_full = (
        lax.all_gather(held[0], ("heads", "blk"), axis=0, tiled=True),
        lax.all_gather(held[1], ("heads", "blk"), axis=0, tiled=True),
        lax.all_gather(held[2], ("heads", "blk"), axis=0, tiled=True),
    )
    branch_grad = residual_grad.astype(jnp.bfloat16)
    out_proj_grad = jnp.dot(attended_tok.T, branch_grad, preferred_element_type=jnp.float32)
    attended_grad = jnp.dot(branch_grad, out_full.T, preferred_element_type=jnp.float32).astype(
        jnp.bfloat16
    )
    attended_grad = attended_grad.reshape(token_count, KV_HEADS, group_size * head_dim)
    attended_grad_blk = lax.all_to_all(
        attended_grad, "heads", split_axis=1, concat_axis=0, tiled=True
    )
    attended_grad_blk = attended_grad_blk.reshape(block_len, local_groups, group_size, head_dim)

    def attend_back(pair_sum, element):
        row_start, log_sum = element
        query_part, key_part, value_part, window_start, scores = scores_at(row_start)
        probs = jnp.exp(scores - log_sum)
        grad_part = lax.dynamic_slice_in_dim(attended_grad_blk, row_start, query_rows, 0)
        prob_grad = jnp.einsum(
            "qcgd,kcd->cgqk", grad_part, value_part, preferred_element_type=jnp.float32
        )
        inner = jnp.sum(probs * prob_grad, axis=-1, keepdims=True)
        score_grad = (probs * (prob_grad - inner)).astype(jnp.bfloat16)
        query_grad = (
            jnp.einsum("cgqk,kcd->qcgd", score_grad, key_part, preferred_element_type=jnp.float32)
            * score_scale
        )
        key_grad = (
            jnp.einsum("cgqk,qcgd->kcd", score_grad, query_part, preferred_element_type=jnp.float32)
            * score_scale
        )
        value_grad = jnp.einsum(
            "cgqk,qcgd->kcd",
            probs.astype(jnp.bfloat16),
            grad_part,
            preferred_element_type=jnp.float32,
        )
        window_sum = lax.dynamic_slice_in_dim(
            pair_sum, window_start, key_span, 0
        ) + jnp.concatenate([key_grad, value_grad], axis=-1)
        return (lax.dynamic_update_slice_in_dim(pair_sum, window_sum, window_start, 0), query_grad)

    pair_zero = jnp.zeros((2 * block_len, local_groups, 2 * head_dim), jnp.float32)
    pair_sum, query_grads = lax.scan(attend_back, pair_zero, (starts, log_sums))
    returned = from_behind(pair_sum[:block_len], "blk", -1)
    pair_grad_blk = (pair_sum[block_len:] + returned).astype(jnp.bfloat16)
    query_grad_blk = query_grads.reshape(block_len, local_groups, group_size * head_dim).astype(
        jnp.bfloat16
    )
    query_grad_tok, pair_grad_tok = (
        lax.all_to_all(query_grad_blk, "heads", split_axis=0, concat_axis=1, tiled=True),
        lax.all_to_all(pair_grad_blk, "heads", split_axis=0, concat_axis=1, tiled=True),
    )
    query_rot_grad = query_grad_tok.reshape(token_count, HEADS, head_dim).astype(jnp.float32)
    key_rot_grad = pair_grad_tok[..., :head_dim].astype(jnp.float32)
    value_grad_tok = pair_grad_tok[..., head_dim:].astype(jnp.float32)
    query_raw_grad, query_gain_terms = norm_back(
        query_raw, query_scaling, rotate(query_rot_grad, cosine, -sine)
    )
    key_raw_grad, key_gain_terms = norm_back(
        key_raw, key_scaling, rotate(key_rot_grad, cosine, -sine)
    )
    projected_grad = jnp.concatenate(
        [
            query_raw_grad.reshape(token_count, query_width),
            key_raw_grad.reshape(token_count, key_width),
            value_grad_tok.reshape(token_count, key_width),
        ],
        axis=-1,
    ).astype(jnp.bfloat16)
    qkv_grad_full = jnp.dot(normed.T, projected_grad, preferred_element_type=jnp.float32)
    normed_in_grad = jnp.dot(projected_grad, qkv_full.T, preferred_element_type=jnp.float32)
    input_norm_grad, attn_gain_terms = norm_back(
        hidden_in, attn_norm_gain.astype(jnp.float32), normed_in_grad
    )
    input_grad = residual_grad + input_norm_grad
    q_gain_grad, k_gain_grad = lax.psum(
        (jnp.sum(query_gain_terms, axis=(0, 1)), jnp.sum(key_gain_terms, axis=(0, 1))),
        ("heads", "blk"),
    )
    attn_gain_grad, ffn_gain_grad, qkv_grad, out_grad = (
        lax.psum_scatter(
            jnp.sum(attn_gain_terms, axis=0), ("heads", "blk"), scatter_dimension=0, tiled=True
        ),
        lax.psum_scatter(
            jnp.sum(ffn_gain_terms, axis=0), ("heads", "blk"), scatter_dimension=0, tiled=True
        ),
        lax.psum_scatter(qkv_grad_full, ("heads", "blk"), scatter_dimension=0, tiled=True),
        lax.psum_scatter(out_proj_grad, ("heads", "blk"), scatter_dimension=0, tiled=True),
    )
    return (
        layer_out,
        input_grad,
        attn_gain_grad,
        qkv_grad,
        q_gain_grad,
        k_gain_grad,
        out_grad,
        ffn_gain_grad,
        ffn_in_grad,
        ffn_out_grad,
    )


def solution(mesh):
    placed = (
        P(("blk", "heads"), None),
        P("blk"),
        P(("heads", "blk")),
        P(("heads", "blk"), None),
        P(),
        P(),
        P(("heads", "blk"), None),
        P(("heads", "blk")),
        P(("heads", "blk"), None),
        P(("heads", "blk"), None),
        P(("blk", "heads"), None),
    )
    return jax.shard_map(
        local,
        mesh=mesh,
        in_specs=placed,
        out_specs=(
            P(("blk", "heads"), None),
            P(("blk", "heads"), None),
            P(("heads", "blk")),
            P(("heads", "blk"), None),
            P(),
            P(),
            P(("heads", "blk"), None),
            P(("heads", "blk")),
            P(("heads", "blk"), None),
            P(("heads", "blk"), None),
        ),
        check_vma=False,
    )
```

profile of v0, /device:TPU:0, one launch (start us, length us, event | category | flops | bytes accessed | tf_op | source)
XLA Modules:
  0.0 2751.7 jit_solution(7532567946664295950)
XLA Ops:
  13.0 42.3 %all-reduce.6 = (bf16[2048]{0:T(1024)(128)(2,1)S(1)}, bf16[2048]{0:T(1024)(128)(2,1)}) all-reduce(bf16[2048]{0:T(1024)(128)(2,1)S(1)} %dynamic-update-slice, bf16[2048]{0:T(1024)(128)(2,1)S(1)} %dynamic-update-slice.1), channel_id=1, replica_groups=mesh['heads'=4,'blk'=8] {'heads','blk'}, use_global_device_ids=true, to_apply=%add | all-reduce | flops 4096 | bytes 16384
  59.1 24.4 all-gather.9.cloned.1.call-done
  131.1 89.0 %while.32 = (s32[]{:T(128)}, bf16[4,512,1,4,64]{1,4,3,2,0:T(8,128)(2,1)}, f32[4,1,4,512,1]{3,2,4,1,0:T(4,128)}, s32[4]{0:T(128)S(1)}, bf16[4096,1,128]{0,2,1:T(8...) while((s32[]{:T(128)}, ...), condition=%wide.region_6.7_spmd, body=%wide.region_3.6_spmd.sunk | while | flops 1409156608 | bytes 69433592 | solution.py:158
  278.7 109.1 %all-gather.13.cloned.1.call-done = bf16[2048,10240]{1,0:T(8,128)(2,1)} async-done(((bf16[64,10240]{1,0:T(8,128)(2,1)}), bf16[2048,10240]{1,0:T(8,128)(2,1)}) %all-gather.13.cloned.1.call-update) | async-done | bytes 41943056 | tf_op jit(solution)/shard_map/all_gather | solution.py:167
  387.7 32.5 %fusion.92 = f32[512,10240]{1,0:T(8,128)} fusion(bf16[2048,10240]{1,0:T(8,128)(2,1)} %all-gather.13.cloned.1.call-done, f32[512,2048]{1,0:T(8,128)} %get-tuple-element.500, f32[2048]{0:T(1024)S(1)} %convert_element_type.137, f32[512]{0:T(512)S(1)} %add_rsqrt_fusion.2), kind=kOutput, calls=%fused_computation.164 | convolution fusion | flops 21477982208 | bytes 67119104 | tf_op jit(solution)/shard_map/dot_general | solution.py:53
  431.2 92.1 %all-gather.15.cloned.1.call-done = bf16[5120,2048]{1,0:T(8,128)(2,1)} async-done(((bf16[160,2048]{1,0:T(8,128)(2,1)}), bf16[5120,2048]{1,0:T(8,128)(2,1)}) %all-gather.15.cloned.1.call-update) | async-done | bytes 20971536 | tf_op jit(solution)/shard_map/all_gather | solution.py:168
  523.2 18.2 convolution_add_fusion
  542.1 132.3 %all-gather.17.cloned.1.call-done = bf16[5120,2048]{1,0:T(8,128)(2,1)} async-done(((bf16[160,2048]{1,0:T(8,128)(2,1)}), bf16[5120,2048]{1,0:T(8,128)(2,1)}) %all-gather.17.cloned.1.call-update) | async-done | bytes 20971536 | tf_op jit(solution)/shard_map/all_gather | solution.py:177
  674.3 34.4 %fusion.57 = (bf16[512,5120]{1,0:T(8,128)(2,1)}, bf16[512,5120]{1,0:T(8,128)(2,1)}) fusion(f32[512,10240]{1,0:T(8,128)} %fusion.92, bf16[5120,2048]{1,0:T(8,128)(2,1)} %all-gather.17.cloned.1.call-done, bf16[512,2048]{1,0:T(8,128)(2,1)S(1)} %copy-done.17), kind=kOutput, calls=%fused_computation.75 | convolution fusion | flops 10771496960 | bytes 54525952 | tf_op jit(solution)/shard_map/dot_general | solution.py:179
  708.7 201.8 %all-gather.19.cloned.1.call-done = bf16[2048,10240]{1,0:T(8,128)(2,1)} async-done(((bf16[64,10240]{1,0:T(8,128)(2,1)}), bf16[2048,10240]{1,0:T(8,128)(2,1)}) %all-gather.19.cloned.1.call-update) | async-done | bytes 41943056 | tf_op jit(solution)/shard_map/all_gather | solution.py:176
  910.5 31.9 %multiply_reduce_fusion = (f32[2048]{0:T(1024)}, f32[512]{0:T(512)S(1)}, f32[512,2048]{1,0:T(8,128)}) fusion(f32[512,2048]{1,0:T(8,128)} %get-tuple-element.500, f32[512]{0:T(512)S(1)} %add_rsqrt_fusion.2, f32[2048]{0:T(1024)S(1)} %convert_element_type.137, bf16[2048,10240]{1,0:T(8,128)(2,1)} %all-gather.19.cloned.1.call-done, ...), kind=kOutput, calls=%fused_computation.98 | convolution fusion | flops 21502097408 | bytes 60837888 | tf_op jit(solution)/shard_map/dot_general | solution.py:183
  950.0 19.4 fusion.93
  969.4 40.2 %all-gather.21.cloned.1.call-done = bf16[1024,2048]{1,0:T(8,128)(2,1)} async-done(((bf16[32,2048]{1,0:T(8,128)(2,1)}), bf16[1024,2048]{1,0:T(8,128)(2,1)}) %all-gather.21.cloned.1.call-update) | async-done | bytes 4194320 | tf_op jit(solution)/shard_map/all_gather | solution.py:194
  1039.3 298.3 %while.33 = (s32[]{:T(128)}, f32[4096,1,128]{2,0,1:T(8,128)}, bf16[4,512,1,4,64]{1,4,3,2,0:T(8,128)(2,1)}, s32[4]{0:T(128)S(1)}, bf16[2048,1,4,64]{0,3,2,1:T(8,1...) while((s32[]{:T(128)}, f32[4096,1,128]{2,0,1:T(8,128)}, ...), condition=%wide.region_11.12_spmd, body=%wide.region_9.11_spmd.sunk | while | flops 3438970368 | bytes 202922400 | solution.py:237
  1086.8 15.5 fusion.139
  1146.7 15.0 fusion.138
  1220.9 15.0 fusion.138
  1295.3 15.0 fusion.138
  1441.8 38.8 %fusion.60 = f32[2048,10240]{1,0:T(8,128)} fusion(bf16[512,5120]{1,0:T(8,128)(2,1)} %get-tuple-element.477, bf16[512,5120]{1,0:T(8,128)(2,1)} %get-tuple-element.476, f32[512,2048]{1,0:T(8,128)} %get-tuple-element.500, f32[2048]{0:T(1024)S(1)} %copy-done.24, f32[512]{0:T(512)S(1)} %copy-done.26), kind=kOutput, calls=%fused_computation.85 | convolution fusion | flops 21498953728 | bytes 98576384 | tf_op jit(solution)/shard_map/dot_general | solution.py:182
  1481.4 44.7 %all-reduce.2 = bf16[2048]{0:T(1024)(128)(2,1)S(1)} all-reduce(bf16[2048]{0:T(1024)(128)(2,1)S(1)} %dynamic-update-slice.2), channel_id=1, replica_groups=mesh['heads'=4,'blk'=8] {'heads','blk'}, use_global_device_ids=true, to_apply=%add.2 | all-reduce | flops 2048 | bytes 8192
  1535.0 41.3 %all-reduce.5 = (f32[2048]{0:T(1024)S(1)}, f32[64]{0:T(128)}, f32[64]{0:T(128)}, f32[2048]{0:T(1024)S(1)}) all-reduce(f32[2048]{0:T(1024)S(1)} %get-tuple-element.428, f32[64]{0:T(128)S(1)} %reduce_sum.167, f32[64]{0:T(128)S(1)} %reduce_sum.170, f32[2048]{0:T(1024)S(1)} %copy-done.36), channel_id=2, replica_groups=mesh['heads'=4,'blk'=8] {'heads','blk'}, use_global_device_ids=true, to_apply=%region_16.17.clone | all-reduce | flops 4224 | bytes 33792
  1584.5 114.7 %reduce-scatter.7.cloned.1.call-done = f32[32,2048]{1,0:T(8,128)} async-done(((f32[1024,2048]{1,0:T(8,128)}), f32[32,2048]{1,0:T(8,128)}) %reduce-scatter.7.cloned.1.call-update) | async-done | bytes 262160 | tf_op jit(solution)/shard_map/reduce_scatter | solution.py:282
  1699.1 159.9 %reduce-scatter.5.cloned.1.call-done = f32[64,1536]{1,0:T(8,128)} async-done(((f32[2048,1536]{1,0:T(8,128)}), f32[64,1536]{1,0:T(8,128)}) %reduce-scatter.5.cloned.1.call-update) | async-done | bytes 393232 | tf_op jit(solution)/shard_map/reduce_scatter | solution.py:281
  1859.0 885.7 %reduce-scatter.9.cloned.1.call-done = f32[64,10240]{1,0:T(8,128)} async-done(((f32[2048,10240]{1,0:T(8,128)}), f32[64,10240]{1,0:T(8,128)}) %reduce-scatter.9.cloned.1.call-update) | async-done | bytes 2621456 | tf_op jit(solution)/shard_map/reduce_scatter | solution.py:185
  (371 shorter events, 585.8 us)
Async XLA Ops:
  7.2 76.3 %all-gather.9.cloned.1.call-start = ((), (), s32[]{:S(2)}) async-start(), calls=%async_computation.10 | async-start | bytes 6488064 | tf_op jit(solution)/shard_map/all_gather | solution.py:95
  7.9 263.2 %all-gather.11.cloned.1.call-start = ((), (), s32[]{:S(2)}) async-start(), calls=%async_computation.11 | async-start | bytes 4325376 | tf_op jit(solution)/shard_map/all_gather | solution.py:96
  8.7 379.1 %all-gather.13.cloned.1.call-start = ((), (), s32[]{:S(2)}) async-start(), calls=%async_computation.12 | async-start | bytes 43253760 | tf_op jit(solution)/shard_map/all_gather | solution.py:167
  9.4 513.8 %all-gather.15.cloned.1.call-start = ((), (), s32[]{:S(2)}) async-start(), calls=%async_computation.13 | async-start | bytes 21626880 | tf_op jit(solution)/shard_map/all_gather | solution.py:168
  10.7 89.4 %copy-start.41 = (f32[64]{0:T(128)}, f32[64]{0:T(128)S(1)}, u32[]{:S(2)}) copy-start(f32[64]{0:T(128)S(1)} %convert_element_type.135) | copy-start | bytes 772
  94.3 12.2 all-to-all-start
  106.5 20.7 all-to-all-start.1
  111.0 18.2 collective-permute-start
  246.4 17.1 all-to-all-start.2
  249.9 424.4 %all-gather.17.cloned.1.call-start = ((), (), s32[]{:S(2)}) async-start(), calls=%async_computation.14 | async-start | bytes 21626880 | tf_op jit(solution)/shard_map/all_gather | solution.py:177
  250.0 692.4 %copy-start.23 = (f32[2048]{0:T(1024)}, f32[2048]{0:T(1024)S(1)}, u32[]{:S(2)}) copy-start(f32[2048]{0:T(1024)S(1)} %convert_element_type.137) | copy-start | bytes 24580
  278.7 663.7 %copy-start.25 = (f32[512]{0:T(512)}, f32[512]{0:T(512)S(1)}, u32[]{:S(2)}) copy-start(f32[512]{0:T(512)S(1)} %add_rsqrt_fusion.2) | copy-start | bytes 6148
  431.1 243.2 %copy-start.17 = (bf16[512,2048]{1,0:T(8,128)(2,1)S(1)}, bf16[512,2048]{1,0:T(8,128)(2,1)}, u32[]{:S(2)}) copy-start(bf16[512,2048]{1,0:T(8,128)(2,1)} %param.25) | copy-start | bytes 6291460
  541.4 369.0 %all-gather.19.cloned.1.call-start = ((), (), s32[]{:S(2)}) async-start(), calls=%async_computation.15 | async-start | bytes 43253760 | tf_op jit(solution)/shard_map/all_gather | solution.py:176
  542.0 467.7 %all-gather.21.cloned.1.call-start = ((), (), s32[]{:S(2)}) async-start(), calls=%async_computation.16 | async-start | bytes 4325376 | tf_op jit(solution)/shard_map/all_gather | solution.py:194
  949.2 577.0 %all-gather.23.cloned.1.call-start = ((), (), s32[]{:S(2)}) async-start(), calls=%async_computation.17 | async-start | bytes 6488064 | tf_op jit(solution)/shard_map/all_gather | solution.py:193
  950.0 634.5 %reduce-scatter.11.cloned.1.call-start = ((), (), s32[]{:S(2)}) async-start(), calls=%async_computation.21 | async-start | bytes 43253760 | tf_op jit(solution)/shard_map/reduce_scatter | solution.py:186
  1016.6 18.7 all-to-all-start.3
  1020.1 679.0 %reduce-scatter.7.cloned.1.call-start = ((), (), s32[]{:S(2)}) async-start(), calls=%async_computation.19 | async-start | bytes 8650752 | tf_op jit(solution)/shard_map/reduce_scatter | solution.py:282
  1357.5 26.8 all-to-all-start.4
  1370.2 34.1 %collective-permute-start.1 = (f32[2048,1,128]{2,0,1:T(8,128)}, f32[2048,1,128]{2,0,1:T(8,128)}, u32[]{:S(2)}, u32[]{:S(2)}) collective-permute-start(f32[2048,1,128]{2,0,1:T(8,128)} %slice.100), channel_id=1, source_target_pairs={{1,0},{2,1},{3,2},{4,3},{5,4},{6,5},{7,6},{9,8},{10,9},{11,10},{12... | collective-permute-start | bytes 3145736 | tf_op jit(solution)/shard_map/ppermute | solution.py:19
  1411.3 14.5 all-to-all-start.5
  1415.5 443.6 %reduce-scatter.5.cloned.1.call-start = ((), (), s32[]{:S(2)}) async-start(), calls=%async_computation.18 | async-start | bytes 12976128 | tf_op jit(solution)/shard_map/reduce_scatter | solution.py:281
  1441.1 1303.6 %reduce-scatter.9.cloned.1.call-start = ((), (), s32[]{:S(2)}) async-start(), calls=%async_computation.20 | async-start | bytes 86507520 | tf_op jit(solution)/shard_map/reduce_scatter | solution.py:185
  (59 other events, 764.3 us)
Sparse Core Ops, SparseCore 0:
  11.0 72.4 all-gather.8
  86.5 64.4 all-gather.10
  153.9 233.8 all-gather.12
  390.4 132.7 all-gather.14
  541.6 132.7 all-gather.16
  677.0 233.3 all-gather.18
  949.4 60.2 all-gather.20
  1012.7 73.7 all-gather.22
  1089.4 459.0 reduce-scatter.10
  1551.3 147.8 reduce-scatter.6
  1705.7 153.2 reduce-scatter.4
  1861.9 882.7 reduce-scatter.8
where the time goes:
time: 2760 us; the launch traced here: 2750 us
  waiting for transfers between devices  1820 us (66%)
  matrix products  432 us (16%)
  other arithmetic  179 us (6%)
  blocking collectives  128 us (5%)
  local copies, waits for them, and re-layouts  123 us (4%)
    reduce_scatter x1, waiting for transfers between devices, local(): lax.psum_scatter(up_proj_grad, ('heads', 'blk'), scatter_dimension=0, til...  886 us
    all_gather x1, waiting for transfers between devices, local(): lax.all_gather(held[0], ('heads', 'blk'), axis=0, tiled=True)  202 us
    reduce_scatter x1, waiting for transfers between devices, local(): lax.psum_scatter(qkv_grad_full, ('heads', 'blk'), scatter_dimension=0, ti...  160 us
    all_gather x2, waiting for transfers between devices, local(): lax.all_gather(held[1], ('heads', 'blk'), axis=0, tiled=True)  132 us
    unnamed x3, blocking collectives  128 us
    reduce_scatter x1, waiting for transfers between devices, local(): lax.psum_scatter(out_proj_grad, ('heads', 'blk'), scatter_dimension=0, ti...  115 us
    all_gather x1, waiting for transfers between devices, local(): lax.all_gather(ffn_in_weight, ('heads', 'blk'), axis=0, tiled=True)  109 us
    all_gather x1, waiting for transfers between devices, local(): lax.all_gather(ffn_out_weight, ('heads', 'blk'), axis=0, tiled=True)  92.1 us
  transfers between devices with their start and end apart: 20, of which 15 were waited for; matrix products, arithmetic and copies ran while one was open for 24% of the time, Pallas kernels for 0%

commit v1 on v0

v1 whole, which is shorter than its diff:
```python
import jax
import jax.numpy as jnp
from jax import lax
from jax.sharding import PartitionSpec as P

HEADS = 16
KV_HEADS = 4
DOC_MAX = 2000


EPS = 1e-06
ROPE_BASE = 10000.0
NEG = -1e30


def from_behind(block, axis, distance):
    devices = range(lax.axis_size(axis))
    route = [(i - distance, i) for i in devices if i - distance in devices]
    return lax.ppermute(block, axis, route)


def rms_scale(values, scaling):
    return values * lax.rsqrt(jnp.mean(values * values, axis=-1, keepdims=True) + EPS) * scaling


def norm_back(values, scaling, gradient):
    inverse = lax.rsqrt(jnp.mean(values * values, axis=-1, keepdims=True) + EPS)
    scaled = gradient * scaling
    moment = jnp.mean(scaled * values, axis=-1, keepdims=True)
    return (
        inverse * scaled - values * inverse * inverse * inverse * moment,
        gradient * values * inverse,
    )


def rotation(positions, head_dim):
    half_width = head_dim // 2
    frequency = ROPE_BASE ** (-2.0 * jnp.arange(half_width, dtype=jnp.float32) / head_dim)
    angles = positions.astype(jnp.float32)[:, None] * frequency[None, :]
    return (jnp.cos(angles)[:, None, :], jnp.sin(angles)[:, None, :])


def rotate(values, cosine, sine):
    half_width = values.shape[-1] // 2
    front_half = values[..., :half_width]
    second = values[..., half_width:]
    return jnp.concatenate(
        [front_half * cosine - second * sine, second * cosine + front_half * sine], axis=-1
    )


def peers_exchange(pieces, axis):
    size = lax.axis_size(axis)
    return [pieces[0]] + [
        lax.ppermute(pieces[k], axis, [(i, i ^ k) for i in range(size)]) for k in range(1, size)
    ]


def place(parts, axis, dim):
    own = lax.axis_index(axis)
    extent = parts[0].shape[dim]
    shape = list(parts[0].shape)
    shape[dim] = extent * len(parts)
    whole = jnp.zeros(shape, parts[0].dtype)
    for k, part in enumerate(parts):
        whole = lax.dynamic_update_slice_in_dim(whole, part, (own ^ k) * extent, dim)
    return whole


def gather_peers(block, axis, dim):
    return place(peers_exchange([block] * lax.axis_size(axis), axis), axis, dim)


def slices_for(block, axis, dim):
    own = lax.axis_index(axis)
    size = lax.axis_size(axis)
    extent = block.shape[dim] // size
    return [
        lax.dynamic_slice_in_dim(block, (own ^ k) * extent, extent, dim) for k in range(size)
    ]


def local(
    inputs,
    positions,
    attn_gain,
    qkv_weight,
    q_gain,
    k_gain,
    out_weight,
    ffn_gain,
    ffn_in_weight,
    ffn_out_weight,
    cotangent,
):
    token_count, width = inputs.shape
    depth = qkv_weight.shape[0]
    head_dim = q_gain.shape[0]
    group_size = HEADS // KV_HEADS
    score_scale = head_dim ** (-0.5)
    heads_size = lax.axis_size("heads")
    blk_size = lax.axis_size("blk")
    query_width = HEADS * head_dim // heads_size
    key_width = KV_HEADS * head_dim // heads_size
    own_head = lax.axis_index("heads")
    block_len = token_count * heads_size
    hidden_units = ffn_out_weight.shape[0] * blk_size

    qkv_parts = jnp.concatenate(
        [
            qkv_weight[:, : HEADS * head_dim].reshape(depth, heads_size, query_width),
            qkv_weight[:, HEADS * head_dim : (HEADS + KV_HEADS) * head_dim].reshape(
                depth, heads_size, key_width
            ),
            qkv_weight[:, (HEADS + KV_HEADS) * head_dim :].reshape(depth, heads_size, key_width),
            jnp.broadcast_to(attn_gain[:, None, None], (depth, heads_size, 64)),
            jnp.broadcast_to(ffn_gain[:, None, None], (depth, heads_size, 64)),
        ],
        axis=-1,
    )
    joined_width = qkv_parts.shape[-1]
    qkv_parts = qkv_parts.transpose(1, 0, 2)

    def to_group(parts):
        sent = slices_for(parts, "heads", 0)
        return place(peers_exchange(sent, "heads"), "heads", 0)

    qkv_group = lax.all_gather(to_group(qkv_parts), "blk", axis=1, tiled=True).reshape(
        width, joined_width
    )
    qkv_width = query_width + 2 * key_width
    attn_scaling = qkv_group[:, qkv_width].astype(jnp.float32)
    ffn_scaling = qkv_group[:, qkv_width + 64].astype(jnp.float32)
    qkv_group = qkv_group[:, :qkv_width]
    in_parts = ffn_in_weight.reshape(depth, 2, heads_size, hidden_units).transpose(2, 0, 1, 3)
    in_group = lax.all_gather(
        to_group(in_parts.reshape(heads_size, depth, 2 * hidden_units)), "blk", axis=1, tiled=True
    ).reshape(width, 2 * hidden_units)
    out_group = lax.all_gather(out_weight, "blk", axis=0, tiled=True)
    down_group = lax.all_gather(ffn_out_weight, "blk", axis=0, tiled=True)

    inputs_blk = gather_peers(inputs, "heads", 0)
    hidden_in = inputs_blk.astype(jnp.float32)
    cosine, sine = rotation(positions, head_dim)
    normed = rms_scale(hidden_in, attn_scaling).astype(jnp.bfloat16)
    projected = jnp.dot(normed, qkv_group, preferred_element_type=jnp.float32)
    query_raw = projected[:, :query_width].reshape(block_len, -1, head_dim)
    key_raw = projected[:, query_width : query_width + key_width].reshape(block_len, -1, head_dim)
    value_raw = projected[:, query_width + key_width :].reshape(block_len, -1, head_dim)
    query_scaling = q_gain.astype(jnp.float32)
    key_scaling = k_gain.astype(jnp.float32)
    query_low = rotate(rms_scale(query_raw, query_scaling), cosine, sine).astype(jnp.bfloat16)
    key_low = rotate(rms_scale(key_raw, key_scaling), cosine, sine).astype(jnp.bfloat16)
    pair_blk = jnp.concatenate([key_low, value_raw.astype(jnp.bfloat16)], axis=-1)
    local_groups = pair_blk.shape[1]
    prior_pair = from_behind(pair_blk, "blk", 1)
    pair_all = jnp.concatenate([prior_pair, pair_blk], axis=0)
    query_rows = min(512, block_len)
    window = min(block_len, -(-DOC_MAX // 128) * 128)
    key_span = window + query_rows
    queries = query_low.reshape(block_len, local_groups, group_size, head_dim)
    starts = jnp.arange(block_len // query_rows, dtype=jnp.int32) * query_rows

    def scores_at(row_start):
        query_part = lax.dynamic_slice_in_dim(queries, row_start, query_rows, 0)
        window_start = row_start + block_len - window
        pair_part = lax.dynamic_slice_in_dim(pair_all, window_start, key_span, 0)
        key_part = pair_part[..., :head_dim]
        value_part = pair_part[..., head_dim:]
        position_part = lax.dynamic_slice_in_dim(positions, row_start, query_rows, 0)
        query_index = row_start + block_len + jnp.arange(query_rows, dtype=jnp.int32)
        key_index = window_start + jnp.arange(key_span, dtype=jnp.int32)
        allowed = (key_index[None, :] <= query_index[:, None]) & (
            key_index[None, :] >= (query_index - position_part)[:, None]
        )
        scores = (
            jnp.einsum("qcgd,kcd->cgqk", query_part, key_part, preferred_element_type=jnp.float32)
            * score_scale
        )
        return (query_part, key_part, value_part, window_start, jnp.where(allowed, scores, NEG))

    def attend(row_start):
        query_part, key_part, value_part, window_start, scores = scores_at(row_start)
        top = jnp.max(scores, axis=-1, keepdims=True)
        expo = jnp.exp(scores - top)
        total = jnp.sum(expo, axis=-1, keepdims=True)
        probs = (expo / total).astype(jnp.bfloat16)
        mixed = jnp.einsum("cgqk,kcd->qcgd", probs, value_part, preferred_element_type=jnp.float32)
        return (mixed.astype(jnp.bfloat16), top + jnp.log(total))

    attended, log_sums = lax.map(attend, starts)
    attended_blk = attended.reshape(block_len, query_width)
    attended_all = gather_peers(attended_blk, "heads", 1)
    out_full = gather_peers(out_group, "heads", 0)
    residual = hidden_in + jnp.dot(attended_all, out_full, preferred_element_type=jnp.float32)
    ffn_normed = rms_scale(residual, ffn_scaling).astype(jnp.bfloat16)
    residual_own = lax.dynamic_slice_in_dim(residual, own_head * token_count, token_count, 0)
    attended_own = lax.dynamic_slice_in_dim(attended_all, own_head * token_count, token_count, 0)
    cotangent_blk = gather_peers(cotangent, "heads", 0)

    gate_up = jnp.dot(ffn_normed, in_group, preferred_element_type=jnp.float32)
    gate = gate_up[:, :hidden_units]
    upward = gate_up[:, hidden_units:]
    sigmoid = jax.nn.sigmoid(gate)
    activated = gate * sigmoid
    hidden = (activated * upward).astype(jnp.bfloat16)
    hidden_grad = jnp.dot(cotangent_blk, down_group.T, preferred_element_type=jnp.float32)
    gate_up_grad = jnp.concatenate(
        [
            hidden_grad * upward * sigmoid * (1.0 + gate * (1.0 - sigmoid)),
            hidden_grad * activated,
        ],
        axis=-1,
    ).astype(jnp.bfloat16)

    def sum_peers(block):
        got = peers_exchange(slices_for(block, "heads", 0), "heads")
        return sum(part.astype(jnp.float32) for part in got)

    normed_grad_part = jnp.dot(gate_up_grad, in_group.T, preferred_element_type=jnp.float32)
    ffn_normed_grad = sum_peers(normed_grad_part.astype(jnp.bfloat16))
    output_part = jnp.dot(hidden, down_group, preferred_element_type=jnp.float32)
    layer_out = (residual_own + sum_peers(output_part.astype(jnp.bfloat16))).astype(jnp.bfloat16)
    down_grad = jnp.dot(hidden.T, cotangent_blk, preferred_element_type=jnp.float32)
    ffn_out_grad = lax.psum_scatter(
        down_grad.astype(jnp.bfloat16), "blk", scatter_dimension=0, tiled=True
    ).astype(jnp.float32)
    up_grad = jnp.dot(ffn_normed.T, gate_up_grad, preferred_element_type=jnp.float32)
    up_grad = lax.psum_scatter(
        up_grad.astype(jnp.bfloat16).reshape(heads_size, blk_size * depth, 2 * hidden_units),
        "blk",
        scatter_dimension=1,
        tiled=True,
    )
    ffn_in_grad = place(
        [
            part.reshape(depth, 2, 1, hidden_units)
            for part in peers_exchange(
                [piece[0] for piece in slices_for(up_grad, "heads", 0)], "heads"
            )
        ],
        "heads",
        2,
    ).reshape(depth, 2 * heads_size * hidden_units).astype(jnp.float32)

    residual_norm_grad, ffn_gain_terms = norm_back(residual_own, ffn_scaling, ffn_normed_grad)
    residual_grad = cotangent.astype(jnp.float32) + residual_norm_grad
    branch_grad = residual_grad.astype(jnp.bfloat16)
    out_proj_grad = jnp.dot(attended_own.T, branch_grad, preferred_element_type=jnp.float32)
    out_grad = lax.psum_scatter(
        sum_peers(out_proj_grad.astype(jnp.bfloat16)).astype(jnp.bfloat16),
        "blk",
        scatter_dimension=0,
        tiled=True,
    ).astype(jnp.float32)
    attended_grad = jnp.dot(branch_grad, out_full.T, preferred_element_type=jnp.float32).astype(
        jnp.bfloat16
    )
    attended_grad_blk = place(
        peers_exchange(slices_for(attended_grad, "heads", 1), "heads"), "heads", 0
    ).reshape(block_len, local_groups, group_size, head_dim)

    def attend_back(pair_sum, element):
        row_start, log_sum = element
        query_part, key_part, value_part, window_start, scores = scores_at(row_start)
        probs = jnp.exp(scores - log_sum)
        grad_part = lax.dynamic_slice_in_dim(attended_grad_blk, row_start, query_rows, 0)
        prob_grad = jnp.einsum(
            "qcgd,kcd->cgqk", grad_part, value_part, preferred_element_type=jnp.float32
        )
        inner = jnp.sum(probs * prob_grad, axis=-1, keepdims=True)
        score_grad = (probs * (prob_grad - inner)).astype(jnp.bfloat16)
        query_grad = (
            jnp.einsum("cgqk,kcd->qcgd", score_grad, key_part, preferred_element_type=jnp.float32)
            * score_scale
        )
        key_grad = (
            jnp.einsum("cgqk,qcgd->kcd", score_grad, query_part, preferred_element_type=jnp.float32)
            * score_scale
        )
        value_grad = jnp.einsum(
            "cgqk,qcgd->kcd",
            probs.astype(jnp.bfloat16),
            grad_part,
            preferred_element_type=jnp.float32,
        )
        window_sum = lax.dynamic_slice_in_dim(
            pair_sum, window_start, key_span, 0
        ) + jnp.concatenate([key_grad, value_grad], axis=-1)
        return (lax.dynamic_update_slice_in_dim(pair_sum, window_sum, window_start, 0), query_grad)

    pair_zero = jnp.zeros((2 * block_len, local_groups, 2 * head_dim), jnp.float32)
    pair_sum, query_grads = lax.scan(attend_back, pair_zero, (starts, log_sums))
    returned = from_behind(pair_sum[:block_len], "blk", -1)
    pair_grad_blk = (pair_sum[block_len:] + returned).astype(jnp.bfloat16)
    query_rot_grad = (
        query_grads.reshape(block_len, -1, head_dim).astype(jnp.bfloat16).astype(jnp.float32)
    )
    key_rot_grad = pair_grad_blk[..., :head_dim].astype(jnp.float32)
    value_grad = pair_grad_blk[..., head_dim:]
    query_raw_grad, query_gain_terms = norm_back(
        query_raw, query_scaling, rotate(query_rot_grad, cosine, -sine)
    )
    key_raw_grad, key_gain_terms = norm_back(
        key_raw, key_scaling, rotate(key_rot_grad, cosine, -sine)
    )
    projected_grad = jnp.concatenate(
        [
            query_raw_grad.reshape(block_len, query_width).astype(jnp.bfloat16),
            key_raw_grad.reshape(block_len, key_width).astype(jnp.bfloat16),
            value_grad.reshape(block_len, key_width),
        ],
        axis=-1,
    )
    qkv_grad_part = jnp.dot(normed.T, projected_grad, preferred_element_type=jnp.float32)
    qkv_sum = lax.psum_scatter(
        qkv_grad_part.astype(jnp.bfloat16).reshape(heads_size, blk_size * depth, qkv_width),
        "blk",
        scatter_dimension=1,
        tiled=True,
    )
    qkv_got = place(
        [
            part[:, None, :]
            for part in peers_exchange(
                [piece[0] for piece in slices_for(qkv_sum, "heads", 0)], "heads"
            )
        ],
        "heads",
        1,
    ).astype(jnp.float32)
    qkv_grad = jnp.concatenate(
        [
            qkv_got[:, :, :query_width].reshape(depth, -1),
            qkv_got[:, :, query_width : query_width + key_width].reshape(depth, -1),
            qkv_got[:, :, query_width + key_width :].reshape(depth, -1),
        ],
        axis=-1,
    )
    qkv_all = gather_peers(qkv_group, "heads", 1)
    projected_grad_own = place(
        peers_exchange(slices_for(projected_grad, "heads", 0), "heads"), "heads", 1
    )
    normed_in_grad = jnp.dot(projected_grad_own, qkv_all.T, preferred_element_type=jnp.float32)
    input_norm_grad, attn_gain_terms = norm_back(
        inputs.astype(jnp.float32), attn_scaling, normed_in_grad
    )
    input_grad = residual_grad + input_norm_grad
    gains = lax.psum(
        jnp.concatenate(
            [
                jnp.sum(attn_gain_terms, axis=0),
                jnp.sum(ffn_gain_terms, axis=0),
                jnp.sum(query_gain_terms, axis=(0, 1)),
                jnp.sum(key_gain_terms, axis=(0, 1)),
            ]
        ),
        ("heads", "blk"),
    )
    own_rows = (own_head * blk_size + lax.axis_index("blk")) * depth
    attn_gain_grad = lax.dynamic_slice_in_dim(gains, own_rows, depth, 0)
    ffn_gain_grad = lax.dynamic_slice_in_dim(gains, width + own_rows, depth, 0)
    q_gain_grad = gains[2 * width : 2 * width + head_dim]
    k_gain_grad = gains[2 * width + head_dim :]
    return (
        layer_out,
        input_grad,
        attn_gain_grad,
        qkv_grad,
        q_gain_grad,
        k_gain_grad,
        out_grad,
        ffn_gain_grad,
        ffn_in_grad,
        ffn_out_grad,
    )


def solution(mesh):
    placed = (
        P(("blk", "heads"), None),
        P("blk"),
        P(("heads", "blk")),
        P(("heads", "blk"), None),
        P(),
        P(),
        P(("heads", "blk"), None),
        P(("heads", "blk")),
        P(("heads", "blk"), None),
        P(("heads", "blk"), None),
        P(("blk", "heads"), None),
    )
    return jax.shard_map(
        local,
        mesh=mesh,
        in_specs=placed,
        out_specs=(
            P(("blk", "heads"), None),
            P(("blk", "heads"), None),
            P(("heads", "blk")),
            P(("heads", "blk"), None),
            P(),
            P(),
            P(("heads", "blk"), None),
            P(("heads", "blk")),
            P(("heads", "blk"), None),
            P(("heads", "blk"), None),
        ),
        check_vma=False,
    )
```

time: 2760 us -> 1390 us (0.50)
  waiting for transfers between devices: 1820 us -> 400 us
  local copies, waits for them, and re-layouts: 123 us -> 191 us
  other arithmetic: 179 us -> 144 us
  starting transfers between devices: 25.6 us -> 53.2 us
    reduce_scatter x4, waiting for transfers between devices: 1160 us -> 0.03 us  [the longest x1 0.02 us: local(): lax.psum_scatter(up_grad.astype(jnp.bfloat16).reshape(heads_size, blk_siz...]
    all_gather x8 -> x4, waiting for transfers between devices: 600 us -> 0.05 us  [the longest x1 0.02 us: local(): lax.all_gather(to_group(in_parts.reshape(heads_size, depth, 2 * hidden_un...]
    ppermute x0 -> x42, waiting for transfers between devices: none -> 391 us  [peers_exchange(): lax.ppermute(pieces[k], axis, [(i, i ^ k) for i in range(size)])]
    unnamed x3 -> x0, blocking collectives: 128 us -> none
    psum x0 -> x1, blocking collectives: none -> 116 us  [local(): lax.psum(jnp.concatenate([jnp.sum(attn_gain_terms, axis=0), jnp.sum(ffn_g...]
    dynamic_update_slice x0 -> x41, local copies, waits for them, and re-layouts: none -> 70 us  [place(): lax.dynamic_update_slice_in_dim(whole, part, (own ^ k) * extent, dim)]
    all_to_all x6 -> x0, waiting for transfers between devices: 57.3 us -> none  [the longest x1 14 us: local(): lax.all_to_all(query_low.reshape(token_count, KV_HEADS, group_size * head...]
    ppermute x0 -> x42, starting transfers between devices: none -> 48.9 us  [peers_exchange(): lax.ppermute(pieces[k], axis, [(i, i ^ k) for i in range(size)])]
  transfers between devices with their start and end apart: 20 -> 52, of which waited for: 15 -> 27; matrix products, arithmetic and copies ran while one was open for 24% -> 27% of each run, Pallas kernels for 0% -> 0%
where the time goes in v1:
time: 1390 us; the launch traced here: 1380 us
  matrix products  438 us (32%)
  waiting for transfers between devices  400 us (29%)
  local copies, waits for them, and re-layouts  191 us (14%)
  other arithmetic  144 us (10%)
  blocking collectives  116 us (8%)
  starting transfers between devices  53.2 us (4%)
  loops' own time  26.9 us (2%)
  between operations  16 us (1%)
    ppermute x42, waiting for transfers between devices, peers_exchange(): lax.ppermute(pieces[k], axis, [(i, i ^ k) for i in range(size)])  391 us
    psum x1, blocking collectives, local(): lax.psum(jnp.concatenate([jnp.sum(attn_gain_terms, axis=0), jnp.sum(ffn_g...  116 us
    dynamic_update_slice x41, local copies, waits for them, and re-layouts, place(): lax.dynamic_update_slice_in_dim(whole, part, (own ^ k) * extent, dim)  70 us
    dot_general x8, matrix products, scores_at(): jnp.einsum('qcgd,kcd->cgqk', query_part, key_part, preferred_element_type...  60.1 us
    dot_general x4, matrix products, attend_back(): jnp.einsum('qcgd,kcd->cgqk', grad_part, value_part, preferred_element_typ...  59.9 us
    another operation x5, other arithmetic  59.4 us
    ppermute x42, starting transfers between devices, peers_exchange(): lax.ppermute(pieces[k], axis, [(i, i ^ k) for i in range(size)])  48.9 us
    dot_general x4, matrix products, attend(): jnp.einsum('cgqk,kcd->qcgd', probs, value_part, preferred_element_type=jn...  44.3 us
  transfers between devices with their start and end apart: 52, of which 27 were waited for; matrix products, arithmetic and copies ran while one was open for 27% of the time, Pallas kernels for 0%

profile of v1, /device:TPU:0, one launch (start us, length us, event | category | flops | bytes accessed | tf_op | source)
XLA Modules:
  0.0 1384.9 jit_solution(15931319596818193328)
XLA Ops:
  71.6 25.0 %collective-permute-done = bf16[512,2048]{0,1:T(8,128)(2,1)} collective-permute-done((bf16[512,2048]{0,1:T(8,128)(2,1)S(1)}, bf16[512,2048]{0,1:T(8,128)(2,1)}, u32[]{:S(2)}, u32[]{:S(2)}) %collective-permute-start) | collective-permute-done | bytes 2097184 | tf_op jit(solution)/shard_map/ppermute | solution.py:55
  101.3 41.3 %collective-permute-done.1 = bf16[512,2048]{0,1:T(8,128)(2,1)} collective-permute-done((bf16[512,2048]{0,1:T(8,128)(2,1)S(1)}, bf16[512,2048]{0,1:T(8,128)(2,1)}, u32[]{:S(2)}, u32[]{:S(2)}) %collective-permute-start.1) | collective-permute-done | bytes 2097184 | tf_op jit(solution)/shard_map/ppermute | solution.py:55
  156.6 29.9 %collective-permute-done.19 = bf16[512,2048]{0,1:T(8,128)(2,1)} collective-permute-done((bf16[512,2048]{0,1:T(8,128)(2,1)}, bf16[512,2048]{0,1:T(8,128)(2,1)}, u32[]{:S(2)}, u32[]{:S(2)}) %collective-permute-start.19) | collective-permute-done | bytes 2097184 | tf_op jit(solution)/shard_map/ppermute | solution.py:55
  191.2 41.4 %collective-permute-done.20 = bf16[512,2048]{0,1:T(8,128)(2,1)} collective-permute-done((bf16[512,2048]{0,1:T(8,128)(2,1)}, bf16[512,2048]{0,1:T(8,128)(2,1)}, u32[]{:S(2)}, u32[]{:S(2)}) %collective-permute-start.20) | collective-permute-done | bytes 2097184 | tf_op jit(solution)/shard_map/ppermute | solution.py:55
  251.1 114.2 %while.32 = (s32[]{:T(128)}, bf16[4,512,1,4,64]{1,4,3,2,0:T(8,128)(2,1)}, f32[4,1,4,512,1]{3,2,4,1,0:T(4,128)}, s32[4]{0:T(128)S(1)}, bf16[4096,1,128]{0,2,1:T(8...) while((s32[]{:T(128)}, ...), condition=%wide.region_6.7_spmd, body=%wide.region_3.6_spmd.sunk | while | flops 1409156608 | bytes 153320720 | solution.py:191
  396.9 14.7 %collective-permute-done.9 = bf16[2048,256]{0,1:T(8,128)(2,1)S(1)} collective-permute-done((bf16[2048,256]{0,1:T(8,128)(2,1)S(1)}, bf16[2048,256]{0,1:T(8,128)(2,1)S(1)}, u32[]{:S(2)}, u32[]{:S(2)}) %collective-permute-start.9) | collective-permute-done | bytes 1048608 | tf_op jit(solution)/shard_map/ppermute | solution.py:55
  425.7 30.9 %fusion.103 = f32[2048,2560]{1,0:T(8,128)} fusion(bf16[2048,2560]{1,0:T(8,128)(2,1)} %bitcast.339, f32[2048,2048]{0,1:T(8,128)} %get-tuple-element.510, f32[2048]{0:T(1024)S(1)} %copy-done.35, f32[2048]{0:T(1024)S(1)} %add_rsqrt_fusion.1), kind=kOutput, calls=%fused_computation.258 | convolution fusion | flops 21487419392 | bytes 48250880 | tf_op jit(solution)/shard_map/dot_general | solution.py:201
  456.6 23.8 %multiply_convert_fusion.2 = (bf16[2048,1280]{1,0:T(8,128)(2,1)}, bf16[2048,1280]{1,0:T(8,128)(2,1)}, bf16[2048,1280]{1,0:T(8,128)(2,1)}) fusion(f32[2048,2560]{1,0:T(8,128)} %fusion.103, bf16[2048,2048]{0,1:T(8,128)(2,1)} %constant_dynamic-update-slice_fusion.10, bf16[1280,2048]{1,0:T(8,128)(2,1)} %all-gather.11.cloned.1.call-done), kind=kOutput, calls=%fused_computation.80 | convolution fusion | flops 10776739840 | bytes 50331648 | tf_op jit(solution)/shard_map/dot_general | solution.py:207
  480.3 27.6 %convolution_convert_fusion.3 = bf16[2048,2048]{0,1:T(8,128)(2,1)S(1)} fusion(bf16[2048,2560]{1,0:T(8,128)(2,1)} %bitcast.340, bf16[2048,1280]{1,0:T(8,128)(2,1)} %get-tuple-element.445, bf16[2048,1280]{1,0:T(8,128)(2,1)} %get-tuple-element.444), kind=kOutput, calls=%fused_computation.86 | convolution fusion | flops 21500002304 | bytes 29360128 | tf_op jit(solution)/shard_map/dot_general | solution.py:220
  514.6 16.7 %convolution_convert_fusion.1 = bf16[2048,2048]{0,1:T(8,128)(2,1)} fusion(bf16[2048,1280]{1,0:T(8,128)(2,1)} %get-tuple-element.446, bf16[1280,2048]{1,0:T(8,128)(2,1)} %all-gather.11.cloned.1.call-done), kind=kOutput, calls=%fused_computation.84 | convolution fusion | flops 10741612544 | bytes 18874368 | tf_op jit(solution)/shard_map/dot_general | solution.py:222
  554.5 41.8 %collective-permute-done.24 = bf16[512,2048]{0,1:T(8,128)(2,1)} collective-permute-done((bf16[512,2048]{0,1:T(8,128)(2,1)}, bf16[512,2048]{0,1:T(8,128)(2,1)}, u32[]{:S(2)}, u32[]{:S(2)}) %collective-permute-start.24) | collective-permute-done | bytes 2097184 | tf_op jit(solution)/shard_map/ppermute | solution.py:55
  600.7 40.5 %collective-permute-done.16 = bf16[512,2048]{0,1:T(8,128)(2,1)S(1)} collective-permute-done((bf16[512,2048]{0,1:T(8,128)(2,1)}, bf16[512,2048]{0,1:T(8,128)(2,1)S(1)}, u32[]{:S(2)}, u32[]{:S(2)}) %collective-permute-start.16) | collective-permute-done | bytes 2097184 | tf_op jit(solution)/shard_map/ppermute | solution.py:55
  644.2 42.0 %collective-permute-done.18 = bf16[512,2048]{0,1:T(8,128)(2,1)} collective-permute-done((bf16[512,2048]{0,1:T(8,128)(2,1)S(1)}, bf16[512,2048]{0,1:T(8,128)(2,1)}, u32[]{:S(2)}, u32[]{:S(2)}) %collective-permute-start.18) | collective-permute-done | bytes 2097184 | tf_op jit(solution)/shard_map/ppermute | solution.py:55
  706.9 309.0 %while.33 = (s32[]{:T(128)}, f32[4096,1,128]{0,2,1:T(8,128)S(1)}, bf16[4,512,1,4,64]{1,4,3,2,0:T(8,128)(2,1)}, s32[4]{0:T(128)S(1)}, bf16[2048,1,4,64]{0,3,2,1:T...) while((s32[]{:T(128)}, f32[4096,1,128]{0,2,1:T(8,128)S(1)}, ...), condition=%wide.region_13.14_spmd, body=%wide.region_11.13_spmd.sunk | while | flops 3438970368 | bytes 223370080 | solution.py:293
  726.0 15.0 %fusion.151 = (f32[4,512]{1,0:T(4,128)S(1)}, f32[2560,512,4]{1,0,2:T(8,128)}) fusion(f32[2560,512,4]{1,0,2:T(8,128)} %fusion.149, f32[4,512]{1,0:T(4,128)S(1)} %dynamic-slice_bitcast_fusion.25, pred[512,2560]{0,1:T(8,128)(4,1)S(1)} %compare_and_fusion.5, bf16[2048,1,4,64]{0,3,2,1:T(8,128)(2,1)} %copy-done.11, s32[]{:T(128)S(6)} %select_n.251, ...), kind=kOutput, calls=%fused_computation.29.clone.1 | convolution fusion | flops 697300992 | bytes 43859980 | tf_op jit(solution)/shard_map/while/body/eval_jaxpr/qcgd,kcd->cgqk/dot_general | solution.py:268
  740.9 14.6 %fusion.152 = bf16[4,512,2560]{1,2,0:T(8,128)(2,1)S(1)} fusion(f32[2560,512,4]{1,0,2:T(8,128)} %get-tuple-element.624, f32[2560,512,4]{1,0,2:T(8,128)} %fusion.149, f32[4,512]{1,0:T(4,128)S(1)} %get-tuple-element.625, f32[4,512]{1,0:T(4,128)S(1)} %dynamic-slice_bitcast_fusion.25, pred[512,2560]{0,1:T(8,128)(4,1)S(1)} %compare_and_fusion.5), kind=kLoop, calls=%fused_computation.34.clone.1 | loop fusion | flops 31457280 | bytes 53755904 | tf_op jit(solution)/shard_map/reshape.554
  804.3 15.0 %fusion.151 = (f32[4,512]{1,0:T(4,128)S(1)}, f32[2560,512,4]{1,0,2:T(8,128)}) fusion(f32[2560,512,4]{1,0,2:T(8,128)} %fusion.149, f32[4,512]{1,0:T(4,128)S(1)} %dynamic-slice_bitcast_fusion.25, pred[512,2560]{0,1:T(8,128)(4,1)S(1)} %compare_and_fusion.5, bf16[2048,1,4,64]{0,3,2,1:T(8,128)(2,1)} %copy-done.11, s32[]{:T(128)S(6)} %select_n.251, ...), kind=kOutput, calls=%fused_computation.29.clone.1 | convolution fusion | flops 697300992 | bytes 43859980 | tf_op jit(solution)/shard_map/while/body/eval_jaxpr/qcgd,kcd->cgqk/dot_general | solution.py:268
  881.9 15.0 %fusion.151 = (f32[4,512]{1,0:T(4,128)S(1)}, f32[2560,512,4]{1,0,2:T(8,128)}) fusion(f32[2560,512,4]{1,0,2:T(8,128)} %fusion.149, f32[4,512]{1,0:T(4,128)S(1)} %dynamic-slice_bitcast_fusion.25, pred[512,2560]{0,1:T(8,128)(4,1)S(1)} %compare_and_fusion.5, bf16[2048,1,4,64]{0,3,2,1:T(8,128)(2,1)} %copy-done.11, s32[]{:T(128)S(6)} %select_n.251, ...), kind=kOutput, calls=%fused_computation.29.clone.1 | convolution fusion | flops 697300992 | bytes 43859980 | tf_op jit(solution)/shard_map/while/body/eval_jaxpr/qcgd,kcd->cgqk/dot_general | solution.py:268
  958.7 15.0 %fusion.151 = (f32[4,512]{1,0:T(4,128)S(1)}, f32[2560,512,4]{1,0,2:T(8,128)}) fusion(f32[2560,512,4]{1,0,2:T(8,128)} %fusion.149, f32[4,512]{1,0:T(4,128)S(1)} %dynamic-slice_bitcast_fusion.25, pred[512,2560]{0,1:T(8,128)(4,1)S(1)} %compare_and_fusion.5, bf16[2048,1,4,64]{0,3,2,1:T(8,128)(2,1)} %copy-done.11, s32[]{:T(128)S(6)} %select_n.251, ...), kind=kOutput, calls=%fused_computation.29.clone.1 | convolution fusion | flops 697300992 | bytes 43859980 | tf_op jit(solution)/shard_map/while/body/eval_jaxpr/qcgd,kcd->cgqk/dot_general | solution.py:268
  973.6 14.6 %fusion.152 = bf16[4,512,2560]{1,2,0:T(8,128)(2,1)S(1)} fusion(f32[2560,512,4]{1,0,2:T(8,128)} %get-tuple-element.624, f32[2560,512,4]{1,0,2:T(8,128)} %fusion.149, f32[4,512]{1,0:T(4,128)S(1)} %get-tuple-element.625, f32[4,512]{1,0:T(4,128)S(1)} %dynamic-slice_bitcast_fusion.25, pred[512,2560]{0,1:T(8,128)(4,1)S(1)} %compare_and_fusion.5), kind=kLoop, calls=%fused_computation.34.clone.1 | loop fusion | flops 31457280 | bytes 53755904 | tf_op jit(solution)/shard_map/reshape.554
  1078.0 29.8 %convolution_convert_fusion = bf16[2048,2560]{1,0:T(8,128)(2,1)} fusion(bf16[2048,1280]{1,0:T(8,128)(2,1)} %get-tuple-element.445, bf16[2048,1280]{1,0:T(8,128)(2,1)} %get-tuple-element.444, f32[2048,2048]{0,1:T(8,128)} %get-tuple-element.510, f32[2048]{0:T(1024)S(1)} %copy-done.36, f32[2048]{0:T(1024)S(1)} %copy-done.43), kind=kOutput, calls=%fused_computation.77 | convolution fusion | flops 21513633792 | bytes 37765120 | tf_op jit(solution)/shard_map/dot_general | solution.py:228
  1108.2 16.7 %convolution_convert_fusion.2 = bf16[1280,2048]{1,0:T(8,128)(2,1)} fusion(bf16[2048,1280]{1,0:T(8,128)(2,1)} %get-tuple-element.446, bf16[2048,2048]{0,1:T(8,128)(2,1)} %constant_dynamic-update-slice_fusion.10), kind=kOutput, calls=%fused_computation.85 | convolution fusion | flops 10740039680 | bytes 18874368 | tf_op jit(solution)/shard_map/dot_general | solution.py:224
  1135.6 16.7 %collective-permute-done.32 = bf16[2048,384]{1,0:T(8,128)(2,1)} collective-permute-done((bf16[2048,384]{1,0:T(8,128)(2,1)}, bf16[2048,384]{1,0:T(8,128)(2,1)}, u32[]{:S(2)}, u32[]{:S(2)}) %collective-permute-start.32) | collective-permute-done | bytes 1572896 | tf_op jit(solution)/shard_map/ppermute | solution.py:55
  1205.0 116.3 %psum.7 = f32[4224]{0:T(1024)S(1)} all-reduce(f32[4224]{0:T(1024)S(1)} %concatenate.84), channel_id=1, replica_groups=mesh['heads'=4,'blk'=8] {'heads','blk'}, use_global_device_ids=true, to_apply=%region_22.23 | all-reduce | flops 4224 | bytes 33792 | tf_op jit(solution)/shard_map/psum | solution.py:349
  (493 shorter events, 698.1 us)
Async XLA Ops:
  7.2 62.5 %all-gather.7.cloned.1.call-start = ((), (), s32[]{:S(2)}) async-start(), calls=%async_computation.5 | async-start | bytes 1179648 | tf_op jit(solution)/shard_map/all_gather | solution.py:139
  7.9 227.8 %all-gather.5.cloned.1.call-start = ((), (), s32[]{:S(2)}) async-start(), calls=%async_computation.4 | async-start | bytes 2359296 | tf_op jit(solution)/shard_map/all_gather | solution.py:128
  24.5 401.1 %all-gather.9.cloned.1.call-start = ((), (), s32[]{:S(2)}) async-start(), calls=%async_computation.6 | async-start | bytes 11796480 | tf_op jit(solution)/shard_map/all_gather | solution.py:136
  44.9 411.7 %all-gather.11.cloned.1.call-start = ((), (), s32[]{:S(2)}) async-start(), calls=%async_computation.7 | async-start | bytes 5898240 | tf_op jit(solution)/shard_map/all_gather | solution.py:140
  47.8 48.7 %collective-permute-start = (bf16[512,2048]{0,1:T(8,128)(2,1)S(1)}, bf16[512,2048]{0,1:T(8,128)(2,1)}, u32[]{:S(2)}, u32[]{:S(2)}) collective-permute-start(bf16[512,2048]{0,1:T(8,128)(2,1)S(1)} %copy.206), channel_id=1, source_target_pairs={{0,8},{8,0},{16,24},{24,16},{1,9},{9,1},{17,25},{25,17},{2,10},{10... | collective-permute-start | bytes 6291464 | tf_op jit(solution)/shard_map/ppermute | solution.py:55
  49.1 93.6 %collective-permute-start.1 = (bf16[512,2048]{0,1:T(8,128)(2,1)S(1)}, bf16[512,2048]{0,1:T(8,128)(2,1)}, u32[]{:S(2)}, u32[]{:S(2)}) collective-permute-start(bf16[512,2048]{0,1:T(8,128)(2,1)S(1)} %copy.206), channel_id=1, source_target_pairs={{0,16},{8,24},{16,0},{24,8},{1,17},{9,25},{17,1},{25,9},{2,18},{10... | collective-permute-start | bytes 6291464 | tf_op jit(solution)/shard_map/ppermute | solution.py:55
  50.1 96.6 %collective-permute-start.2 = (bf16[512,2048]{0,1:T(8,128)(2,1)S(1)}, bf16[512,2048]{0,1:T(8,128)(2,1)}, u32[]{:S(2)}, u32[]{:S(2)}) collective-permute-start(bf16[512,2048]{0,1:T(8,128)(2,1)S(1)} %copy.206), channel_id=1, source_target_pairs={{0,24},{8,16},{16,8},{24,0},{1,25},{9,17},{17,9},{25,1},{2,26},{10... | collective-permute-start | bytes 6291464 | tf_op jit(solution)/shard_map/ppermute | solution.py:55
  55.3 131.2 %collective-permute-start.19 = (bf16[512,2048]{0,1:T(8,128)(2,1)}, bf16[512,2048]{0,1:T(8,128)(2,1)}, u32[]{:S(2)}, u32[]{:S(2)}) collective-permute-start(bf16[512,2048]{0,1:T(8,128)(2,1)} %copy.218), channel_id=1, source_target_pairs={{0,8},{8,0},{16,24},{24,16},{1,9},{9,1},{17,25},{25,17},{2,10},{10... | collective-permute-start | bytes 6291464 | tf_op jit(solution)/shard_map/ppermute | solution.py:55
  56.5 176.1 %collective-permute-start.20 = (bf16[512,2048]{0,1:T(8,128)(2,1)}, bf16[512,2048]{0,1:T(8,128)(2,1)}, u32[]{:S(2)}, u32[]{:S(2)}) collective-permute-start(bf16[512,2048]{0,1:T(8,128)(2,1)} %copy.218), channel_id=1, source_target_pairs={{0,16},{8,24},{16,0},{24,8},{1,17},{9,25},{17,1},{25,9},{2,18},{10... | collective-permute-start | bytes 6291464 | tf_op jit(solution)/shard_map/ppermute | solution.py:55
  57.5 1269.3 %reduce-scatter.5.cloned.1.call-start = ((), (), s32[]{:S(2)}) async-start(), calls=%async_computation.8 | async-start | bytes 1769472 | tf_op jit(solution)/shard_map/reduce_scatter | solution.py:316
  96.5 272.8 %collective-permute-start.21 = (bf16[512,2048]{0,1:T(8,128)(2,1)}, bf16[512,2048]{0,1:T(8,128)(2,1)}, u32[]{:S(2)}, u32[]{:S(2)}) collective-permute-start(bf16[512,2048]{0,1:T(8,128)(2,1)} %copy.218), channel_id=1, source_target_pairs={{0,24},{8,16},{16,8},{24,0},{1,25},{9,17},{17,9},{25,1},{2,26},{10... | collective-permute-start | bytes 6291464 | tf_op jit(solution)/shard_map/ppermute | solution.py:55
  142.7 231.3 %collective-permute-start.10 = (bf16[256,2048]{1,0:T(8,128)(2,1)}, bf16[256,2048]{1,0:T(8,128)(2,1)}, u32[]{:S(2)}, u32[]{:S(2)}) collective-permute-start(bf16[256,2048]{1,0:T(8,128)(2,1)} %all-gather.7.cloned.1.call-done), channel_id=1, source_target_pairs={{0,8},{8,0},{16,24},{24,16},{1,9},{9,1},{17,25},{25,17},{2,10},{10... | collective-permute-start | bytes 3145736 | tf_op jit(solution)/shard_map/ppermute | solution.py:55
  146.7 230.0 %collective-permute-start.11 = (bf16[256,2048]{1,0:T(8,128)(2,1)}, bf16[256,2048]{1,0:T(8,128)(2,1)}, u32[]{:S(2)}, u32[]{:S(2)}) collective-permute-start(bf16[256,2048]{1,0:T(8,128)(2,1)} %all-gather.7.cloned.1.call-done), channel_id=1, source_target_pairs={{0,16},{8,24},{16,0},{24,8},{1,17},{9,25},{17,1},{25,9},{2,18},{10... | collective-permute-start | bytes 3145736 | tf_op jit(solution)/shard_map/ppermute | solution.py:55
  186.5 191.6 %collective-permute-start.12 = (bf16[256,2048]{1,0:T(8,128)(2,1)}, bf16[256,2048]{1,0:T(8,128)(2,1)}, u32[]{:S(2)}, u32[]{:S(2)}) collective-permute-start(bf16[256,2048]{1,0:T(8,128)(2,1)} %all-gather.7.cloned.1.call-done), channel_id=1, source_target_pairs={{0,24},{8,16},{16,8},{24,0},{1,25},{9,17},{17,9},{25,1},{2,26},{10... | collective-permute-start | bytes 3145736 | tf_op jit(solution)/shard_map/ppermute | solution.py:55
  511.1 40.2 %collective-permute-start.22 = (bf16[512,2048]{0,1:T(8,128)(2,1)}, bf16[512,2048]{0,1:T(8,128)(2,1)S(1)}, u32[]{:S(2)}, u32[]{:S(2)}) collective-permute-start(bf16[512,2048]{0,1:T(8,128)(2,1)} %get-tuple-element.449), channel_id=1, source_target_pairs={{0,8},{8,0},{16,24},{24,16},{1,9},{9,1},{17,25},{25,17},{2,10},{10... | collective-permute-start | bytes 6291464 | tf_op jit(solution)/shard_map/ppermute | solution.py:55
  512.2 42.3 %collective-permute-start.23 = (bf16[512,2048]{0,1:T(8,128)(2,1)}, bf16[512,2048]{0,1:T(8,128)(2,1)S(1)}, u32[]{:S(2)}, u32[]{:S(2)}) collective-permute-start(bf16[512,2048]{0,1:T(8,128)(2,1)} %get-tuple-element.451), channel_id=1, source_target_pairs={{0,16},{8,24},{16,0},{24,8},{1,17},{9,25},{17,1},{25,9},{2,18},{10... | collective-permute-start | bytes 6291464 | tf_op jit(solution)/shard_map/ppermute | solution.py:55
  512.9 83.4 %collective-permute-start.24 = (bf16[512,2048]{0,1:T(8,128)(2,1)}, bf16[512,2048]{0,1:T(8,128)(2,1)}, u32[]{:S(2)}, u32[]{:S(2)}) collective-permute-start(bf16[512,2048]{0,1:T(8,128)(2,1)} %get-tuple-element.450), channel_id=1, source_target_pairs={{0,24},{8,16},{16,8},{24,0},{1,25},{9,17},{17,9},{25,1},{2,26},{10... | collective-permute-start | bytes 6291464 | tf_op jit(solution)/shard_map/ppermute | solution.py:55
  535.9 105.3 %collective-permute-start.16 = (bf16[512,2048]{0,1:T(8,128)(2,1)}, bf16[512,2048]{0,1:T(8,128)(2,1)S(1)}, u32[]{:S(2)}, u32[]{:S(2)}) collective-permute-start(bf16[512,2048]{0,1:T(8,128)(2,1)} %get-tuple-element.452), channel_id=1, source_target_pairs={{0,8},{8,0},{16,24},{24,16},{1,9},{9,1},{17,25},{25,17},{2,10},{10... | collective-permute-start | bytes 6291464 | tf_op jit(solution)/shard_map/ppermute | solution.py:55
  537.0 107.1 %collective-permute-start.17 = (bf16[512,2048]{0,1:T(8,128)(2,1)S(1)}, bf16[512,2048]{0,1:T(8,128)(2,1)S(1)}, u32[]{:S(2)}, u32[]{:S(2)}) collective-permute-start(bf16[512,2048]{0,1:T(8,128)(2,1)S(1)} %get-tuple-element.454), channel_id=1, source_target_pairs={{0,16},{8,24},{16,0},{24,8},{1,17},{9,25},{17,1},{25,9},{2,18},{10... | collective-permute-start | bytes 6291464 | tf_op jit(solution)/shard_map/ppermute | solution.py:55
  551.3 134.9 %collective-permute-start.18 = (bf16[512,2048]{0,1:T(8,128)(2,1)S(1)}, bf16[512,2048]{0,1:T(8,128)(2,1)}, u32[]{:S(2)}, u32[]{:S(2)}) collective-permute-start(bf16[512,2048]{0,1:T(8,128)(2,1)S(1)} %get-tuple-element.453), channel_id=1, source_target_pairs={{0,24},{8,16},{16,8},{24,0},{1,25},{9,17},{17,9},{25,1},{2,26},{10... | collective-permute-start | bytes 6291464 | tf_op jit(solution)/shard_map/ppermute | solution.py:55
  1043.7 293.9 %reduce-scatter.7.cloned.1.call-start = ((), (), s32[]{:S(2)}) async-start(), calls=%async_computation.9 | async-start | bytes 1179648 | tf_op jit(solution)/shard_map/reduce_scatter | solution.py:250
  1077.9 267.9 %reduce-scatter.9.cloned.1.call-start = ((), (), s32[]{:S(2)}) async-start(), calls=%async_computation.10 | async-start | bytes 11796480 | tf_op jit(solution)/shard_map/reduce_scatter | solution.py:229
  1107.8 244.3 %reduce-scatter.11.cloned.1.call-start = ((), (), s32[]{:S(2)}) async-start(), calls=%async_computation.11 | async-start | bytes 5898240 | tf_op jit(solution)/shard_map/reduce_scatter | solution.py:225
  1133.0 43.9 %collective-permute-start.34 = (bf16[2048,384]{1,0:T(8,128)(2,1)}, bf16[2048,384]{1,0:T(8,128)(2,1)}, u32[]{:S(2)}, u32[]{:S(2)}) collective-permute-start(bf16[2048,384]{1,0:T(8,128)(2,1)} %get-tuple-element.466), channel_id=1, source_target_pairs={{0,24},{8,16},{16,8},{24,0},{1,25},{9,17},{17,9},{25,1},{2,26},{10... | collective-permute-start | bytes 4718600 | tf_op jit(solution)/shard_map/ppermute | solution.py:55
  (100 other events, 2299.6 us)
Sparse Core Ops, SparseCore 0:
  9.6 24.7 all-gather.6
  36.6 28.7 all-gather.4
  67.6 98.8 all-gather.8
  168.0 54.3 all-gather.10
  1043.8 58.9 reduce-scatter.4
  1104.9 51.1 reduce-scatter.6
  1158.4 107.8 reduce-scatter.8
  1268.6 59.2 reduce-scatter.10

commit v2 on v0

v2 whole, which is shorter than its diff:
```python
import functools

import jax
import jax.numpy as jnp
from jax import lax
from jax.experimental import pallas as pl
from jax.experimental.pallas import tpu as pltpu
from jax.sharding import PartitionSpec as P

HEADS = 16
KV_HEADS = 4


EPS = 1e-06
ROPE_BASE = 10000.0
NEG = -1e30
MESH = pl.DeviceIdType.MESH
ROWS_IN_BOTH = (((1,), (1,)), ((), ()))


def from_behind(block, axis, distance):
    devices = range(lax.axis_size(axis))
    route = [(i - distance, i) for i in devices if i - distance in devices]
    return lax.ppermute(block, axis, route)


def rotation(positions, head_dim):
    half_width = head_dim // 2
    frequency = ROPE_BASE ** (-2.0 * jnp.arange(half_width, dtype=jnp.float32) / head_dim)
    angles = positions.astype(jnp.float32)[:, None] * frequency[None, :]
    return (jnp.cos(angles)[:, None, :], jnp.sin(angles)[:, None, :])


def stack_heads(tile, heads, first):
    turned = tile.T
    dim = turned.shape[0] // heads
    wide = jnp.concatenate([turned[h * dim : (h + 1) * dim] for h in range(heads)], axis=1)
    zero = jnp.zeros_like(wide)
    return jnp.concatenate([wide, zero] if first else [zero, wide], axis=0)


def unstack_heads(wide, heads):
    count = wide.shape[1] // heads
    return jnp.concatenate([wide[:, h * count : (h + 1) * count] for h in range(heads)], axis=0).T


def scores_at(pair, query_ext, low, first_query, key_start, heads):
    scores = jnp.dot(pair, query_ext, preferred_element_type=jnp.float32)
    rows, columns = scores.shape
    shape = (rows, columns // heads)
    key = key_start + lax.broadcasted_iota(jnp.int32, shape, 0)
    query = first_query + lax.broadcasted_iota(jnp.int32, shape, 1)
    bias = jnp.where((key <= query) & (key >= low), 0.0, NEG)
    return scores + jnp.concatenate([bias] * heads, axis=1)


def transpose_into(pair_ref, turned_ref):
    for start in range(0, pair_ref.shape[0], 512):
        turned_ref[:, start : start + 512] = pair_ref[start : start + 512, :].T


def attend_kernel(
    heads, key_rows, scale, first_ref, query_ref, low_ref, pair_ref, out_ref, log_ref, turned_ref,
    mixed_ref, total_ref
):
    step = pl.program_id(0)
    query_rows = query_ref.shape[0]

    @pl.when(step == 0)
    def _():
        transpose_into(pair_ref, turned_ref)

    query_ext = stack_heads(query_ref[...] * jnp.bfloat16(scale), heads, True)
    low = low_ref[...]
    base = pair_ref.shape[0] // 2 + step * query_rows
    mixed_ref[...] = jnp.zeros_like(mixed_ref)
    total_ref[...] = jnp.zeros_like(total_ref)

    def tile(index, carried):
        start = pl.multiple_of(index * key_rows, key_rows)
        expo = jnp.exp(
            scores_at(pair_ref[pl.ds(start, key_rows), :], query_ext, low, base, start, heads)
        )
        total_ref[...] += jnp.sum(expo, axis=0, keepdims=True)
        mixed_ref[...] += jnp.dot(
            turned_ref[:, pl.ds(start, key_rows)],
            expo.astype(jnp.bfloat16),
            preferred_element_type=jnp.float32,
        )
        return carried

    lax.fori_loop(first_ref[step], (base + query_rows - 1) // key_rows + 1, tile, 0)
    total = total_ref[...]
    dim = pair_ref.shape[1] // 2
    out_ref[...] = unstack_heads(mixed_ref[dim:] / total, heads).astype(out_ref.dtype)
    log_ref[...] = jnp.log(total)[None]


def attend_back_kernel(
    heads, key_rows, scale, first_ref, query_ref, low_ref, pair_ref, out_ref, log_ref, *refs
):
    *grad_refs, query_grad_ref, pair_grad_ref, turned_ref, sum_ref = refs
    step = pl.program_id(0)
    peer = first_ref[pl.num_programs(0)] ^ step
    grad = grad_refs[0][...]
    for k in range(1, len(grad_refs)):
        grad = jnp.where(peer == k, grad_refs[k][...], grad)
    query_rows = query_ref.shape[0]
    dim = pair_ref.shape[1] // 2

    @pl.when(step == 0)
    def _():
        pair_grad_ref[...] = jnp.zeros_like(pair_grad_ref)
        transpose_into(pair_ref, turned_ref)

    query_ext = stack_heads(query_ref[...] * jnp.bfloat16(scale), heads, True)
    grad_ext = stack_heads(grad, heads, False)
    out_ext = stack_heads(out_ref[...], heads, False)
    inner = jnp.sum(
        grad_ext.astype(jnp.float32) * out_ext.astype(jnp.float32), axis=0, keepdims=True
    )
    log_sum = log_ref[0]
    low = low_ref[...]
    base = pair_ref.shape[0] // 2 + step * query_rows
    sum_ref[...] = jnp.zeros_like(sum_ref)

    def tile(index, carried):
        start = pl.multiple_of(index * key_rows, key_rows)
        pair = pair_ref[pl.ds(start, key_rows), :]
        probs = jnp.exp(scores_at(pair, query_ext, low, base, start, heads) - log_sum)
        probs_grad = jnp.dot(pair, grad_ext, preferred_element_type=jnp.float32)
        score_grad = (probs * (probs_grad - inner)).astype(jnp.bfloat16)
        sum_ref[...] += jnp.dot(
            turned_ref[:dim, pl.ds(start, key_rows)], score_grad, preferred_element_type=jnp.float32
        )
        pair_grad_ref[pl.ds(start, key_rows), :] += lax.dot_general(
            score_grad, query_ext, ROWS_IN_BOTH, preferred_element_type=jnp.float32
        ) + lax.dot_general(
            probs.astype(jnp.bfloat16), grad_ext, ROWS_IN_BOTH, preferred_element_type=jnp.float32
        )
        return carried

    lax.fori_loop(first_ref[step], (base + query_rows - 1) // key_rows + 1, tile, 0)
    query_grad_ref[...] = unstack_heads(sum_ref[...] * scale, heads).astype(query_grad_ref.dtype)


def attention_specs(queries, pair, query_rows, heads):
    width = queries.shape[1]
    return (
        pl.BlockSpec((query_rows, width), lambda i, first: (i, 0)),
        pl.BlockSpec((1, query_rows), lambda i, first: (0, i)),
        pl.BlockSpec(pair.shape, lambda i, first: (0, 0)),
        pl.BlockSpec((1, 1, heads * query_rows), lambda i, first: (i, 0, 0)),
    )


def attend(queries, pair, first, low, heads, query_rows, key_rows):
    count, width = queries.shape
    tile, row, whole, logs = attention_specs(queries, pair, query_rows, heads)
    columns = heads * query_rows
    return pl.pallas_call(
        functools.partial(attend_kernel, heads, key_rows, (width // heads) ** -0.5),
        grid_spec=pltpu.PrefetchScalarGridSpec(
            num_scalar_prefetch=1,
            grid=(count // query_rows,),
            in_specs=[tile, row, whole],
            out_specs=[tile, logs],
            scratch_shapes=[
                pltpu.VMEM(pair.shape[::-1], jnp.bfloat16),
                pltpu.VMEM((pair.shape[1], columns), jnp.float32),
                pltpu.VMEM((1, columns), jnp.float32),
            ],
        ),
        out_shape=[
            jax.ShapeDtypeStruct((count, width), jnp.bfloat16),
            jax.ShapeDtypeStruct((count // query_rows, 1, columns), jnp.float32),
        ],
        compiler_params=pltpu.CompilerParams(vmem_limit_bytes=48 << 20),
        cost_estimate=pl.CostEstimate(
            flops=20_000_000_000, bytes_accessed=8_000_000, transcendentals=0
        ),
        name="attend",
    )(first, queries, low, pair)


def attend_back(queries, pair, first, low, grads, out, logs, heads, query_rows, key_rows):
    count, width = queries.shape
    tile, row, whole, log_spec = attention_specs(queries, pair, query_rows, heads)
    columns = heads * query_rows
    return pl.pallas_call(
        functools.partial(attend_back_kernel, heads, key_rows, (width // heads) ** -0.5),
        grid_spec=pltpu.PrefetchScalarGridSpec(
            num_scalar_prefetch=1,
            grid=(count // query_rows,),
            in_specs=[tile, row, whole, tile, log_spec]
            + [pl.BlockSpec((query_rows, width), lambda i, first: (0, 0))] * len(grads),
            out_specs=[tile, whole],
            scratch_shapes=[
                pltpu.VMEM(pair.shape[::-1], jnp.bfloat16),
                pltpu.VMEM((pair.shape[1] // 2, columns), jnp.float32),
            ],
        ),
        out_shape=[
            jax.ShapeDtypeStruct((count, width), jnp.bfloat16),
            jax.ShapeDtypeStruct(pair.shape, jnp.float32),
        ],
        compiler_params=pltpu.CompilerParams(vmem_limit_bytes=48 << 20),
        cost_estimate=pl.CostEstimate(
            flops=40_000_000_000, bytes_accessed=12_000_000, transcendentals=0
        ),
        name="attend_back",
    )(first, queries, low, pair, out, logs, *grads)


def heads_apart(wide, dim):
    rows = wide.shape[0]
    return jnp.concatenate(
        [
            jnp.broadcast_to(
                jnp.mean(jnp.square(wide[:, c : c + dim]), axis=-1, keepdims=True), (rows, dim)
            )
            for c in range(0, wide.shape[1], dim)
        ],
        axis=1,
    )


def spread_mean(wide, dim):
    rows = wide.shape[0]
    return jnp.concatenate(
        [
            jnp.broadcast_to(jnp.mean(wide[:, c : c + dim], axis=-1, keepdims=True), (rows, dim))
            for c in range(0, wide.shape[1], dim)
        ],
        axis=1,
    )


def turn(wide, cosine, sine, dim):
    count = wide.shape[1] // dim
    half = dim // 2
    swapped = jnp.concatenate(
        [
            wide[:, c + shift : c + shift + half]
            for c in range(0, wide.shape[1], dim)
            for shift in (half, 0)
        ],
        axis=1,
    )
    return wide * jnp.concatenate([cosine] * count, axis=1) + swapped * jnp.concatenate(
        [sine] * count, axis=1
    )


def project_kernel(
    dim, own_ref, x_ref, weight_ref, head_gain_ref, cosine_ref, sine_ref, query_ref, pair_ref,
    raw_ref, normed_ref, gain_ref, ffn_gain_ref
):
    columns = raw_ref.shape[1]

    @pl.when(pl.program_id(0) == 0)
    def _():
        gains = weight_ref[:, columns:].T.astype(jnp.float32)
        gain_ref[...] = gains[:1]
        ffn_gain_ref[...] = gains[64:65]

    values = x_ref[...].astype(jnp.float32)
    normed = values * lax.rsqrt(jnp.mean(values * values, axis=-1, keepdims=True) + EPS)
    normed = (normed * gain_ref[...]).astype(jnp.bfloat16)
    normed_ref[...] = normed
    raw = jnp.dot(normed, weight_ref[:, :columns], preferred_element_type=jnp.float32)
    raw_ref[...] = raw
    turned_width = raw.shape[1] - pair_ref.shape[1] // 2
    heads = raw[:, :turned_width]
    heads = heads * lax.rsqrt(heads_apart(heads, dim) + EPS) * head_gain_ref[...]
    heads = turn(heads, cosine_ref[...], sine_ref[...], dim).astype(jnp.bfloat16)
    query_width = query_ref.shape[1]
    query_ref[...] = heads[:, :query_width]
    pair_ref[...] = jnp.concatenate(
        [heads[:, query_width:], raw[:, turned_width:].astype(jnp.bfloat16)], axis=1
    )


def project(own, x, weight, head_gain, cosine, sine, size, query_width, rows):
    count, width = x.shape
    out_width = weight.shape[1] - 128
    pair_width = out_width - query_width
    dim = cosine.shape[1]
    tiles = count // size // rows

    def apart(i, own):
        return ((own[0] ^ (i // tiles)) * tiles + i % tiles, 0)

    def there(i, own):
        return (i, 0)

    def whole(i, own):
        return (0, 0)

    return pl.pallas_call(
        functools.partial(project_kernel, dim),
        grid_spec=pltpu.PrefetchScalarGridSpec(
            num_scalar_prefetch=1,
            grid=(count // rows,),
            in_specs=[
                pl.BlockSpec((rows, width), there),
                pl.BlockSpec(weight.shape, whole),
                pl.BlockSpec(head_gain.shape, whole),
                pl.BlockSpec((rows, dim), apart),
                pl.BlockSpec((rows, dim), apart),
            ],
            out_specs=[
                pl.BlockSpec((rows, query_width), apart),
                pl.BlockSpec((rows, pair_width), apart),
                pl.BlockSpec((rows, out_width), apart),
                pl.BlockSpec((rows, width), there),
                pl.BlockSpec((1, width), whole),
                pl.BlockSpec((1, width), whole),
            ],
        ),
        out_shape=[
            jax.ShapeDtypeStruct((count, query_width), jnp.bfloat16),
            jax.ShapeDtypeStruct((count, pair_width), jnp.bfloat16),
            jax.ShapeDtypeStruct((count, out_width), jnp.float32),
            jax.ShapeDtypeStruct((count, width), jnp.bfloat16),
            jax.ShapeDtypeStruct((1, width), jnp.float32),
            jax.ShapeDtypeStruct((1, width), jnp.float32),
        ],
        compiler_params=pltpu.CompilerParams(vmem_limit_bytes=48 << 20),
        cost_estimate=pl.CostEstimate(
            flops=4 * count * width * out_width, bytes_accessed=30_000_000, transcendentals=0
        ),
        name="project",
    )(own, x, weight, head_gain, cosine, sine)


def project_back_kernel(
    dim, own_ref, query_grad_ref, pair_grad_ref, returned_ref, raw_ref, head_gain_ref, cosine_ref,
    sine_ref, grad_ref, gain_grad_ref
):
    @pl.when(pl.program_id(0) == 0)
    def _():
        gain_grad_ref[...] = jnp.zeros_like(gain_grad_ref)

    pair_grad = pair_grad_ref[...] + returned_ref[...].astype(jnp.float32)
    pair_grad = pair_grad.astype(jnp.bfloat16)
    half = pair_grad.shape[1] // 2
    grads = jnp.concatenate([query_grad_ref[...], pair_grad[:, :half]], axis=1).astype(jnp.float32)
    grads = turn(grads, cosine_ref[...], -sine_ref[...], dim)
    values = raw_ref[:, : grads.shape[1]]
    inverse = lax.rsqrt(heads_apart(values, dim) + EPS)
    gain_grad_ref[...] += jnp.sum(grads * values * inverse, axis=0, keepdims=True)
    scaled = grads * head_gain_ref[...]
    moment = spread_mean(scaled * values, dim)
    back = inverse * scaled - values * inverse * inverse * inverse * moment
    grad_ref[...] = jnp.concatenate([back.astype(jnp.bfloat16), pair_grad[:, half:]], axis=1)


def project_back(own, query_grad, pair_sum, returned, raw, head_gain, cosine, sine, size, rows):
    count, query_width = query_grad.shape
    pair_width = pair_sum.shape[1]
    out_width = raw.shape[1]
    dim = cosine.shape[1]
    tiles = count // size // rows

    def apart(i, own):
        return ((own[0] ^ (i // tiles)) * tiles + i % tiles, 0)

    def behind(i, own):
        return (apart(i, own)[0] + count // rows, 0)

    def whole(i, own):
        return (0, 0)

    return pl.pallas_call(
        functools.partial(project_back_kernel, dim),
        grid_spec=pltpu.PrefetchScalarGridSpec(
            num_scalar_prefetch=1,
            grid=(count // rows,),
            in_specs=[
                pl.BlockSpec((rows, query_width), apart),
                pl.BlockSpec((rows, pair_width), behind),
                pl.BlockSpec((rows, pair_width), apart),
                pl.BlockSpec((rows, out_width), apart),
                pl.BlockSpec(head_gain.shape, whole),
                pl.BlockSpec((rows, dim), apart),
                pl.BlockSpec((rows, dim), apart),
            ],
            out_specs=[
                pl.BlockSpec((rows, out_width), lambda i, own: (i, 0)),
                pl.BlockSpec(head_gain.shape, whole),
            ],
        ),
        out_shape=[
            jax.ShapeDtypeStruct((count, out_width), jnp.bfloat16),
            jax.ShapeDtypeStruct(head_gain.shape, jnp.float32),
        ],
        compiler_params=pltpu.CompilerParams(vmem_limit_bytes=48 << 20),
        cost_estimate=pl.CostEstimate(
            flops=8_000_000_000, bytes_accessed=8_000_000, transcendentals=0
        ),
        name="project_back",
    )(own, query_grad, pair_sum, returned, raw, head_gain, cosine, sine)


def join_kernel(half_tiles, x_ref, *refs):
    *part_refs, top_ref, bottom_ref, weight_ref, gain_ref, residual_ref, normed_ref = refs
    tile = pl.program_id(0)
    far = jnp.where((tile // half_tiles) % 2 == 1, top_ref[...], bottom_ref[...])
    attended = jnp.concatenate([ref[...] for ref in part_refs] + [far], axis=1)
    residual = x_ref[...].astype(jnp.float32) + jnp.dot(
        attended, weight_ref[...], preferred_element_type=jnp.float32
    )
    residual_ref[...] = residual
    normed = residual * lax.rsqrt(jnp.mean(residual * residual, axis=-1, keepdims=True) + EPS)
    normed_ref[...] = (normed * gain_ref[...]).astype(jnp.bfloat16)


def join(x, parts, top, bottom, weight, gain, rows):
    count, width = x.shape
    columns = parts[0].shape[1]
    tiles = count // 4 // rows

    def part_map(k):
        return lambda i: ((k ^ (i // tiles)) * tiles + i % tiles, 0)

    def far_map(i):
        return (((3 ^ (i // tiles)) % 2) * tiles + i % tiles, 0)

    def there(i):
        return (i, 0)

    def whole(i):
        return (0, 0)

    return pl.pallas_call(
        functools.partial(join_kernel, 2 * tiles),
        grid=(count // rows,),
        in_specs=[pl.BlockSpec((rows, width), there)]
        + [pl.BlockSpec((rows, columns), part_map(k)) for k in range(3)]
        + [pl.BlockSpec((rows, columns), far_map)] * 2
        + [pl.BlockSpec(weight.shape, whole), pl.BlockSpec((1, width), whole)],
        out_specs=[pl.BlockSpec((rows, width), there)] * 2,
        out_shape=[
            jax.ShapeDtypeStruct((count, width), jnp.float32),
            jax.ShapeDtypeStruct((count, width), jnp.bfloat16),
        ],
        compiler_params=pltpu.CompilerParams(vmem_limit_bytes=48 << 20),
        cost_estimate=pl.CostEstimate(
            flops=2 * count * width * weight.shape[0],
            bytes_accessed=50_000_000,
            transcendentals=0,
        ),
        name="join",
    )(x, *parts, top, bottom, weight, gain)


def settle_kernel(size, own_ref, *refs):
    *part_refs, out_ref = refs
    for k, part_ref in enumerate(part_refs):

        @pl.when(pl.program_id(0) % size == k)
        def _(part_ref=part_ref):
            out_ref[...] = part_ref[...].astype(out_ref.dtype)


def settle(own, parts, pieces):
    size = len(parts)
    rows, width = parts[0].shape
    piece = width // pieces
    return pl.pallas_call(
        functools.partial(settle_kernel, size),
        grid_spec=pltpu.PrefetchScalarGridSpec(
            num_scalar_prefetch=1,
            grid=(pieces * size,),
            in_specs=[pl.BlockSpec((rows, piece), lambda i, own: (0, i // size))] * size,
            out_specs=pl.BlockSpec(
                (rows, piece), lambda i, own: (0, i // size * size + (own[0] ^ (i % size)))
            ),
        ),
        out_shape=jax.ShapeDtypeStruct((rows, width * size), jnp.float32),
        name="settle",
    )(own, *parts)


def begin_kernel(
    x_ref, qkv_ref, in_ref, x_out, qkv_out, in_out, local_sem, x_send, x_recv, q_send, q_recv,
    w_send, w_recv, b_send, b_recv
):
    head, blk = lax.axis_index("heads"), lax.axis_index("blk")
    size, blk_size = lax.axis_size("heads"), lax.axis_size("blk")
    count, depth = x_ref.shape[0], qkv_ref.shape[1]
    half = count // 2
    units = in_out.shape[2] // 2
    barrier = pltpu.get_barrier_semaphore()
    for k in range(1, size):
        pl.semaphore_signal(barrier, inc=1, device_id=(head ^ k, blk), device_id_type=MESH)

    def greet(k, carried):
        pl.semaphore_signal(
            barrier, inc=1, device_id=(head, lax.rem(blk + k, blk_size)), device_id_type=MESH
        )
        return carried

    lax.fori_loop(1, blk_size, greet, 0)
    pl.semaphore_wait(barrier, size + blk_size - 2)

    def send(source, target, k, send_sem, recv_sem):
        return pltpu.make_async_remote_copy(
            src_ref=source,
            dst_ref=target,
            send_sem=send_sem,
            recv_sem=recv_sem,
            device_id=(head ^ k, blk),
            device_id_type=MESH,
        )

    rows = pl.ds(pl.multiple_of(blk * depth, depth), depth)
    qkv_copies = [
        send(
            qkv_ref.at[head ^ k], qkv_out.at[head, rows], k, q_send.at[k - 1], q_recv.at[k - 1]
        )
        for k in range(1, size)
    ]

    def columns(part, owner):
        return pl.ds(pl.multiple_of((part * size + owner) * units, units), units)

    in_copies = [
        send(
            in_ref.at[:, columns(part, head ^ k)],
            in_out.at[head, :, pl.ds(part * units, units)],
            k,
            w_send.at[2 * k - 2 + part],
            w_recv.at[2 * k - 2 + part],
        )
        for k in range(1, size)
        for part in range(2)
    ]
    near = [
        send(x_ref, x_out.at[pl.ds(k * count, count)], k, x_send.at[k - 1], x_recv.at[k - 1])
        for k in (1, 2)
    ]
    far = [
        send(
            x_out.at[pl.ds(count, half)],
            x_out.at[pl.ds(3 * count, half)],
            2,
            x_send.at[2],
            x_recv.at[2],
        ),
        send(
            x_out.at[pl.ds(2 * count + half, half)],
            x_out.at[pl.ds(3 * count + half, half)],
            1,
            x_send.at[3],
            x_recv.at[3],
        ),
    ]
    own = [
        pltpu.make_async_copy(qkv_ref.at[head], qkv_out.at[head, rows], local_sem.at[0]),
        pltpu.make_async_copy(x_ref, x_out.at[pl.ds(0, count)], local_sem.at[1]),
    ] + [
        pltpu.make_async_copy(
            in_ref.at[:, columns(part, head)],
            in_out.at[head, :, pl.ds(part * units, units)],
            local_sem.at[2 + part],
        )
        for part in range(2)
    ]
    for copy in qkv_copies + near + in_copies + own:
        copy.start()

    def along(k):
        return pltpu.make_async_remote_copy(
            src_ref=qkv_out.at[:, rows],
            dst_ref=qkv_out.at[:, rows],
            send_sem=b_send.at[k],
            recv_sem=b_recv.at[k],
            device_id=(head, lax.rem(blk + k, blk_size)),
            device_id_type=MESH,
        )

    def arrived(k):
        source = pl.ds(
            pl.multiple_of(lax.rem(blk + blk_size - k, blk_size) * depth, depth), depth
        )
        return pltpu.make_async_remote_copy(
            src_ref=qkv_out.at[:, rows],
            dst_ref=qkv_out.at[:, source],
            send_sem=b_send.at[k],
            recv_sem=b_recv.at[k],
            device_id=(head, lax.rem(blk + k, blk_size)),
            device_id_type=MESH,
        )

    def start(k, carried):
        along(k).start()
        return carried

    def finish(k, carried):
        along(k).wait_send()
        arrived(k).wait_recv()
        return carried

    own[0].wait()
    for copy in qkv_copies:
        copy.wait_recv()
    lax.fori_loop(1, blk_size, start, 0)
    for first, second in zip(near, far):
        first.wait_recv()
        second.start()
    for copy in qkv_copies + near:
        copy.wait_send()
    for copy in in_copies + far:
        copy.wait()
    for copy in own[1:]:
        copy.wait()
    lax.fori_loop(1, blk_size, finish, 0)


def begin(x, qkv_parts, in_weight):
    size, blk_size = lax.axis_size("heads"), lax.axis_size("blk")
    count, width = x.shape
    depth, joined = qkv_parts.shape[1:]
    anywhere = pl.BlockSpec(memory_space=pl.ANY)
    sems = pltpu.SemaphoreType.DMA
    return pl.pallas_call(
        begin_kernel,
        out_shape=[
            jax.ShapeDtypeStruct((size * count, width), x.dtype),
            jax.ShapeDtypeStruct((size, blk_size * depth, joined), x.dtype),
            jax.ShapeDtypeStruct((size, depth, in_weight.shape[1] // size), x.dtype),
        ],
        in_specs=[anywhere] * 3,
        out_specs=[anywhere] * 3,
        scratch_shapes=[
            sems((4,)),
            sems((4,)),
            sems((4,)),
            sems((size - 1,)),
            sems((size - 1,)),
            sems((2 * size - 2,)),
            sems((2 * size - 2,)),
            sems((blk_size,)),
            sems((blk_size,)),
        ],
        compiler_params=pltpu.CompilerParams(collective_id=1, has_side_effects=True),
        name="begin",
    )(x, qkv_parts, in_weight)


def hidden_kernel(
    normed_ref, gate_ref, up_ref, cot_ref, down_ref, hidden_ref, gate_grad_ref, up_grad_ref
):
    normed = normed_ref[...]
    gate = jnp.dot(normed, gate_ref[...], preferred_element_type=jnp.float32)
    upward = jnp.dot(normed, up_ref[...], preferred_element_type=jnp.float32)
    grad = lax.dot_general(
        cot_ref[...], down_ref[...], ROWS_IN_BOTH, preferred_element_type=jnp.float32
    )
    sigmoid = jax.nn.sigmoid(gate)
    activated = gate * sigmoid
    hidden_ref[...] = (activated * upward).astype(jnp.bfloat16)
    gate_grad_ref[...] = (grad * upward * sigmoid * (1.0 + gate * (1.0 - sigmoid))).astype(
        jnp.bfloat16
    )
    up_grad_ref[...] = (grad * activated).astype(jnp.bfloat16)


def hidden_pass(normed, weight, cot, down, rows, units):
    count, width = normed.shape
    total = down.shape[0]
    tiles = total // units
    out_spec = pl.BlockSpec((rows, units), lambda i, j: (i, j))
    out_shape = jax.ShapeDtypeStruct((count, total), jnp.bfloat16)
    return pl.pallas_call(
        hidden_kernel,
        grid=(count // rows, tiles),
        in_specs=[
            pl.BlockSpec((rows, width), lambda i, j: (i, 0)),
            pl.BlockSpec((width, units), lambda i, j: (0, j)),
            pl.BlockSpec((width, units), lambda i, j: (0, tiles + j)),
            pl.BlockSpec((rows, width), lambda i, j: (i, 0)),
            pl.BlockSpec((units, width), lambda i, j: (j, 0)),
        ],
        out_specs=[out_spec] * 3,
        out_shape=[out_shape] * 3,
        compiler_params=pltpu.CompilerParams(vmem_limit_bytes=58 << 20),
        cost_estimate=pl.CostEstimate(
            flops=6 * count * width * total, bytes_accessed=70_000_000, transcendentals=0
        ),
        name="hidden_pass",
    )(normed, weight, weight, cot, down)


def shares_kernel(compute, order_ref, *refs):
    *in_refs, one_ref, two_ref, rest_ref = refs
    step = pl.program_id(0)
    value = compute(*in_refs).astype(jnp.bfloat16)

    @pl.when(step < 2)
    def _():
        one_ref[...] = value

    @pl.when((step >= 2) & (step < 4))
    def _():
        two_ref[...] = value

    @pl.when(step >= 4)
    def _():
        rest_ref[...] = value


def shares(compute, left, right, right_specs, flops, name):
    rows = left[0].shape[0] // 8
    width = right[0].shape[0] if name == "back_pass" else right[0].shape[1]
    order = jnp.array([2, 6, 5, 7, 0, 1, 4, 3], jnp.int32)
    return pl.pallas_call(
        functools.partial(shares_kernel, compute),
        grid_spec=pltpu.PrefetchScalarGridSpec(
            num_scalar_prefetch=1,
            grid=(8,),
            in_specs=[
                pl.BlockSpec((rows, a.shape[1]), lambda i, order: (order[i], 0)) for a in left
            ]
            + right_specs,
            out_specs=[
                pl.BlockSpec((rows, width), lambda i, order: (jnp.minimum(i, 1), 0)),
                pl.BlockSpec((rows, width), lambda i, order: (jnp.clip(i - 2, 0, 1), 0)),
                pl.BlockSpec((rows, width), lambda i, order: (jnp.clip(i - 4, 0, 3), 0)),
            ],
        ),
        out_shape=[
            jax.ShapeDtypeStruct((count * rows, width), jnp.bfloat16) for count in (2, 2, 4)
        ],
        compiler_params=pltpu.CompilerParams(vmem_limit_bytes=58 << 20),
        cost_estimate=pl.CostEstimate(flops=flops, bytes_accessed=40_000_000, transcendentals=0),
        name=name,
    )(order, *left, *right)


def back_product(gate_ref, up_ref, gate_weight_ref, up_weight_ref):
    return lax.dot_general(
        gate_ref[...], gate_weight_ref[...], ROWS_IN_BOTH, preferred_element_type=jnp.float32
    ) + lax.dot_general(
        up_ref[...], up_weight_ref[...], ROWS_IN_BOTH, preferred_element_type=jnp.float32
    )


def back_pass(gate_grad, up_grad, weight):
    width, total = weight.shape[0], gate_grad.shape[1]
    specs = [
        pl.BlockSpec((width, total), lambda i, order: (0, 0)),
        pl.BlockSpec((width, total), lambda i, order: (0, 1)),
    ]
    flops = 4 * gate_grad.shape[0] * width * total
    return shares(back_product, [gate_grad, up_grad], [weight] * 2, specs, flops, "back_pass")


def down_product(hidden_ref, weight_ref):
    return jnp.dot(hidden_ref[...], weight_ref[...], preferred_element_type=jnp.float32)


def down_pass(hidden, weight):
    specs = [pl.BlockSpec(weight.shape, lambda i, order: (0, 0))]
    flops = 2 * hidden.shape[0] * weight.shape[0] * weight.shape[1]
    return shares(down_product, [hidden], [weight], specs, flops, "down_pass")


def residual_back_kernel(
    keep_ref, top_ref, bottom_ref, top_last_ref, bottom_last_ref, residual_ref, cot_ref, gain_ref,
    *refs
):
    *weight_refs, grad_ref, branch_ref, gain_grad_ref, attended_ref = refs
    step = pl.program_id(0)
    first = step < pl.num_programs(0) // 2

    @pl.when(step == 0)
    def _():
        gain_grad_ref[...] = jnp.zeros_like(gain_grad_ref)

    def wide(ref):
        return ref[...].astype(jnp.float32)

    gradient = wide(keep_ref) + jnp.where(
        first, wide(top_ref) + wide(top_last_ref), wide(bottom_ref) + wide(bottom_last_ref)
    )
    values = residual_ref[...]
    inverse = lax.rsqrt(jnp.mean(values * values, axis=-1, keepdims=True) + EPS)
    gain_grad_ref[...] += jnp.sum(gradient * values * inverse, axis=0, keepdims=True)
    scaled = gradient * gain_ref[...]
    moment = jnp.mean(scaled * values, axis=-1, keepdims=True)
    total = wide(cot_ref) + inverse * scaled - values * (inverse * inverse * inverse * moment)
    grad_ref[...] = total
    branch = total.astype(jnp.bfloat16)
    branch_ref[...] = branch
    for k, weight_ref in enumerate(weight_refs):
        attended_ref[k] = lax.dot_general(
            branch, weight_ref[...], ROWS_IN_BOTH, preferred_element_type=jnp.float32
        ).astype(jnp.bfloat16)


def residual_back(keep, top, bottom, top_last, bottom_last, residual, cot, gain, weights, rows):
    count, width = cot.shape
    columns = weights[0].shape[0]
    tiles = count // 2 // rows

    def there(i):
        return (i, 0)

    def in_half(i):
        return (i % tiles, 0)

    def whole(i):
        return (0, 0)

    tile = pl.BlockSpec((rows, width), there)
    half = pl.BlockSpec((rows, width), in_half)
    row = pl.BlockSpec((1, width), whole)
    return pl.pallas_call(
        residual_back_kernel,
        grid=(count // rows,),
        in_specs=[tile, half, half, half, half, tile, tile, row]
        + [pl.BlockSpec(weight.shape, whole) for weight in weights],
        out_specs=[
            tile,
            tile,
            row,
            pl.BlockSpec((len(weights), rows, columns), lambda i: (0, i, 0)),
        ],
        out_shape=[
            jax.ShapeDtypeStruct((count, width), jnp.float32),
            jax.ShapeDtypeStruct((count, width), jnp.bfloat16),
            jax.ShapeDtypeStruct((1, width), jnp.float32),
            jax.ShapeDtypeStruct((len(weights), count, columns), jnp.bfloat16),
        ],
        compiler_params=pltpu.CompilerParams(vmem_limit_bytes=48 << 20),
        cost_estimate=pl.CostEstimate(
            flops=2 * count * width * columns * len(weights),
            bytes_accessed=30_000_000,
            transcendentals=0,
        ),
        name="residual_back",
    )(keep, top, bottom, top_last, bottom_last, residual, cot, gain, *weights)


def turned_kernel(left_ref, right_ref, out_ref):
    out_ref[...] = lax.dot_general(
        left_ref[...], right_ref[...], (((0,), (0,)), ((), ())), preferred_element_type=jnp.float32
    ).astype(out_ref.dtype)


def turned_product(left, right, rows):
    count, height = left.shape
    width = right.shape[1]
    return pl.pallas_call(
        turned_kernel,
        grid=(height // rows,),
        in_specs=[
            pl.BlockSpec((count, rows), lambda i: (0, i)),
            pl.BlockSpec((count, width), lambda i: (0, 0)),
        ],
        out_specs=pl.BlockSpec((rows, width), lambda i: (i, 0)),
        out_shape=jax.ShapeDtypeStruct((height, width), jnp.bfloat16),
        compiler_params=pltpu.CompilerParams(vmem_limit_bytes=58 << 20),
        cost_estimate=pl.CostEstimate(
            flops=2 * count * height * width, bytes_accessed=20_000_000, transcendentals=0
        ),
        name="turned_product",
    )(left, right)


def finish_kernel(
    query_width, dim, sent_ref, qkv_ref, x_ref, residual_ref, gain_ref, ffn_ref, head_ref, *refs
):
    size, blk_size = lax.axis_size("heads"), lax.axis_size("blk")
    weight_refs, refs = refs[:size], refs[size:]
    (
        grad_ref, qkv_grad_ref, gains_ref, got_ref, qkv_got_ref, part_ref, gain_got_ref, s_send,
        s_recv, q_send, q_recv, g_send, g_recv,
    ) = refs
    devices = size * blk_size
    head, blk = lax.axis_index("heads"), lax.axis_index("blk")
    own = head * blk_size + blk
    count, width = x_ref.shape
    depth = width // devices
    barrier = pltpu.get_barrier_semaphore()

    def place_of(index):
        return (index // blk_size, lax.rem(index, blk_size))

    def greet(k, carried):
        pl.semaphore_signal(
            barrier, inc=1, device_id=place_of(lax.rem(own + k, devices)), device_id_type=MESH
        )
        return carried

    lax.fori_loop(1, devices, greet, 0)
    pl.semaphore_wait(barrier, devices - 1)

    sends = [
        pltpu.make_async_remote_copy(
            src_ref=sent_ref.at[pl.ds(k * count, count)],
            dst_ref=got_ref.at[k - 1],
            send_sem=s_send.at[k - 1],
            recv_sem=s_recv.at[k - 1],
            device_id=(head ^ k, blk),
            device_id_type=MESH,
        )
        for k in range(1, size)
    ]
    for copy in sends:
        copy.start()

    def rows_of(index):
        return pl.ds(pl.multiple_of(index * depth, depth), depth)

    def qkv_copy(k, slot):
        other = lax.rem(own + k, devices)
        return pltpu.make_async_remote_copy(
            src_ref=qkv_ref.at[rows_of(other)],
            dst_ref=qkv_got_ref.at[slot],
            send_sem=q_send.at[k],
            recv_sem=q_recv.at[slot],
            device_id=place_of(other),
            device_id_type=MESH,
        )

    def gain_copy(k, slot):
        other = lax.rem(own + k, devices)
        return pltpu.make_async_remote_copy(
            src_ref=part_ref.at[other],
            dst_ref=gain_got_ref.at[slot],
            send_sem=g_send.at[k],
            recv_sem=g_recv.at[slot],
            device_id=place_of(other),
            device_id_type=MESH,
        )

    def start_qkv(k, carried):
        qkv_copy(k, own).start()
        return carried

    lax.fori_loop(1, devices, start_qkv, 0)
    qkv_got_ref[own] = qkv_ref[rows_of(own)]
    for copy in sends:
        copy.wait_recv()

    rows = min(128, count)

    def tile(index, gain_sum):
        here = pl.ds(pl.multiple_of(index * rows, rows), rows)
        normed_grad = lax.dot_general(
            sent_ref[here], weight_refs[0][...], ROWS_IN_BOTH, preferred_element_type=jnp.float32
        )
        for k in range(1, size):
            normed_grad += lax.dot_general(
                got_ref[k - 1, here],
                weight_refs[k][...],
                ROWS_IN_BOTH,
                preferred_element_type=jnp.float32,
            )
        values = x_ref[here].astype(jnp.float32)
        inverse = lax.rsqrt(jnp.mean(values * values, axis=-1, keepdims=True) + EPS)
        scaled = normed_grad * gain_ref[...]
        moment = jnp.mean(scaled * values, axis=-1, keepdims=True)
        grad_ref[here] = (
            residual_ref[here]
            + inverse * scaled
            - values * (inverse * inverse * inverse * moment)
        )
        return gain_sum + jnp.sum(normed_grad * values * inverse, axis=0, keepdims=True)

    attn_sum = lax.fori_loop(0, count // rows, tile, jnp.zeros((1, width), jnp.float32))

    def by_device(row):
        lanes = jnp.concatenate(
            [row[:, d * depth : (d + 1) * depth] for d in range(devices)], axis=0
        )
        if depth < 64:
            lanes = jnp.concatenate(
                [lanes, jnp.zeros((devices, 64 - depth), jnp.float32)], axis=1
            )
        return lanes

    head_row = head_ref[...]
    query_sum = head_row[:, :dim]
    for c in range(dim, query_width, dim):
        query_sum += head_row[:, c : c + dim]
    key_sum = head_row[:, query_width : query_width + dim]
    for c in range(query_width + dim, head_row.shape[1], dim):
        key_sum += head_row[:, c : c + dim]
    both = jnp.concatenate([query_sum, key_sum], axis=1)
    part_ref[...] = jnp.zeros_like(part_ref)
    part_ref[:, 0, :] = jnp.concatenate([by_device(attn_sum), by_device(ffn_ref[...])], axis=1)
    part_ref[:, 1, :] = jnp.broadcast_to(both, (devices, 2 * dim))

    def start_gain(k, carried):
        gain_copy(k, own).start()
        return carried

    lax.fori_loop(1, devices, start_gain, 0)
    gain_got_ref[own] = part_ref[own]

    def finish(k, carried):
        source = lax.rem(own + devices - k, devices)
        qkv_copy(k, source).wait()
        gain_copy(k, source).wait()
        return carried

    lax.fori_loop(1, devices, finish, 0)
    for copy in sends:
        copy.wait_send()
    gains_ref[...] = jnp.sum(gain_got_ref[...], axis=0)

    def group_sum(h):
        total = qkv_got_ref[h * blk_size].astype(jnp.float32)
        for b in range(1, blk_size):
            total += qkv_got_ref[h * blk_size + b].astype(jnp.float32)
        return total

    sums = [group_sum(h) for h in range(size)]
    key_end = query_width + (sums[0].shape[1] - query_width) // 2
    qkv_grad_ref[...] = jnp.concatenate(
        [total[:, :query_width] for total in sums]
        + [total[:, query_width:key_end] for total in sums]
        + [total[:, key_end:] for total in sums],
        axis=1,
    )


def finish(sent, qkv_part, x, residual_grad, gain, ffn_sum, head_sum, weights, query_width, dim):
    size, blk_size = lax.axis_size("heads"), lax.axis_size("blk")
    devices = size * blk_size
    count, width = x.shape
    depth, joined = width // devices, sent.shape[1]
    vmem = pl.BlockSpec(memory_space=pltpu.VMEM)
    sems = pltpu.SemaphoreType.DMA
    return pl.pallas_call(
        functools.partial(finish_kernel, query_width, dim),
        out_shape=[
            jax.ShapeDtypeStruct((count, width), jnp.float32),
            jax.ShapeDtypeStruct((depth, size * joined), jnp.float32),
            jax.ShapeDtypeStruct((8, 128), jnp.float32),
        ],
        in_specs=[vmem] * (7 + size),
        out_specs=[vmem] * 3,
        scratch_shapes=[
            pltpu.VMEM((size - 1, count, joined), jnp.bfloat16),
            pltpu.VMEM((devices, depth, joined), jnp.bfloat16),
            pltpu.VMEM((devices, 8, 128), jnp.float32),
            pltpu.VMEM((devices, 8, 128), jnp.float32),
            sems((size - 1,)),
            sems((size - 1,)),
            sems((devices,)),
            sems((devices,)),
            sems((devices,)),
            sems((devices,)),
        ],
        compiler_params=pltpu.CompilerParams(
            collective_id=0, has_side_effects=True, vmem_limit_bytes=56 << 20
        ),
        name="finish",
    )(sent, qkv_part, x, residual_grad, gain, ffn_sum, head_sum, *weights)


def permute(block, axis, k):
    return lax.ppermute(block, axis, [(i, i ^ k) for i in range(lax.axis_size(axis))])


def after(value, *done):
    return lax.optimization_barrier((value, *done))[0]


def pick(block, k, axis, dim):
    extent = block.shape[dim] // lax.axis_size(axis)
    return lax.dynamic_slice_in_dim(block, (lax.axis_index(axis) ^ k) * extent, extent, dim)


def gather_near(block, *done):
    half = block.shape[0] // 2
    one, two = permute(block, "heads", 1), permute(block, "heads", 2)
    if done:
        one, two = lax.optimization_barrier((one, two, *done))[:2]
    top = permute(one[:half], "heads", 2)
    bottom = permute(two[half:], "heads", 1)
    return block, one, two, top, bottom


def wide(block):
    return block.astype(jnp.float32)


def local(
    inputs,
    positions,
    attn_gain,
    qkv_weight,
    q_gain,
    k_gain,
    out_weight,
    ffn_gain,
    ffn_in_weight,
    ffn_out_weight,
    cotangent,
):
    token_count, width = inputs.shape
    depth = qkv_weight.shape[0]
    head_dim = q_gain.shape[0]
    group_size = HEADS // KV_HEADS
    size = lax.axis_size("heads")
    blk_size = lax.axis_size("blk")
    query_all, key_all = HEADS * head_dim, KV_HEADS * head_dim
    query_width, key_width = query_all // size, key_all // size
    qkv_width = query_width + 2 * key_width
    block_len = token_count * size
    half = token_count // 2
    own = lax.axis_index("heads").astype(jnp.int32).reshape(1)

    qkv_parts = jnp.concatenate(
        [
            qkv_weight[:, :query_all].reshape(depth, size, query_width),
            qkv_weight[:, query_all : query_all + key_all].reshape(depth, size, key_width),
            qkv_weight[:, query_all + key_all :].reshape(depth, size, key_width),
            jnp.broadcast_to(attn_gain[:, None, None], (depth, size, 64)),
            jnp.broadcast_to(ffn_gain[:, None, None], (depth, size, 64)),
        ],
        axis=-1,
    ).transpose(1, 0, 2)
    out_group = lax.all_gather(out_weight, "blk", axis=0, tiled=True)
    down_group = lax.all_gather(ffn_out_weight, "blk", axis=0, tiled=True)

    inputs_blk, qkv_rows, in_rows = begin(inputs, qkv_parts, ffn_in_weight)
    in_group = lax.all_gather(in_rows, "blk", axis=1, tiled=True).reshape(width, -1)
    qkv_rows = qkv_rows.reshape(width, -1)
    cosine, sine = rotation(positions, head_dim)
    cosine = jnp.concatenate([cosine[:, 0], cosine[:, 0]], axis=-1)
    sine = jnp.concatenate([-sine[:, 0], sine[:, 0]], axis=-1)
    head_gain = jnp.concatenate(
        [jnp.tile(q_gain, HEADS // size), jnp.tile(k_gain, KV_HEADS // size)]
    ).astype(jnp.float32)[None, :]
    query_low, pair_blk, raw, normed, attn_scaling, ffn_scaling = project(
        own, inputs_blk, qkv_rows, head_gain, cosine, sine, size, query_width, 256
    )
    pair_all = jnp.concatenate([from_behind(pair_blk, "blk", 1), pair_blk], axis=0)
    query_rows, key_rows = token_count, 256
    low = block_len + jnp.arange(block_len, dtype=jnp.int32) - positions
    first = jnp.concatenate([low[::query_rows] // key_rows, own])
    low = low[None, :]
    attended_blk, logs = attend(query_low, pair_all, first, low, group_size, query_rows, key_rows)

    mine = jnp.concatenate([pick(attended_blk, k, "heads", 0) for k in range(size)], axis=0)
    out_near = gather_near(after(out_group, inputs_blk))
    out_all = (*out_near[:3], jnp.concatenate(out_near[3:], axis=0))
    near = gather_near(mine)
    residual, ffn_normed = join(
        inputs_blk, near[:3], *near[3:], jnp.concatenate(out_all, axis=0), ffn_scaling, 256
    )
    residual_own = residual[:token_count]
    cotangent_near = gather_near(after(cotangent, inputs_blk), near[1])
    cotangent_blk = jnp.concatenate(cotangent_near, axis=0)

    hidden, gate_grad, up_grad = hidden_pass(
        ffn_normed, in_group, cotangent_blk, down_group, block_len // 2, 256
    )
    one, two, rest = back_pass(gate_grad, up_grad, in_group)
    top, bottom = permute(one, "heads", 1), permute(two, "heads", 2)
    down_sum = turned_product(after(hidden, rest), cotangent_blk, 256)
    ffn_out_grad = wide(lax.psum_scatter(down_sum, "blk", scatter_dimension=0, tiled=True))
    gate_up_grad = jnp.concatenate([gate_grad, up_grad], axis=1)
    in_sum = turned_product(ffn_normed, after(gate_up_grad, down_sum), 256)
    in_part = lax.psum_scatter(
        in_sum.reshape(size, blk_size * depth, -1), "blk", scatter_dimension=1, tiled=True
    )
    top, bottom, in_sum = lax.optimization_barrier((top, bottom, in_sum))
    top_send = (wide(rest[2 * half : 3 * half]) + wide(top[half:])).astype(jnp.bfloat16)
    bottom_send = (wide(rest[3 * half :]) + wide(bottom[half:])).astype(jnp.bfloat16)
    top_last, bottom_last = permute(top_send, "heads", 2), permute(bottom_send, "heads", 1)
    out_one, out_two, out_rest = down_pass(after(hidden, top_send, bottom_send), down_group)
    top_last, bottom_last, out_rest = lax.optimization_barrier((top_last, bottom_last, out_rest))

    residual_grad, branch_grad, ffn_sum, attended_grad = residual_back(
        rest, top, bottom, top_last, bottom_last, residual_own, cotangent, ffn_scaling, out_all,
        min(128, half)
    )
    grads = [attended_grad[0]] + [permute(attended_grad[k], "heads", k) for k in range(1, size)]
    attended_own = jnp.concatenate(
        [
            near[0][:token_count],
            near[1][token_count : 2 * token_count],
            near[2][2 * token_count : 3 * token_count],
            near[4][token_count:],
        ],
        axis=1,
    )
    out_sum = turned_product(attended_own, branch_grad, 256)
    *grads, out_sum, out_one, out_two = lax.optimization_barrier(
        (*grads, out_sum, out_one, out_two)
    )
    out_top, out_bottom = permute(out_one, "heads", 1), permute(out_two, "heads", 2)
    query_grad, pair_sum = attend_back(
        query_low, pair_all, first, low, grads, attended_blk, logs, group_size, query_rows, key_rows
    )
    returned = from_behind(pair_sum[:block_len].astype(jnp.bfloat16), "blk", -1)
    out_peers = [
        permute(out_sum[k * query_width : (k + 1) * query_width], "heads", k)
        for k in range(1, size)
    ]
    out_part = sum(wide(part) for part in out_peers) + wide(out_sum[:query_width])
    out_grad = wide(
        lax.psum_scatter(out_part.astype(jnp.bfloat16), "blk", scatter_dimension=0, tiled=True)
    )
    out_top, out_bottom, returned = lax.optimization_barrier((out_top, out_bottom, returned))
    top_send = (wide(out_rest[2 * half : 3 * half]) + wide(out_top[half:])).astype(jnp.bfloat16)
    bottom_send = (wide(out_rest[3 * half :]) + wide(out_bottom[half:])).astype(jnp.bfloat16)
    out_top_last = permute(top_send, "heads", 2)
    out_bottom_last = permute(bottom_send, "heads", 1)
    layer_out = jnp.concatenate(
        [
            residual_own[:half] + wide(out_rest[:half]) + wide(out_top[:half]) + wide(out_top_last),
            residual_own[half:]
            + wide(out_rest[half : 2 * half])
            + wide(out_bottom[:half])
            + wide(out_bottom_last),
        ],
        axis=0,
    ).astype(jnp.bfloat16)

    projected_grad, head_sum = project_back(
        own, query_grad, pair_sum, returned, raw, head_gain, cosine, sine, size, 256
    )
    qkv_part = turned_product(normed, projected_grad, 512)
    qkv_near = gather_near(after(qkv_rows[:, :qkv_width], out_near[1], near[1], cotangent_blk))
    qkv_all = (*qkv_near[:3], jnp.concatenate(qkv_near[3:], axis=0))
    input_grad, qkv_grad, gains = finish(
        projected_grad, qkv_part, inputs, residual_grad, attn_scaling, ffn_sum, head_sum, qkv_all,
        query_width, head_dim
    )
    in_pieces = [pick(in_part, k, "heads", 0)[0] for k in range(size)]
    ffn_in_grad = settle(
        own,
        [in_pieces[0]] + [permute(in_pieces[k], "heads", k) for k in range(1, size)],
        2,
    )
    return (
        layer_out,
        input_grad,
        gains[0, :depth],
        qkv_grad,
        gains[1, :head_dim],
        gains[1, head_dim : 2 * head_dim],
        out_grad,
        gains[0, 64 : 64 + depth],
        ffn_in_grad,
        ffn_out_grad,
    )


def solution(mesh):
    placed = (
        P(("blk", "heads"), None),
        P("blk"),
        P(("heads", "blk")),
        P(("heads", "blk"), None),
        P(),
        P(),
        P(("heads", "blk"), None),
        P(("heads", "blk")),
        P(("heads", "blk"), None),
        P(("heads", "blk"), None),
        P(("blk", "heads"), None),
    )
    return jax.shard_map(
        local,
        mesh=mesh,
        in_specs=placed,
        out_specs=(
            P(("blk", "heads"), None),
            P(("blk", "heads"), None),
            P(("heads", "blk")),
            P(("heads", "blk"), None),
            P(),
            P(),
            P(("heads", "blk"), None),
            P(("heads", "blk")),
            P(("heads", "blk"), None),
            P(("heads", "blk"), None),
        ),
        check_vma=False,
    )
```

time: 2760 us -> 824 us (0.30)
  waiting for transfers between devices: 1820 us -> 244 us
  matrix products: 432 us -> 0 us
  Pallas kernels: 0 us -> 424 us
  other arithmetic: 179 us -> 42.6 us
  blocking collectives: 128 us -> 0 us
  local copies, waits for them, and re-layouts: 123 us -> 46.7 us
    reduce_scatter x4 -> x3, waiting for transfers between devices: 1160 us -> 0.02 us  [the longest x1 0.02 us: local(): lax.psum_scatter(out_part.astype(jnp.bfloat16), 'blk', scatter_dimension=...]
    all_gather x8 -> x3, waiting for transfers between devices: 600 us -> 0.01 us  [the longest x1 0.01 us: local(): out_group = lax.all_gather(out_weight, 'blk', axis=0, tiled=True)]
    dot_general x40 -> x0, matrix products: 432 us -> none  [the longest x8 60.8 us: scores_at(): jnp.einsum('qcgd,kcd->cgqk', query_part, key_part, preferred_element_type...]
    pallas_call x0 -> x16, Pallas kernels: none -> 424 us  [the longest x1 92.6 us: begin(): pl.pallas_call(begin_kernel, out_shape=[jax.ShapeDtypeStruct((size * coun...]
    ppermute x0 -> x33, waiting for transfers between devices: none -> 242 us  [permute(): lax.ppermute(block, axis, [(i, i ^ k) for i in range(lax.axis_size(axis))])]
    unnamed x3 -> x0, blocking collectives: 128 us -> none
    all_to_all x6 -> x0, waiting for transfers between devices: 57.3 us -> none  [the longest x1 14 us: local(): lax.all_to_all(query_low.reshape(token_count, KV_HEADS, group_size * head...]
    another operation x6 -> x1, other arithmetic: 60.5 us -> 5.53 us
  transfers between devices with their start and end apart: 20 -> 41, of which waited for: 15 -> 15; matrix products, arithmetic and copies ran while one was open for 24% -> 8% of each run, Pallas kernels for 0% -> 37%
where the time goes in v2:
time: 824 us; the launch traced here: 813 us
  Pallas kernels  424 us (51%)
  waiting for transfers between devices  244 us (30%)
  local copies, waits for them, and re-layouts  46.7 us (6%)
  other arithmetic  42.6 us (5%)
  starting transfers between devices  40.8 us (5%)
  between operations  15.3 us (2%)
    ppermute x33, waiting for transfers between devices, permute(): lax.ppermute(block, axis, [(i, i ^ k) for i in range(lax.axis_size(axis))])  242 us
    pallas_call x1, Pallas kernels, begin(): pl.pallas_call(begin_kernel, out_shape=[jax.ShapeDtypeStruct((size * coun...  92.6 us
    pallas_call x1, Pallas kernels, finish(): pl.pallas_call(functools.partial(finish_kernel, query_width, dim), out_sh...  60.7 us
    pallas_call x4, Pallas kernels, turned_product(): pl.pallas_call(turned_kernel, grid=(height // rows,), in_specs=[pl.BlockS...  60.3 us
    pallas_call x2, Pallas kernels, shares(): pl.pallas_call(functools.partial(shares_kernel, compute), grid_spec=pltpu...  50 us
    pallas_call x1, Pallas kernels, hidden_pass(): pl.pallas_call(hidden_kernel, grid=(count // rows, tiles), in_specs=[pl.B...  43 us
    ppermute x33, starting transfers between devices, permute(): lax.ppermute(block, axis, [(i, i ^ k) for i in range(lax.axis_size(axis))])  37.2 us
    pallas_call x1, Pallas kernels, attend_back(): pl.pallas_call(functools.partial(attend_back_kernel, heads, key_rows, (wi...  34.4 us
  transfers between devices with their start and end apart: 41, of which 15 were waited for; matrix products, arithmetic and copies ran while one was open for 8% of the time, Pallas kernels for 37%

profile of v2, /device:TPU:0, one launch (start us, length us, event | category | flops | bytes accessed | tf_op | source)
XLA Modules:
  0.0 813.5 jit_solution(4432773008766723384)
XLA Ops:
  13.0 92.6 %begin.1 = (bf16[2048,2048]{1,0:T(8,128)(2,1)}, bf16[4,512,512]{2,1,0:T(8,128)(2,1)}, bf16[4,64,2560]{2,1,0:T(8,128)(2,1)}) custom-call(bf16[512,2048]{1,0:T(8,128)(2,1)} %x_ref.3, bf16[4,64,512]{2,1,0:T(8,128)(2,1)} %bitcast.40, bf16[64,10240]{1,0:T(8,128)(2,1)} %in_ref.1), custom_call_target="tpu_custom_call" | custom-call | tf_op jit(solution)/shard_map/begin/pallas_call | solution.py:628
  111.2 22.5 %project.1 = (bf16[2048,256]{1,0:T(8,128)(2,1)S(1)}, bf16[2048,128]{1,0:T(8,128)(2,1)S(1)}, f32[2048,384]{1,0:T(8,128)}, bf16[2048,2048]{1,0:T(8,128)(2,1)}, f32...) custom-call(s32[1]{0:T(128)} %bitcast.1.own_ref, bf16[2048,2048]{1,0:T(8,128)(2,1)} %get-tuple-element.66.x_ref, ...), custom_call_target="tpu_custom_call" | custom-call | flops 6442450944 | bytes 30000000 | tf_op jit(solution)/shard_map/project/pallas_call | solution.py:300
  138.1 15.9 %attend.1 = (bf16[2048,256]{1,0:T(8,128)(2,1)S(1)}, f32[4,1,2048]{2,1,0:T(1,128)S(1)}) custom-call(s32[5]{0:T(128)S(1)} %pad_add_fusion.first_ref, bf16[2048,256]{1,0:T(8,128)(2,1)S(1)} %get-tuple-element.68.query_ref, s32[1,2048]{1,0:T(1,128)S(1)} %bitcast.37, bf16[4096,128]{1,0:T(8,128)(2,1)S(1)} %constant_dynamic-update-slice_fusion.pair_ref), custom_call_target="tpu_custom_call" | custom-call | flops 20000000000 | bytes 8000000 | tf_op jit(solution)/shard_map/attend/pallas_call | solution.py:161
  160.9 45.8 %collective-permute-done.1.refs_1_ = bf16[2048,256]{1,0:T(8,128)(2,1)} collective-permute-done((bf16[2048,256]{1,0:T(8,128)(2,1)}, bf16[2048,256]{1,0:T(8,128)(2,1)}, u32[]{:S(2)}, u32[]{:S(2)}) %collective-permute-start.1) | collective-permute-done | bytes 1048608 | tf_op jit(solution)/shard_map/ppermute | solution.py:1069
  219.6 9.5 %collective-permute-done.5.refs_1_ = bf16[256,2048]{1,0:T(8,128)(2,1)S(1)} collective-permute-done((bf16[256,2048]{1,0:T(8,128)(2,1)}, bf16[256,2048]{1,0:T(8,128)(2,1)S(1)}, u32[]{:S(2)}, u32[]{:S(2)}) %collective-permute-start.5) | collective-permute-done | bytes 1048608 | tf_op jit(solution)/shard_map/ppermute | solution.py:1069
  230.7 14.4 %collective-permute-done.6.refs_2_ = bf16[256,2048]{1,0:T(8,128)(2,1)S(1)} collective-permute-done((bf16[256,2048]{1,0:T(8,128)(2,1)S(1)}, bf16[256,2048]{1,0:T(8,128)(2,1)S(1)}, u32[]{:S(2)}, u32[]{:S(2)}) %collective-permute-start.6) | collective-permute-done | bytes 1048608 | tf_op jit(solution)/shard_map/ppermute | solution.py:1069
  246.7 20.9 %collective-permute-done.11 = bf16[256,2048]{1,0:T(8,128)(2,1)S(1)} collective-permute-done((bf16[256,2048]{1,0:T(8,128)(2,1)S(1)}, bf16[256,2048]{1,0:T(8,128)(2,1)S(1)}, u32[]{:S(2)}, u32[]{:S(2)}) %collective-permute-start.11) | collective-permute-done | bytes 1048608 | tf_op jit(solution)/shard_map/ppermute | solution.py:1069
  269.3 8.9 %collective-permute-done.7 = bf16[128,2048]{1,0:T(8,128)(2,1)S(1)} collective-permute-done((bf16[128,2048]{1,0:T(8,128)(2,1)S(1)}, bf16[128,2048]{1,0:T(8,128)(2,1)S(1)}, u32[]{:S(2)}, u32[]{:S(2)}) %collective-permute-start.7) | collective-permute-done | bytes 524320 | tf_op jit(solution)/shard_map/ppermute | solution.py:1069
  282.4 18.5 %join.1 = (f32[2048,2048]{1,0:T(8,128)}, bf16[2048,2048]{1,0:T(8,128)(2,1)}) custom-call(bf16[2048,2048]{1,0:T(8,128)(2,1)} %get-tuple-element.66.x_ref, bf16[2048,256]{1,0:T(8,128)(2,1)} %pad_maximum_fusion.5.refs_0_, bf16[2048,256]{1,0:T(8,128)(2,1)} %collective-permute-done.1.refs_1_, bf16[2048,256]{1,0:T(8,128)(2,1)} %collective-permute-done.2.refs_2_, ...), custom_call_target="tpu_custom_call" | custom-call | flops 8589934592 | bytes 50000000 | tf_op jit(solution)/shard_map/join/pallas_call | solution.py:436
  301.7 43.0 %hidden_pass.1 = (bf16[2048,1280]{1,0:T(8,128)(2,1)}, bf16[2048,1280]{1,0:T(8,128)(2,1)}, bf16[2048,1280]{1,0:T(8,128)(2,1)}) custom-call(bf16[2048,2048]{1,0:T(8,128)(2,1)} %get-tuple-element.74.normed_ref.left_ref, bf16[2048,2560]{1,0:T(8,128)(2,1)} %bitcast.44, bf16[2048,2560]{1,0:T(8,128)(2,1)} %bitcast.45, bf16[2048,2048]{1,0:T(8,128)(2,1)} %copy-done.38, ...), custom_call_target="tpu_custom_call" | custom-call | flops 32212254720 | bytes 70000000 | tf_op jit(solution)/shard_map/hidden_pass/pallas_call | solution.py:677
  344.7 9.6 %pad_maximum_fusion.right_ref = bf16[2048,2560]{1,0:T(8,128)(2,1)} fusion(bf16[2048,1280]{1,0:T(8,128)(2,1)} %get-tuple-element.80.refs_1_, bf16[2048,1280]{1,0:T(8,128)(2,1)} %get-tuple-element.79.refs_0_), kind=kLoop, calls=%fused_computation | loop fusion | flops 20971520 | bytes 20971520 | tf_op jit(solution)/shard_map/concatenate | solution.py:1171
  354.3 31.4 %back_pass.1 = (bf16[512,2048]{1,0:T(8,128)(2,1)}, bf16[512,2048]{1,0:T(8,128)(2,1)}, bf16[1024,2048]{1,0:T(8,128)(2,1)}) custom-call(s32[8]{0:T(128)} %constant.43.clone.order_ref, bf16[2048,1280]{1,0:T(8,128)(2,1)} %get-tuple-element.79.refs_0_, bf16[2048,1280]{1,0:T(8,128)(2,1)} %get-tuple-element.80.refs_1_, bf16[2048,2560]{1,0:T(8,128)(2,1)} %bitcast.46, ...), custom_call_target="tpu_custom_call" | custom-call | flops 21474836480 | bytes 40000000 | tf_op jit(solution)/shard_map/back_pass/pallas_call | solution.py:719
  385.7 16.6 %turned_product.4 = bf16[1280,2048]{1,0:T(8,128)(2,1)} custom-call(bf16[2048,1280]{1,0:T(8,128)(2,1)} %get-tuple-element.89.left_ref.refs_0_, bf16[2048,2048]{1,0:T(8,128)(2,1)} %copy-done.38), custom_call_target="tpu_custom_call" | custom-call | flops 10737418240 | bytes 20000000 | tf_op jit(solution)/shard_map/turned_product/pallas_call | solution.py:857
  402.3 28.9 %turned_product.5 = bf16[2048,2560]{1,0:T(8,128)(2,1)} custom-call(bf16[2048,2048]{1,0:T(8,128)(2,1)} %get-tuple-element.74.normed_ref.left_ref, bf16[2048,2560]{1,0:T(8,128)(2,1)} %pad_maximum_fusion.right_ref), custom_call_target="tpu_custom_call" | custom-call | flops 21474836480 | bytes 20000000 | tf_op jit(solution)/shard_map/turned_product/pallas_call | solution.py:857
  436.5 40.4 %collective-permute-done.13.top_ref = bf16[512,2048]{1,0:T(8,128)(2,1)S(1)} collective-permute-done((bf16[512,2048]{1,0:T(8,128)(2,1)}, bf16[512,2048]{1,0:T(8,128)(2,1)S(1)}, u32[]{:S(2)}, u32[]{:S(2)}) %collective-permute-start.13) | collective-permute-done | bytes 2097184 | tf_op jit(solution)/shard_map/ppermute | solution.py:1069
  490.5 18.6 %down_pass.1 = (bf16[512,2048]{1,0:T(8,128)(2,1)}, bf16[512,2048]{1,0:T(8,128)(2,1)}, bf16[1024,2048]{1,0:T(8,128)(2,1)}) custom-call(s32[8]{0:T(128)} %constant.43.clone.order_ref, bf16[2048,1280]{1,0:T(8,128)(2,1)} %get-tuple-element.89.left_ref.refs_0_, bf16[1280,2048]{1,0:T(8,128)(2,1)} %all-gather.8.cloned.1.call-done.down_ref.refs_1_), custom_call_target="tpu_custom_call" | custom-call | flops 10737418240 | bytes 40000000 | tf_op jit(solution)/shard_map/down_pass/pallas_call | solution.py:719
  509.1 12.3 %residual_back.1 = (f32[512,2048]{1,0:T(8,128)}, bf16[512,2048]{1,0:T(8,128)(2,1)}, f32[1,2048]{1,0:T(1,128)S(1)}, bf16[4,512,256]{2,1,0:T(8,128)(2,1)S(1)}) custom-call(bf16[1024,2048]{1,0:T(8,128)(2,1)} %get-tuple-element.81.keep_ref, bf16[512,2048]{1,0:T(8,128)(2,1)} %copy-done.26, bf16[512,2048]{1,0:T(8,128)(2,1)} %copy-done.27, ...), custom_call_target="tpu_custom_call" | custom-call | flops 2147483648 | bytes 30000000 | tf_op jit(solution)/shard_map/residual_back/pallas_call | solution.py:821
  538.7 23.5 %collective-permute-done.31 = bf16[256,2048]{1,0:T(8,128)(2,1)S(1)} collective-permute-done((bf16[256,2048]{1,0:T(8,128)(2,1)S(1)}, bf16[256,2048]{1,0:T(8,128)(2,1)S(1)}, u32[]{:S(2)}, u32[]{:S(2)}) %collective-permute-start.31) | collective-permute-done | bytes 1048608 | tf_op jit(solution)/shard_map/ppermute | solution.py:1069
  562.2 16.7 %collective-permute-done.30 = bf16[256,2048]{1,0:T(8,128)(2,1)S(1)} collective-permute-done((bf16[256,2048]{1,0:T(8,128)(2,1)S(1)}, bf16[256,2048]{1,0:T(8,128)(2,1)S(1)}, u32[]{:S(2)}, u32[]{:S(2)}) %collective-permute-start.30) | collective-permute-done | bytes 1048608 | tf_op jit(solution)/shard_map/ppermute | solution.py:1069
  586.0 34.1 %collective-permute-done.26.refs_2_ = bf16[2048,384]{1,0:T(8,128)(2,1)S(1)} collective-permute-done((bf16[2048,384]{1,0:T(8,128)(2,1)S(1)}, bf16[2048,384]{1,0:T(8,128)(2,1)S(1)}, u32[]{:S(2)}, u32[]{:S(2)}) %collective-permute-start.26) | collective-permute-done | bytes 1572896 | tf_op jit(solution)/shard_map/ppermute | solution.py:1069
  626.3 34.4 %attend_back.1 = (bf16[2048,256]{1,0:T(8,128)(2,1)S(1)}, f32[4096,128]{1,0:T(8,128)}) custom-call(s32[5]{0:T(128)S(1)} %pad_add_fusion.first_ref, bf16[2048,256]{1,0:T(8,128)(2,1)S(1)} %copy-done.23, s32[1,2048]{1,0:T(1,128)S(1)} %bitcast.38, bf16[4096,128]{1,0:T(8,128)(2,1)S(1)} %copy-done.9, bf16[2048,256]{1,0:T(8,128)(2,1)S(1)} %get-tuple-element.70.out_ref, ...), custom_call_target="tpu_custom_call" | custom-call | flops 40000000000 | bytes 12000000 | tf_op jit(solution)/shard_map/attend_back/pallas_call | solution.py:190
  666.3 18.7 %collective-permute-done.20 = bf16[512,2048]{1,0:T(8,128)(2,1)} collective-permute-done((bf16[512,2048]{1,0:T(8,128)(2,1)}, bf16[512,2048]{1,0:T(8,128)(2,1)}, u32[]{:S(2)}, u32[]{:S(2)}) %collective-permute-start.20) | collective-permute-done | bytes 2097184 | tf_op jit(solution)/shard_map/ppermute | solution.py:1069
  693.5 9.2 %project_back.1 = (bf16[2048,384]{1,0:T(8,128)(2,1)S(1)}, f32[1,320]{1,0:T(1,128)S(1)}) custom-call(s32[1]{0:T(128)} %bitcast.1.own_ref, bf16[2048,256]{1,0:T(8,128)(2,1)S(1)} %get-tuple-element.108.query_grad_ref, f32[4096,128]{1,0:T(8,128)} %get-tuple-element.105.pair_grad_ref, bf16[2048,128]{1,0:T(8,128)(2,1)S(1)} %collective-permute-done.22.returned_ref, ...), custom_call_target="tpu_custom_call" | custom-call | flops 8000000000 | bytes 8000000 | tf_op jit(solution)/shard_map/project_back/pallas_call | solution.py:375
  713.0 60.7 %finish.1 = (f32[512,2048]{1,0:T(8,128)}, f32[64,1536]{1,0:T(8,128)}, f32[8,128]{1,0:T(8,128)}) custom-call(bf16[2048,384]{1,0:T(8,128)(2,1)} %copy-done.1, bf16[2048,384]{1,0:T(8,128)(2,1)} %turned_product.7.qkv_ref, bf16[512,2048]{1,0:T(8,128)(2,1)} %x_ref.3, f32[512,2048]{1,0:T(8,128)} %get-tuple-element.113.residual_ref, f32[1,2048]{1,0:T(1,128)} %copy-done.11, ...), custom_call_target="tpu_custom_call" | custom-call | tf_op jit(solution)/shard_map/finish/pallas_call | solution.py:1040
  (240 shorter events, 151.0 us)
Async XLA Ops:
  7.2 150.5 %all-gather.4.cloned.1.call-start = ((), (), s32[]{:S(2)}) async-start(), calls=%async_computation.3 | async-start | bytes 1179648 | tf_op jit(solution)/shard_map/all_gather | solution.py:1131
  7.9 293.8 %all-gather.8.cloned.1.call-start = ((), (), s32[]{:S(2)}) async-start(), calls=%async_computation.5 | async-start | bytes 5898240 | tf_op jit(solution)/shard_map/all_gather | solution.py:1132
  8.7 293.1 %all-gather.6.cloned.1.call-start = ((), (), s32[]{:S(2)}) async-start(), calls=%async_computation.4 | async-start | bytes 11796480 | tf_op jit(solution)/shard_map/all_gather | solution.py:1135
  105.7 669.4 %reduce-scatter.6.cloned.1.call-start = ((), (), s32[]{:S(2)}) async-start(), calls=%async_computation.7 | async-start | bytes 11796480 | tf_op jit(solution)/shard_map/reduce_scatter | solution.py:1173
  135.5 75.7 %collective-permute-start.9 = (bf16[512,2048]{1,0:T(8,128)(2,1)}, bf16[512,2048]{1,0:T(8,128)(2,1)}, u32[]{:S(2)}, u32[]{:S(2)}) collective-permute-start(bf16[512,2048]{1,0:T(8,128)(2,1)} %cot_ref.1), channel_id=1, source_target_pairs={{0,8},{8,0},{16,24},{24,16},{1,9},{9,1},{17,25},{25,17},{2,10},{10... | collective-permute-start | bytes 6291464 | tf_op jit(solution)/shard_map/ppermute | solution.py:1069
  137.0 74.2 %collective-permute-start.10 = (bf16[512,2048]{1,0:T(8,128)(2,1)}, bf16[512,2048]{1,0:T(8,128)(2,1)}, u32[]{:S(2)}, u32[]{:S(2)}) collective-permute-start(bf16[512,2048]{1,0:T(8,128)(2,1)} %cot_ref.1), channel_id=1, source_target_pairs={{0,16},{8,24},{16,0},{24,8},{1,17},{9,25},{17,1},{25,9},{2,18},{10... | collective-permute-start | bytes 6291464 | tf_op jit(solution)/shard_map/ppermute | solution.py:1069
  155.9 50.9 %collective-permute-start.1 = (bf16[2048,256]{1,0:T(8,128)(2,1)}, bf16[2048,256]{1,0:T(8,128)(2,1)}, u32[]{:S(2)}, u32[]{:S(2)}) collective-permute-start(bf16[2048,256]{1,0:T(8,128)(2,1)} %pad_maximum_fusion.5.refs_0_), channel_id=1, source_target_pairs={{0,8},{8,0},{16,24},{24,16},{1,9},{9,1},{17,25},{25,17},{2,10},{10... | collective-permute-start | bytes 3145736 | tf_op jit(solution)/shard_map/ppermute | solution.py:1069
  157.1 52.2 %collective-permute-start.2 = (bf16[2048,256]{1,0:T(8,128)(2,1)}, bf16[2048,256]{1,0:T(8,128)(2,1)}, u32[]{:S(2)}, u32[]{:S(2)}) collective-permute-start(bf16[2048,256]{1,0:T(8,128)(2,1)} %pad_maximum_fusion.5.refs_0_), channel_id=1, source_target_pairs={{0,16},{8,24},{16,0},{24,8},{1,17},{9,25},{17,1},{25,9},{2,18},{10... | collective-permute-start | bytes 3145736 | tf_op jit(solution)/shard_map/ppermute | solution.py:1069
  157.7 71.4 %collective-permute-start.5 = (bf16[256,2048]{1,0:T(8,128)(2,1)}, bf16[256,2048]{1,0:T(8,128)(2,1)S(1)}, u32[]{:S(2)}, u32[]{:S(2)}) collective-permute-start(bf16[256,2048]{1,0:T(8,128)(2,1)} %all-gather.4.cloned.1.call-done.refs_0_), channel_id=1, source_target_pairs={{0,8},{8,0},{16,24},{24,16},{1,9},{9,1},{17,25},{25,17},{2,10},{10... | collective-permute-start | bytes 3145736 | tf_op jit(solution)/shard_map/ppermute | solution.py:1069
  207.8 72.4 %collective-permute-start.3 = (bf16[1024,256]{1,0:T(8,128)(2,1)S(1)}, bf16[1024,256]{1,0:T(8,128)(2,1)S(1)}, u32[]{:S(2)}, u32[]{:S(2)}) collective-permute-start(bf16[1024,256]{1,0:T(8,128)(2,1)S(1)} %slice.179), channel_id=1, source_target_pairs={{0,16},{8,24},{16,0},{24,8},{1,17},{9,25},{17,1},{25,9},{2,18},{10... | collective-permute-start | bytes 1572872 | tf_op jit(solution)/shard_map/ppermute | solution.py:1069
  212.5 55.1 %collective-permute-start.11 = (bf16[256,2048]{1,0:T(8,128)(2,1)S(1)}, bf16[256,2048]{1,0:T(8,128)(2,1)S(1)}, u32[]{:S(2)}, u32[]{:S(2)}) collective-permute-start(bf16[256,2048]{1,0:T(8,128)(2,1)S(1)} %slice.144), channel_id=1, source_target_pairs={{0,16},{8,24},{16,0},{24,8},{1,17},{9,25},{17,1},{25,9},{2,18},{10... | collective-permute-start | bytes 3145736 | tf_op jit(solution)/shard_map/ppermute | solution.py:1069
  215.3 53.9 %collective-permute-start.12 = (bf16[256,2048]{1,0:T(8,128)(2,1)S(1)}, bf16[256,2048]{1,0:T(8,128)(2,1)S(1)}, u32[]{:S(2)}, u32[]{:S(2)}) collective-permute-start(bf16[256,2048]{1,0:T(8,128)(2,1)S(1)} %slice.145), channel_id=1, source_target_pairs={{0,8},{8,0},{16,24},{24,16},{1,9},{9,1},{17,25},{25,17},{2,10},{10... | collective-permute-start | bytes 3145736 | tf_op jit(solution)/shard_map/ppermute | solution.py:1069
  229.1 51.2 %collective-permute-start.4 = (bf16[1024,256]{1,0:T(8,128)(2,1)S(1)}, bf16[1024,256]{1,0:T(8,128)(2,1)S(1)}, u32[]{:S(2)}, u32[]{:S(2)}) collective-permute-start(bf16[1024,256]{1,0:T(8,128)(2,1)S(1)} %slice.180), channel_id=1, source_target_pairs={{0,8},{8,0},{16,24},{24,16},{1,9},{9,1},{17,25},{25,17},{2,10},{10... | collective-permute-start | bytes 1572872 | tf_op jit(solution)/shard_map/ppermute | solution.py:1069
  431.2 355.2 %reduce-scatter.4.cloned.1.call-start = ((), (), s32[]{:S(2)}) async-start(), calls=%async_computation.6 | async-start | bytes 1179648 | tf_op jit(solution)/shard_map/reduce_scatter | solution.py:1212
  431.3 45.7 %collective-permute-start.13 = (bf16[512,2048]{1,0:T(8,128)(2,1)}, bf16[512,2048]{1,0:T(8,128)(2,1)S(1)}, u32[]{:S(2)}, u32[]{:S(2)}) collective-permute-start(bf16[512,2048]{1,0:T(8,128)(2,1)} %get-tuple-element.82), channel_id=1, source_target_pairs={{0,8},{8,0},{16,24},{24,16},{1,9},{9,1},{17,25},{25,17},{2,10},{10... | collective-permute-start | bytes 6291464 | tf_op jit(solution)/shard_map/ppermute | solution.py:1069
  432.8 45.4 %collective-permute-start.14 = (bf16[512,2048]{1,0:T(8,128)(2,1)}, bf16[512,2048]{1,0:T(8,128)(2,1)S(1)}, u32[]{:S(2)}, u32[]{:S(2)}) collective-permute-start(bf16[512,2048]{1,0:T(8,128)(2,1)} %get-tuple-element.83), channel_id=1, source_target_pairs={{0,16},{8,24},{16,0},{24,8},{1,17},{9,25},{17,1},{25,9},{2,18},{10... | collective-permute-start | bytes 6291464 | tf_op jit(solution)/shard_map/ppermute | solution.py:1069
  536.6 42.3 %collective-permute-start.30 = (bf16[256,2048]{1,0:T(8,128)(2,1)S(1)}, bf16[256,2048]{1,0:T(8,128)(2,1)S(1)}, u32[]{:S(2)}, u32[]{:S(2)}) collective-permute-start(bf16[256,2048]{1,0:T(8,128)(2,1)S(1)} %get-tuple-element.126), channel_id=1, source_target_pairs={{0,16},{8,24},{16,0},{24,8},{1,17},{9,25},{17,1},{25,9},{2,18},{10... | collective-permute-start | bytes 3145736 | tf_op jit(solution)/shard_map/ppermute | solution.py:1069
  537.6 41.3 %collective-permute-start.29 = (bf16[256,2048]{1,0:T(8,128)(2,1)S(1)}, bf16[256,2048]{1,0:T(8,128)(2,1)S(1)}, u32[]{:S(2)}, u32[]{:S(2)}) collective-permute-start(bf16[256,2048]{1,0:T(8,128)(2,1)S(1)} %get-tuple-element.124), channel_id=1, source_target_pairs={{0,8},{8,0},{16,24},{24,16},{1,9},{9,1},{17,25},{25,17},{2,10},{10... | collective-permute-start | bytes 3145736 | tf_op jit(solution)/shard_map/ppermute | solution.py:1069
  581.9 207.6 %reduce-scatter.8.cloned.1.call-start = ((), (), s32[]{:S(2)}) async-start(), calls=%async_computation.8 | async-start | bytes 5898240 | tf_op jit(solution)/shard_map/reduce_scatter | solution.py:1170
  621.2 42.4 %collective-permute-start.28 = (bf16[1024,384]{1,0:T(8,128)(2,1)}, bf16[1024,384]{1,0:T(8,128)(2,1)}, u32[]{:S(2)}, u32[]{:S(2)}) collective-permute-start(bf16[1024,384]{1,0:T(8,128)(2,1)} %slice.189), channel_id=1, source_target_pairs={{0,8},{8,0},{16,24},{24,16},{1,9},{9,1},{17,25},{25,17},{2,10},{10... | collective-permute-start | bytes 2359304 | tf_op jit(solution)/shard_map/ppermute | solution.py:1069
  624.4 60.6 %collective-permute-start.20 = (bf16[512,2048]{1,0:T(8,128)(2,1)}, bf16[512,2048]{1,0:T(8,128)(2,1)}, u32[]{:S(2)}, u32[]{:S(2)}) collective-permute-start(bf16[512,2048]{1,0:T(8,128)(2,1)} %get-tuple-element.98), channel_id=1, source_target_pairs={{0,8},{8,0},{16,24},{24,16},{1,9},{9,1},{17,25},{25,17},{2,10},{10... | collective-permute-start | bytes 6291464 | tf_op jit(solution)/shard_map/ppermute | solution.py:1069
  625.5 61.7 %collective-permute-start.21 = (bf16[512,2048]{1,0:T(8,128)(2,1)}, bf16[512,2048]{1,0:T(8,128)(2,1)}, u32[]{:S(2)}, u32[]{:S(2)}) collective-permute-start(bf16[512,2048]{1,0:T(8,128)(2,1)} %get-tuple-element.99), channel_id=1, source_target_pairs={{0,16},{8,24},{16,0},{24,8},{1,17},{9,25},{17,1},{25,9},{2,18},{10... | collective-permute-start | bytes 6291464 | tf_op jit(solution)/shard_map/ppermute | solution.py:1069
  691.6 89.3 %collective-permute-start.23 = (bf16[256,2048]{1,0:T(8,128)(2,1)}, bf16[256,2048]{1,0:T(8,128)(2,1)}, u32[]{:S(2)}, u32[]{:S(2)}) collective-permute-start(bf16[256,2048]{1,0:T(8,128)(2,1)} %get-tuple-element.127), channel_id=1, source_target_pairs={{0,16},{8,24},{16,0},{24,8},{1,17},{9,25},{17,1},{25,9},{2,18},{10... | collective-permute-start | bytes 3145736 | tf_op jit(solution)/shard_map/ppermute | solution.py:1069
  692.4 88.5 %collective-permute-start.24 = (bf16[256,2048]{1,0:T(8,128)(2,1)}, bf16[256,2048]{1,0:T(8,128)(2,1)}, u32[]{:S(2)}, u32[]{:S(2)}) collective-permute-start(bf16[256,2048]{1,0:T(8,128)(2,1)} %get-tuple-element.128), channel_id=1, source_target_pairs={{0,8},{8,0},{16,24},{24,16},{1,9},{9,1},{17,25},{25,17},{2,10},{10... | collective-permute-start | bytes 3145736 | tf_op jit(solution)/shard_map/ppermute | solution.py:1069
  (65 other events, 1384.9 us)
Sparse Core Ops, SparseCore 0:
  9.6 49.3 all-gather.3
  60.7 60.0 all-gather.7
  122.3 98.6 all-gather.5
  431.3 106.6 reduce-scatter.5
  582.0 29.4 reduce-scatter.3
  613.7 59.1 reduce-scatter.7

commit v3 on v2

--- a/solution.py
+++ b/solution.py
@@ -99,12 +99,9 @@
 def attend_back_kernel(
     heads, key_rows, scale, first_ref, query_ref, low_ref, pair_ref, out_ref, log_ref, *refs
 ):
-    *grad_refs, query_grad_ref, pair_grad_ref, turned_ref, sum_ref = refs
+    grads_ref, query_grad_ref, pair_grad_ref, turned_ref, sum_ref = refs
     step = pl.program_id(0)
-    peer = first_ref[pl.num_programs(0)] ^ step
-    grad = grad_refs[0][...]
-    for k in range(1, len(grad_refs)):
-        grad = jnp.where(peer == k, grad_refs[k][...], grad)
+    grad = grads_ref[first_ref[pl.num_programs(0)] ^ step]
     query_rows = query_ref.shape[0]
     dim = pair_ref.shape[1] // 2
 
@@ -193,7 +190,7 @@
             num_scalar_prefetch=1,
             grid=(count // query_rows,),
             in_specs=[tile, row, whole, tile, log_spec]
-            + [pl.BlockSpec((query_rows, width), lambda i, first: (0, 0))] * len(grads),
+            + [pl.BlockSpec(grads.shape, lambda i, first: (0, 0, 0))],
             out_specs=[tile, whole],
             scratch_shapes=[
                 pltpu.VMEM(pair.shape[::-1], jnp.bfloat16),
@@ -209,7 +206,7 @@
             flops=40_000_000_000, bytes_accessed=12_000_000, transcendentals=0
         ),
         name="attend_back",
-    )(first, queries, low, pair, out, logs, *grads)
+    )(first, queries, low, pair, out, logs, grads)
 
 
 def heads_apart(wide, dim):
@@ -650,9 +647,93 @@
     )(x, qkv_parts, in_weight)
 
 
+def spread_copies(source_ref, target_ref, send_sem, recv_sem):
+    head, blk = lax.axis_index("heads"), lax.axis_index("blk")
+    rows = source_ref.shape[0] // 2
+    quarter = rows // 2
+    start = pl.multiple_of(lax.rem(blk, 2) * rows, rows)
+    half = pl.ds(start, rows)
+    count = [0]
+
+    def copy(source, target, place):
+        index = count[0]
+        count[0] += 1
+        return pltpu.make_async_remote_copy(
+            src_ref=source,
+            dst_ref=target,
+            send_sem=send_sem.at[index],
+            recv_sem=recv_sem.at[index],
+            device_id=place,
+            device_id_type=MESH,
+        )
+
+    near = [
+        copy(source_ref.at[half], target_ref.at[k - 1, half], (head ^ k, blk)) for k in (1, 2)
+    ]
+    upper = pl.ds(start, quarter)
+    lower = pl.ds(pl.multiple_of(start + quarter, quarter), quarter)
+    far = [
+        copy(target_ref.at[0, upper], target_ref.at[2, upper], (head ^ 2, blk)),
+        copy(target_ref.at[1, lower], target_ref.at[2, lower], (head ^ 1, blk)),
+    ]
+    other = [
+        copy(target_ref.at[k, half], target_ref.at[k, half], (head, blk ^ 1)) for k in range(3)
+    ]
+    return near, far, other
+
+
+def greet_near(partner):
+    head, blk = lax.axis_index("heads"), lax.axis_index("blk")
+    barrier = pltpu.get_barrier_semaphore()
+    places = [(head ^ 1, blk), (head ^ 2, blk)] + ([(head, blk ^ 1)] if partner else [])
+    for place in places:
+        pl.semaphore_signal(barrier, inc=1, device_id=place, device_id_type=MESH)
+    pl.semaphore_wait(barrier, len(places))
+
+
+def spread_job(step, marks, source_ref, target_ref, send_sem, recv_sem):
+    near, far, other = spread_copies(source_ref, target_ref, send_sem, recv_sem)
+    begin_at, far_at, other_at = marks
+
+    @pl.when(step == begin_at)
+    def _():
+        greet_near(True)
+        for copy in near:
+            copy.start()
+
+    @pl.when(step == far_at)
+    def _():
+        for k in range(2):
+            near[k].wait_recv()
+            far[k].start()
+            other[k].start()
+
+    @pl.when(step == other_at)
+    def _():
+        for copy in far:
+            copy.wait_recv()
+        other[2].start()
+
+    def end():
+        for copy in near + far:
+            copy.wait_send()
+        for copy in other:
+            copy.wait()
+
+    return end
+
+
+SPREAD_COUNT = 7
+
+
 def hidden_kernel(
-    normed_ref, gate_ref, up_ref, cot_ref, down_ref, hidden_ref, gate_grad_ref, up_grad_ref
+    normed_ref, gate_ref, up_ref, cot_ref, down_ref, side_ref, hidden_ref, gate_grad_ref,
+    up_grad_ref, spread_ref, send_sem, recv_sem
 ):
+    steps = pl.num_programs(0) * pl.num_programs(1)
+    step = pl.program_id(0) * pl.num_programs(1) + pl.program_id(1)
+    marks = (0, steps // 2, steps - 2)
+    end = spread_job(step, marks, side_ref, spread_ref, send_sem, recv_sem)
     normed = normed_ref[...]
     gate = jnp.dot(normed, gate_ref[...], preferred_element_type=jnp.float32)
     upward = jnp.dot(normed, up_ref[...], preferred_element_type=jnp.float32)
@@ -666,14 +747,16 @@
         jnp.bfloat16
     )
     up_grad_ref[...] = (grad * activated).astype(jnp.bfloat16)
-
-
-def hidden_pass(normed, weight, cot, down, rows, units):
+    pl.when(step == steps - 1)(end)
+
+
+def hidden_pass(normed, weight, cot, down, side, rows, units):
     count, width = normed.shape
     total = down.shape[0]
     tiles = total // units
     out_spec = pl.BlockSpec((rows, units), lambda i, j: (i, j))
     out_shape = jax.ShapeDtypeStruct((count, total), jnp.bfloat16)
+    anywhere = pl.BlockSpec(memory_space=pl.ANY)
     return pl.pallas_call(
         hidden_kernel,
         grid=(count // rows, tiles),
@@ -683,166 +766,322 @@
             pl.BlockSpec((width, units), lambda i, j: (0, tiles + j)),
             pl.BlockSpec((rows, width), lambda i, j: (i, 0)),
             pl.BlockSpec((units, width), lambda i, j: (j, 0)),
-        ],
-        out_specs=[out_spec] * 3,
-        out_shape=[out_shape] * 3,
-        compiler_params=pltpu.CompilerParams(vmem_limit_bytes=58 << 20),
+            anywhere,
+        ],
+        out_specs=[out_spec] * 3 + [anywhere],
+        out_shape=[out_shape] * 3 + [jax.ShapeDtypeStruct((3, *side.shape), side.dtype)],
+        scratch_shapes=[pltpu.SemaphoreType.DMA((SPREAD_COUNT,))] * 2,
+        compiler_params=pltpu.CompilerParams(
+            collective_id=2, has_side_effects=True, vmem_limit_bytes=58 << 20
+        ),
         cost_estimate=pl.CostEstimate(
             flops=6 * count * width * total, bytes_accessed=70_000_000, transcendentals=0
         ),
         name="hidden_pass",
-    )(normed, weight, weight, cot, down)
-
-
-def shares_kernel(compute, order_ref, *refs):
-    *in_refs, one_ref, two_ref, rest_ref = refs
+    )(normed, weight, weight, cot, down, side)
+
+
+def in_order(step):
+    value = 3
+    for index, half in enumerate((2, 6, 5, 7, 0, 1, 4)):
+        value = jnp.where(step == index, half, value)
+    return value
+
+
+def tail_kernel(
+    normed_ref, gate_ref, up_ref, hidden_ref, in_hbm, down_hbm, in_sum_ref, out_ref, grad_ref,
+    weight_ref, one_ref, two_ref, rest_ref, top_ref, bottom_ref, last_ref, last_got_ref,
+    weight_sem, send_sem, recv_sem
+):
     step = pl.program_id(0)
-    value = compute(*in_refs).astype(jnp.bfloat16)
-
-    @pl.when(step < 2)
+    head, blk = lax.axis_index("heads"), lax.axis_index("blk")
+    rows, total = hidden_ref.shape
+    width = grad_ref.shape[1]
+    load_in = pltpu.make_async_copy(in_hbm, weight_ref, weight_sem.at[0])
+    load_down = pltpu.make_async_copy(
+        down_hbm, weight_ref.at[pl.ds(0, total), pl.ds(0, width)], weight_sem.at[1]
+    )
+
+    def copy(source, target, k, index):
+        return pltpu.make_async_remote_copy(
+            src_ref=source,
+            dst_ref=target,
+            send_sem=send_sem.at[index],
+            recv_sem=recv_sem.at[index],
+            device_id=(head ^ k, blk),
+            device_id_type=MESH,
+        )
+
+    send_one = copy(one_ref, top_ref, 1, 0)
+    send_two = copy(two_ref, bottom_ref, 2, 1)
+    send_top = copy(last_ref.at[0], last_got_ref.at[0], 2, 2)
+    send_bottom = copy(last_ref.at[1], last_got_ref.at[1], 1, 3)
+
+    def wide_of(block):
+        return block.astype(jnp.float32)
+
+    @pl.when(step == 0)
     def _():
-        one_ref[...] = value
-
-    @pl.when((step >= 2) & (step < 4))
+        load_in.start()
+        greet_near(False)
+        load_in.wait()
+
+    @pl.when(step < 8)
     def _():
-        two_ref[...] = value
-
-    @pl.when(step >= 4)
+        here = pl.ds(pl.multiple_of(in_order(step) * rows, rows), rows)
+        value = lax.dot_general(
+            gate_ref[here], weight_ref[:, :total], ROWS_IN_BOTH, preferred_element_type=jnp.float32
+        ) + lax.dot_general(
+            up_ref[here], weight_ref[:, total:], ROWS_IN_BOTH, preferred_element_type=jnp.float32
+        )
+        value = value.astype(jnp.bfloat16)
+
+        def rows_from(first):
+            return pl.ds(pl.multiple_of((step - first) * rows, rows), rows)
+
+        @pl.when(step < 2)
+        def _():
+            one_ref[rows_from(0)] = value
+
+        @pl.when((step >= 2) & (step < 4))
+        def _():
+            two_ref[rows_from(2)] = value
+
+        @pl.when(step >= 4)
+        def _():
+            rest_ref[rows_from(4)] = value
+
+        @pl.when(step == 1)
+        def _():
+            send_one.start()
+
+        @pl.when(step == 3)
+        def _():
+            send_two.start()
+
+        @pl.when(step == 7)
+        def _():
+            load_down.start()
+
+    @pl.when((step >= 8) & (step < 16))
     def _():
-        rest_ref[...] = value
-
-
-def shares(compute, left, right, right_specs, flops, name):
-    rows = left[0].shape[0] // 8
-    width = right[0].shape[0] if name == "back_pass" else right[0].shape[1]
-    order = jnp.array([2, 6, 5, 7, 0, 1, 4, 3], jnp.int32)
+        for part, ref in enumerate((gate_ref, up_ref)):
+            in_sum_ref[:, part * total : (part + 1) * total] = lax.dot_general(
+                normed_ref[...], ref[...], (((0,), (0,)), ((), ())),
+                preferred_element_type=jnp.float32,
+            ).astype(jnp.bfloat16)
+
+        @pl.when(step == 13)
+        def _():
+            send_one.wait_recv()
+            last_ref[0] = (
+                wide_of(rest_ref[2 * rows : 3 * rows]) + wide_of(top_ref[rows:])
+            ).astype(jnp.bfloat16)
+            send_top.start()
+
+        @pl.when(step == 15)
+        def _():
+            send_two.wait_recv()
+            last_ref[1] = (wide_of(rest_ref[3 * rows :]) + wide_of(bottom_ref[rows:])).astype(
+                jnp.bfloat16
+            )
+            send_bottom.start()
+            load_down.wait()
+
+    @pl.when(step >= 16)
+    def _():
+        out_ref[...] = jnp.dot(
+            hidden_ref[...], weight_ref[:total, :width], preferred_element_type=jnp.float32
+        ).astype(jnp.bfloat16)
+
+    @pl.when(step == pl.num_programs(0) - 1)
+    def _():
+        send_top.wait_recv()
+        send_bottom.wait_recv()
+        grad_ref[:rows] = (
+            wide_of(rest_ref[:rows]) + wide_of(top_ref[:rows]) + wide_of(last_got_ref[0])
+        )
+        grad_ref[rows:] = (
+            wide_of(rest_ref[rows : 2 * rows]) + wide_of(bottom_ref[:rows]) + wide_of(last_got_ref[1])
+        )
+        for sent in (send_one, send_two, send_top, send_bottom):
+            sent.wait_send()
+
+
+def feed_tail(normed, gate_grad, up_grad, hidden, weight, down):
+    count, width = normed.shape
+    total = hidden.shape[1]
+    rows = count // 8
+    anywhere = pl.BlockSpec(memory_space=pl.ANY)
+    once = pl.Buffered(1)
+
+    def stage(i, first):
+        return jnp.clip(i - first, 0, 7)
+
+    low = jnp.bfloat16
     return pl.pallas_call(
-        functools.partial(shares_kernel, compute),
-        grid_spec=pltpu.PrefetchScalarGridSpec(
-            num_scalar_prefetch=1,
-            grid=(8,),
-            in_specs=[
-                pl.BlockSpec((rows, a.shape[1]), lambda i, order: (order[i], 0)) for a in left
-            ]
-            + right_specs,
-            out_specs=[
-                pl.BlockSpec((rows, width), lambda i, order: (jnp.minimum(i, 1), 0)),
-                pl.BlockSpec((rows, width), lambda i, order: (jnp.clip(i - 2, 0, 1), 0)),
-                pl.BlockSpec((rows, width), lambda i, order: (jnp.clip(i - 4, 0, 3), 0)),
-            ],
-        ),
+        tail_kernel,
+        grid=(24,),
+        in_specs=[
+            pl.BlockSpec((count, rows), lambda i: (0, stage(i, 8))),
+            pl.BlockSpec((count, total), lambda i: (0, 0), pipeline_mode=once),
+            pl.BlockSpec((count, total), lambda i: (0, 0), pipeline_mode=once),
+            pl.BlockSpec((rows, total), lambda i: (in_order(stage(i, 16)), 0)),
+            anywhere,
+            anywhere,
+        ],
+        out_specs=[
+            pl.BlockSpec((rows, 2 * total), lambda i: (stage(i, 8), 0)),
+            pl.BlockSpec((rows, width), lambda i: (stage(i, 16), 0)),
+            pl.BlockSpec((2 * rows, width), lambda i: (0, 0), pipeline_mode=once),
+        ],
         out_shape=[
-            jax.ShapeDtypeStruct((count * rows, width), jnp.bfloat16) for count in (2, 2, 4)
-        ],
-        compiler_params=pltpu.CompilerParams(vmem_limit_bytes=58 << 20),
-        cost_estimate=pl.CostEstimate(flops=flops, bytes_accessed=40_000_000, transcendentals=0),
-        name=name,
-    )(order, *left, *right)
-
-
-def back_product(gate_ref, up_ref, gate_weight_ref, up_weight_ref):
-    return lax.dot_general(
-        gate_ref[...], gate_weight_ref[...], ROWS_IN_BOTH, preferred_element_type=jnp.float32
-    ) + lax.dot_general(
-        up_ref[...], up_weight_ref[...], ROWS_IN_BOTH, preferred_element_type=jnp.float32
-    )
-
-
-def back_pass(gate_grad, up_grad, weight):
-    width, total = weight.shape[0], gate_grad.shape[1]
-    specs = [
-        pl.BlockSpec((width, total), lambda i, order: (0, 0)),
-        pl.BlockSpec((width, total), lambda i, order: (0, 1)),
+            jax.ShapeDtypeStruct((width, 2 * total), low),
+            jax.ShapeDtypeStruct((count, width), low),
+            jax.ShapeDtypeStruct((2 * rows, width), jnp.float32),
+        ],
+        scratch_shapes=[
+            pltpu.VMEM(weight.shape, low),
+            pltpu.VMEM((2 * rows, width), low),
+            pltpu.VMEM((2 * rows, width), low),
+            pltpu.VMEM((4 * rows, width), low),
+            pltpu.VMEM((2 * rows, width), low),
+            pltpu.VMEM((2 * rows, width), low),
+            pltpu.VMEM((2, rows, width), low),
+            pltpu.VMEM((2, rows, width), low),
+            pltpu.SemaphoreType.DMA((2,)),
+            pltpu.SemaphoreType.DMA((4,)),
+            pltpu.SemaphoreType.DMA((4,)),
+        ],
+        compiler_params=pltpu.CompilerParams(
+            collective_id=3, has_side_effects=True, vmem_limit_bytes=60 << 20
+        ),
+        cost_estimate=pl.CostEstimate(
+            flops=10 * count * width * total, bytes_accessed=70_000_000, transcendentals=0
+        ),
+        name="feed_tail",
+    )(normed, gate_grad, up_grad, hidden, weight, down)
+
+
+def residual_back_kernel(
+    grad_sum_ref, residual_ref, cot_ref, gain_ref, attended_ref, *refs
+):
+    size = lax.axis_size("heads")
+    weight_refs, refs = refs[:size], refs[size:]
+    (
+        grad_ref, gain_grad_ref, out_sum_ref, pieces_ref, branch_ref, mine_ref, own_sem, send_sem,
+        recv_sem,
+    ) = refs
+    step = pl.program_id(0)
+    last = pl.num_programs(0) - 1
+    head, blk = lax.axis_index("heads"), lax.axis_index("blk")
+    rows = cot_ref.shape[0]
+    copies = [
+        pltpu.make_async_remote_copy(
+            src_ref=mine_ref.at[k],
+            dst_ref=pieces_ref.at[k],
+            send_sem=send_sem.at[k - 1],
+            recv_sem=recv_sem.at[k - 1],
+            device_id=(head ^ k, blk),
+            device_id_type=MESH,
+        )
+        for k in range(1, size)
     ]
-    flops = 4 * gate_grad.shape[0] * width * total
-    return shares(back_product, [gate_grad, up_grad], [weight] * 2, specs, flops, "back_pass")
-
-
-def down_product(hidden_ref, weight_ref):
-    return jnp.dot(hidden_ref[...], weight_ref[...], preferred_element_type=jnp.float32)
-
-
-def down_pass(hidden, weight):
-    specs = [pl.BlockSpec(weight.shape, lambda i, order: (0, 0))]
-    flops = 2 * hidden.shape[0] * weight.shape[0] * weight.shape[1]
-    return shares(down_product, [hidden], [weight], specs, flops, "down_pass")
-
-
-def residual_back_kernel(
-    keep_ref, top_ref, bottom_ref, top_last_ref, bottom_last_ref, residual_ref, cot_ref, gain_ref,
-    *refs
-):
-    *weight_refs, grad_ref, branch_ref, gain_grad_ref, attended_ref = refs
-    step = pl.program_id(0)
-    first = step < pl.num_programs(0) // 2
+    keep = pltpu.make_async_copy(mine_ref.at[0], pieces_ref.at[0], own_sem)
 
     @pl.when(step == 0)
     def _():
         gain_grad_ref[...] = jnp.zeros_like(gain_grad_ref)
-
-    def wide(ref):
-        return ref[...].astype(jnp.float32)
-
-    gradient = wide(keep_ref) + jnp.where(
-        first, wide(top_ref) + wide(top_last_ref), wide(bottom_ref) + wide(bottom_last_ref)
-    )
-    values = residual_ref[...]
-    inverse = lax.rsqrt(jnp.mean(values * values, axis=-1, keepdims=True) + EPS)
-    gain_grad_ref[...] += jnp.sum(gradient * values * inverse, axis=0, keepdims=True)
-    scaled = gradient * gain_ref[...]
-    moment = jnp.mean(scaled * values, axis=-1, keepdims=True)
-    total = wide(cot_ref) + inverse * scaled - values * (inverse * inverse * inverse * moment)
-    grad_ref[...] = total
-    branch = total.astype(jnp.bfloat16)
-    branch_ref[...] = branch
-    for k, weight_ref in enumerate(weight_refs):
-        attended_ref[k] = lax.dot_general(
-            branch, weight_ref[...], ROWS_IN_BOTH, preferred_element_type=jnp.float32
-        ).astype(jnp.bfloat16)
-
-
-def residual_back(keep, top, bottom, top_last, bottom_last, residual, cot, gain, weights, rows):
+        barrier = pltpu.get_barrier_semaphore()
+        for k in range(1, size):
+            pl.semaphore_signal(barrier, inc=1, device_id=(head ^ k, blk), device_id_type=MESH)
+        pl.semaphore_wait(barrier, size - 1)
+
+    @pl.when(step < last)
+    def _():
+        here = pl.ds(pl.multiple_of(step * rows, rows), rows)
+        gradient = grad_sum_ref[...]
+        values = residual_ref[...]
+        inverse = lax.rsqrt(jnp.mean(values * values, axis=-1, keepdims=True) + EPS)
+        gain_grad_ref[...] += jnp.sum(gradient * values * inverse, axis=0, keepdims=True)
+        scaled = gradient * gain_ref[...]
+        moment = jnp.mean(scaled * values, axis=-1, keepdims=True)
+        total = cot_ref[...].astype(jnp.float32) + (
+            inverse * scaled - values * (inverse * inverse * inverse * moment)
+        )
+        grad_ref[...] = total
+        branch = total.astype(jnp.bfloat16)
+        branch_ref[here] = branch
+        for k, weight_ref in enumerate(weight_refs):
+            mine_ref[k, here] = lax.dot_general(
+                branch, weight_ref[...], ROWS_IN_BOTH, preferred_element_type=jnp.float32
+            ).astype(jnp.bfloat16)
+
+    @pl.when(step == last)
+    def _():
+        for copy in copies:
+            copy.start()
+        keep.start()
+        columns = attended_ref.shape[1] // size
+        for k in range(size):
+            out_sum_ref[k * columns : (k + 1) * columns] = lax.dot_general(
+                attended_ref[:, k * columns : (k + 1) * columns],
+                branch_ref[...],
+                (((0,), (0,)), ((), ())),
+                preferred_element_type=jnp.float32,
+            ).astype(jnp.bfloat16)
+        for copy in copies:
+            copy.wait()
+        keep.wait()
+
+
+def residual_back(grad_sum, residual, cot, gain, attended, weights, rows):
     count, width = cot.shape
+    size = len(weights)
     columns = weights[0].shape[0]
-    tiles = count // 2 // rows
+    tiles = count // rows
 
     def there(i):
-        return (i, 0)
-
-    def in_half(i):
-        return (i % tiles, 0)
+        return (jnp.minimum(i, tiles - 1), 0)
 
     def whole(i):
         return (0, 0)
 
     tile = pl.BlockSpec((rows, width), there)
-    half = pl.BlockSpec((rows, width), in_half)
     row = pl.BlockSpec((1, width), whole)
+    pieces = (size, count, columns)
     return pl.pallas_call(
         residual_back_kernel,
-        grid=(count // rows,),
-        in_specs=[tile, half, half, half, half, tile, tile, row]
+        grid=(tiles + 1,),
+        in_specs=[tile, tile, tile, row, pl.BlockSpec(attended.shape, whole)]
         + [pl.BlockSpec(weight.shape, whole) for weight in weights],
         out_specs=[
             tile,
-            tile,
             row,
-            pl.BlockSpec((len(weights), rows, columns), lambda i: (0, i, 0)),
+            pl.BlockSpec((size * columns, width), whole),
+            pl.BlockSpec(memory_space=pl.ANY),
         ],
         out_shape=[
             jax.ShapeDtypeStruct((count, width), jnp.float32),
-            jax.ShapeDtypeStruct((count, width), jnp.bfloat16),
             jax.ShapeDtypeStruct((1, width), jnp.float32),
-            jax.ShapeDtypeStruct((len(weights), count, columns), jnp.bfloat16),
-        ],
-        compiler_params=pltpu.CompilerParams(vmem_limit_bytes=48 << 20),
+            jax.ShapeDtypeStruct((size * columns, width), jnp.bfloat16),
+            jax.ShapeDtypeStruct(pieces, jnp.bfloat16),
+        ],
+        scratch_shapes=[
+            pltpu.VMEM((count, width), jnp.bfloat16),
+            pltpu.VMEM(pieces, jnp.bfloat16),
+            pltpu.SemaphoreType.DMA,
+            pltpu.SemaphoreType.DMA((size - 1,)),
+            pltpu.SemaphoreType.DMA((size - 1,)),
+        ],
+        compiler_params=pltpu.CompilerParams(
+            collective_id=4, has_side_effects=True, vmem_limit_bytes=56 << 20
+        ),
         cost_estimate=pl.CostEstimate(
-            flops=2 * count * width * columns * len(weights),
-            bytes_accessed=30_000_000,
-            transcendentals=0,
+            flops=4 * count * width * columns * size, bytes_accessed=30_000_000, transcendentals=0
         ),
         name="residual_back",
-    )(keep, top, bottom, top_last, bottom_last, residual, cot, gain, *weights)
+    )(grad_sum, residual, cot, gain, attended, *weights)
 
 
 def turned_kernel(left_ref, right_ref, out_ref):
@@ -872,13 +1111,15 @@
 
 
 def finish_kernel(
-    query_width, dim, sent_ref, qkv_ref, x_ref, residual_ref, gain_ref, ffn_ref, head_ref, *refs
+    query_width, dim, sent_ref, qkv_ref, x_ref, residual_ref, gain_ref, ffn_ref, head_ref,
+    weight_ref, weights_ref, *refs
 ):
     size, blk_size = lax.axis_size("heads"), lax.axis_size("blk")
-    weight_refs, refs = refs[:size], refs[size:]
+    out_refs, refs = refs[:size], refs[size:]
     (
-        grad_ref, qkv_grad_ref, gains_ref, got_ref, qkv_got_ref, part_ref, gain_got_ref, s_send,
-        s_recv, q_send, q_recv, g_send, g_recv,
+        grad_ref, qkv_grad_ref, gains_ref, out_grad_ref, got_ref, qkv_got_ref, part_ref,
+        gain_got_ref, out_part_ref, out_got_ref, s_send, s_recv, q_send, q_recv, g_send, g_recv,
+        o_send, o_recv,
     ) = refs
     devices = size * blk_size
     head, blk = lax.axis_index("heads"), lax.axis_index("blk")
@@ -927,6 +1168,19 @@
             device_id_type=MESH,
         )
 
+    out_rows = out_grad_ref.shape[0]
+
+    def out_copy(k, slot):
+        other = lax.rem(blk + k, blk_size)
+        return pltpu.make_async_remote_copy(
+            src_ref=out_part_ref.at[other],
+            dst_ref=out_got_ref.at[slot],
+            send_sem=o_send.at[k],
+            recv_sem=o_recv.at[slot],
+            device_id=(head, other),
+            device_id_type=MESH,
+        )
+
     def gain_copy(k, slot):
         other = lax.rem(own + k, devices)
         return pltpu.make_async_remote_copy(
@@ -944,6 +1198,23 @@
 
     lax.fori_loop(1, devices, start_qkv, 0)
     qkv_got_ref[own] = qkv_ref[rows_of(own)]
+
+    def out_sum(index, carried):
+        here = pl.ds(pl.multiple_of(index * out_rows, out_rows), out_rows)
+        total = out_refs[0][here].astype(jnp.float32)
+        for ref in out_refs[1:]:
+            total += ref[here].astype(jnp.float32)
+        out_part_ref[index, :out_rows] = total.astype(jnp.bfloat16)
+        return carried
+
+    lax.fori_loop(0, blk_size, out_sum, 0)
+
+    def start_out(k, carried):
+        out_copy(k, blk).start()
+        return carried
+
+    lax.fori_loop(1, blk_size, start_out, 0)
+    out_got_ref[blk] = out_part_ref[blk]
     for copy in sends:
         copy.wait_recv()
 
@@ -952,12 +1223,12 @@
     def tile(index, gain_sum):
         here = pl.ds(pl.multiple_of(index * rows, rows), rows)
         normed_grad = lax.dot_general(
-            sent_ref[here], weight_refs[0][...], ROWS_IN_BOTH, preferred_element_type=jnp.float32
+            sent_ref[here], weight_ref[...], ROWS_IN_BOTH, preferred_element_type=jnp.float32
         )
         for k in range(1, size):
             normed_grad += lax.dot_general(
                 got_ref[k - 1, here],
-                weight_refs[k][...],
+                weights_ref[k - 1],
                 ROWS_IN_BOTH,
                 preferred_element_type=jnp.float32,
             )
@@ -1010,8 +1281,18 @@
         return carried
 
     lax.fori_loop(1, devices, finish, 0)
+
+    def finish_out(k, carried):
+        out_copy(k, lax.rem(blk + blk_size - k, blk_size)).wait()
+        return carried
+
+    lax.fori_loop(1, blk_size, finish_out, 0)
     for copy in sends:
         copy.wait_send()
+    out_total = out_got_ref[0, :out_rows].astype(jnp.float32)
+    for b in range(1, blk_size):
+        out_total += out_got_ref[b, :out_rows].astype(jnp.float32)
+    out_grad_ref[...] = out_total
     gains_ref[...] = jnp.sum(gain_got_ref[...], axis=0)
 
     def group_sum(h):
@@ -1030,11 +1311,15 @@
     )
 
 
-def finish(sent, qkv_part, x, residual_grad, gain, ffn_sum, head_sum, weights, query_width, dim):
+def finish(
+    sent, qkv_part, x, residual_grad, gain, ffn_sum, head_sum, weight, weights, outs, query_width, dim
+):
     size, blk_size = lax.axis_size("heads"), lax.axis_size("blk")
     devices = size * blk_size
     count, width = x.shape
     depth, joined = width // devices, sent.shape[1]
+    out_rows = outs[0].shape[0] // blk_size
+    held_rows = -(-out_rows // 16) * 16
     vmem = pl.BlockSpec(memory_space=pltpu.VMEM)
     sems = pltpu.SemaphoreType.DMA
     return pl.pallas_call(
@@ -1043,26 +1328,31 @@
             jax.ShapeDtypeStruct((count, width), jnp.float32),
             jax.ShapeDtypeStruct((depth, size * joined), jnp.float32),
             jax.ShapeDtypeStruct((8, 128), jnp.float32),
-        ],
-        in_specs=[vmem] * (7 + size),
-        out_specs=[vmem] * 3,
+            jax.ShapeDtypeStruct((out_rows, width), jnp.float32),
+        ],
+        in_specs=[vmem] * (9 + size),
+        out_specs=[vmem] * 4,
         scratch_shapes=[
             pltpu.VMEM((size - 1, count, joined), jnp.bfloat16),
             pltpu.VMEM((devices, depth, joined), jnp.bfloat16),
             pltpu.VMEM((devices, 8, 128), jnp.float32),
             pltpu.VMEM((devices, 8, 128), jnp.float32),
+            pltpu.VMEM((blk_size, held_rows, width), jnp.bfloat16),
+            pltpu.VMEM((blk_size, held_rows, width), jnp.bfloat16),
             sems((size - 1,)),
             sems((size - 1,)),
             sems((devices,)),
             sems((devices,)),
             sems((devices,)),
             sems((devices,)),
+            sems((blk_size,)),
+            sems((blk_size,)),
         ],
         compiler_params=pltpu.CompilerParams(
             collective_id=0, has_side_effects=True, vmem_limit_bytes=56 << 20
         ),
         name="finish",
-    )(sent, qkv_part, x, residual_grad, gain, ffn_sum, head_sum, *weights)
+    )(sent, qkv_part, x, residual_grad, gain, ffn_sum, head_sum, weight, weights, *outs)
 
 
 def permute(block, axis, k):
@@ -1161,30 +1451,20 @@
     cotangent_near = gather_near(after(cotangent, inputs_blk), near[1])
     cotangent_blk = jnp.concatenate(cotangent_near, axis=0)
 
-    hidden, gate_grad, up_grad = hidden_pass(
-        ffn_normed, in_group, cotangent_blk, down_group, block_len // 2, 256
-    )
-    one, two, rest = back_pass(gate_grad, up_grad, in_group)
-    top, bottom = permute(one, "heads", 1), permute(two, "heads", 2)
-    down_sum = turned_product(after(hidden, rest), cotangent_blk, 256)
-    ffn_out_grad = wide(lax.psum_scatter(down_sum, "blk", scatter_dimension=0, tiled=True))
-    gate_up_grad = jnp.concatenate([gate_grad, up_grad], axis=1)
-    in_sum = turned_product(ffn_normed, after(gate_up_grad, down_sum), 256)
+    qkv_group = qkv_rows[:, :qkv_width]
+    hidden, gate_grad, up_grad, qkv_peers = hidden_pass(
+        ffn_normed, in_group, cotangent_blk, down_group, qkv_group, block_len // 2, 256
+    )
+    down_sum = turned_product(hidden, cotangent_blk, 256)
+    ffn_out_grad = lax.psum_scatter(down_sum, "blk", scatter_dimension=0, tiled=True)
+    in_sum, out_terms, grad_sum = feed_tail(
+        ffn_normed, gate_grad, up_grad, after(hidden, down_sum), in_group, down_group
+    )
+    in_sum, ffn_out_grad = lax.optimization_barrier((in_sum, ffn_out_grad))
     in_part = lax.psum_scatter(
         in_sum.reshape(size, blk_size * depth, -1), "blk", scatter_dimension=1, tiled=True
     )
-    top, bottom, in_sum = lax.optimization_barrier((top, bottom, in_sum))
-    top_send = (wide(rest[2 * half : 3 * half]) + wide(top[half:])).astype(jnp.bfloat16)
-    bottom_send = (wide(rest[3 * half :]) + wide(bottom[half:])).astype(jnp.bfloat16)
-    top_last, bottom_last = permute(top_send, "heads", 2), permute(bottom_send, "heads", 1)
-    out_one, out_two, out_rest = down_pass(after(hidden, top_send, bottom_send), down_group)
-    top_last, bottom_last, out_rest = lax.optimization_barrier((top_last, bottom_last, out_rest))
-
-    residual_grad, branch_grad, ffn_sum, attended_grad = residual_back(
-        rest, top, bottom, top_last, bottom_last, residual_own, cotangent, ffn_scaling, out_all,
-        min(128, half)
-    )
-    grads = [attended_grad[0]] + [permute(attended_grad[k], "heads", k) for k in range(1, size)]
+    ffn_out_grad = wide(ffn_out_grad)
     attended_own = jnp.concatenate(
         [
             near[0][:token_count],
@@ -1194,23 +1474,22 @@
         ],
         axis=1,
     )
-    out_sum = turned_product(attended_own, branch_grad, 256)
-    *grads, out_sum, out_one, out_two = lax.optimization_barrier(
-        (*grads, out_sum, out_one, out_two)
-    )
+    residual_grad, ffn_sum, out_sum, grads = residual_back(
+        grad_sum, residual_own, cotangent, ffn_scaling, attended_own, out_all, min(128, half)
+    )
+    out_one, out_two, out_rest = (
+        out_terms[: 2 * half],
+        out_terms[2 * half : 4 * half],
+        out_terms[4 * half :],
+    )
+    out_one, out_two, grads = lax.optimization_barrier((out_one, out_two, grads))
     out_top, out_bottom = permute(out_one, "heads", 1), permute(out_two, "heads", 2)
+    out_slices = [out_sum[k * query_width : (k + 1) * query_width] for k in range(size)]
+    out_slices = [out_slices[0]] + [permute(out_slices[k], "heads", k) for k in range(1, size)]
     query_grad, pair_sum = attend_back(
         query_low, pair_all, first, low, grads, attended_blk, logs, group_size, query_rows, key_rows
     )
     returned = from_behind(pair_sum[:block_len].astype(jnp.bfloat16), "blk", -1)
-    out_peers = [
-        permute(out_sum[k * query_width : (k + 1) * query_width], "heads", k)
-        for k in range(1, size)
-    ]
-    out_part = sum(wide(part) for part in out_peers) + wide(out_sum[:query_width])
-    out_grad = wide(
-        lax.psum_scatter(out_part.astype(jnp.bfloat16), "blk", scatter_dimension=0, tiled=True)
-    )
     out_top, out_bottom, returned = lax.optimization_barrier((out_top, out_bottom, returned))
     top_send = (wide(out_rest[2 * half : 3 * half]) + wide(out_top[half:])).astype(jnp.bfloat16)
     bottom_send = (wide(out_rest[3 * half :]) + wide(out_bottom[half:])).astype(jnp.bfloat16)
@@ -1231,11 +1510,9 @@
         own, query_grad, pair_sum, returned, raw, head_gain, cosine, sine, size, 256
     )
     qkv_part = turned_product(normed, projected_grad, 512)
-    qkv_near = gather_near(after(qkv_rows[:, :qkv_width], out_near[1], near[1], cotangent_blk))
-    qkv_all = (*qkv_near[:3], jnp.concatenate(qkv_near[3:], axis=0))
-    input_grad, qkv_grad, gains = finish(
-        projected_grad, qkv_part, inputs, residual_grad, attn_scaling, ffn_sum, head_sum, qkv_all,
-        query_width, head_dim
+    input_grad, qkv_grad, gains, out_grad = finish(
+        projected_grad, qkv_part, inputs, residual_grad, attn_scaling, ffn_sum, head_sum, qkv_group,
+        qkv_peers, out_slices, query_width, head_dim
     )
     in_pieces = [pick(in_part, k, "heads", 0)[0] for k in range(size)]
     ffn_in_grad = settle(

time: 824 us -> 722 us (0.88)
  waiting for transfers between devices: 244 us -> 132 us
  Pallas kernels: 424 us -> 476 us
  other arithmetic: 42.6 us -> 19.2 us
  starting transfers between devices: 40.8 us -> 25.1 us
    ppermute x33 -> x22, waiting for transfers between devices: 242 us -> 130 us  [permute(): lax.ppermute(block, axis, [(i, i ^ k) for i in range(lax.axis_size(axis))])]
    pallas_call x3 -> x2, Pallas kernels: 62.3 us -> 124 us  [the longest x1 96.3 us: feed_tail(): pl.pallas_call(tail_kernel, grid=(24,), in_specs=[pl.BlockSpec((count, ro...]
    pallas_call x4 -> x2, Pallas kernels: 60.3 us -> 25.1 us  [turned_product(): pl.pallas_call(turned_kernel, grid=(height // rows,), in_specs=[pl.BlockS...]
    pallas_call x1, Pallas kernels: 60.7 us -> 82.4 us  [finish(): pl.pallas_call(functools.partial(finish_kernel, query_width, dim), out_sh...]
    ppermute x33 -> x22, starting transfers between devices: 37.2 us -> 21.6 us  [permute(): lax.ppermute(block, axis, [(i, i ^ k) for i in range(lax.axis_size(axis))])]
    concatenate x2 -> x0, other arithmetic: 12.3 us -> none  [the longest x1 9.6 us: local(): gate_up_grad = jnp.concatenate([gate_grad, up_grad], axis=1)]
    unnamed x105 -> x80, local copies, waits for them, and re-layouts: 19.4 us -> 19.4 us
  transfers between devices with their start and end apart: 41 -> 29, of which waited for: 15 -> 9; matrix products, arithmetic and copies ran while one was open for 8% -> 8% of each run, Pallas kernels for 37% -> 57%
where the time goes in v3:
time: 722 us; the launch traced here: 715 us
  Pallas kernels  476 us (66%)
  waiting for transfers between devices  132 us (18%)
  local copies, waits for them, and re-layouts  48.8 us (7%)
  starting transfers between devices  25.1 us (3%)
  other arithmetic  19.2 us (3%)
  between operations  14.9 us (2%)
    ppermute x22, waiting for transfers between devices, permute(): lax.ppermute(block, axis, [(i, i ^ k) for i in range(lax.axis_size(axis))])  130 us
    pallas_call x1, Pallas kernels, feed_tail(): pl.pallas_call(tail_kernel, grid=(24,), in_specs=[pl.BlockSpec((count, ro...  96.3 us
    pallas_call x1, Pallas kernels, begin(): pl.pallas_call(begin_kernel, out_shape=[jax.ShapeDtypeStruct((size * coun...  92.6 us
    pallas_call x1, Pallas kernels, finish(): pl.pallas_call(functools.partial(finish_kernel, query_width, dim), out_sh...  82.4 us
    pallas_call x1, Pallas kernels, hidden_pass(): pl.pallas_call(hidden_kernel, grid=(count // rows, tiles), in_specs=[pl.B...  44.3 us
    pallas_call x1, Pallas kernels, attend_back(): pl.pallas_call(functools.partial(attend_back_kernel, heads, key_rows, (wi...  34.8 us
    pallas_call x1, Pallas kernels, residual_back(): pl.pallas_call(residual_back_kernel, grid=(tiles + 1,), in_specs=[tile, t...  28.1 us
    pallas_call x2, Pallas kernels, turned_product(): pl.pallas_call(turned_kernel, grid=(height // rows,), in_specs=[pl.BlockS...  25.1 us
  transfers between devices with their start and end apart: 29, of which 9 were waited for; matrix products, arithmetic and copies ran while one was open for 8% of the time, Pallas kernels for 57%

profile of v3, /device:TPU:0, one launch (start us, length us, event | category | flops | bytes accessed | tf_op | source)
XLA Modules:
  0.0 715.4 jit_solution(11052843685643709614)
XLA Ops:
  13.0 92.6 %begin.1 = (bf16[2048,2048]{1,0:T(8,128)(2,1)}, bf16[4,512,512]{2,1,0:T(8,128)(2,1)}, bf16[4,64,2560]{2,1,0:T(8,128)(2,1)}) custom-call(bf16[512,2048]{1,0:T(8,128)(2,1)} %x_ref.3, bf16[4,64,512]{2,1,0:T(8,128)(2,1)} %bitcast.32, bf16[64,10240]{1,0:T(8,128)(2,1)} %in_ref.1), custom_call_target="tpu_custom_call" | custom-call | tf_op jit(solution)/shard_map/begin/pallas_call | solution.py:625
  111.2 22.8 %project.1 = (bf16[2048,256]{1,0:T(8,128)(2,1)S(1)}, bf16[2048,128]{1,0:T(8,128)(2,1)S(1)}, f32[2048,384]{1,0:T(8,128)}, bf16[2048,2048]{1,0:T(8,128)(2,1)}, f32...) custom-call(s32[1]{0:T(128)} %bitcast.1.own_ref, bf16[2048,2048]{1,0:T(8,128)(2,1)} %get-tuple-element.55.x_ref, ...), custom_call_target="tpu_custom_call" | custom-call | flops 6442450944 | bytes 30000000 | tf_op jit(solution)/shard_map/project/pallas_call | solution.py:297
  141.3 16.2 %attend.1 = (bf16[2048,256]{1,0:T(8,128)(2,1)S(1)}, f32[4,1,2048]{2,1,0:T(1,128)S(1)}) custom-call(s32[5]{0:T(128)S(1)} %pad_add_fusion.first_ref, bf16[2048,256]{1,0:T(8,128)(2,1)S(1)} %copy-done.15, s32[1,2048]{1,0:T(1,128)S(1)} %bitcast.29, bf16[4096,128]{1,0:T(8,128)(2,1)S(1)} %constant_dynamic-update-slice_fusion.pair_ref), custom_call_target="tpu_custom_call" | custom-call | flops 20000000000 | bytes 8000000 | tf_op jit(solution)/shard_map/attend/pallas_call | solution.py:158
  165.1 45.1 %collective-permute-done.1.refs_1_ = bf16[2048,256]{1,0:T(8,128)(2,1)} collective-permute-done((bf16[2048,256]{1,0:T(8,128)(2,1)}, bf16[2048,256]{1,0:T(8,128)(2,1)}, u32[]{:S(2)}, u32[]{:S(2)}) %collective-permute-start.1) | collective-permute-done | bytes 1048608 | tf_op jit(solution)/shard_map/ppermute | solution.py:1359
  223.1 9.6 %collective-permute-done.5.refs_1_ = bf16[256,2048]{1,0:T(8,128)(2,1)S(1)} collective-permute-done((bf16[256,2048]{1,0:T(8,128)(2,1)}, bf16[256,2048]{1,0:T(8,128)(2,1)S(1)}, u32[]{:S(2)}, u32[]{:S(2)}) %collective-permute-start.5) | collective-permute-done | bytes 1048608 | tf_op jit(solution)/shard_map/ppermute | solution.py:1359
  233.4 15.3 %collective-permute-done.6.refs_2_ = bf16[256,2048]{1,0:T(8,128)(2,1)S(1)} collective-permute-done((bf16[256,2048]{1,0:T(8,128)(2,1)S(1)}, bf16[256,2048]{1,0:T(8,128)(2,1)S(1)}, u32[]{:S(2)}, u32[]{:S(2)}) %collective-permute-start.6) | collective-permute-done | bytes 1048608 | tf_op jit(solution)/shard_map/ppermute | solution.py:1359
  249.4 21.8 %collective-permute-done.11 = bf16[256,2048]{1,0:T(8,128)(2,1)S(1)} collective-permute-done((bf16[256,2048]{1,0:T(8,128)(2,1)S(1)}, bf16[256,2048]{1,0:T(8,128)(2,1)S(1)}, u32[]{:S(2)}, u32[]{:S(2)}) %collective-permute-start.11) | collective-permute-done | bytes 1048608 | tf_op jit(solution)/shard_map/ppermute | solution.py:1359
  272.1 9.0 %collective-permute-done.7 = bf16[128,2048]{1,0:T(8,128)(2,1)S(1)} collective-permute-done((bf16[128,2048]{1,0:T(8,128)(2,1)S(1)}, bf16[128,2048]{1,0:T(8,128)(2,1)S(1)}, u32[]{:S(2)}, u32[]{:S(2)}) %collective-permute-start.7) | collective-permute-done | bytes 524320 | tf_op jit(solution)/shard_map/ppermute | solution.py:1359
  284.5 18.5 %join.1 = (f32[2048,2048]{1,0:T(8,128)}, bf16[2048,2048]{1,0:T(8,128)(2,1)}) custom-call(bf16[2048,2048]{1,0:T(8,128)(2,1)} %get-tuple-element.55.x_ref, bf16[2048,256]{1,0:T(8,128)(2,1)} %pad_maximum_fusion.3.refs_0_, bf16[2048,256]{1,0:T(8,128)(2,1)} %collective-permute-done.1.refs_1_, bf16[2048,256]{1,0:T(8,128)(2,1)} %collective-permute-done.2.refs_2_, ...), custom_call_target="tpu_custom_call" | custom-call | flops 8589934592 | bytes 50000000 | tf_op jit(solution)/shard_map/join/pallas_call | solution.py:433
  303.0 44.3 %hidden_pass.1 = (bf16[2048,1280]{1,0:T(8,128)(2,1)}, bf16[2048,1280]{1,0:T(8,128)(2,1)}, bf16[2048,1280]{1,0:T(8,128)(2,1)}, bf16[3,2048,384]{2,1,0:T(8,128)(2,1)}) custom-call(bf16[2048,2048]{1,0:T(8,128)(2,1)} %get-tuple-element.63.normed_ref, bf16[2048,2560]{1,0:T(8,128)(2,1)} %bitcast.36, bf16[2048,2560]{1,0:T(8,128)(2,1)} %bitcast.37, ...), custom_call_target="tpu_custom_call" | custom-call | flops 32212254720 | bytes 70000000 | tf_op jit(solution)/shard_map/hidden_pass/pallas_call | solution.py:760
  347.4 16.6 %turned_product.2 = bf16[1280,2048]{1,0:T(8,128)(2,1)} custom-call(bf16[2048,1280]{1,0:T(8,128)(2,1)} %get-tuple-element.71.left_ref.hidden_ref, bf16[2048,2048]{1,0:T(8,128)(2,1)} %copy-done.26), custom_call_target="tpu_custom_call" | custom-call | flops 10737418240 | bytes 20000000 | tf_op jit(solution)/shard_map/turned_product/pallas_call | solution.py:1096
  364.3 96.3 %feed_tail.1 = (bf16[2048,2560]{1,0:T(8,128)(2,1)}, bf16[2048,2048]{1,0:T(8,128)(2,1)}, f32[512,2048]{1,0:T(8,128)}) custom-call(bf16[2048,2048]{1,0:T(8,128)(2,1)} %get-tuple-element.63.normed_ref, bf16[2048,1280]{1,0:T(8,128)(2,1)} %get-tuple-element.68.gate_ref, bf16[2048,1280]{1,0:T(8,128)(2,1)} %get-tuple-element.69.up_ref, ...), custom_call_target="tpu_custom_call" | custom-call | flops 53687091200 | bytes 70000000 | tf_op jit(solution)/shard_map/feed_tail/pallas_call | solution.py:922
  463.8 5.1 slice.131.residual_ref
  470.0 28.1 %residual_back.1 = (f32[512,2048]{1,0:T(8,128)}, f32[1,2048]{1,0:T(1,128)}, bf16[1024,2048]{1,0:T(8,128)(2,1)}, bf16[4,512,256]{2,1,0:T(8,128)(2,1)}) custom-call(f32[512,2048]{1,0:T(8,128)} %get-tuple-element.73.grad_sum_ref, f32[512,2048]{1,0:T(8,128)} %slice.131.residual_ref, bf16[512,2048]{1,0:T(8,128)(2,1)} %cot_ref.1, f32[1,2048]{1,0:T(1,128)} %copy-done.13, ...), custom_call_target="tpu_custom_call" | custom-call | flops 4294967296 | bytes 30000000 | tf_op jit(solution)/shard_map/residual_back/pallas_call | solution.py:1053
  503.7 34.8 %attend_back.1 = (bf16[2048,256]{1,0:T(8,128)(2,1)S(1)}, f32[4096,128]{1,0:T(8,128)}) custom-call(s32[5]{0:T(128)S(1)} %pad_add_fusion.first_ref, bf16[2048,256]{1,0:T(8,128)(2,1)S(1)} %copy-done.16, s32[1,2048]{1,0:T(1,128)S(1)} %bitcast.30, bf16[4096,128]{1,0:T(8,128)(2,1)S(1)} %copy-done.7, bf16[2048,256]{1,0:T(8,128)(2,1)S(1)} %get-tuple-element.59.out_ref, ...), custom_call_target="tpu_custom_call" | custom-call | flops 40000000000 | bytes 12000000 | tf_op jit(solution)/shard_map/attend_back/pallas_call | solution.py:187
  549.8 4.5 add_convert_fusion.3
  555.7 9.3 %project_back.1 = (bf16[2048,384]{1,0:T(8,128)(2,1)S(1)}, f32[1,320]{1,0:T(1,128)S(1)}) custom-call(s32[1]{0:T(128)} %bitcast.1.own_ref, bf16[2048,256]{1,0:T(8,128)(2,1)S(1)} %get-tuple-element.82.query_grad_ref, f32[4096,128]{1,0:T(8,128)} %get-tuple-element.79.pair_grad_ref, bf16[2048,128]{1,0:T(8,128)(2,1)S(1)} %collective-permute-done.15.returned_ref, ...), custom_call_target="tpu_custom_call" | custom-call | flops 8000000000 | bytes 8000000 | tf_op jit(solution)/shard_map/project_back/pallas_call | solution.py:372
  566.7 8.5 %turned_product.3.qkv_ref = bf16[2048,384]{1,0:T(8,128)(2,1)} custom-call(bf16[2048,2048]{1,0:T(8,128)(2,1)} %get-tuple-element.86.left_ref, bf16[2048,384]{1,0:T(8,128)(2,1)} %copy-done), custom_call_target="tpu_custom_call" | custom-call | flops 3221225472 | bytes 20000000 | tf_op jit(solution)/shard_map/turned_product/pallas_call | solution.py:1096
  575.2 18.5 %collective-permute-done.20.refs_3_ = bf16[256,2048]{1,0:T(8,128)(2,1)} collective-permute-done((bf16[256,2048]{1,0:T(8,128)(2,1)}, bf16[256,2048]{1,0:T(8,128)(2,1)}, u32[]{:S(2)}, u32[]{:S(2)}) %collective-permute-start.20) | collective-permute-done | bytes 1048608 | tf_op jit(solution)/shard_map/ppermute | solution.py:1359
  593.7 82.4 %finish.1 = (f32[512,2048]{1,0:T(8,128)}, f32[64,1536]{1,0:T(8,128)}, f32[8,128]{1,0:T(8,128)}, f32[32,2048]{1,0:T(8,128)}) custom-call(bf16[2048,384]{1,0:T(8,128)(2,1)} %copy-done, bf16[2048,384]{1,0:T(8,128)(2,1)} %turned_product.3.qkv_ref, bf16[512,2048]{1,0:T(8,128)(2,1)} %x_ref.3, f32[512,2048]{1,0:T(8,128)} %get-tuple-element.87.residual_ref, ...), custom_call_target="tpu_custom_call" | custom-call | tf_op jit(solution)/shard_map/finish/pallas_call | solution.py:1325
  683.3 4.4 add_convert_fusion.2
  690.4 6.8 collective-permute-done.22.refs_2_
  697.2 5.0 settle.1
  702.2 4.8 copy.43
  (179 shorter events, 80.0 us)
Async XLA Ops:
  7.2 154.6 %all-gather.4.cloned.1.call-start = ((), (), s32[]{:S(2)}) async-start(), calls=%async_computation.2 | async-start | bytes 1179648 | tf_op jit(solution)/shard_map/all_gather | solution.py:1421
  7.9 295.1 %all-gather.8.cloned.1.call-start = ((), (), s32[]{:S(2)}) async-start(), calls=%async_computation.4 | async-start | bytes 5898240 | tf_op jit(solution)/shard_map/all_gather | solution.py:1422
  8.7 294.4 %all-gather.6.cloned.1.call-start = ((), (), s32[]{:S(2)}) async-start(), calls=%async_computation.3 | async-start | bytes 11796480 | tf_op jit(solution)/shard_map/all_gather | solution.py:1425
  105.7 355.0 %reduce-scatter.3.cloned.1.call-start = ((), (), s32[]{:S(2)}) async-start(), calls=%async_computation.5 | async-start | bytes 5898240 | tf_op jit(solution)/shard_map/reduce_scatter | solution.py:1459
  137.4 77.3 %collective-permute-start.10 = (bf16[512,2048]{1,0:T(8,128)(2,1)}, bf16[512,2048]{1,0:T(8,128)(2,1)}, u32[]{:S(2)}, u32[]{:S(2)}) collective-permute-start(bf16[512,2048]{1,0:T(8,128)(2,1)} %cot_ref.1), channel_id=1, source_target_pairs={{0,16},{8,24},{16,0},{24,8},{1,17},{9,25},{17,1},{25,9},{2,18},{10... | collective-permute-start | bytes 6291464 | tf_op jit(solution)/shard_map/ppermute | solution.py:1359
  139.0 75.7 %collective-permute-start.9 = (bf16[512,2048]{1,0:T(8,128)(2,1)}, bf16[512,2048]{1,0:T(8,128)(2,1)}, u32[]{:S(2)}, u32[]{:S(2)}) collective-permute-start(bf16[512,2048]{1,0:T(8,128)(2,1)} %cot_ref.1), channel_id=1, source_target_pairs={{0,8},{8,0},{16,24},{24,16},{1,9},{9,1},{17,25},{25,17},{2,10},{10... | collective-permute-start | bytes 6291464 | tf_op jit(solution)/shard_map/ppermute | solution.py:1359
  158.6 51.6 %collective-permute-start.1 = (bf16[2048,256]{1,0:T(8,128)(2,1)}, bf16[2048,256]{1,0:T(8,128)(2,1)}, u32[]{:S(2)}, u32[]{:S(2)}) collective-permute-start(bf16[2048,256]{1,0:T(8,128)(2,1)} %pad_maximum_fusion.3.refs_0_), channel_id=1, source_target_pairs={{0,8},{8,0},{16,24},{24,16},{1,9},{9,1},{17,25},{25,17},{2,10},{10... | collective-permute-start | bytes 3145736 | tf_op jit(solution)/shard_map/ppermute | solution.py:1359
  159.9 52.0 %collective-permute-start.2 = (bf16[2048,256]{1,0:T(8,128)(2,1)}, bf16[2048,256]{1,0:T(8,128)(2,1)}, u32[]{:S(2)}, u32[]{:S(2)}) collective-permute-start(bf16[2048,256]{1,0:T(8,128)(2,1)} %pad_maximum_fusion.3.refs_0_), channel_id=1, source_target_pairs={{0,16},{8,24},{16,0},{24,8},{1,17},{9,25},{17,1},{25,9},{2,18},{10... | collective-permute-start | bytes 3145736 | tf_op jit(solution)/shard_map/ppermute | solution.py:1359
  161.8 70.8 %collective-permute-start.5 = (bf16[256,2048]{1,0:T(8,128)(2,1)}, bf16[256,2048]{1,0:T(8,128)(2,1)S(1)}, u32[]{:S(2)}, u32[]{:S(2)}) collective-permute-start(bf16[256,2048]{1,0:T(8,128)(2,1)} %all-gather.4.cloned.1.call-done.refs_0_), channel_id=1, source_target_pairs={{0,8},{8,0},{16,24},{24,16},{1,9},{9,1},{17,25},{25,17},{2,10},{10... | collective-permute-start | bytes 3145736 | tf_op jit(solution)/shard_map/ppermute | solution.py:1359
  211.3 71.2 %collective-permute-start.3 = (bf16[1024,256]{1,0:T(8,128)(2,1)S(1)}, bf16[1024,256]{1,0:T(8,128)(2,1)S(1)}, u32[]{:S(2)}, u32[]{:S(2)}) collective-permute-start(bf16[1024,256]{1,0:T(8,128)(2,1)S(1)} %slice.152), channel_id=1, source_target_pairs={{0,16},{8,24},{16,0},{24,8},{1,17},{9,25},{17,1},{25,9},{2,18},{10... | collective-permute-start | bytes 1572872 | tf_op jit(solution)/shard_map/ppermute | solution.py:1359
  213.0 35.7 %collective-permute-start.6 = (bf16[256,2048]{1,0:T(8,128)(2,1)S(1)}, bf16[256,2048]{1,0:T(8,128)(2,1)S(1)}, u32[]{:S(2)}, u32[]{:S(2)}) collective-permute-start(bf16[256,2048]{1,0:T(8,128)(2,1)S(1)} %copy-done.24), channel_id=1, source_target_pairs={{0,16},{8,24},{16,0},{24,8},{1,17},{9,25},{17,1},{25,9},{2,18},{10... | collective-permute-start | bytes 3145736 | tf_op jit(solution)/shard_map/ppermute | solution.py:1359
  216.0 55.2 %collective-permute-start.11 = (bf16[256,2048]{1,0:T(8,128)(2,1)S(1)}, bf16[256,2048]{1,0:T(8,128)(2,1)S(1)}, u32[]{:S(2)}, u32[]{:S(2)}) collective-permute-start(bf16[256,2048]{1,0:T(8,128)(2,1)S(1)} %slice.125), channel_id=1, source_target_pairs={{0,16},{8,24},{16,0},{24,8},{1,17},{9,25},{17,1},{25,9},{2,18},{10... | collective-permute-start | bytes 3145736 | tf_op jit(solution)/shard_map/ppermute | solution.py:1359
  217.9 54.0 %collective-permute-start.12 = (bf16[256,2048]{1,0:T(8,128)(2,1)S(1)}, bf16[256,2048]{1,0:T(8,128)(2,1)S(1)}, u32[]{:S(2)}, u32[]{:S(2)}) collective-permute-start(bf16[256,2048]{1,0:T(8,128)(2,1)S(1)} %slice.126), channel_id=1, source_target_pairs={{0,8},{8,0},{16,24},{24,16},{1,9},{9,1},{17,25},{25,17},{2,10},{10... | collective-permute-start | bytes 3145736 | tf_op jit(solution)/shard_map/ppermute | solution.py:1359
  232.6 49.9 %collective-permute-start.4 = (bf16[1024,256]{1,0:T(8,128)(2,1)S(1)}, bf16[1024,256]{1,0:T(8,128)(2,1)S(1)}, u32[]{:S(2)}, u32[]{:S(2)}) collective-permute-start(bf16[1024,256]{1,0:T(8,128)(2,1)S(1)} %slice.153), channel_id=1, source_target_pairs={{0,8},{8,0},{16,24},{24,16},{1,9},{9,1},{17,25},{25,17},{2,10},{10... | collective-permute-start | bytes 1572872 | tf_op jit(solution)/shard_map/ppermute | solution.py:1359
  248.7 32.4 %collective-permute-start.7 = (bf16[128,2048]{1,0:T(8,128)(2,1)S(1)}, bf16[128,2048]{1,0:T(8,128)(2,1)S(1)}, u32[]{:S(2)}, u32[]{:S(2)}) collective-permute-start(bf16[128,2048]{1,0:T(8,128)(2,1)S(1)} %slice.154), channel_id=1, source_target_pairs={{0,16},{8,24},{16,0},{24,8},{1,17},{9,25},{17,1},{25,9},{2,18},{10... | collective-permute-start | bytes 1572872 | tf_op jit(solution)/shard_map/ppermute | solution.py:1359
  364.0 313.5 %reduce-scatter.5.cloned.1.call-start = ((), (), s32[]{:S(2)}) async-start(), calls=%async_computation.6 | async-start | bytes 11796480 | tf_op jit(solution)/shard_map/reduce_scatter | solution.py:1464
  502.5 47.4 %collective-permute-start.13 = (bf16[512,2048]{1,0:T(8,128)(2,1)}, bf16[512,2048]{1,0:T(8,128)(2,1)S(1)}, u32[]{:S(2)}, u32[]{:S(2)}) collective-permute-start(bf16[512,2048]{1,0:T(8,128)(2,1)} %get-tuple-element.75), channel_id=1, source_target_pairs={{0,8},{8,0},{16,24},{24,16},{1,9},{9,1},{17,25},{25,17},{2,10},{10... | collective-permute-start | bytes 6291464 | tf_op jit(solution)/shard_map/ppermute | solution.py:1359
  503.0 46.8 %collective-permute-start.14 = (bf16[512,2048]{1,0:T(8,128)(2,1)S(1)}, bf16[512,2048]{1,0:T(8,128)(2,1)S(1)}, u32[]{:S(2)}, u32[]{:S(2)}) collective-permute-start(bf16[512,2048]{1,0:T(8,128)(2,1)S(1)} %get-tuple-element.76), channel_id=1, source_target_pairs={{0,16},{8,24},{16,0},{24,8},{1,17},{9,25},{17,1},{25,9},{2,18},{10... | collective-permute-start | bytes 6291464 | tf_op jit(solution)/shard_map/ppermute | solution.py:1359
  543.4 31.8 %collective-permute-start.18 = (bf16[256,2048]{1,0:T(8,128)(2,1)}, bf16[256,2048]{1,0:T(8,128)(2,1)S(1)}, u32[]{:S(2)}, u32[]{:S(2)}) collective-permute-start(bf16[256,2048]{1,0:T(8,128)(2,1)} %get-tuple-element.108), channel_id=1, source_target_pairs={{0,8},{8,0},{16,24},{24,16},{1,9},{9,1},{17,25},{25,17},{2,10},{10... | collective-permute-start | bytes 3145736 | tf_op jit(solution)/shard_map/ppermute | solution.py:1359
  544.7 30.5 %collective-permute-start.19 = (bf16[256,2048]{1,0:T(8,128)(2,1)}, bf16[256,2048]{1,0:T(8,128)(2,1)S(1)}, u32[]{:S(2)}, u32[]{:S(2)}) collective-permute-start(bf16[256,2048]{1,0:T(8,128)(2,1)} %get-tuple-element.107), channel_id=1, source_target_pairs={{0,16},{8,24},{16,0},{24,8},{1,17},{9,25},{17,1},{25,9},{2,18},{10... | collective-permute-start | bytes 3145736 | tf_op jit(solution)/shard_map/ppermute | solution.py:1359
  546.2 47.5 %collective-permute-start.20 = (bf16[256,2048]{1,0:T(8,128)(2,1)}, bf16[256,2048]{1,0:T(8,128)(2,1)}, u32[]{:S(2)}, u32[]{:S(2)}) collective-permute-start(bf16[256,2048]{1,0:T(8,128)(2,1)} %get-tuple-element.106), channel_id=1, source_target_pairs={{0,24},{8,16},{16,8},{24,0},{1,25},{9,17},{17,9},{25,1},{2,26},{10... | collective-permute-start | bytes 3145736 | tf_op jit(solution)/shard_map/ppermute | solution.py:1359
  554.4 128.9 %collective-permute-start.16 = (bf16[256,2048]{1,0:T(8,128)(2,1)}, bf16[256,2048]{1,0:T(8,128)(2,1)S(1)}, u32[]{:S(2)}, u32[]{:S(2)}) collective-permute-start(bf16[256,2048]{1,0:T(8,128)(2,1)} %get-tuple-element.102), channel_id=1, source_target_pairs={{0,16},{8,24},{16,0},{24,8},{1,17},{9,25},{17,1},{25,9},{2,18},{10... | collective-permute-start | bytes 3145736 | tf_op jit(solution)/shard_map/ppermute | solution.py:1359
  554.4 128.9 %collective-permute-start.17 = (bf16[256,2048]{1,0:T(8,128)(2,1)}, bf16[256,2048]{1,0:T(8,128)(2,1)}, u32[]{:S(2)}, u32[]{:S(2)}) collective-permute-start(bf16[256,2048]{1,0:T(8,128)(2,1)} %get-tuple-element.103), channel_id=1, source_target_pairs={{0,8},{8,0},{16,24},{24,16},{1,9},{9,1},{17,25},{25,17},{2,10},{10... | collective-permute-start | bytes 3145736 | tf_op jit(solution)/shard_map/ppermute | solution.py:1359
  680.6 16.6 %collective-permute-start.22 = (bf16[64,2560]{1,0:T(8,128)(2,1)S(1)}, bf16[64,2560]{1,0:T(8,128)(2,1)}, u32[]{:S(2)}, u32[]{:S(2)}) collective-permute-start(bf16[64,2560]{1,0:T(8,128)(2,1)S(1)} %get-tuple-element.111), channel_id=1, source_target_pairs={{0,16},{8,24},{16,0},{24,8},{1,17},{9,25},{17,1},{25,9},{2,18},{10... | collective-permute-start | bytes 983048 | tf_op jit(solution)/shard_map/ppermute | solution.py:1359
  (39 other events, 799.9 us)
Sparse Core Ops, SparseCore 0:
  9.6 49.3 all-gather.3
  60.7 60.0 all-gather.7
  122.4 98.6 all-gather.5
  364.2 57.3 reduce-scatter.2
  460.8 112.2 reduce-scatter.4

commit v4 on v3

--- a/solution.py
+++ b/solution.py
@@ -250,10 +250,13 @@
 
 
 def project_kernel(
-    dim, own_ref, x_ref, weight_ref, head_gain_ref, cosine_ref, sine_ref, query_ref, pair_ref,
-    raw_ref, normed_ref, gain_ref, ffn_gain_ref
+    dim, x_ref, weight_ref, head_gain_ref, cosine_ref, sine_ref, side_ref, query_ref, pair_ref,
+    raw_ref, normed_ref, gain_ref, ffn_gain_ref, spread_ref, send_sem, recv_sem
 ):
     columns = raw_ref.shape[1]
+    step, steps = pl.program_id(0), pl.num_programs(0)
+    marks = (0, steps // 2, steps - 2)
+    end = spread_job(step, marks, side_ref, spread_ref, send_sem, recv_sem)
 
     @pl.when(pl.program_id(0) == 0)
     def _():
@@ -276,45 +279,47 @@
     pair_ref[...] = jnp.concatenate(
         [heads[:, query_width:], raw[:, turned_width:].astype(jnp.bfloat16)], axis=1
     )
-
-
-def project(own, x, weight, head_gain, cosine, sine, size, query_width, rows):
+    pl.when(step == steps - 1)(end)
+
+
+def project(x, weight, head_gain, cosine, sine, side, size, query_width, rows):
     count, width = x.shape
     out_width = weight.shape[1] - 128
     pair_width = out_width - query_width
     dim = cosine.shape[1]
     tiles = count // size // rows
 
-    def apart(i, own):
-        return ((own[0] ^ (i // tiles)) * tiles + i % tiles, 0)
-
-    def there(i, own):
+    def apart(i):
+        return ((lax.axis_index("heads") ^ (i // tiles)) * tiles + i % tiles, 0)
+
+    def there(i):
         return (i, 0)
 
-    def whole(i, own):
+    def whole(i):
         return (0, 0)
+
+    anywhere = pl.BlockSpec(memory_space=pl.ANY)
 
     return pl.pallas_call(
         functools.partial(project_kernel, dim),
-        grid_spec=pltpu.PrefetchScalarGridSpec(
-            num_scalar_prefetch=1,
-            grid=(count // rows,),
-            in_specs=[
-                pl.BlockSpec((rows, width), there),
-                pl.BlockSpec(weight.shape, whole),
-                pl.BlockSpec(head_gain.shape, whole),
-                pl.BlockSpec((rows, dim), apart),
-                pl.BlockSpec((rows, dim), apart),
-            ],
-            out_specs=[
-                pl.BlockSpec((rows, query_width), apart),
-                pl.BlockSpec((rows, pair_width), apart),
-                pl.BlockSpec((rows, out_width), apart),
-                pl.BlockSpec((rows, width), there),
-                pl.BlockSpec((1, width), whole),
-                pl.BlockSpec((1, width), whole),
-            ],
-        ),
+        grid=(count // rows,),
+        in_specs=[
+            pl.BlockSpec((rows, width), there),
+            pl.BlockSpec(weight.shape, whole),
+            pl.BlockSpec(head_gain.shape, whole),
+            pl.BlockSpec((rows, dim), apart),
+            pl.BlockSpec((rows, dim), apart),
+            anywhere,
+        ],
+        out_specs=[
+            pl.BlockSpec((rows, query_width), apart),
+            pl.BlockSpec((rows, pair_width), apart),
+            pl.BlockSpec((rows, out_width), apart),
+            pl.BlockSpec((rows, width), there),
+            pl.BlockSpec((1, width), whole),
+            pl.BlockSpec((1, width), whole),
+            anywhere,
+        ],
         out_shape=[
             jax.ShapeDtypeStruct((count, query_width), jnp.bfloat16),
             jax.ShapeDtypeStruct((count, pair_width), jnp.bfloat16),
@@ -322,13 +327,17 @@
             jax.ShapeDtypeStruct((count, width), jnp.bfloat16),
             jax.ShapeDtypeStruct((1, width), jnp.float32),
             jax.ShapeDtypeStruct((1, width), jnp.float32),
-        ],
-        compiler_params=pltpu.CompilerParams(vmem_limit_bytes=48 << 20),
+            jax.ShapeDtypeStruct((3, *side.shape), side.dtype),
+        ],
+        scratch_shapes=[pltpu.SemaphoreType.DMA((SPREAD_COUNT,))] * 2,
+        compiler_params=pltpu.CompilerParams(
+            collective_id=5, has_side_effects=True, vmem_limit_bytes=48 << 20
+        ),
         cost_estimate=pl.CostEstimate(
             flops=4 * count * width * out_width, bytes_accessed=30_000_000, transcendentals=0
         ),
         name="project",
-    )(own, x, weight, head_gain, cosine, sine)
+    )(x, weight, head_gain, cosine, sine, side)
 
 
 def project_back_kernel(
@@ -400,29 +409,85 @@
     )(own, query_grad, pair_sum, returned, raw, head_gain, cosine, sine)
 
 
-def join_kernel(half_tiles, x_ref, *refs):
-    *part_refs, top_ref, bottom_ref, weight_ref, gain_ref, residual_ref, normed_ref = refs
-    tile = pl.program_id(0)
-    far = jnp.where((tile // half_tiles) % 2 == 1, top_ref[...], bottom_ref[...])
-    attended = jnp.concatenate([ref[...] for ref in part_refs] + [far], axis=1)
-    residual = x_ref[...].astype(jnp.float32) + jnp.dot(
-        attended, weight_ref[...], preferred_element_type=jnp.float32
-    )
-    residual_ref[...] = residual
-    normed = residual * lax.rsqrt(jnp.mean(residual * residual, axis=-1, keepdims=True) + EPS)
+def join_kernel(
+    x_ref, weight_ref, weights_ref, gain_ref, mine_ref, cot_ref, residual_ref,
+    normed_ref, attended_ref, cot_one_ref, cot_two_ref, held_ref, local_sem, send_sem, recv_sem
+):
+    step = pl.program_id(0)
+    head, blk = lax.axis_index("heads"), lax.axis_index("blk")
+    rows = x_ref.shape[0]
+    count = held_ref.shape[1] // 4
+    tiles = count // rows
+
+    def copy(source, target, k, index):
+        return pltpu.make_async_remote_copy(
+            src_ref=source,
+            dst_ref=target,
+            send_sem=send_sem.at[index],
+            recv_sem=recv_sem.at[index],
+            device_id=(head ^ k, blk),
+            device_id_type=MESH,
+        )
+
+    upper, lower = pl.ds(0, 2 * count), pl.ds(2 * count, 2 * count)
+    near = [copy(mine_ref, held_ref.at[k], k, k - 1) for k in (1, 2)]
+    far = [
+        copy(held_ref.at[1, upper], held_ref.at[3, upper], 2, 2),
+        copy(held_ref.at[2, lower], held_ref.at[3, lower], 1, 3),
+    ]
+    half = count // 2
+    cot_near = [
+        copy(cot_ref.at[pl.ds(half, half)], cot_one_ref, 1, 4),
+        copy(cot_ref.at[pl.ds(0, half)], cot_two_ref, 2, 5),
+    ]
+    own = pltpu.make_async_copy(mine_ref, held_ref.at[0], local_sem)
+
+    @pl.when(step == 0)
+    def _():
+        own.start()
+        greet_near(False)
+        for first in near:
+            first.start()
+        for first, second in zip(near, far):
+            first.wait_recv()
+            second.start()
+        own.wait()
+        for second in far:
+            second.wait_recv()
+        for last in cot_near:
+            last.start()
+
+    chunk = step // tiles
+    parts = []
+    total = x_ref[...].astype(jnp.float32)
+    for k in range(4):
+        start = ((chunk ^ k) * tiles + lax.rem(step, tiles)) * rows
+        part = held_ref[k, pl.ds(pl.multiple_of(start, rows), rows)]
+        weight = weight_ref[...] if k == 0 else weights_ref[k - 1]
+        total += jnp.dot(part, weight, preferred_element_type=jnp.float32)
+        parts.append(part)
+    residual_ref[...] = total
+    normed = total * lax.rsqrt(jnp.mean(total * total, axis=-1, keepdims=True) + EPS)
     normed_ref[...] = (normed * gain_ref[...]).astype(jnp.bfloat16)
 
-
-def join(x, parts, top, bottom, weight, gain, rows):
+    @pl.when(chunk == 0)
+    def _():
+        attended_ref[...] = jnp.concatenate(parts, axis=1)
+
+    @pl.when(step == pl.num_programs(0) - 1)
+    def _():
+        for first in near + far:
+            first.wait_send()
+        for last in cot_near:
+            last.wait()
+
+
+def join(x, mine, weight, weights, gain, cot, rows):
     count, width = x.shape
-    columns = parts[0].shape[1]
-    tiles = count // 4 // rows
-
-    def part_map(k):
-        return lambda i: ((k ^ (i // tiles)) * tiles + i % tiles, 0)
-
-    def far_map(i):
-        return (((3 ^ (i // tiles)) % 2) * tiles + i % tiles, 0)
+    tokens = count // 4
+    columns = mine.shape[1]
+    tiles = tokens // rows
+    anywhere = pl.BlockSpec(memory_space=pl.ANY)
 
     def there(i):
         return (i, 0)
@@ -430,54 +495,46 @@
     def whole(i):
         return (0, 0)
 
+    sems = pltpu.SemaphoreType.DMA
     return pl.pallas_call(
-        functools.partial(join_kernel, 2 * tiles),
+        join_kernel,
         grid=(count // rows,),
-        in_specs=[pl.BlockSpec((rows, width), there)]
-        + [pl.BlockSpec((rows, columns), part_map(k)) for k in range(3)]
-        + [pl.BlockSpec((rows, columns), far_map)] * 2
-        + [pl.BlockSpec(weight.shape, whole), pl.BlockSpec((1, width), whole)],
-        out_specs=[pl.BlockSpec((rows, width), there)] * 2,
+        in_specs=[
+            pl.BlockSpec((rows, width), there),
+            pl.BlockSpec(weight.shape, whole),
+            pl.BlockSpec(weights.shape, lambda i: (0, 0, 0)),
+            pl.BlockSpec((1, width), whole),
+            anywhere,
+            anywhere,
+        ],
+        out_specs=[
+            pl.BlockSpec((rows, width), there),
+            pl.BlockSpec((rows, width), there),
+            pl.BlockSpec((rows, 4 * columns), lambda i: (jnp.minimum(i, tiles - 1), 0)),
+            anywhere,
+            anywhere,
+        ],
         out_shape=[
             jax.ShapeDtypeStruct((count, width), jnp.float32),
             jax.ShapeDtypeStruct((count, width), jnp.bfloat16),
-        ],
-        compiler_params=pltpu.CompilerParams(vmem_limit_bytes=48 << 20),
+            jax.ShapeDtypeStruct((tokens, 4 * columns), jnp.bfloat16),
+            jax.ShapeDtypeStruct((tokens // 2, width), jnp.bfloat16),
+            jax.ShapeDtypeStruct((tokens // 2, width), jnp.bfloat16),
+        ],
+        scratch_shapes=[
+            pltpu.VMEM((4, count, columns), jnp.bfloat16),
+            sems,
+            sems((6,)),
+            sems((6,)),
+        ],
+        compiler_params=pltpu.CompilerParams(
+            collective_id=6, has_side_effects=True, vmem_limit_bytes=56 << 20
+        ),
         cost_estimate=pl.CostEstimate(
-            flops=2 * count * width * weight.shape[0],
-            bytes_accessed=50_000_000,
-            transcendentals=0,
+            flops=16 * count * width * columns, bytes_accessed=50_000_000, transcendentals=0
         ),
         name="join",
-    )(x, *parts, top, bottom, weight, gain)
-
-
-def settle_kernel(size, own_ref, *refs):
-    *part_refs, out_ref = refs
-    for k, part_ref in enumerate(part_refs):
-
-        @pl.when(pl.program_id(0) % size == k)
-        def _(part_ref=part_ref):
-            out_ref[...] = part_ref[...].astype(out_ref.dtype)
-
-
-def settle(own, parts, pieces):
-    size = len(parts)
-    rows, width = parts[0].shape
-    piece = width // pieces
-    return pl.pallas_call(
-        functools.partial(settle_kernel, size),
-        grid_spec=pltpu.PrefetchScalarGridSpec(
-            num_scalar_prefetch=1,
-            grid=(pieces * size,),
-            in_specs=[pl.BlockSpec((rows, piece), lambda i, own: (0, i // size))] * size,
-            out_specs=pl.BlockSpec(
-                (rows, piece), lambda i, own: (0, i // size * size + (own[0] ^ (i % size)))
-            ),
-        ),
-        out_shape=jax.ShapeDtypeStruct((rows, width * size), jnp.float32),
-        name="settle",
-    )(own, *parts)
+    )(x, weight, weights, gain, mine, cot)
 
 
 def begin_kernel(
@@ -691,13 +748,14 @@
     pl.semaphore_wait(barrier, len(places))
 
 
-def spread_job(step, marks, source_ref, target_ref, send_sem, recv_sem):
+def spread_job(step, marks, source_ref, target_ref, send_sem, recv_sem, greet=True):
     near, far, other = spread_copies(source_ref, target_ref, send_sem, recv_sem)
     begin_at, far_at, other_at = marks
 
     @pl.when(step == begin_at)
     def _():
-        greet_near(True)
+        if greet:
+            greet_near(True)
         for copy in near:
             copy.start()
 
@@ -727,58 +785,137 @@
 
 
 def hidden_kernel(
-    normed_ref, gate_ref, up_ref, cot_ref, down_ref, side_ref, hidden_ref, gate_grad_ref,
-    up_grad_ref, spread_ref, send_sem, recv_sem
+    tiles, normed_ref, gate_ref, up_ref, down_ref, side_ref, cot_ref, one_top_ref, one_bottom_ref,
+    two_top_ref, two_bottom_ref, hidden_ref, gate_grad_ref, up_grad_ref, down_sum_ref, spread_ref,
+    held_ref, hidden_all_ref, load_sem, far_send, far_recv, send_sem, recv_sem
 ):
-    steps = pl.num_programs(0) * pl.num_programs(1)
-    step = pl.program_id(0) * pl.num_programs(1) + pl.program_id(1)
-    marks = (0, steps // 2, steps - 2)
-    end = spread_job(step, marks, side_ref, spread_ref, send_sem, recv_sem)
-    normed = normed_ref[...]
-    gate = jnp.dot(normed, gate_ref[...], preferred_element_type=jnp.float32)
-    upward = jnp.dot(normed, up_ref[...], preferred_element_type=jnp.float32)
-    grad = lax.dot_general(
-        cot_ref[...], down_ref[...], ROWS_IN_BOTH, preferred_element_type=jnp.float32
-    )
-    sigmoid = jax.nn.sigmoid(gate)
-    activated = gate * sigmoid
-    hidden_ref[...] = (activated * upward).astype(jnp.bfloat16)
-    gate_grad_ref[...] = (grad * upward * sigmoid * (1.0 + gate * (1.0 - sigmoid))).astype(
-        jnp.bfloat16
-    )
-    up_grad_ref[...] = (grad * activated).astype(jnp.bfloat16)
+    step, steps = pl.program_id(0), pl.num_programs(0)
+    head, blk = lax.axis_index("heads"), lax.axis_index("blk")
+    count = cot_ref.shape[0]
+    half = count // 2
+    rows, units = hidden_ref.shape
+    far = [
+        pltpu.make_async_remote_copy(
+            src_ref=ref,
+            dst_ref=held_ref.at[pl.ds(3 * count + part * half, half)],
+            send_sem=far_send.at[part],
+            recv_sem=far_recv.at[part],
+            device_id=(head ^ k, blk),
+            device_id_type=MESH,
+        )
+        for part, (ref, k) in enumerate(((one_top_ref, 2), (two_bottom_ref, 1)))
+    ]
+    near = ((one_top_ref, 2), (one_bottom_ref, 3), (two_top_ref, 4), (two_bottom_ref, 5))
+    loads = [pltpu.make_async_copy(cot_ref, held_ref.at[pl.ds(0, count)], load_sem.at[0])] + [
+        pltpu.make_async_copy(ref, held_ref.at[pl.ds(half * place, half)], load_sem.at[place - 1])
+        for ref, place in near
+    ]
+
+    @pl.when(step == 0)
+    def _():
+        for load in loads:
+            load.start()
+        greet_near(True)
+        for copy in far:
+            copy.start()
+        for load in loads:
+            load.wait()
+
+    @pl.when(step == tiles)
+    def _():
+        for copy in far:
+            copy.wait()
+
+    marks = (tiles, 2 * tiles, 2 * tiles + 2)
+    end = spread_job(step, marks, side_ref, spread_ref, send_sem, recv_sem, False)
+
+    @pl.when(step < 2 * tiles)
+    def _():
+        here = pl.ds(pl.multiple_of(step // tiles * rows, rows), rows)
+        normed = normed_ref[...]
+        gate = jnp.dot(normed, gate_ref[...], preferred_element_type=jnp.float32)
+        upward = jnp.dot(normed, up_ref[...], preferred_element_type=jnp.float32)
+        grad = lax.dot_general(
+            held_ref[here], down_ref[...], ROWS_IN_BOTH, preferred_element_type=jnp.float32
+        )
+        sigmoid = jax.nn.sigmoid(gate)
+        activated = gate * sigmoid
+        hidden = (activated * upward).astype(jnp.bfloat16)
+        hidden_ref[...] = hidden
+        hidden_all_ref[here, pl.ds(pl.multiple_of(lax.rem(step, tiles) * units, units), units)] = (
+            hidden
+        )
+        gate_grad_ref[...] = (grad * upward * sigmoid * (1.0 + gate * (1.0 - sigmoid))).astype(
+            jnp.bfloat16
+        )
+        up_grad_ref[...] = (grad * activated).astype(jnp.bfloat16)
+
+    @pl.when(step >= 2 * tiles)
+    def _():
+        there = pl.ds(pl.multiple_of((step - 2 * tiles) * units, units), units)
+        down_sum_ref[...] = lax.dot_general(
+            hidden_all_ref[:, there],
+            held_ref[...],
+            (((0,), (0,)), ((), ())),
+            preferred_element_type=jnp.float32,
+        ).astype(jnp.bfloat16)
+
     pl.when(step == steps - 1)(end)
 
 
-def hidden_pass(normed, weight, cot, down, side, rows, units):
+def hidden_pass(normed, weight, cot, cot_near, down, side, units):
     count, width = normed.shape
     total = down.shape[0]
     tiles = total // units
-    out_spec = pl.BlockSpec((rows, units), lambda i, j: (i, j))
+    rows = count // 2
+
+    def row(s):
+        return jnp.minimum(s // tiles, 1)
+
+    def column(s):
+        return jnp.where(s < 2 * tiles, lax.rem(s, tiles), tiles - 1)
+
+    out_spec = pl.BlockSpec((rows, units), lambda s: (row(s), column(s)))
     out_shape = jax.ShapeDtypeStruct((count, total), jnp.bfloat16)
     anywhere = pl.BlockSpec(memory_space=pl.ANY)
+    sems = pltpu.SemaphoreType.DMA
     return pl.pallas_call(
-        hidden_kernel,
-        grid=(count // rows, tiles),
+        functools.partial(hidden_kernel, tiles),
+        grid=(3 * tiles,),
         in_specs=[
-            pl.BlockSpec((rows, width), lambda i, j: (i, 0)),
-            pl.BlockSpec((width, units), lambda i, j: (0, j)),
-            pl.BlockSpec((width, units), lambda i, j: (0, tiles + j)),
-            pl.BlockSpec((rows, width), lambda i, j: (i, 0)),
-            pl.BlockSpec((units, width), lambda i, j: (j, 0)),
+            pl.BlockSpec((rows, width), lambda s: (row(s), 0)),
+            pl.BlockSpec((width, units), lambda s: (0, column(s))),
+            pl.BlockSpec((width, units), lambda s: (0, tiles + column(s))),
+            pl.BlockSpec((units, width), lambda s: (column(s), 0)),
+        ]
+        + [anywhere] * 6,
+        out_specs=[out_spec] * 3
+        + [
+            pl.BlockSpec((units, width), lambda s: (jnp.maximum(s - 2 * tiles, 0), 0)),
             anywhere,
         ],
-        out_specs=[out_spec] * 3 + [anywhere],
-        out_shape=[out_shape] * 3 + [jax.ShapeDtypeStruct((3, *side.shape), side.dtype)],
-        scratch_shapes=[pltpu.SemaphoreType.DMA((SPREAD_COUNT,))] * 2,
+        out_shape=[out_shape] * 3
+        + [
+            jax.ShapeDtypeStruct((total, width), jnp.bfloat16),
+            jax.ShapeDtypeStruct((3, *side.shape), side.dtype),
+        ],
+        scratch_shapes=[
+            pltpu.VMEM((count, width), jnp.bfloat16),
+            pltpu.VMEM((count, total), jnp.bfloat16),
+            sems((5,)),
+            sems((2,)),
+            sems((2,)),
+            sems((SPREAD_COUNT,)),
+            sems((SPREAD_COUNT,)),
+        ],
         compiler_params=pltpu.CompilerParams(
             collective_id=2, has_side_effects=True, vmem_limit_bytes=58 << 20
         ),
         cost_estimate=pl.CostEstimate(
-            flops=6 * count * width * total, bytes_accessed=70_000_000, transcendentals=0
+            flops=8 * count * width * total, bytes_accessed=70_000_000, transcendentals=0
         ),
         name="hidden_pass",
-    )(normed, weight, weight, cot, down, side)
+    )(normed, weight, weight, down, side, cot, *cot_near)
 
 
 def in_order(step):
@@ -789,7 +926,8 @@
 
 
 def tail_kernel(
-    normed_ref, gate_ref, up_ref, hidden_ref, in_hbm, down_hbm, in_sum_ref, out_ref, grad_ref,
+    normed_ref, gate_ref, up_ref, hidden_ref, in_hbm, down_hbm, in_sum_ref, out_one_ref,
+    out_two_ref, out_rest_ref, grad_ref,
     weight_ref, one_ref, two_ref, rest_ref, top_ref, bottom_ref, last_ref, last_got_ref,
     weight_sem, send_sem, recv_sem
 ):
@@ -890,9 +1028,21 @@
 
     @pl.when(step >= 16)
     def _():
-        out_ref[...] = jnp.dot(
+        terms = jnp.dot(
             hidden_ref[...], weight_ref[:total, :width], preferred_element_type=jnp.float32
         ).astype(jnp.bfloat16)
+
+        @pl.when(step < 18)
+        def _():
+            out_one_ref[...] = terms
+
+        @pl.when((step >= 18) & (step < 20))
+        def _():
+            out_two_ref[...] = terms
+
+        @pl.when(step >= 20)
+        def _():
+            out_rest_ref[...] = terms
 
     @pl.when(step == pl.num_programs(0) - 1)
     def _():
@@ -932,12 +1082,16 @@
         ],
         out_specs=[
             pl.BlockSpec((rows, 2 * total), lambda i: (stage(i, 8), 0)),
-            pl.BlockSpec((rows, width), lambda i: (stage(i, 16), 0)),
+            pl.BlockSpec((rows, width), lambda i: (jnp.clip(i - 16, 0, 1), 0)),
+            pl.BlockSpec((rows, width), lambda i: (jnp.clip(i - 18, 0, 1), 0)),
+            pl.BlockSpec((rows, width), lambda i: (jnp.clip(i - 20, 0, 3), 0)),
             pl.BlockSpec((2 * rows, width), lambda i: (0, 0), pipeline_mode=once),
         ],
         out_shape=[
             jax.ShapeDtypeStruct((width, 2 * total), low),
-            jax.ShapeDtypeStruct((count, width), low),
+            jax.ShapeDtypeStruct((2 * rows, width), low),
+            jax.ShapeDtypeStruct((2 * rows, width), low),
+            jax.ShapeDtypeStruct((4 * rows, width), low),
             jax.ShapeDtypeStruct((2 * rows, width), jnp.float32),
         ],
         scratch_shapes=[
@@ -964,14 +1118,12 @@
 
 
 def residual_back_kernel(
-    grad_sum_ref, residual_ref, cot_ref, gain_ref, attended_ref, *refs
+    grad_sum_ref, residual_ref, cot_ref, gain_ref, attended_ref, weight_ref, weights_ref, grad_ref,
+    gain_grad_ref, out_sum_ref, pieces_ref, branch_ref, mine_ref, terms_ref, terms_got_ref, own_sem,
+    send_sem, recv_sem
 ):
     size = lax.axis_size("heads")
-    weight_refs, refs = refs[:size], refs[size:]
-    (
-        grad_ref, gain_grad_ref, out_sum_ref, pieces_ref, branch_ref, mine_ref, own_sem, send_sem,
-        recv_sem,
-    ) = refs
+    core = lax.rem(lax.axis_index("blk"), 2)
     step = pl.program_id(0)
     last = pl.num_programs(0) - 1
     head, blk = lax.axis_index("heads"), lax.axis_index("blk")
@@ -988,6 +1140,14 @@
         for k in range(1, size)
     ]
     keep = pltpu.make_async_copy(mine_ref.at[0], pieces_ref.at[0], own_sem)
+    across = pltpu.make_async_remote_copy(
+        src_ref=terms_ref.at[:, 1 - core],
+        dst_ref=terms_got_ref,
+        send_sem=send_sem.at[size - 1],
+        recv_sem=recv_sem.at[size - 1],
+        device_id=(head, blk ^ 1),
+        device_id_type=MESH,
+    )
 
     @pl.when(step == 0)
     def _():
@@ -995,7 +1155,8 @@
         barrier = pltpu.get_barrier_semaphore()
         for k in range(1, size):
             pl.semaphore_signal(barrier, inc=1, device_id=(head ^ k, blk), device_id_type=MESH)
-        pl.semaphore_wait(barrier, size - 1)
+        pl.semaphore_signal(barrier, inc=1, device_id=(head, blk ^ 1), device_id_type=MESH)
+        pl.semaphore_wait(barrier, size)
 
     @pl.when(step < last)
     def _():
@@ -1012,9 +1173,10 @@
         grad_ref[...] = total
         branch = total.astype(jnp.bfloat16)
         branch_ref[here] = branch
-        for k, weight_ref in enumerate(weight_refs):
+        for k in range(size):
+            weight = weight_ref[...] if k == 0 else weights_ref[k - 1]
             mine_ref[k, here] = lax.dot_general(
-                branch, weight_ref[...], ROWS_IN_BOTH, preferred_element_type=jnp.float32
+                branch, weight, ROWS_IN_BOTH, preferred_element_type=jnp.float32
             ).astype(jnp.bfloat16)
 
     @pl.when(step == last)
@@ -1023,22 +1185,36 @@
             copy.start()
         keep.start()
         columns = attended_ref.shape[1] // size
+        pairs = terms_ref.shape[0] // size
         for k in range(size):
-            out_sum_ref[k * columns : (k + 1) * columns] = lax.dot_general(
+            terms = lax.dot_general(
                 attended_ref[:, k * columns : (k + 1) * columns],
                 branch_ref[...],
                 (((0,), (0,)), ((), ())),
                 preferred_element_type=jnp.float32,
             ).astype(jnp.bfloat16)
+            terms_ref[k * pairs : (k + 1) * pairs] = terms.reshape(pairs, *terms_ref.shape[1:])
+        across.start()
+        across.wait()
+
+        def add(index, carried):
+            out_sum_ref[index] = (
+                terms_ref[index, core].astype(jnp.float32)
+                + terms_got_ref[index].astype(jnp.float32)
+            ).astype(jnp.bfloat16)
+            return carried
+
+        lax.fori_loop(0, terms_ref.shape[0], add, 0)
         for copy in copies:
             copy.wait()
         keep.wait()
 
 
-def residual_back(grad_sum, residual, cot, gain, attended, weights, rows):
+def residual_back(grad_sum, residual, cot, gain, attended, weight, weights, rows):
     count, width = cot.shape
-    size = len(weights)
-    columns = weights[0].shape[0]
+    size, blk_size = lax.axis_size("heads"), lax.axis_size("blk")
+    columns = weight.shape[0]
+    pairs, held = size * blk_size // 2, columns // blk_size
     tiles = count // rows
 
     def there(i):
@@ -1053,26 +1229,35 @@
     return pl.pallas_call(
         residual_back_kernel,
         grid=(tiles + 1,),
-        in_specs=[tile, tile, tile, row, pl.BlockSpec(attended.shape, whole)]
-        + [pl.BlockSpec(weight.shape, whole) for weight in weights],
+        in_specs=[
+            tile,
+            tile,
+            tile,
+            row,
+            pl.BlockSpec(attended.shape, whole),
+            pl.BlockSpec(weight.shape, whole),
+            pl.BlockSpec(weights.shape, lambda i: (0, 0, 0)),
+        ],
         out_specs=[
             tile,
             row,
-            pl.BlockSpec((size * columns, width), whole),
+            pl.BlockSpec((pairs, held, width), lambda i: (0, 0, 0)),
             pl.BlockSpec(memory_space=pl.ANY),
         ],
         out_shape=[
             jax.ShapeDtypeStruct((count, width), jnp.float32),
             jax.ShapeDtypeStruct((1, width), jnp.float32),
-            jax.ShapeDtypeStruct((size * columns, width), jnp.bfloat16),
+            jax.ShapeDtypeStruct((pairs, held, width), jnp.bfloat16),
             jax.ShapeDtypeStruct(pieces, jnp.bfloat16),
         ],
         scratch_shapes=[
             pltpu.VMEM((count, width), jnp.bfloat16),
             pltpu.VMEM(pieces, jnp.bfloat16),
+            pltpu.VMEM((pairs, 2, held, width), jnp.bfloat16),
+            pltpu.VMEM((pairs, held, width), jnp.bfloat16),
             pltpu.SemaphoreType.DMA,
-            pltpu.SemaphoreType.DMA((size - 1,)),
-            pltpu.SemaphoreType.DMA((size - 1,)),
+            pltpu.SemaphoreType.DMA((size,)),
+            pltpu.SemaphoreType.DMA((size,)),
         ],
         compiler_params=pltpu.CompilerParams(
             collective_id=4, has_side_effects=True, vmem_limit_bytes=56 << 20
@@ -1081,52 +1266,83 @@
             flops=4 * count * width * columns * size, bytes_accessed=30_000_000, transcendentals=0
         ),
         name="residual_back",
-    )(grad_sum, residual, cot, gain, attended, *weights)
-
-
-def turned_kernel(left_ref, right_ref, out_ref):
+    )(grad_sum, residual, cot, gain, attended, weight, weights)
+
+
+def turned_kernel(left_ref, *refs):
+    *right_refs, out_ref, held_ref, load_sem = refs
+    count = right_refs[0].shape[0]
+
+    @pl.when(pl.program_id(0) == 0)
+    def _():
+        loads = [
+            pltpu.make_async_copy(ref, held_ref.at[pl.ds(k * count, count)], load_sem.at[k])
+            for k, ref in enumerate(right_refs)
+        ]
+        for load in loads:
+            load.start()
+        for load in loads:
+            load.wait()
+
     out_ref[...] = lax.dot_general(
-        left_ref[...], right_ref[...], (((0,), (0,)), ((), ())), preferred_element_type=jnp.float32
+        left_ref[...], held_ref[...], (((0,), (0,)), ((), ())), preferred_element_type=jnp.float32
     ).astype(out_ref.dtype)
 
 
-def turned_product(left, right, rows):
+def turned_product(left, rights, rows):
     count, height = left.shape
-    width = right.shape[1]
+    width = rights[0].shape[1]
     return pl.pallas_call(
         turned_kernel,
         grid=(height // rows,),
-        in_specs=[
-            pl.BlockSpec((count, rows), lambda i: (0, i)),
-            pl.BlockSpec((count, width), lambda i: (0, 0)),
-        ],
+        in_specs=[pl.BlockSpec((count, rows), lambda i: (0, i))]
+        + [pl.BlockSpec(memory_space=pl.ANY)] * len(rights),
         out_specs=pl.BlockSpec((rows, width), lambda i: (i, 0)),
         out_shape=jax.ShapeDtypeStruct((height, width), jnp.bfloat16),
+        scratch_shapes=[
+            pltpu.VMEM((count, width), jnp.bfloat16),
+            pltpu.SemaphoreType.DMA((len(rights),)),
+        ],
         compiler_params=pltpu.CompilerParams(vmem_limit_bytes=58 << 20),
         cost_estimate=pl.CostEstimate(
             flops=2 * count * height * width, bytes_accessed=20_000_000, transcendentals=0
         ),
         name="turned_product",
-    )(left, right)
+    )(left, *rights)
 
 
 def finish_kernel(
-    query_width, dim, sent_ref, qkv_ref, x_ref, residual_ref, gain_ref, ffn_ref, head_ref,
-    weight_ref, weights_ref, *refs
+    query_width, dim, sent_ref, qkv_ref, gain_ref, ffn_ref, head_ref, weight_ref, out_own_ref,
+    out_one_ref, out_two_ref, out_three_ref, *refs
 ):
     size, blk_size = lax.axis_size("heads"), lax.axis_size("blk")
-    out_refs, refs = refs[:size], refs[size:]
+    out_refs = (out_own_ref, out_one_ref, out_two_ref, out_three_ref)
+    sources, refs = refs[:4], refs[4:]
     (
-        grad_ref, qkv_grad_ref, gains_ref, out_grad_ref, got_ref, qkv_got_ref, part_ref,
-        gain_got_ref, out_part_ref, out_got_ref, s_send, s_recv, q_send, q_recv, g_send, g_recv,
-        o_send, o_recv,
+        grad_ref, qkv_grad_ref, gains_ref, out_grad_ref, in_grad_ref, *refs
+    ) = refs
+    held, refs = refs[:4], refs[4:]
+    weights_ref, x_ref, residual_grad_ref, in_ref = held
+    (
+        got_ref, qkv_other_ref, qkv_sum_ref, qkv_got_ref, part_ref, gain_got_ref, out_part_ref,
+        out_got_ref, in_got_ref, load_sem, s_send, s_recv, c_send, c_recv, q_send, q_recv, g_send,
+        g_recv, o_send, o_recv, i_send, i_recv,
     ) = refs
     devices = size * blk_size
+    pairs = blk_size // 2
     head, blk = lax.axis_index("heads"), lax.axis_index("blk")
+    core, pair = lax.rem(blk, 2), blk // 2
     own = head * blk_size + blk
+    own_pair = head * pairs + pair
     count, width = x_ref.shape
     depth = width // devices
     barrier = pltpu.get_barrier_semaphore()
+    loads = [
+        pltpu.make_async_copy(source, target, load_sem.at[index])
+        for index, (source, target) in enumerate(zip(sources, held))
+    ]
+    for load in loads:
+        load.start()
 
     def place_of(index):
         return (index // blk_size, lax.rem(index, blk_size))
@@ -1140,84 +1356,106 @@
     lax.fori_loop(1, devices, greet, 0)
     pl.semaphore_wait(barrier, devices - 1)
 
+    def copy(source, target, place, send, recv):
+        return pltpu.make_async_remote_copy(
+            src_ref=source,
+            dst_ref=target,
+            send_sem=send,
+            recv_sem=recv,
+            device_id=place,
+            device_id_type=MESH,
+        )
+
+    across = copy(qkv_ref.at[:, 1 - core], qkv_other_ref, (head, blk ^ 1), c_send, c_recv)
+    across.start()
     sends = [
-        pltpu.make_async_remote_copy(
-            src_ref=sent_ref.at[pl.ds(k * count, count)],
-            dst_ref=got_ref.at[k - 1],
-            send_sem=s_send.at[k - 1],
-            recv_sem=s_recv.at[k - 1],
-            device_id=(head ^ k, blk),
-            device_id_type=MESH,
+        copy(
+            sent_ref.at[pl.ds(k * count, count)],
+            got_ref.at[k - 1],
+            (head ^ k, blk),
+            s_send.at[k - 1],
+            s_recv.at[k - 1],
         )
         for k in range(1, size)
     ]
-    for copy in sends:
-        copy.start()
-
-    def rows_of(index):
-        return pl.ds(pl.multiple_of(index * depth, depth), depth)
+    for sent in sends:
+        sent.start()
+
+    def wide_of(block):
+        return block.astype(jnp.float32)
+
+    across.wait_recv()
 
     def qkv_copy(k, slot):
-        other = lax.rem(own + k, devices)
-        return pltpu.make_async_remote_copy(
-            src_ref=qkv_ref.at[rows_of(other)],
-            dst_ref=qkv_got_ref.at[slot],
-            send_sem=q_send.at[k],
-            recv_sem=q_recv.at[slot],
-            device_id=place_of(other),
-            device_id_type=MESH,
+        other = lax.rem(own_pair + k, size * pairs)
+        return copy(
+            qkv_sum_ref.at[other],
+            qkv_got_ref.at[slot],
+            (other // pairs, lax.rem(other, pairs) * 2 + core),
+            q_send.at[k],
+            q_recv.at[slot],
+        )
+
+    def qkv_sum(index, carried):
+        qkv_sum_ref[index] = (
+            wide_of(qkv_ref[index, core]) + wide_of(qkv_other_ref[index])
+        ).astype(jnp.bfloat16)
+        return carried
+
+    def start_qkv(k, carried):
+        qkv_copy(k, own_pair).start()
+        return carried
+
+    lax.fori_loop(0, size * pairs, qkv_sum, 0)
+    lax.fori_loop(1, size * pairs, start_qkv, 0)
+    qkv_got_ref[own_pair] = qkv_sum_ref[own_pair]
+
+    def out_copy(k, slot):
+        other = lax.rem(pair + k, pairs)
+        return copy(
+            out_part_ref.at[other],
+            out_got_ref.at[slot],
+            (head, other * 2 + core),
+            o_send.at[k],
+            o_recv.at[slot],
         )
 
     out_rows = out_grad_ref.shape[0]
-
-    def out_copy(k, slot):
-        other = lax.rem(blk + k, blk_size)
-        return pltpu.make_async_remote_copy(
-            src_ref=out_part_ref.at[other],
-            dst_ref=out_got_ref.at[slot],
-            send_sem=o_send.at[k],
-            recv_sem=o_recv.at[slot],
-            device_id=(head, other),
-            device_id_type=MESH,
-        )
-
-    def gain_copy(k, slot):
-        other = lax.rem(own + k, devices)
-        return pltpu.make_async_remote_copy(
-            src_ref=part_ref.at[other],
-            dst_ref=gain_got_ref.at[slot],
-            send_sem=g_send.at[k],
-            recv_sem=g_recv.at[slot],
-            device_id=place_of(other),
-            device_id_type=MESH,
-        )
-
-    def start_qkv(k, carried):
-        qkv_copy(k, own).start()
-        return carried
-
-    lax.fori_loop(1, devices, start_qkv, 0)
-    qkv_got_ref[own] = qkv_ref[rows_of(own)]
 
     def out_sum(index, carried):
         here = pl.ds(pl.multiple_of(index * out_rows, out_rows), out_rows)
-        total = out_refs[0][here].astype(jnp.float32)
+        total = wide_of(out_refs[0][here])
         for ref in out_refs[1:]:
-            total += ref[here].astype(jnp.float32)
+            total += wide_of(ref[here])
         out_part_ref[index, :out_rows] = total.astype(jnp.bfloat16)
         return carried
 
-    lax.fori_loop(0, blk_size, out_sum, 0)
-
     def start_out(k, carried):
-        out_copy(k, blk).start()
+        out_copy(k, pair).start()
         return carried
 
-    lax.fori_loop(1, blk_size, start_out, 0)
-    out_got_ref[blk] = out_part_ref[blk]
-    for copy in sends:
-        copy.wait_recv()
-
+    lax.fori_loop(0, pairs, out_sum, 0)
+    lax.fori_loop(1, pairs, start_out, 0)
+    out_got_ref[pair] = out_part_ref[pair]
+
+    loads[3].wait()
+    in_sends = [
+        copy(
+            in_ref.at[head ^ k],
+            in_got_ref.at[k - 1],
+            (head ^ k, blk),
+            i_send.at[k - 1],
+            i_recv.at[k - 1],
+        )
+        for k in range(1, size)
+    ]
+    for sent in in_sends:
+        sent.start()
+
+    for index in (0, 1, 2):
+        loads[index].wait()
+    for sent in sends:
+        sent.wait_recv()
     rows = min(128, count)
 
     def tile(index, gain_sum):
@@ -1232,12 +1470,12 @@
                 ROWS_IN_BOTH,
                 preferred_element_type=jnp.float32,
             )
-        values = x_ref[here].astype(jnp.float32)
+        values = wide_of(x_ref[here])
         inverse = lax.rsqrt(jnp.mean(values * values, axis=-1, keepdims=True) + EPS)
         scaled = normed_grad * gain_ref[...]
         moment = jnp.mean(scaled * values, axis=-1, keepdims=True)
         grad_ref[here] = (
-            residual_ref[here]
+            residual_grad_ref[here]
             + inverse * scaled
             - values * (inverse * inverse * inverse * moment)
         )
@@ -1267,6 +1505,12 @@
     part_ref[:, 0, :] = jnp.concatenate([by_device(attn_sum), by_device(ffn_ref[...])], axis=1)
     part_ref[:, 1, :] = jnp.broadcast_to(both, (devices, 2 * dim))
 
+    def gain_copy(k, slot):
+        other = lax.rem(own + k, devices)
+        return copy(
+            part_ref.at[other], gain_got_ref.at[slot], place_of(other), g_send.at[k], g_recv.at[slot]
+        )
+
     def start_gain(k, carried):
         gain_copy(k, own).start()
         return carried
@@ -1274,31 +1518,26 @@
     lax.fori_loop(1, devices, start_gain, 0)
     gain_got_ref[own] = part_ref[own]
 
-    def finish(k, carried):
-        source = lax.rem(own + devices - k, devices)
-        qkv_copy(k, source).wait()
-        gain_copy(k, source).wait()
+    units = in_ref.shape[2] // 2
+    for k in range(size):
+        if k:
+            in_sends[k - 1].wait_recv()
+        for part in range(2):
+            columns = pl.ds(pl.multiple_of((part * size + (head ^ k)) * units, units), units)
+            piece = slice(part * units, (part + 1) * units)
+            got = in_got_ref[k - 1, :, piece] if k else in_ref[head, :, piece]
+            in_grad_ref[:, columns] = wide_of(got)
+
+    def finish_qkv(k, carried):
+        qkv_copy(k, lax.rem(own_pair + size * pairs - k, size * pairs)).wait()
         return carried
 
-    lax.fori_loop(1, devices, finish, 0)
-
-    def finish_out(k, carried):
-        out_copy(k, lax.rem(blk + blk_size - k, blk_size)).wait()
-        return carried
-
-    lax.fori_loop(1, blk_size, finish_out, 0)
-    for copy in sends:
-        copy.wait_send()
-    out_total = out_got_ref[0, :out_rows].astype(jnp.float32)
-    for b in range(1, blk_size):
-        out_total += out_got_ref[b, :out_rows].astype(jnp.float32)
-    out_grad_ref[...] = out_total
-    gains_ref[...] = jnp.sum(gain_got_ref[...], axis=0)
+    lax.fori_loop(1, size * pairs, finish_qkv, 0)
 
     def group_sum(h):
-        total = qkv_got_ref[h * blk_size].astype(jnp.float32)
-        for b in range(1, blk_size):
-            total += qkv_got_ref[h * blk_size + b].astype(jnp.float32)
+        total = wide_of(qkv_got_ref[h * pairs])
+        for b in range(1, pairs):
+            total += wide_of(qkv_got_ref[h * pairs + b])
         return total
 
     sums = [group_sum(h) for h in range(size)]
@@ -1310,18 +1549,44 @@
         axis=1,
     )
 
+    def finish_out(k, carried):
+        out_copy(k, lax.rem(pair + pairs - k, pairs)).wait()
+        return carried
+
+    lax.fori_loop(1, pairs, finish_out, 0)
+    out_total = wide_of(out_got_ref[0, :out_rows])
+    for b in range(1, pairs):
+        out_total += wide_of(out_got_ref[b, :out_rows])
+    out_grad_ref[...] = out_total
+
+    def finish_gain(k, carried):
+        gain_copy(k, lax.rem(own + devices - k, devices)).wait()
+        return carried
+
+    lax.fori_loop(1, devices, finish_gain, 0)
+    gains_ref[...] = jnp.sum(gain_got_ref[...], axis=0)
+    across.wait_send()
+    for sent in sends + in_sends:
+        sent.wait_send()
+
 
 def finish(
-    sent, qkv_part, x, residual_grad, gain, ffn_sum, head_sum, weight, weights, outs, query_width, dim
+    sent, qkv_part, x, residual_grad, gain, ffn_sum, head_sum, weight, weights, outs, in_part,
+    query_width, dim
 ):
     size, blk_size = lax.axis_size("heads"), lax.axis_size("blk")
     devices = size * blk_size
+    pairs = blk_size // 2
     count, width = x.shape
     depth, joined = width // devices, sent.shape[1]
-    out_rows = outs[0].shape[0] // blk_size
+    out_rows = outs[0].shape[0] // pairs
     held_rows = -(-out_rows // 16) * 16
+    units = in_part.shape[2]
     vmem = pl.BlockSpec(memory_space=pltpu.VMEM)
+    anywhere = pl.BlockSpec(memory_space=pl.ANY)
     sems = pltpu.SemaphoreType.DMA
+    low = jnp.bfloat16
+    loaded = (weights, x, residual_grad, in_part)
     return pl.pallas_call(
         functools.partial(finish_kernel, query_width, dim),
         out_shape=[
@@ -1329,30 +1594,43 @@
             jax.ShapeDtypeStruct((depth, size * joined), jnp.float32),
             jax.ShapeDtypeStruct((8, 128), jnp.float32),
             jax.ShapeDtypeStruct((out_rows, width), jnp.float32),
-        ],
-        in_specs=[vmem] * (9 + size),
-        out_specs=[vmem] * 4,
-        scratch_shapes=[
-            pltpu.VMEM((size - 1, count, joined), jnp.bfloat16),
-            pltpu.VMEM((devices, depth, joined), jnp.bfloat16),
+            jax.ShapeDtypeStruct((depth, size * units), jnp.float32),
+        ],
+        in_specs=[vmem] * (6 + size) + [anywhere] * 4,
+        out_specs=[vmem] * 5,
+        scratch_shapes=[pltpu.VMEM(array.shape, array.dtype) for array in loaded]
+        + [
+            pltpu.VMEM((size - 1, count, joined), low),
+            pltpu.VMEM((size * pairs, depth, joined), low),
+            pltpu.VMEM((size * pairs, depth, joined), low),
+            pltpu.VMEM((size * pairs, depth, joined), low),
             pltpu.VMEM((devices, 8, 128), jnp.float32),
             pltpu.VMEM((devices, 8, 128), jnp.float32),
-            pltpu.VMEM((blk_size, held_rows, width), jnp.bfloat16),
-            pltpu.VMEM((blk_size, held_rows, width), jnp.bfloat16),
+            pltpu.VMEM((pairs, held_rows, width), low),
+            pltpu.VMEM((pairs, held_rows, width), low),
+            pltpu.VMEM((size - 1, depth, units), low),
+            sems((4,)),
             sems((size - 1,)),
             sems((size - 1,)),
+            sems,
+            sems,
+            sems((size * pairs,)),
+            sems((size * pairs,)),
             sems((devices,)),
             sems((devices,)),
-            sems((devices,)),
-            sems((devices,)),
-            sems((blk_size,)),
-            sems((blk_size,)),
+            sems((pairs,)),
+            sems((pairs,)),
+            sems((size - 1,)),
+            sems((size - 1,)),
         ],
         compiler_params=pltpu.CompilerParams(
-            collective_id=0, has_side_effects=True, vmem_limit_bytes=56 << 20
+            collective_id=0, has_side_effects=True, vmem_limit_bytes=60 << 20
         ),
         name="finish",
-    )(sent, qkv_part, x, residual_grad, gain, ffn_sum, head_sum, weight, weights, *outs)
+    )(
+        sent, qkv_part.reshape(size * pairs, 2, depth, joined), gain, ffn_sum, head_sum, weight,
+        *outs, *loaded
+    )
 
 
 def permute(block, axis, k):
@@ -1366,16 +1644,6 @@
 def pick(block, k, axis, dim):
     extent = block.shape[dim] // lax.axis_size(axis)
     return lax.dynamic_slice_in_dim(block, (lax.axis_index(axis) ^ k) * extent, extent, dim)
-
-
-def gather_near(block, *done):
-    half = block.shape[0] // 2
-    one, two = permute(block, "heads", 1), permute(block, "heads", 2)
-    if done:
-        one, two = lax.optimization_barrier((one, two, *done))[:2]
-    top = permute(one[:half], "heads", 2)
-    bottom = permute(two[half:], "heads", 1)
-    return block, one, two, top, bottom
 
 
 def wide(block):
@@ -1430,8 +1698,8 @@
     head_gain = jnp.concatenate(
         [jnp.tile(q_gain, HEADS // size), jnp.tile(k_gain, KV_HEADS // size)]
     ).astype(jnp.float32)[None, :]
-    query_low, pair_blk, raw, normed, attn_scaling, ffn_scaling = project(
-        own, inputs_blk, qkv_rows, head_gain, cosine, sine, size, query_width, 256
+    query_low, pair_blk, raw, normed, attn_scaling, ffn_scaling, out_peers = project(
+        inputs_blk, qkv_rows, head_gain, cosine, sine, out_group, size, query_width, 256
     )
     pair_all = jnp.concatenate([from_behind(pair_blk, "blk", 1), pair_blk], axis=0)
     query_rows, key_rows = token_count, 256
@@ -1441,50 +1709,39 @@
     attended_blk, logs = attend(query_low, pair_all, first, low, group_size, query_rows, key_rows)
 
     mine = jnp.concatenate([pick(attended_blk, k, "heads", 0) for k in range(size)], axis=0)
-    out_near = gather_near(after(out_group, inputs_blk))
-    out_all = (*out_near[:3], jnp.concatenate(out_near[3:], axis=0))
-    near = gather_near(mine)
-    residual, ffn_normed = join(
-        inputs_blk, near[:3], *near[3:], jnp.concatenate(out_all, axis=0), ffn_scaling, 256
+    late = after(cotangent, inputs_blk)
+    one_top, two_bottom = permute(late[:half], "heads", 1), permute(late[half:], "heads", 2)
+    residual, ffn_normed, attended_own, one_bottom, two_top = join(
+        inputs_blk, mine, out_group, out_peers, ffn_scaling, cotangent, 256
     )
     residual_own = residual[:token_count]
-    cotangent_near = gather_near(after(cotangent, inputs_blk), near[1])
-    cotangent_blk = jnp.concatenate(cotangent_near, axis=0)
-
     qkv_group = qkv_rows[:, :qkv_width]
-    hidden, gate_grad, up_grad, qkv_peers = hidden_pass(
-        ffn_normed, in_group, cotangent_blk, down_group, qkv_group, block_len // 2, 256
-    )
-    down_sum = turned_product(hidden, cotangent_blk, 256)
+    hidden, gate_grad, up_grad, down_sum, qkv_peers = hidden_pass(
+        ffn_normed,
+        in_group,
+        cotangent,
+        (one_top, one_bottom, two_top, two_bottom),
+        down_group,
+        qkv_group,
+        256,
+    )
     ffn_out_grad = lax.psum_scatter(down_sum, "blk", scatter_dimension=0, tiled=True)
-    in_sum, out_terms, grad_sum = feed_tail(
-        ffn_normed, gate_grad, up_grad, after(hidden, down_sum), in_group, down_group
+    in_sum, out_one, out_two, out_rest, grad_sum = feed_tail(
+        ffn_normed, gate_grad, up_grad, hidden, in_group, down_group
     )
     in_sum, ffn_out_grad = lax.optimization_barrier((in_sum, ffn_out_grad))
     in_part = lax.psum_scatter(
         in_sum.reshape(size, blk_size * depth, -1), "blk", scatter_dimension=1, tiled=True
     )
     ffn_out_grad = wide(ffn_out_grad)
-    attended_own = jnp.concatenate(
-        [
-            near[0][:token_count],
-            near[1][token_count : 2 * token_count],
-            near[2][2 * token_count : 3 * token_count],
-            near[4][token_count:],
-        ],
-        axis=1,
-    )
     residual_grad, ffn_sum, out_sum, grads = residual_back(
-        grad_sum, residual_own, cotangent, ffn_scaling, attended_own, out_all, min(128, half)
-    )
-    out_one, out_two, out_rest = (
-        out_terms[: 2 * half],
-        out_terms[2 * half : 4 * half],
-        out_terms[4 * half :],
+        grad_sum, residual, cotangent, ffn_scaling, attended_own, out_group, out_peers,
+        min(128, half)
     )
     out_one, out_two, grads = lax.optimization_barrier((out_one, out_two, grads))
     out_top, out_bottom = permute(out_one, "heads", 1), permute(out_two, "heads", 2)
-    out_slices = [out_sum[k * query_width : (k + 1) * query_width] for k in range(size)]
+    out_slices = jnp.split(out_sum.reshape(size, -1, width), size, axis=0)
+    out_slices = [piece[0] for piece in out_slices]
     out_slices = [out_slices[0]] + [permute(out_slices[k], "heads", k) for k in range(1, size)]
     query_grad, pair_sum = attend_back(
         query_low, pair_all, first, low, grads, attended_blk, logs, group_size, query_rows, key_rows
@@ -1509,16 +1766,10 @@
     projected_grad, head_sum = project_back(
         own, query_grad, pair_sum, returned, raw, head_gain, cosine, sine, size, 256
     )
-    qkv_part = turned_product(normed, projected_grad, 512)
-    input_grad, qkv_grad, gains, out_grad = finish(
+    qkv_part = turned_product(normed, [projected_grad], 512)
+    input_grad, qkv_grad, gains, out_grad, ffn_in_grad = finish(
         projected_grad, qkv_part, inputs, residual_grad, attn_scaling, ffn_sum, head_sum, qkv_group,
-        qkv_peers, out_slices, query_width, head_dim
-    )
-    in_pieces = [pick(in_part, k, "heads", 0)[0] for k in range(size)]
-    ffn_in_grad = settle(
-        own,
-        [in_pieces[0]] + [permute(in_pieces[k], "heads", k) for k in range(1, size)],
-        2,
+        qkv_peers, out_slices, in_part, query_width, head_dim
     )
     return (
         layer_out,

time: 722 us -> 623 us (0.86)
  waiting for transfers between devices: 132 us -> 26.2 us
  Pallas kernels: 476 us -> 515 us
  local copies, waits for them, and re-layouts: 48.8 us -> 27.7 us
  starting transfers between devices: 25.1 us -> 13 us
    ppermute x22 -> x9, waiting for transfers between devices: 130 us -> 7.54 us  [permute(): lax.ppermute(block, axis, [(i, i ^ k) for i in range(lax.axis_size(axis))])]
    pallas_call x4 -> x3, Pallas kernels: 90.7 us -> 162 us  [the longest x1 72.9 us: hidden_pass(): pl.pallas_call(functools.partial(hidden_kernel, tiles), grid=(3 * tiles,)...]
    reduce_scatter x1, waiting for transfers between devices: 0.01 us -> 17.2 us  [local(): lax.psum_scatter(in_sum.reshape(size, blk_size * depth, -1), 'blk', scatt...]
    slice x12 -> x1, local copies, waits for them, and re-layouts: 18.5 us -> 1.44 us  [local(): late[half:]]
    pallas_call x2 -> x1, Pallas kernels: 25.1 us -> 9.85 us  [turned_product(): pl.pallas_call(turned_kernel, grid=(height // rows,), in_specs=[pl.BlockS...]
    pallas_call x1, Pallas kernels: 82.4 us -> 69.1 us  [finish(): pl.pallas_call(functools.partial(finish_kernel, query_width, dim), out_sh...]
    ppermute x22 -> x9, starting transfers between devices: 21.6 us -> 9.76 us  [permute(): lax.ppermute(block, axis, [(i, i ^ k) for i in range(lax.axis_size(axis))])]
    unnamed x80 -> x53, local copies, waits for them, and re-layouts: 19.4 us -> 13.3 us
  transfers between devices with their start and end apart: 29 -> 16, of which waited for: 9 -> 2; matrix products, arithmetic and copies ran while one was open for 8% -> 5% of each run, Pallas kernels for 57% -> 61%
where the time goes in v4:
time: 623 us; the launch traced here: 614 us
  Pallas kernels  515 us (83%)
  local copies, waits for them, and re-layouts  27.7 us (4%)
  waiting for transfers between devices  26.2 us (4%)
  other arithmetic  17 us (3%)
  between operations  14.7 us (2%)
  starting transfers between devices  13 us (2%)
    pallas_call x1, Pallas kernels, feed_tail(): pl.pallas_call(tail_kernel, grid=(24,), in_specs=[pl.BlockSpec((count, ro...  94.4 us
    pallas_call x1, Pallas kernels, begin(): pl.pallas_call(begin_kernel, out_shape=[jax.ShapeDtypeStruct((size * coun...  92.6 us
    pallas_call x1, Pallas kernels, hidden_pass(): pl.pallas_call(functools.partial(hidden_kernel, tiles), grid=(3 * tiles,)...  72.9 us
    pallas_call x1, Pallas kernels, finish(): pl.pallas_call(functools.partial(finish_kernel, query_width, dim), out_sh...  69.1 us
    pallas_call x1, Pallas kernels, join(): pl.pallas_call(join_kernel, grid=(count // rows,), in_specs=[pl.BlockSpec...  60.2 us
    pallas_call x1, Pallas kernels, attend_back(): pl.pallas_call(functools.partial(attend_back_kernel, heads, key_rows, (wi...  34.4 us
    pallas_call x1, Pallas kernels, project(): pl.pallas_call(functools.partial(project_kernel, dim), grid=(count // row...  29 us
    pallas_call x1, Pallas kernels, residual_back(): pl.pallas_call(residual_back_kernel, grid=(tiles + 1,), in_specs=[tile, t...  27.5 us
  transfers between devices with their start and end apart: 16, of which 2 were waited for; matrix products, arithmetic and copies ran while one was open for 5% of the time, Pallas kernels for 61%

profile of v4, /device:TPU:0, one launch (start us, length us, event | category | flops | bytes accessed | tf_op | source)
XLA Modules:
  0.0 613.7 jit_solution(18212902002185495975)
XLA Ops:
  13.0 92.6 %begin.1 = (bf16[2048,2048]{1,0:T(8,128)(2,1)}, bf16[4,512,512]{2,1,0:T(8,128)(2,1)}, bf16[4,64,2560]{2,1,0:T(8,128)(2,1)}) custom-call(bf16[512,2048]{1,0:T(8,128)(2,1)} %refs_1_.1, bf16[4,64,512]{2,1,0:T(8,128)(2,1)} %bitcast.31, bf16[64,10240]{1,0:T(8,128)(2,1)} %in_ref.1), custom_call_target="tpu_custom_call" | custom-call | tf_op jit(solution)/shard_map/begin/pallas_call | solution.py:682
  105.9 3.7 fusion
  111.5 29.0 %project.1 = (bf16[2048,256]{1,0:T(8,128)(2,1)S(1)}, bf16[2048,128]{1,0:T(8,128)(2,1)S(1)}, f32[2048,384]{1,0:T(8,128)}, bf16[2048,2048]{1,0:T(8,128)(2,1)}, f32...) custom-call(bf16[2048,2048]{1,0:T(8,128)(2,1)} %get-tuple-element.59.x_ref, ...), custom_call_target="tpu_custom_call" | custom-call | flops 6442450944 | bytes 30000000 | tf_op jit(solution)/shard_map/project/pallas_call | solution.py:303
  140.5 1.5 collective-permute-start
  143.5 1.9 collective-permute-start.2
  145.6 2.7 slice.96.side_ref.weight_ref
  149.8 15.9 %attend.1 = (bf16[2048,256]{1,0:T(8,128)(2,1)S(1)}, f32[4,1,2048]{2,1,0:T(1,128)S(1)}) custom-call(s32[5]{0:T(128)S(1)} %pad_add_fusion.first_ref, bf16[2048,256]{1,0:T(8,128)(2,1)S(1)} %copy-done.11, s32[1,2048]{1,0:T(1,128)S(1)} %bitcast.24, bf16[4096,128]{1,0:T(8,128)(2,1)S(1)} %constant_dynamic-update-slice_fusion.pair_ref), custom_call_target="tpu_custom_call" | custom-call | flops 20000000000 | bytes 8000000 | tf_op jit(solution)/shard_map/attend/pallas_call | solution.py:158
  166.9 60.2 %join.1 = (f32[2048,2048]{1,0:T(8,128)}, bf16[2048,2048]{1,0:T(8,128)(2,1)}, bf16[512,1024]{1,0:T(8,128)(2,1)}, bf16[256,2048]{1,0:T(8,128)(2,1)}, bf16[256,2048]{1,0:T(8,128)(2,1)}) custom-call(bf16[2048,2048]{1,0:T(8,128)(2,1)} %get-tuple-element.59.x_ref, bf16[256,2048]{1,0:T(8,128)(2,1)} %all-gather.4.cloned.1.call-done.side_ref.weight_ref, ...), custom_call_target="tpu_custom_call" | custom-call | flops 17179869184 | bytes 50000000 | tf_op jit(solution)/shard_map/join/pallas_call | solution.py:499
  227.3 72.9 %hidden_pass.1 = (bf16[2048,1280]{1,0:T(8,128)(2,1)}, bf16[2048,1280]{1,0:T(8,128)(2,1)}, bf16[2048,1280]{1,0:T(8,128)(2,1)}, bf16[1280,2048]{1,0:T(8,128)(2,1)}, bf16[3,2048,384]{2,1,0:T(8,128)(2,1)}) custom-call(bf16[2048,2048]{1,0:T(8,128)(2,1)} %get-tuple-element.67.normed_ref, bf16[2048,2560]{1,0:T(8,128)(2,1)} %bitcast.35, ...), custom_call_target="tpu_custom_call" | custom-call | flops 42949672960 | bytes 70000000 | tf_op jit(solution)/shard_map/hidden_pass/pallas_call | solution.py:882
  300.4 94.4 %feed_tail.1 = (bf16[2048,2560]{1,0:T(8,128)(2,1)}, bf16[512,2048]{1,0:T(8,128)(2,1)}, bf16[512,2048]{1,0:T(8,128)(2,1)}, bf16[1024,2048]{1,0:T(8,128)(2,1)}, f32[512,2048]{1,0:T(8,128)}) custom-call(bf16[2048,2048]{1,0:T(8,128)(2,1)} %get-tuple-element.67.normed_ref, bf16[2048,1280]{1,0:T(8,128)(2,1)} %get-tuple-element.72.gate_ref, ...), custom_call_target="tpu_custom_call" | custom-call | flops 53687091200 | bytes 70000000 | tf_op jit(solution)/shard_map/feed_tail/pallas_call | solution.py:1072
  394.9 27.5 %residual_back.1 = (f32[512,2048]{1,0:T(8,128)}, f32[1,2048]{1,0:T(1,128)}, bf16[16,32,2048]{2,1,0:T(8,128)(2,1)}, bf16[4,512,256]{2,1,0:T(8,128)(2,1)}) custom-call(f32[512,2048]{1,0:T(8,128)} %get-tuple-element.78.grad_sum_ref, f32[2048,2048]{1,0:T(8,128)} %get-tuple-element.66.residual_ref, bf16[512,2048]{1,0:T(8,128)(2,1)} %cot_ref.5, ...), custom_call_target="tpu_custom_call" | custom-call | flops 4294967296 | bytes 30000000 | tf_op jit(solution)/shard_map/residual_back/pallas_call | solution.py:1229
  425.7 34.4 %attend_back.1 = (bf16[2048,256]{1,0:T(8,128)(2,1)S(1)}, f32[4096,128]{1,0:T(8,128)}) custom-call(s32[5]{0:T(128)S(1)} %pad_add_fusion.first_ref, bf16[2048,256]{1,0:T(8,128)(2,1)S(1)} %copy-done.12, s32[1,2048]{1,0:T(1,128)S(1)} %bitcast.25, bf16[4096,128]{1,0:T(8,128)(2,1)S(1)} %copy-done.3, bf16[2048,256]{1,0:T(8,128)(2,1)S(1)} %get-tuple-element.65.out_ref, ...), custom_call_target="tpu_custom_call" | custom-call | flops 40000000000 | bytes 12000000 | tf_op jit(solution)/shard_map/attend_back/pallas_call | solution.py:187
  462.7 3.1 fusion.1
  466.7 1.5 collective-permute-start.10
  469.3 4.3 add_convert_fusion.3
  475.6 9.2 %project_back.1 = (bf16[2048,384]{1,0:T(8,128)(2,1)S(1)}, f32[1,320]{1,0:T(1,128)S(1)}) custom-call(s32[1]{0:T(128)} %bitcast.3.own_ref, bf16[2048,256]{1,0:T(8,128)(2,1)S(1)} %get-tuple-element.88.query_grad_ref, f32[4096,128]{1,0:T(8,128)} %get-tuple-element.85.pair_grad_ref, bf16[2048,128]{1,0:T(8,128)(2,1)S(1)} %collective-permute-done.5.returned_ref, ...), custom_call_target="tpu_custom_call" | custom-call | flops 8000000000 | bytes 8000000 | tf_op jit(solution)/shard_map/project_back/pallas_call | solution.py:381
  486.6 9.9 %turned_product.1 = bf16[2048,384]{1,0:T(8,128)(2,1)} custom-call(bf16[2048,2048]{1,0:T(8,128)(2,1)} %get-tuple-element.92.left_ref, bf16[2048,384]{1,0:T(8,128)(2,1)} %copy-done), custom_call_target="tpu_custom_call" | custom-call | flops 3221225472 | bytes 20000000 | tf_op jit(solution)/shard_map/turned_product/pallas_call | solution.py:1295
  496.4 7.5 %collective-permute-done.6 = bf16[256,2048]{1,0:T(8,128)(2,1)S(1)} collective-permute-done((bf16[256,2048]{1,0:T(8,128)(2,1)}, bf16[256,2048]{1,0:T(8,128)(2,1)S(1)}, u32[]{:S(2)}, u32[]{:S(2)}) %collective-permute-start.6) | collective-permute-done | bytes 1048608 | tf_op jit(solution)/shard_map/ppermute | solution.py:1637
  504.0 4.6 add_convert_fusion.2
  508.6 1.5 pad_maximum_fusion
  511.2 17.2 %reduce-scatter.5.cloned.1.call-done.refs_3_ = bf16[4,64,2560]{2,1,0:T(8,128)(2,1)} async-done(((bf16[4,512,2560]{2,1,0:T(8,128)(2,1)}), bf16[4,64,2560]{2,1,0:T(8,128)(2,1)}) %reduce-scatter.5.cloned.1.call-update) | async-done | bytes 1310736 | tf_op jit(solution)/shard_map/reduce_scatter | solution.py:1733
  528.4 69.1 %finish.1 = (f32[512,2048]{1,0:T(8,128)}, f32[64,1536]{1,0:T(8,128)}, f32[8,128]{1,0:T(8,128)}, f32[32,2048]{1,0:T(8,128)}, f32[64,10240]{1,0:T(8,128)}) custom-call(bf16[2048,384]{1,0:T(8,128)(2,1)} %copy-done, bf16[16,2,64,384]{3,2,1,0:T(8,128)(2,1)} %bitcast.28, f32[1,2048]{1,0:T(1,128)} %copy-done.4, f32[1,2048]{1,0:T(1,128)} %get-tuple-element.94.ffn_ref, ...), custom_call_target="tpu_custom_call" | custom-call | tf_op jit(solution)/shard_map/finish/pallas_call | solution.py:1590
  599.0 4.8 copy.36
  605.3 1.5 copy.39
  (109 shorter events, 28.2 us)
Async XLA Ops:
  7.2 103.1 %all-gather.4.cloned.1.call-start = ((), (), s32[]{:S(2)}) async-start(), calls=%async_computation.2 | async-start | bytes 1179648 | tf_op jit(solution)/shard_map/all_gather | solution.py:1689
  7.9 219.3 %all-gather.8.cloned.1.call-start = ((), (), s32[]{:S(2)}) async-start(), calls=%async_computation.4 | async-start | bytes 5898240 | tf_op jit(solution)/shard_map/all_gather | solution.py:1690
  8.7 218.6 %all-gather.6.cloned.1.call-start = ((), (), s32[]{:S(2)}) async-start(), calls=%async_computation.3 | async-start | bytes 11796480 | tf_op jit(solution)/shard_map/all_gather | solution.py:1693
  13.0 92.7 %copy-start.23 = (bf16[64]{0:T(256)(128)(2,1)S(1)}, bf16[64]{0:T(256)(128)(2,1)}, u32[]{:S(2)}) copy-start(bf16[64]{0:T(256)(128)(2,1)} %param.15) | copy-start | bytes 388
  13.0 92.8 %copy-start.22 = (bf16[64]{0:T(256)(128)(2,1)S(1)}, bf16[64]{0:T(256)(128)(2,1)}, u32[]{:S(2)}) copy-start(bf16[64]{0:T(256)(128)(2,1)} %param.16) | copy-start | bytes 388
  13.0 92.8 %copy-start.21 = (s32[2048]{0:T(1024)S(1)}, s32[2048]{0:T(1024)}, u32[]{:S(2)}) copy-start(s32[2048]{0:T(1024)} %param.12) | copy-start | bytes 24580
  105.7 289.2 %reduce-scatter.3.cloned.1.call-start = ((), (), s32[]{:S(2)}) async-start(), calls=%async_computation.5 | async-start | bytes 5898240 | tf_op jit(solution)/shard_map/reduce_scatter | solution.py:1728
  111.5 30.5 %copy-start.13 = (bf16[512,2048]{1,0:T(8,128)(2,1)S(1)}, bf16[512,2048]{1,0:T(8,128)(2,1)}, u32[]{:S(2)}) copy-start(bf16[512,2048]{1,0:T(8,128)(2,1)} %cot_ref.5) | copy-start | bytes 6291460
  140.5 8.0 %collective-permute-start = (bf16[2048,128]{1,0:T(8,128)(2,1)S(1)}, bf16[2048,128]{1,0:T(8,128)(2,1)S(1)}, u32[]{:S(2)}, u32[]{:S(2)}) collective-permute-start(bf16[2048,128]{1,0:T(8,128)(2,1)S(1)} %get-tuple-element.64), channel_id=1, source_target_pairs={{0,1},{1,2},{2,3},{3,4},{4,5},{5,6},{6,7},{8,9},{9,10},{10,11},{11... | collective-permute-start | bytes 1572872 | tf_op jit(solution)/shard_map/ppermute | solution.py:24
  143.5 83.7 %collective-permute-start.2 = (bf16[256,2048]{1,0:T(8,128)(2,1)}, bf16[256,2048]{1,0:T(8,128)(2,1)}, u32[]{:S(2)}, u32[]{:S(2)}) collective-permute-start(bf16[256,2048]{1,0:T(8,128)(2,1)} %get-tuple-element.116), channel_id=1, source_target_pairs={{0,16},{8,24},{16,0},{24,8},{1,17},{9,25},{17,1},{25,9},{2,18},{10... | collective-permute-start | bytes 3145736 | tf_op jit(solution)/shard_map/ppermute | solution.py:1637
  145.4 81.8 %collective-permute-start.1 = (bf16[256,2048]{1,0:T(8,128)(2,1)}, bf16[256,2048]{1,0:T(8,128)(2,1)}, u32[]{:S(2)}, u32[]{:S(2)}) collective-permute-start(bf16[256,2048]{1,0:T(8,128)(2,1)} %get-tuple-element.117), channel_id=1, source_target_pairs={{0,8},{8,0},{16,24},{24,16},{1,9},{9,1},{17,25},{25,17},{2,10},{10... | collective-permute-start | bytes 3145736 | tf_op jit(solution)/shard_map/ppermute | solution.py:1637
  148.6 17.2 %copy-start.2 = (bf16[4096,128]{1,0:T(8,128)(2,1)}, bf16[4096,128]{1,0:T(8,128)(2,1)S(1)}, u32[]{:S(2)}) copy-start(bf16[4096,128]{1,0:T(8,128)(2,1)S(1)} %constant_dynamic-update-slice_fusion.pair_ref) | copy-start | bytes 3145732
  300.2 228.2 %reduce-scatter.5.cloned.1.call-start = ((), (), s32[]{:S(2)}) async-start(), calls=%async_computation.6 | async-start | bytes 11796480 | tf_op jit(solution)/shard_map/reduce_scatter | solution.py:1733
  394.9 29.6 %copy-start.3 = (bf16[4096,128]{1,0:T(8,128)(2,1)S(1)}, bf16[4096,128]{1,0:T(8,128)(2,1)}, u32[]{:S(2)}) copy-start(bf16[4096,128]{1,0:T(8,128)(2,1)} %copy-done.2) | copy-start | bytes 3145732
  394.9 29.6 %copy-start.12 = (bf16[2048,256]{1,0:T(8,128)(2,1)S(1)}, bf16[2048,256]{1,0:T(8,128)(2,1)}, u32[]{:S(2)}) copy-start(bf16[2048,256]{1,0:T(8,128)(2,1)} %copy-done.10) | copy-start | bytes 3145732
  422.4 46.9 %collective-permute-start.3 = (bf16[512,2048]{1,0:T(8,128)(2,1)}, bf16[512,2048]{1,0:T(8,128)(2,1)S(1)}, u32[]{:S(2)}, u32[]{:S(2)}) collective-permute-start(bf16[512,2048]{1,0:T(8,128)(2,1)} %get-tuple-element.81), channel_id=1, source_target_pairs={{0,8},{8,0},{16,24},{24,16},{1,9},{9,1},{17,25},{25,17},{2,10},{10... | collective-permute-start | bytes 6291464 | tf_op jit(solution)/shard_map/ppermute | solution.py:1637
  423.3 46.0 %collective-permute-start.4 = (bf16[512,2048]{1,0:T(8,128)(2,1)}, bf16[512,2048]{1,0:T(8,128)(2,1)}, u32[]{:S(2)}, u32[]{:S(2)}) collective-permute-start(bf16[512,2048]{1,0:T(8,128)(2,1)} %get-tuple-element.82), channel_id=1, source_target_pairs={{0,16},{8,24},{16,0},{24,8},{1,17},{9,25},{17,1},{25,9},{2,18},{10... | collective-permute-start | bytes 6291464 | tf_op jit(solution)/shard_map/ppermute | solution.py:1637
  461.4 6.7 %collective-permute-start.5 = (bf16[2048,128]{1,0:T(8,128)(2,1)S(1)}, bf16[2048,128]{1,0:T(8,128)(2,1)S(1)}, u32[]{:S(2)}, u32[]{:S(2)}) collective-permute-start(bf16[2048,128]{1,0:T(8,128)(2,1)S(1)} %slice.113), channel_id=1, source_target_pairs={{1,0},{2,1},{3,2},{4,3},{5,4},{6,5},{7,6},{9,8},{10,9},{11,10},{12... | collective-permute-start | bytes 1572872 | tf_op jit(solution)/shard_map/ppermute | solution.py:24
  465.8 45.5 %collective-permute-start.9 = (bf16[128,2048]{1,0:T(8,128)(2,1)}, bf16[128,2048]{1,0:T(8,128)(2,1)}, u32[]{:S(2)}, u32[]{:S(2)}) collective-permute-start(bf16[128,2048]{1,0:T(8,128)(2,1)} %bitcast.9), channel_id=1, source_target_pairs={{0,16},{8,24},{16,0},{24,8},{1,17},{9,25},{17,1},{25,9},{2,18},{10... | collective-permute-start | bytes 1572872 | tf_op jit(solution)/shard_map/ppermute | solution.py:1637
  466.7 44.6 %collective-permute-start.10 = (bf16[128,2048]{1,0:T(8,128)(2,1)}, bf16[128,2048]{1,0:T(8,128)(2,1)}, u32[]{:S(2)}, u32[]{:S(2)}) collective-permute-start(bf16[128,2048]{1,0:T(8,128)(2,1)} %bitcast.10), channel_id=1, source_target_pairs={{0,24},{8,16},{16,8},{24,0},{1,25},{9,17},{17,9},{25,1},{2,26},{10... | collective-permute-start | bytes 1572872 | tf_op jit(solution)/shard_map/ppermute | solution.py:1637
  468.1 43.1 %collective-permute-start.8 = (bf16[128,2048]{1,0:T(8,128)(2,1)}, bf16[128,2048]{1,0:T(8,128)(2,1)}, u32[]{:S(2)}, u32[]{:S(2)}) collective-permute-start(bf16[128,2048]{1,0:T(8,128)(2,1)} %bitcast.8), channel_id=1, source_target_pairs={{0,8},{8,0},{16,24},{24,16},{1,9},{9,1},{17,25},{25,17},{2,10},{10... | collective-permute-start | bytes 1572872 | tf_op jit(solution)/shard_map/ppermute | solution.py:1637
  473.6 30.4 %collective-permute-start.6 = (bf16[256,2048]{1,0:T(8,128)(2,1)}, bf16[256,2048]{1,0:T(8,128)(2,1)S(1)}, u32[]{:S(2)}, u32[]{:S(2)}) collective-permute-start(bf16[256,2048]{1,0:T(8,128)(2,1)} %get-tuple-element.110), channel_id=1, source_target_pairs={{0,16},{8,24},{16,0},{24,8},{1,17},{9,25},{17,1},{25,9},{2,18},{10... | collective-permute-start | bytes 3145736 | tf_op jit(solution)/shard_map/ppermute | solution.py:1637
  474.4 29.5 %collective-permute-start.7 = (bf16[256,2048]{1,0:T(8,128)(2,1)}, bf16[256,2048]{1,0:T(8,128)(2,1)}, u32[]{:S(2)}, u32[]{:S(2)}) collective-permute-start(bf16[256,2048]{1,0:T(8,128)(2,1)} %get-tuple-element.111), channel_id=1, source_target_pairs={{0,8},{8,0},{16,24},{24,16},{1,9},{9,1},{17,25},{25,17},{2,10},{10... | collective-permute-start | bytes 3145736 | tf_op jit(solution)/shard_map/ppermute | solution.py:1637
  486.6 17.4 %copy-start.15 = (bf16[1024,2048]{1,0:T(8,128)(2,1)S(1)}, bf16[1024,2048]{1,0:T(8,128)(2,1)}, u32[]{:S(2)}) copy-start(bf16[1024,2048]{1,0:T(8,128)(2,1)} %get-tuple-element.75) | copy-start | bytes 12582916
  (16 other events, 54.4 us)
Sparse Core Ops, SparseCore 0:
  9.6 49.3 all-gather.3
  60.7 60.0 all-gather.7
  122.3 98.6 all-gather.5
  300.3 77.3 reduce-scatter.2
  395.0 133.3 reduce-scatter.4

commit v5 on v4

--- a/solution.py
+++ b/solution.py
@@ -99,7 +99,7 @@
 def attend_back_kernel(
     heads, key_rows, scale, first_ref, query_ref, low_ref, pair_ref, out_ref, log_ref, *refs
 ):
-    grads_ref, query_grad_ref, pair_grad_ref, turned_ref, sum_ref = refs
+    grads_ref, query_grad_ref, pair_grad_ref, behind_ref, turned_ref, sum_ref = refs
     step = pl.program_id(0)
     grad = grads_ref[first_ref[pl.num_programs(0)] ^ step]
     query_rows = query_ref.shape[0]
@@ -139,6 +139,10 @@
 
     lax.fori_loop(first_ref[step], (base + query_rows - 1) // key_rows + 1, tile, 0)
     query_grad_ref[...] = unstack_heads(sum_ref[...] * scale, heads).astype(query_grad_ref.dtype)
+
+    @pl.when(step == pl.num_programs(0) - 1)
+    def _():
+        behind_ref[...] = pair_grad_ref[: behind_ref.shape[0]].astype(behind_ref.dtype)
 
 
 def attention_specs(queries, pair, query_rows, heads):
@@ -184,6 +188,7 @@
     count, width = queries.shape
     tile, row, whole, log_spec = attention_specs(queries, pair, query_rows, heads)
     columns = heads * query_rows
+    behind = (pair.shape[0] // 2, pair.shape[1])
     return pl.pallas_call(
         functools.partial(attend_back_kernel, heads, key_rows, (width // heads) ** -0.5),
         grid_spec=pltpu.PrefetchScalarGridSpec(
@@ -191,7 +196,7 @@
             grid=(count // query_rows,),
             in_specs=[tile, row, whole, tile, log_spec]
             + [pl.BlockSpec(grads.shape, lambda i, first: (0, 0, 0))],
-            out_specs=[tile, whole],
+            out_specs=[tile, whole, pl.BlockSpec(behind, lambda i, first: (0, 0))],
             scratch_shapes=[
                 pltpu.VMEM(pair.shape[::-1], jnp.bfloat16),
                 pltpu.VMEM((pair.shape[1] // 2, columns), jnp.float32),
@@ -200,6 +205,7 @@
         out_shape=[
             jax.ShapeDtypeStruct((count, width), jnp.bfloat16),
             jax.ShapeDtypeStruct(pair.shape, jnp.float32),
+            jax.ShapeDtypeStruct(behind, jnp.bfloat16),
         ],
         compiler_params=pltpu.CompilerParams(vmem_limit_bytes=48 << 20),
         cost_estimate=pl.CostEstimate(
@@ -341,14 +347,51 @@
 
 
 def project_back_kernel(
-    dim, own_ref, query_grad_ref, pair_grad_ref, returned_ref, raw_ref, head_gain_ref, cosine_ref,
-    sine_ref, grad_ref, gain_grad_ref
+    dim, size, query_grad_ref, pair_grad_ref, raw_ref, head_gain_ref, cosine_ref, sine_ref,
+    behind_ref, grad_ref, gain_grad_ref, returned_ref, send_sem, recv_sem
 ):
-    @pl.when(pl.program_id(0) == 0)
-    def _():
+    step = pl.program_id(0)
+    head, blk = lax.axis_index("heads"), lax.axis_index("blk")
+    last = lax.axis_size("blk") - 1
+    rows = raw_ref.shape[0]
+    tiles = returned_ref.shape[0] // size // rows
+    back = pltpu.make_async_remote_copy(
+        src_ref=behind_ref,
+        dst_ref=returned_ref,
+        send_sem=send_sem,
+        recv_sem=recv_sem,
+        device_id=(head, jnp.maximum(blk - 1, 0)),
+        device_id_type=MESH,
+    )
+
+    @pl.when(step == 0)
+    def _():
+        barrier = pltpu.get_barrier_semaphore()
+
+        @pl.when(blk < last)
+        def _():
+            pl.semaphore_signal(
+                barrier, inc=1, device_id=(head, blk + 1), device_id_type=MESH
+            )
+
+        @pl.when(blk > 0)
+        def _():
+            pl.semaphore_wait(barrier, 1)
+            back.start()
+
+        @pl.when(blk == last)
+        def _():
+            returned_ref[...] = jnp.zeros_like(returned_ref)
+
+        @pl.when(blk < last)
+        def _():
+            back.wait_recv()
+
         gain_grad_ref[...] = jnp.zeros_like(gain_grad_ref)
 
-    pair_grad = pair_grad_ref[...] + returned_ref[...].astype(jnp.float32)
+    place = ((head ^ (step // tiles)) * tiles + lax.rem(step, tiles)) * rows
+    returned = returned_ref[pl.ds(pl.multiple_of(place, rows), rows)]
+    pair_grad = pair_grad_ref[...] + returned.astype(jnp.float32)
     pair_grad = pair_grad.astype(jnp.bfloat16)
     half = pair_grad.shape[1] // 2
     grads = jnp.concatenate([query_grad_ref[...], pair_grad[:, :half]], axis=1).astype(jnp.float32)
@@ -358,55 +401,63 @@
     gain_grad_ref[...] += jnp.sum(grads * values * inverse, axis=0, keepdims=True)
     scaled = grads * head_gain_ref[...]
     moment = spread_mean(scaled * values, dim)
-    back = inverse * scaled - values * inverse * inverse * inverse * moment
-    grad_ref[...] = jnp.concatenate([back.astype(jnp.bfloat16), pair_grad[:, half:]], axis=1)
-
-
-def project_back(own, query_grad, pair_sum, returned, raw, head_gain, cosine, sine, size, rows):
+    values_grad = inverse * scaled - values * inverse * inverse * inverse * moment
+    grad_ref[...] = jnp.concatenate([values_grad.astype(jnp.bfloat16), pair_grad[:, half:]], axis=1)
+
+    @pl.when((step == pl.num_programs(0) - 1) & (blk > 0))
+    def _():
+        back.wait_send()
+
+
+def project_back(query_grad, pair_sum, behind, raw, head_gain, cosine, sine, size, rows):
     count, query_width = query_grad.shape
     pair_width = pair_sum.shape[1]
     out_width = raw.shape[1]
     dim = cosine.shape[1]
     tiles = count // size // rows
 
-    def apart(i, own):
-        return ((own[0] ^ (i // tiles)) * tiles + i % tiles, 0)
-
-    def behind(i, own):
-        return (apart(i, own)[0] + count // rows, 0)
-
-    def whole(i, own):
+    def apart(i):
+        return ((lax.axis_index("heads") ^ (i // tiles)) * tiles + i % tiles, 0)
+
+    def after_behind(i):
+        return (apart(i)[0] + count // rows, 0)
+
+    def whole(i):
         return (0, 0)
 
     return pl.pallas_call(
-        functools.partial(project_back_kernel, dim),
-        grid_spec=pltpu.PrefetchScalarGridSpec(
-            num_scalar_prefetch=1,
-            grid=(count // rows,),
-            in_specs=[
-                pl.BlockSpec((rows, query_width), apart),
-                pl.BlockSpec((rows, pair_width), behind),
-                pl.BlockSpec((rows, pair_width), apart),
-                pl.BlockSpec((rows, out_width), apart),
-                pl.BlockSpec(head_gain.shape, whole),
-                pl.BlockSpec((rows, dim), apart),
-                pl.BlockSpec((rows, dim), apart),
-            ],
-            out_specs=[
-                pl.BlockSpec((rows, out_width), lambda i, own: (i, 0)),
-                pl.BlockSpec(head_gain.shape, whole),
-            ],
-        ),
+        functools.partial(project_back_kernel, dim, size),
+        grid=(count // rows,),
+        in_specs=[
+            pl.BlockSpec((rows, query_width), apart),
+            pl.BlockSpec((rows, pair_width), after_behind),
+            pl.BlockSpec((rows, out_width), apart),
+            pl.BlockSpec(head_gain.shape, whole),
+            pl.BlockSpec((rows, dim), apart),
+            pl.BlockSpec((rows, dim), apart),
+            pl.BlockSpec(memory_space=pl.ANY),
+        ],
+        out_specs=[
+            pl.BlockSpec((rows, out_width), lambda i: (i, 0)),
+            pl.BlockSpec(head_gain.shape, whole),
+        ],
+        scratch_shapes=[
+            pltpu.VMEM(behind.shape, behind.dtype),
+            pltpu.SemaphoreType.DMA,
+            pltpu.SemaphoreType.DMA,
+        ],
         out_shape=[
             jax.ShapeDtypeStruct((count, out_width), jnp.bfloat16),
             jax.ShapeDtypeStruct(head_gain.shape, jnp.float32),
         ],
-        compiler_params=pltpu.CompilerParams(vmem_limit_bytes=48 << 20),
+        compiler_params=pltpu.CompilerParams(
+            collective_id=9, has_side_effects=True, vmem_limit_bytes=48 << 20
+        ),
         cost_estimate=pl.CostEstimate(
             flops=8_000_000_000, bytes_accessed=8_000_000, transcendentals=0
         ),
         name="project_back",
-    )(own, query_grad, pair_sum, returned, raw, head_gain, cosine, sine)
+    )(query_grad, pair_sum, raw, head_gain, cosine, sine, behind)
 
 
 def join_kernel(
@@ -537,27 +588,78 @@
     )(x, weight, weights, gain, mine, cot)
 
 
+def trade_kernel(in_ref, out_ref, send_sem, recv_sem):
+    head, blk = lax.axis_index("heads"), lax.axis_index("blk")
+    size = lax.axis_size("heads")
+    units = out_ref.shape[2] // 2
+    barrier = pltpu.get_barrier_semaphore()
+    for k in range(1, size):
+        pl.semaphore_signal(barrier, inc=1, device_id=(head ^ k, blk), device_id_type=MESH)
+    pl.semaphore_wait(barrier, size - 1)
+
+    def columns(part, owner):
+        return pl.ds(pl.multiple_of((part * size + owner) * units, units), units)
+
+    copies = [
+        pltpu.make_async_remote_copy(
+            src_ref=in_ref.at[:, columns(part, head ^ k)],
+            dst_ref=out_ref.at[head, :, pl.ds(part * units, units)],
+            send_sem=send_sem.at[2 * k - 2 + part],
+            recv_sem=recv_sem.at[2 * k - 2 + part],
+            device_id=(head ^ k, blk),
+            device_id_type=MESH,
+        )
+        for k in range(1, size)
+        for part in range(2)
+    ]
+    for copy in copies:
+        copy.start()
+    for part in range(2):
+        out_ref[head, :, part * units : (part + 1) * units] = in_ref[:, columns(part, head)]
+    for copy in copies:
+        copy.wait()
+
+
+def trade(weight):
+    size = lax.axis_size("heads")
+    depth, width = weight.shape
+    vmem = pl.BlockSpec(memory_space=pltpu.VMEM)
+    return pl.pallas_call(
+        trade_kernel,
+        out_shape=jax.ShapeDtypeStruct((size, depth, width // size), weight.dtype),
+        in_specs=[vmem],
+        out_specs=vmem,
+        scratch_shapes=[pltpu.SemaphoreType.DMA((2 * size - 2,))] * 2,
+        compiler_params=pltpu.CompilerParams(
+            collective_id=8, has_side_effects=True, vmem_limit_bytes=16 << 20
+        ),
+        name="trade",
+    )(weight)
+
+
 def begin_kernel(
-    x_ref, qkv_ref, in_ref, x_out, qkv_out, in_out, local_sem, x_send, x_recv, q_send, q_recv,
-    w_send, w_recv, b_send, b_recv
+    x_ref, qkv_ref, x_out, qkv_out, local_sem, x_send, x_recv, q_send, q_recv, b_send, b_recv,
+    c_send, c_recv
 ):
     head, blk = lax.axis_index("heads"), lax.axis_index("blk")
     size, blk_size = lax.axis_size("heads"), lax.axis_size("blk")
+    pairs = blk_size // 2
     count, depth = x_ref.shape[0], qkv_ref.shape[1]
     half = count // 2
-    units = in_out.shape[2] // 2
     barrier = pltpu.get_barrier_semaphore()
     for k in range(1, size):
         pl.semaphore_signal(barrier, inc=1, device_id=(head ^ k, blk), device_id_type=MESH)
+    pl.semaphore_signal(barrier, inc=1, device_id=(head, blk ^ 1), device_id_type=MESH)
+
+    def same_core(k):
+        return lax.rem(blk + 2 * k, blk_size)
 
     def greet(k, carried):
-        pl.semaphore_signal(
-            barrier, inc=1, device_id=(head, lax.rem(blk + k, blk_size)), device_id_type=MESH
-        )
+        pl.semaphore_signal(barrier, inc=1, device_id=(head, same_core(k)), device_id_type=MESH)
         return carried
 
-    lax.fori_loop(1, blk_size, greet, 0)
-    pl.semaphore_wait(barrier, size + blk_size - 2)
+    lax.fori_loop(1, pairs, greet, 0)
+    pl.semaphore_wait(barrier, size + pairs - 1)
 
     def send(source, target, k, send_sem, recv_sem):
         return pltpu.make_async_remote_copy(
@@ -569,27 +671,15 @@
             device_id_type=MESH,
         )
 
-    rows = pl.ds(pl.multiple_of(blk * depth, depth), depth)
+    def rows_of(index):
+        return pl.ds(pl.multiple_of(index * depth, depth), depth)
+
+    rows = rows_of(blk)
     qkv_copies = [
         send(
             qkv_ref.at[head ^ k], qkv_out.at[head, rows], k, q_send.at[k - 1], q_recv.at[k - 1]
         )
         for k in range(1, size)
-    ]
-
-    def columns(part, owner):
-        return pl.ds(pl.multiple_of((part * size + owner) * units, units), units)
-
-    in_copies = [
-        send(
-            in_ref.at[:, columns(part, head ^ k)],
-            in_out.at[head, :, pl.ds(part * units, units)],
-            k,
-            w_send.at[2 * k - 2 + part],
-            w_recv.at[2 * k - 2 + part],
-        )
-        for k in range(1, size)
-        for part in range(2)
     ]
     near = [
         send(x_ref, x_out.at[pl.ds(k * count, count)], k, x_send.at[k - 1], x_recv.at[k - 1])
@@ -614,66 +704,71 @@
     own = [
         pltpu.make_async_copy(qkv_ref.at[head], qkv_out.at[head, rows], local_sem.at[0]),
         pltpu.make_async_copy(x_ref, x_out.at[pl.ds(0, count)], local_sem.at[1]),
-    ] + [
-        pltpu.make_async_copy(
-            in_ref.at[:, columns(part, head)],
-            in_out.at[head, :, pl.ds(part * units, units)],
-            local_sem.at[2 + part],
-        )
-        for part in range(2)
     ]
-    for copy in qkv_copies + near + in_copies + own:
+    for copy in qkv_copies + near + own:
         copy.start()
 
-    def along(k):
+    def along(k, source):
         return pltpu.make_async_remote_copy(
             src_ref=qkv_out.at[:, rows],
-            dst_ref=qkv_out.at[:, rows],
+            dst_ref=qkv_out.at[:, rows_of(source)],
             send_sem=b_send.at[k],
             recv_sem=b_recv.at[k],
-            device_id=(head, lax.rem(blk + k, blk_size)),
+            device_id=(head, same_core(k)),
             device_id_type=MESH,
         )
 
-    def arrived(k):
-        source = pl.ds(
-            pl.multiple_of(lax.rem(blk + blk_size - k, blk_size) * depth, depth), depth
-        )
+    def behind(k):
+        return lax.rem(blk + blk_size - 2 * k, blk_size)
+
+    def across(k, core):
+        source = behind(k) ^ core
         return pltpu.make_async_remote_copy(
-            src_ref=qkv_out.at[:, rows],
-            dst_ref=qkv_out.at[:, source],
-            send_sem=b_send.at[k],
-            recv_sem=b_recv.at[k],
-            device_id=(head, lax.rem(blk + k, blk_size)),
+            src_ref=qkv_out.at[:, rows_of(behind(k))],
+            dst_ref=qkv_out.at[:, rows_of(source)],
+            send_sem=c_send.at[k],
+            recv_sem=c_recv.at[k],
+            device_id=(head, blk ^ 1),
             device_id_type=MESH,
         )
 
     def start(k, carried):
-        along(k).start()
+        along(k, blk).start()
         return carried
 
+    def pass_on(k, carried):
+        along(k, behind(k)).wait_recv()
+        across(k, 0).start()
+        return carried
+
     def finish(k, carried):
-        along(k).wait_send()
-        arrived(k).wait_recv()
+        across(k, 0).wait_send()
+        across(k, 1).wait_recv()
+        return carried
+
+    def sent(k, carried):
+        along(k, blk).wait_send()
         return carried
 
     own[0].wait()
     for copy in qkv_copies:
         copy.wait_recv()
-    lax.fori_loop(1, blk_size, start, 0)
+    lax.fori_loop(1, pairs, start, 0)
+    across(0, 0).start()
+    lax.fori_loop(1, pairs, pass_on, 0)
     for first, second in zip(near, far):
         first.wait_recv()
         second.start()
     for copy in qkv_copies + near:
         copy.wait_send()
-    for copy in in_copies + far:
+    for copy in far:
         copy.wait()
-    for copy in own[1:]:
-        copy.wait()
-    lax.fori_loop(1, blk_size, finish, 0)
-
-
-def begin(x, qkv_parts, in_weight):
+    own[1].wait()
+    lax.fori_loop(1, pairs, sent, 0)
+    lax.fori_loop(0, pairs, finish, 0)
+
+
+def begin(x, qkv_parts):
     size, blk_size = lax.axis_size("heads"), lax.axis_size("blk")
     count, width = x.shape
     depth, joined = qkv_parts.shape[1:]
@@ -684,24 +779,23 @@
         out_shape=[
             jax.ShapeDtypeStruct((size * count, width), x.dtype),
             jax.ShapeDtypeStruct((size, blk_size * depth, joined), x.dtype),
-            jax.ShapeDtypeStruct((size, depth, in_weight.shape[1] // size), x.dtype),
-        ],
-        in_specs=[anywhere] * 3,
-        out_specs=[anywhere] * 3,
+        ],
+        in_specs=[anywhere] * 2,
+        out_specs=[anywhere] * 2,
         scratch_shapes=[
-            sems((4,)),
+            sems((2,)),
             sems((4,)),
             sems((4,)),
             sems((size - 1,)),
             sems((size - 1,)),
-            sems((2 * size - 2,)),
-            sems((2 * size - 2,)),
-            sems((blk_size,)),
-            sems((blk_size,)),
+            sems((blk_size // 2,)),
+            sems((blk_size // 2,)),
+            sems((blk_size // 2,)),
+            sems((blk_size // 2,)),
         ],
         compiler_params=pltpu.CompilerParams(collective_id=1, has_side_effects=True),
         name="begin",
-    )(x, qkv_parts, in_weight)
+    )(x, qkv_parts)
 
 
 def spread_copies(source_ref, target_ref, send_sem, recv_sem):
@@ -710,6 +804,7 @@
     quarter = rows // 2
     start = pl.multiple_of(lax.rem(blk, 2) * rows, rows)
     half = pl.ds(start, rows)
+    first = source_ref.at[half, pl.ds(0, target_ref.shape[2])]
     count = [0]
 
     def copy(source, target, place):
@@ -725,7 +820,7 @@
         )
 
     near = [
-        copy(source_ref.at[half], target_ref.at[k - 1, half], (head ^ k, blk)) for k in (1, 2)
+        copy(first, target_ref.at[k - 1, half], (head ^ k, blk)) for k in (1, 2)
     ]
     upper = pl.ds(start, quarter)
     lower = pl.ds(pl.multiple_of(start + quarter, quarter), quarter)
@@ -785,9 +880,9 @@
 
 
 def hidden_kernel(
-    tiles, normed_ref, gate_ref, up_ref, down_ref, side_ref, cot_ref, one_top_ref, one_bottom_ref,
-    two_top_ref, two_bottom_ref, hidden_ref, gate_grad_ref, up_grad_ref, down_sum_ref, spread_ref,
-    held_ref, hidden_all_ref, load_sem, far_send, far_recv, send_sem, recv_sem
+    tiles, normed_ref, gate_ref, up_ref, down_ref, turned_ref, side_ref, cot_ref, one_top_ref,
+    one_bottom_ref, two_top_ref, two_bottom_ref, hidden_ref, gate_grad_ref, up_grad_ref, in_sum_ref,
+    cot_far_ref, spread_ref, held_ref, grads_ref, load_sem, far_send, far_recv, send_sem, recv_sem
 ):
     step, steps = pl.program_id(0), pl.num_programs(0)
     head, blk = lax.axis_index("heads"), lax.axis_index("blk")
@@ -805,6 +900,9 @@
         )
         for part, (ref, k) in enumerate(((one_top_ref, 2), (two_bottom_ref, 1)))
     ]
+    keep = pltpu.make_async_copy(
+        held_ref.at[pl.ds(3 * count, count)], cot_far_ref, load_sem.at[5]
+    )
     near = ((one_top_ref, 2), (one_bottom_ref, 3), (two_top_ref, 4), (two_bottom_ref, 5))
     loads = [pltpu.make_async_copy(cot_ref, held_ref.at[pl.ds(0, count)], load_sem.at[0])] + [
         pltpu.make_async_copy(ref, held_ref.at[pl.ds(half * place, half)], load_sem.at[place - 1])
@@ -825,8 +923,9 @@
     def _():
         for copy in far:
             copy.wait()
-
-    marks = (tiles, 2 * tiles, 2 * tiles + 2)
+        keep.start()
+
+    marks = (tiles, 2 * tiles, 2 * tiles + 4)
     end = spread_job(step, marks, side_ref, spread_ref, send_sem, recv_sem, False)
 
     @pl.when(step < 2 * tiles)
@@ -840,34 +939,36 @@
         )
         sigmoid = jax.nn.sigmoid(gate)
         activated = gate * sigmoid
-        hidden = (activated * upward).astype(jnp.bfloat16)
-        hidden_ref[...] = hidden
-        hidden_all_ref[here, pl.ds(pl.multiple_of(lax.rem(step, tiles) * units, units), units)] = (
-            hidden
-        )
-        gate_grad_ref[...] = (grad * upward * sigmoid * (1.0 + gate * (1.0 - sigmoid))).astype(
-            jnp.bfloat16
-        )
-        up_grad_ref[...] = (grad * activated).astype(jnp.bfloat16)
+        hidden_ref[...] = (activated * upward).astype(jnp.bfloat16)
+        gate_grad = (grad * upward * sigmoid * (1.0 + gate * (1.0 - sigmoid))).astype(jnp.bfloat16)
+        up_grad = (grad * activated).astype(jnp.bfloat16)
+        gate_grad_ref[...] = gate_grad
+        up_grad_ref[...] = up_grad
+        for part, value in enumerate((gate_grad, up_grad)):
+            place = (part * tiles + lax.rem(step, tiles)) * units
+            grads_ref[here, pl.ds(pl.multiple_of(place, units), units)] = value
 
     @pl.when(step >= 2 * tiles)
     def _():
-        there = pl.ds(pl.multiple_of((step - 2 * tiles) * units, units), units)
-        down_sum_ref[...] = lax.dot_general(
-            hidden_all_ref[:, there],
-            held_ref[...],
+        in_sum_ref[...] = lax.dot_general(
+            turned_ref[...],
+            grads_ref[...],
             (((0,), (0,)), ((), ())),
             preferred_element_type=jnp.float32,
         ).astype(jnp.bfloat16)
 
-    pl.when(step == steps - 1)(end)
-
-
-def hidden_pass(normed, weight, cot, cot_near, down, side, units):
+    @pl.when(step == steps - 1)
+    def _():
+        end()
+        keep.wait()
+
+
+def hidden_pass(normed, weight, cot, cot_near, down, side, side_columns, units):
     count, width = normed.shape
     total = down.shape[0]
     tiles = total // units
     rows = count // 2
+    columns = width // 8
 
     def row(s):
         return jnp.minimum(s // tiles, 1)
@@ -881,28 +982,31 @@
     sems = pltpu.SemaphoreType.DMA
     return pl.pallas_call(
         functools.partial(hidden_kernel, tiles),
-        grid=(3 * tiles,),
+        grid=(2 * tiles + 8,),
         in_specs=[
             pl.BlockSpec((rows, width), lambda s: (row(s), 0)),
             pl.BlockSpec((width, units), lambda s: (0, column(s))),
             pl.BlockSpec((width, units), lambda s: (0, tiles + column(s))),
             pl.BlockSpec((units, width), lambda s: (column(s), 0)),
+            pl.BlockSpec((count, columns), lambda s: (0, jnp.maximum(s - 2 * tiles, 0))),
         ]
         + [anywhere] * 6,
         out_specs=[out_spec] * 3
         + [
-            pl.BlockSpec((units, width), lambda s: (jnp.maximum(s - 2 * tiles, 0), 0)),
+            pl.BlockSpec((columns, 2 * total), lambda s: (jnp.maximum(s - 2 * tiles, 0), 0)),
+            anywhere,
             anywhere,
         ],
         out_shape=[out_shape] * 3
         + [
-            jax.ShapeDtypeStruct((total, width), jnp.bfloat16),
-            jax.ShapeDtypeStruct((3, *side.shape), side.dtype),
+            jax.ShapeDtypeStruct((width, 2 * total), jnp.bfloat16),
+            jax.ShapeDtypeStruct(cot.shape, jnp.bfloat16),
+            jax.ShapeDtypeStruct((3, side.shape[0], side_columns), side.dtype),
         ],
         scratch_shapes=[
             pltpu.VMEM((count, width), jnp.bfloat16),
-            pltpu.VMEM((count, total), jnp.bfloat16),
-            sems((5,)),
+            pltpu.VMEM((count, 2 * total), jnp.bfloat16),
+            sems((6,)),
             sems((2,)),
             sems((2,)),
             sems((SPREAD_COUNT,)),
@@ -912,33 +1016,50 @@
             collective_id=2, has_side_effects=True, vmem_limit_bytes=58 << 20
         ),
         cost_estimate=pl.CostEstimate(
-            flops=8 * count * width * total, bytes_accessed=70_000_000, transcendentals=0
+            flops=10 * count * width * total, bytes_accessed=70_000_000, transcendentals=0
         ),
         name="hidden_pass",
-    )(normed, weight, weight, down, side, cot, *cot_near)
+    )(normed, weight, weight, down, normed, side, cot, *cot_near)
 
 
 def in_order(step):
-    value = 3
-    for index, half in enumerate((2, 6, 5, 7, 0, 1, 4)):
+    value = 1
+    for index, half in enumerate((6, 7, 2, 5, 4, 3, 0)):
         value = jnp.where(step == index, half, value)
     return value
 
 
 def tail_kernel(
-    normed_ref, gate_ref, up_ref, hidden_ref, in_hbm, down_hbm, in_sum_ref, out_one_ref,
-    out_two_ref, out_rest_ref, grad_ref,
-    weight_ref, one_ref, two_ref, rest_ref, top_ref, bottom_ref, last_ref, last_got_ref,
-    weight_sem, send_sem, recv_sem
+    gate_ref, up_ref, hidden_ref, turned_ref, in_hbm, down_hbm, cot_ref, one_top_ref, one_bottom_ref,
+    two_top_ref, two_bottom_ref, cot_far_ref, down_sum_ref, *refs
 ):
+    first_refs, (out_rest_ref, grad_ref, *refs) = refs[:4], refs[4:]
+    (
+        weight_ref, down_ref, first_ref, rest_ref, got_ref, last_ref, last_got_ref, weight_sem,
+        send_sem, recv_sem,
+    ) = refs
     step = pl.program_id(0)
     head, blk = lax.axis_index("heads"), lax.axis_index("blk")
     rows, total = hidden_ref.shape
     width = grad_ref.shape[1]
     load_in = pltpu.make_async_copy(in_hbm, weight_ref, weight_sem.at[0])
-    load_down = pltpu.make_async_copy(
-        down_hbm, weight_ref.at[pl.ds(0, total), pl.ds(0, width)], weight_sem.at[1]
-    )
+    load_down = pltpu.make_async_copy(down_hbm, down_ref, weight_sem.at[1])
+    pieces = (
+        (cot_ref, 0, 2),
+        (one_top_ref, 2, 1),
+        (one_bottom_ref, 3, 1),
+        (two_top_ref, 4, 1),
+        (two_bottom_ref, 5, 1),
+        (cot_far_ref, 6, 2),
+    )
+    cot_loads = [
+        pltpu.make_async_copy(
+            ref,
+            weight_ref.at[pl.ds(place * rows, length * rows), pl.ds(0, width)],
+            weight_sem.at[2 + index],
+        )
+        for index, (ref, place, length) in enumerate(pieces)
+    ]
 
     def copy(source, target, k, index):
         return pltpu.make_async_remote_copy(
@@ -950,10 +1071,11 @@
             device_id_type=MESH,
         )
 
-    send_one = copy(one_ref, top_ref, 1, 0)
-    send_two = copy(two_ref, bottom_ref, 2, 1)
-    send_top = copy(last_ref.at[0], last_got_ref.at[0], 2, 2)
-    send_bottom = copy(last_ref.at[1], last_got_ref.at[1], 1, 3)
+    firsts = [
+        copy(first_ref.at[index], got_ref.at[index], k, index)
+        for index, k in enumerate((1, 2, 1, 2))
+    ]
+    lasts = [copy(last_ref.at[part], last_got_ref.at[part], 2 - part, 4 + part) for part in range(2)]
 
     def wide_of(block):
         return block.astype(jnp.float32)
@@ -961,167 +1083,153 @@
     @pl.when(step == 0)
     def _():
         load_in.start()
+        load_down.start()
         greet_near(False)
         load_in.wait()
 
     @pl.when(step < 8)
     def _():
-        here = pl.ds(pl.multiple_of(in_order(step) * rows, rows), rows)
         value = lax.dot_general(
-            gate_ref[here], weight_ref[:, :total], ROWS_IN_BOTH, preferred_element_type=jnp.float32
+            gate_ref[...], weight_ref[:, :total], ROWS_IN_BOTH, preferred_element_type=jnp.float32
         ) + lax.dot_general(
-            up_ref[here], weight_ref[:, total:], ROWS_IN_BOTH, preferred_element_type=jnp.float32
+            up_ref[...], weight_ref[:, total:], ROWS_IN_BOTH, preferred_element_type=jnp.float32
         )
         value = value.astype(jnp.bfloat16)
 
-        def rows_from(first):
-            return pl.ds(pl.multiple_of((step - first) * rows, rows), rows)
-
-        @pl.when(step < 2)
-        def _():
-            one_ref[rows_from(0)] = value
-
-        @pl.when((step >= 2) & (step < 4))
-        def _():
-            two_ref[rows_from(2)] = value
+        for index in range(4):
+
+            @pl.when(step == index)
+            def _(index=index):
+                first_ref[index] = value
+                firsts[index].start()
 
         @pl.when(step >= 4)
         def _():
-            rest_ref[rows_from(4)] = value
-
-        @pl.when(step == 1)
-        def _():
-            send_one.start()
-
-        @pl.when(step == 3)
-        def _():
-            send_two.start()
+            rest_ref[pl.ds(pl.multiple_of((step - 4) * rows, rows), rows)] = value
 
         @pl.when(step == 7)
         def _():
-            load_down.start()
+            load_down.wait()
+            for load in cot_loads:
+                load.start()
 
     @pl.when((step >= 8) & (step < 16))
     def _():
-        for part, ref in enumerate((gate_ref, up_ref)):
-            in_sum_ref[:, part * total : (part + 1) * total] = lax.dot_general(
-                normed_ref[...], ref[...], (((0,), (0,)), ((), ())),
-                preferred_element_type=jnp.float32,
-            ).astype(jnp.bfloat16)
-
-        @pl.when(step == 13)
+        terms = jnp.dot(
+            hidden_ref[...], down_ref[...], preferred_element_type=jnp.float32
+        ).astype(jnp.bfloat16)
+
+        for index, ref in enumerate(first_refs):
+
+            @pl.when(step == 8 + index)
+            def _(ref=ref):
+                ref[...] = terms
+
+        @pl.when(step >= 12)
         def _():
-            send_one.wait_recv()
-            last_ref[0] = (
-                wide_of(rest_ref[2 * rows : 3 * rows]) + wide_of(top_ref[rows:])
-            ).astype(jnp.bfloat16)
-            send_top.start()
+            out_rest_ref[...] = terms
 
         @pl.when(step == 15)
         def _():
-            send_two.wait_recv()
-            last_ref[1] = (wide_of(rest_ref[3 * rows :]) + wide_of(bottom_ref[rows:])).astype(
-                jnp.bfloat16
+            for load in cot_loads:
+                load.wait()
+
+    @pl.when(step >= 16)
+    def _():
+        down_sum_ref[...] = lax.dot_general(
+            turned_ref[...],
+            weight_ref[:, :width],
+            (((0,), (0,)), ((), ())),
+            preferred_element_type=jnp.float32,
+        ).astype(jnp.bfloat16)
+
+    for part, when in enumerate((8, 9)):
+
+        @pl.when(step == when)
+        def _(part=part):
+            firsts[part].wait_recv()
+            last_ref[part] = (
+                wide_of(rest_ref[part * rows : (part + 1) * rows]) + wide_of(got_ref[part])
+            ).astype(jnp.bfloat16)
+            lasts[part].start()
+
+    @pl.when(step == pl.num_programs(0) - 1)
+    def _():
+        for part in range(2):
+            firsts[2 + part].wait_recv()
+            lasts[part].wait_recv()
+            grad_ref[part * rows : (part + 1) * rows] = (
+                wide_of(rest_ref[(2 + part) * rows : (3 + part) * rows])
+                + wide_of(got_ref[2 + part])
+                + wide_of(last_got_ref[part])
             )
-            send_bottom.start()
-            load_down.wait()
-
-    @pl.when(step >= 16)
-    def _():
-        terms = jnp.dot(
-            hidden_ref[...], weight_ref[:total, :width], preferred_element_type=jnp.float32
-        ).astype(jnp.bfloat16)
-
-        @pl.when(step < 18)
-        def _():
-            out_one_ref[...] = terms
-
-        @pl.when((step >= 18) & (step < 20))
-        def _():
-            out_two_ref[...] = terms
-
-        @pl.when(step >= 20)
-        def _():
-            out_rest_ref[...] = terms
-
-    @pl.when(step == pl.num_programs(0) - 1)
-    def _():
-        send_top.wait_recv()
-        send_bottom.wait_recv()
-        grad_ref[:rows] = (
-            wide_of(rest_ref[:rows]) + wide_of(top_ref[:rows]) + wide_of(last_got_ref[0])
-        )
-        grad_ref[rows:] = (
-            wide_of(rest_ref[rows : 2 * rows]) + wide_of(bottom_ref[:rows]) + wide_of(last_got_ref[1])
-        )
-        for sent in (send_one, send_two, send_top, send_bottom):
+        for sent in firsts + lasts:
             sent.wait_send()
 
 
-def feed_tail(normed, gate_grad, up_grad, hidden, weight, down):
-    count, width = normed.shape
-    total = hidden.shape[1]
+def feed_tail(gate_grad, up_grad, hidden, weight, down, cots):
+    count, total = hidden.shape
+    width = weight.shape[0]
     rows = count // 8
+    units = 256
     anywhere = pl.BlockSpec(memory_space=pl.ANY)
-    once = pl.Buffered(1)
-
-    def stage(i, first):
-        return jnp.clip(i - first, 0, 7)
+
+    def stage(i, first, last):
+        return jnp.clip(i - first, 0, last)
+
+    def first_rows(i):
+        return (in_order(stage(i, 0, 7)), 0)
 
     low = jnp.bfloat16
     return pl.pallas_call(
         tail_kernel,
-        grid=(24,),
+        grid=(16 + total // units,),
         in_specs=[
-            pl.BlockSpec((count, rows), lambda i: (0, stage(i, 8))),
-            pl.BlockSpec((count, total), lambda i: (0, 0), pipeline_mode=once),
-            pl.BlockSpec((count, total), lambda i: (0, 0), pipeline_mode=once),
-            pl.BlockSpec((rows, total), lambda i: (in_order(stage(i, 16)), 0)),
-            anywhere,
-            anywhere,
-        ],
+            pl.BlockSpec((rows, total), first_rows),
+            pl.BlockSpec((rows, total), first_rows),
+            pl.BlockSpec((rows, total), lambda i: (in_order(stage(i, 8, 7)), 0)),
+            pl.BlockSpec((count, units), lambda i: (0, jnp.maximum(i - 16, 0))),
+        ]
+        + [anywhere] * 8,
         out_specs=[
-            pl.BlockSpec((rows, 2 * total), lambda i: (stage(i, 8), 0)),
-            pl.BlockSpec((rows, width), lambda i: (jnp.clip(i - 16, 0, 1), 0)),
-            pl.BlockSpec((rows, width), lambda i: (jnp.clip(i - 18, 0, 1), 0)),
-            pl.BlockSpec((rows, width), lambda i: (jnp.clip(i - 20, 0, 3), 0)),
-            pl.BlockSpec((2 * rows, width), lambda i: (0, 0), pipeline_mode=once),
+            pl.BlockSpec((units, width), lambda i: (jnp.maximum(i - 16, 0), 0)),
+            *[pl.BlockSpec((rows, width), lambda i: (0, 0), pipeline_mode=pl.Buffered(1))] * 4,
+            pl.BlockSpec((rows, width), lambda i: (stage(i, 12, 3), 0)),
+            pl.BlockSpec((2 * rows, width), lambda i: (0, 0), pipeline_mode=pl.Buffered(1)),
         ],
         out_shape=[
-            jax.ShapeDtypeStruct((width, 2 * total), low),
-            jax.ShapeDtypeStruct((2 * rows, width), low),
-            jax.ShapeDtypeStruct((2 * rows, width), low),
+            jax.ShapeDtypeStruct((total, width), low),
+            *[jax.ShapeDtypeStruct((rows, width), low)] * 4,
             jax.ShapeDtypeStruct((4 * rows, width), low),
             jax.ShapeDtypeStruct((2 * rows, width), jnp.float32),
         ],
         scratch_shapes=[
             pltpu.VMEM(weight.shape, low),
-            pltpu.VMEM((2 * rows, width), low),
-            pltpu.VMEM((2 * rows, width), low),
+            pltpu.VMEM(down.shape, low),
+            pltpu.VMEM((4, rows, width), low),
             pltpu.VMEM((4 * rows, width), low),
-            pltpu.VMEM((2 * rows, width), low),
-            pltpu.VMEM((2 * rows, width), low),
+            pltpu.VMEM((4, rows, width), low),
             pltpu.VMEM((2, rows, width), low),
             pltpu.VMEM((2, rows, width), low),
-            pltpu.SemaphoreType.DMA((2,)),
-            pltpu.SemaphoreType.DMA((4,)),
-            pltpu.SemaphoreType.DMA((4,)),
+            pltpu.SemaphoreType.DMA((8,)),
+            pltpu.SemaphoreType.DMA((6,)),
+            pltpu.SemaphoreType.DMA((6,)),
         ],
         compiler_params=pltpu.CompilerParams(
             collective_id=3, has_side_effects=True, vmem_limit_bytes=60 << 20
         ),
         cost_estimate=pl.CostEstimate(
-            flops=10 * count * width * total, bytes_accessed=70_000_000, transcendentals=0
+            flops=8 * count * width * total, bytes_accessed=70_000_000, transcendentals=0
         ),
         name="feed_tail",
-    )(normed, gate_grad, up_grad, hidden, weight, down)
+    )(gate_grad, up_grad, hidden, hidden, weight, down, *cots)
 
 
 def residual_back_kernel(
     grad_sum_ref, residual_ref, cot_ref, gain_ref, attended_ref, weight_ref, weights_ref, grad_ref,
-    gain_grad_ref, out_sum_ref, pieces_ref, branch_ref, mine_ref, terms_ref, terms_got_ref, own_sem,
-    send_sem, recv_sem
+    gain_grad_ref, pieces_ref, *refs
 ):
+    *out_refs, branch_ref, mine_ref, terms_ref, terms_got_ref, own_sem, send_sem, recv_sem = refs
     size = lax.axis_size("heads")
     core = lax.rem(lax.axis_index("blk"), 2)
     step = pl.program_id(0)
@@ -1197,14 +1305,16 @@
         across.start()
         across.wait()
 
-        def add(index, carried):
-            out_sum_ref[index] = (
-                terms_ref[index, core].astype(jnp.float32)
-                + terms_got_ref[index].astype(jnp.float32)
-            ).astype(jnp.bfloat16)
-            return carried
-
-        lax.fori_loop(0, terms_ref.shape[0], add, 0)
+        for k, out_ref in enumerate(out_refs):
+
+            def add(index, carried, k=k, out_ref=out_ref):
+                out_ref[index] = (
+                    terms_ref[k * pairs + index, core].astype(jnp.float32)
+                    + terms_got_ref[k * pairs + index].astype(jnp.float32)
+                ).astype(jnp.bfloat16)
+                return carried
+
+            lax.fori_loop(0, pairs, add, 0)
         for copy in copies:
             copy.wait()
         keep.wait()
@@ -1241,14 +1351,14 @@
         out_specs=[
             tile,
             row,
-            pl.BlockSpec((pairs, held, width), lambda i: (0, 0, 0)),
             pl.BlockSpec(memory_space=pl.ANY),
+            *[pl.BlockSpec((pairs // size, held, width), lambda i: (0, 0, 0))] * size,
         ],
         out_shape=[
             jax.ShapeDtypeStruct((count, width), jnp.float32),
             jax.ShapeDtypeStruct((1, width), jnp.float32),
-            jax.ShapeDtypeStruct((pairs, held, width), jnp.bfloat16),
             jax.ShapeDtypeStruct(pieces, jnp.bfloat16),
+            *[jax.ShapeDtypeStruct((pairs // size, held, width), jnp.bfloat16)] * size,
         ],
         scratch_shapes=[
             pltpu.VMEM((count, width), jnp.bfloat16),
@@ -1269,63 +1379,86 @@
     )(grad_sum, residual, cot, gain, attended, weight, weights)
 
 
-def turned_kernel(left_ref, *refs):
-    *right_refs, out_ref, held_ref, load_sem = refs
-    count = right_refs[0].shape[0]
-
-    @pl.when(pl.program_id(0) == 0)
-    def _():
-        loads = [
-            pltpu.make_async_copy(ref, held_ref.at[pl.ds(k * count, count)], load_sem.at[k])
-            for k, ref in enumerate(right_refs)
-        ]
-        for load in loads:
-            load.start()
-        for load in loads:
-            load.wait()
-
-    out_ref[...] = lax.dot_general(
-        left_ref[...], held_ref[...], (((0,), (0,)), ((), ())), preferred_element_type=jnp.float32
-    ).astype(out_ref.dtype)
-
-
-def turned_product(left, rights, rows):
-    count, height = left.shape
-    width = rights[0].shape[1]
+def qkv_terms_kernel(normed_ref, grad_ref, terms_ref, got_ref, send_sem, recv_sem):
+    step = pl.program_id(0)
+    size = lax.axis_size("heads")
+    head, blk = lax.axis_index("heads"), lax.axis_index("blk")
+    count = got_ref.shape[1]
+    copies = [
+        pltpu.make_async_remote_copy(
+            src_ref=grad_ref.at[pl.ds(k * count, count)],
+            dst_ref=got_ref.at[k - 1],
+            send_sem=send_sem.at[k - 1],
+            recv_sem=recv_sem.at[k - 1],
+            device_id=(head ^ k, blk),
+            device_id_type=MESH,
+        )
+        for k in range(1, size)
+    ]
+
+    @pl.when(step == 0)
+    def _():
+        barrier = pltpu.get_barrier_semaphore()
+        for k in range(1, size):
+            pl.semaphore_signal(barrier, inc=1, device_id=(head ^ k, blk), device_id_type=MESH)
+        pl.semaphore_wait(barrier, size - 1)
+        for copy in copies:
+            copy.start()
+
+    terms_ref[...] = lax.dot_general(
+        normed_ref[...], grad_ref[...], (((0,), (0,)), ((), ())), preferred_element_type=jnp.float32
+    ).astype(terms_ref.dtype)
+
+    @pl.when(step == pl.num_programs(0) - 1)
+    def _():
+        for copy in copies:
+            copy.wait()
+
+
+def qkv_terms(normed, grad, rows):
+    count, height = normed.shape
+    width = grad.shape[1]
+    size = lax.axis_size("heads")
     return pl.pallas_call(
-        turned_kernel,
+        qkv_terms_kernel,
         grid=(height // rows,),
-        in_specs=[pl.BlockSpec((count, rows), lambda i: (0, i))]
-        + [pl.BlockSpec(memory_space=pl.ANY)] * len(rights),
-        out_specs=pl.BlockSpec((rows, width), lambda i: (i, 0)),
-        out_shape=jax.ShapeDtypeStruct((height, width), jnp.bfloat16),
-        scratch_shapes=[
-            pltpu.VMEM((count, width), jnp.bfloat16),
-            pltpu.SemaphoreType.DMA((len(rights),)),
-        ],
-        compiler_params=pltpu.CompilerParams(vmem_limit_bytes=58 << 20),
+        in_specs=[
+            pl.BlockSpec((count, rows), lambda i: (0, i)),
+            pl.BlockSpec((count, width), lambda i: (0, 0)),
+        ],
+        out_specs=[
+            pl.BlockSpec((rows, width), lambda i: (i, 0)),
+            pl.BlockSpec(memory_space=pl.ANY),
+        ],
+        out_shape=[
+            jax.ShapeDtypeStruct((height, width), jnp.bfloat16),
+            jax.ShapeDtypeStruct((size - 1, count // size, width), jnp.bfloat16),
+        ],
+        scratch_shapes=[pltpu.SemaphoreType.DMA((size - 1,))] * 2,
+        compiler_params=pltpu.CompilerParams(
+            collective_id=7, has_side_effects=True, vmem_limit_bytes=48 << 20
+        ),
         cost_estimate=pl.CostEstimate(
-            flops=2 * count * height * width, bytes_accessed=20_000_000, transcendentals=0
-        ),
-        name="turned_product",
-    )(left, *rights)
+            flops=4 * count * height * width, bytes_accessed=20_000_000, transcendentals=0
+        ),
+        name="qkv_terms",
+    )(normed, grad)
 
 
 def finish_kernel(
-    query_width, dim, sent_ref, qkv_ref, gain_ref, ffn_ref, head_ref, weight_ref, out_own_ref,
-    out_one_ref, out_two_ref, out_three_ref, *refs
+    query_width, dim, got_ref, qkv_ref, gain_ref, ffn_ref, head_ref, out_own_ref, out_one_ref, out_two_ref, out_three_ref, *refs
 ):
     size, blk_size = lax.axis_size("heads"), lax.axis_size("blk")
     out_refs = (out_own_ref, out_one_ref, out_two_ref, out_three_ref)
-    sources, refs = refs[:4], refs[4:]
+    sources, refs = refs[:12], refs[12:]
     (
-        grad_ref, qkv_grad_ref, gains_ref, out_grad_ref, in_grad_ref, *refs
+        grad_ref, qkv_grad_ref, gains_ref, out_grad_ref, in_grad_ref, layer_ref, *refs
     ) = refs
-    held, refs = refs[:4], refs[4:]
-    weights_ref, x_ref, residual_grad_ref, in_ref = held
+    held, refs = refs[:12], refs[12:]
+    weight_ref, weights_ref, x_ref, residual_grad_ref, sent_ref, in_ref, residual_ref, rest_ref = held[:8]
     (
-        got_ref, qkv_other_ref, qkv_sum_ref, qkv_got_ref, part_ref, gain_got_ref, out_part_ref,
-        out_got_ref, in_got_ref, load_sem, s_send, s_recv, c_send, c_recv, q_send, q_recv, g_send,
+        qkv_other_ref, qkv_sum_ref, qkv_got_ref, part_ref, gain_got_ref, out_part_ref,
+        out_got_ref, in_got_ref, load_sem, c_send, c_recv, q_send, q_recv, g_send,
         g_recv, o_send, o_recv, i_send, i_recv,
     ) = refs
     devices = size * blk_size
@@ -1338,7 +1471,15 @@
     depth = width // devices
     barrier = pltpu.get_barrier_semaphore()
     loads = [
-        pltpu.make_async_copy(source, target, load_sem.at[index])
+        pltpu.make_async_copy(
+            source.at[pl.ds(0, target.shape[0]), pl.ds(0, target.shape[1])]
+            if index in (0, 4, 6)
+            else source.at[pl.ds(target.shape[0], target.shape[0])]
+            if index == 7
+            else source,
+            target,
+            load_sem.at[index],
+        )
         for index, (source, target) in enumerate(zip(sources, held))
     ]
     for load in loads:
@@ -1368,19 +1509,6 @@
 
     across = copy(qkv_ref.at[:, 1 - core], qkv_other_ref, (head, blk ^ 1), c_send, c_recv)
     across.start()
-    sends = [
-        copy(
-            sent_ref.at[pl.ds(k * count, count)],
-            got_ref.at[k - 1],
-            (head ^ k, blk),
-            s_send.at[k - 1],
-            s_recv.at[k - 1],
-        )
-        for k in range(1, size)
-    ]
-    for sent in sends:
-        sent.start()
-
     def wide_of(block):
         return block.astype(jnp.float32)
 
@@ -1438,7 +1566,7 @@
     lax.fori_loop(1, pairs, start_out, 0)
     out_got_ref[pair] = out_part_ref[pair]
 
-    loads[3].wait()
+    loads[5].wait()
     in_sends = [
         copy(
             in_ref.at[head ^ k],
@@ -1452,10 +1580,8 @@
     for sent in in_sends:
         sent.start()
 
-    for index in (0, 1, 2):
-        loads[index].wait()
-    for sent in sends:
-        sent.wait_recv()
+    for load in loads[:5]:
+        load.wait()
     rows = min(128, count)
 
     def tile(index, gain_sum):
@@ -1528,6 +1654,16 @@
             got = in_got_ref[k - 1, :, piece] if k else in_ref[head, :, piece]
             in_grad_ref[:, columns] = wide_of(got)
 
+    for load in loads[6:]:
+        load.wait()
+    half = count // 2
+    for part in range(2):
+        here = slice(part * half, (part + 1) * half)
+        layer_ref[here] = (
+            residual_ref[here] + wide_of(rest_ref[here]) + wide_of(held[8 + part][...])
+            + wide_of(held[10 + part][...])
+        ).astype(jnp.bfloat16)
+
     def finish_qkv(k, carried):
         qkv_copy(k, lax.rem(own_pair + size * pairs - k, size * pairs)).wait()
         return carried
@@ -1566,13 +1702,13 @@
     lax.fori_loop(1, devices, finish_gain, 0)
     gains_ref[...] = jnp.sum(gain_got_ref[...], axis=0)
     across.wait_send()
-    for sent in sends + in_sends:
+    for sent in in_sends:
         sent.wait_send()
 
 
 def finish(
-    sent, qkv_part, x, residual_grad, gain, ffn_sum, head_sum, weight, weights, outs, in_part,
-    query_width, dim
+    sent, got, qkv_part, x, residual_grad, gain, ffn_sum, head_sum, weight, weights, outs, in_part,
+    residual, rest, terms, query_width, dim
 ):
     size, blk_size = lax.axis_size("heads"), lax.axis_size("blk")
     devices = size * blk_size
@@ -1586,7 +1722,7 @@
     anywhere = pl.BlockSpec(memory_space=pl.ANY)
     sems = pltpu.SemaphoreType.DMA
     low = jnp.bfloat16
-    loaded = (weights, x, residual_grad, in_part)
+    loaded = (weights, x, residual_grad)
     return pl.pallas_call(
         functools.partial(finish_kernel, query_width, dim),
         out_shape=[
@@ -1595,12 +1731,16 @@
             jax.ShapeDtypeStruct((8, 128), jnp.float32),
             jax.ShapeDtypeStruct((out_rows, width), jnp.float32),
             jax.ShapeDtypeStruct((depth, size * units), jnp.float32),
-        ],
-        in_specs=[vmem] * (6 + size) + [anywhere] * 4,
-        out_specs=[vmem] * 5,
-        scratch_shapes=[pltpu.VMEM(array.shape, array.dtype) for array in loaded]
+            jax.ShapeDtypeStruct((count, width), low),
+        ],
+        in_specs=[vmem] * (5 + size) + [anywhere] * 12,
+        out_specs=[vmem] * 6,
+        scratch_shapes=[pltpu.VMEM((width, joined), low)]
+        + [pltpu.VMEM(array.shape, array.dtype) for array in loaded]
+        + [pltpu.VMEM((count, joined), low), pltpu.VMEM(in_part.shape, low)]
+        + [pltpu.VMEM((count, width), jnp.float32), pltpu.VMEM((count, width), low)]
+        + [pltpu.VMEM((count // 2, width), low)] * 4
         + [
-            pltpu.VMEM((size - 1, count, joined), low),
             pltpu.VMEM((size * pairs, depth, joined), low),
             pltpu.VMEM((size * pairs, depth, joined), low),
             pltpu.VMEM((size * pairs, depth, joined), low),
@@ -1609,9 +1749,7 @@
             pltpu.VMEM((pairs, held_rows, width), low),
             pltpu.VMEM((pairs, held_rows, width), low),
             pltpu.VMEM((size - 1, depth, units), low),
-            sems((4,)),
-            sems((size - 1,)),
-            sems((size - 1,)),
+            sems((12,)),
             sems,
             sems,
             sems((size * pairs,)),
@@ -1628,8 +1766,8 @@
         ),
         name="finish",
     )(
-        sent, qkv_part.reshape(size * pairs, 2, depth, joined), gain, ffn_sum, head_sum, weight,
-        *outs, *loaded
+        got, qkv_part.reshape(size * pairs, 2, depth, joined), gain, ffn_sum, head_sum, *outs,
+        weight, *loaded, sent, in_part, residual, rest, *terms
     )
 
 
@@ -1687,10 +1825,10 @@
         axis=-1,
     ).transpose(1, 0, 2)
     out_group = lax.all_gather(out_weight, "blk", axis=0, tiled=True)
-    down_group = lax.all_gather(ffn_out_weight, "blk", axis=0, tiled=True)
-
-    inputs_blk, qkv_rows, in_rows = begin(inputs, qkv_parts, ffn_in_weight)
+    in_rows = trade(ffn_in_weight)
     in_group = lax.all_gather(in_rows, "blk", axis=1, tiled=True).reshape(width, -1)
+
+    inputs_blk, qkv_rows = begin(after(inputs, in_rows), qkv_parts)
     qkv_rows = qkv_rows.reshape(width, -1)
     cosine, sine = rotation(positions, head_dim)
     cosine = jnp.concatenate([cosine[:, 0], cosine[:, 0]], axis=-1)
@@ -1701,7 +1839,10 @@
     query_low, pair_blk, raw, normed, attn_scaling, ffn_scaling, out_peers = project(
         inputs_blk, qkv_rows, head_gain, cosine, sine, out_group, size, query_width, 256
     )
-    pair_all = jnp.concatenate([from_behind(pair_blk, "blk", 1), pair_blk], axis=0)
+    pair_behind = from_behind(pair_blk, "blk", 1)
+    pair_all = jnp.concatenate([pair_behind, pair_blk], axis=0)
+    down_weight, pair_all = lax.optimization_barrier((ffn_out_weight, pair_all))
+    down_group = lax.all_gather(down_weight, "blk", axis=0, tiled=True)
     query_rows, key_rows = token_count, 256
     low = block_len + jnp.arange(block_len, dtype=jnp.int32) - positions
     first = jnp.concatenate([low[::query_rows] // key_rows, own])
@@ -1711,65 +1852,51 @@
     mine = jnp.concatenate([pick(attended_blk, k, "heads", 0) for k in range(size)], axis=0)
     late = after(cotangent, inputs_blk)
     one_top, two_bottom = permute(late[:half], "heads", 1), permute(late[half:], "heads", 2)
+    mine, in_group = lax.optimization_barrier((mine, in_group))
     residual, ffn_normed, attended_own, one_bottom, two_top = join(
         inputs_blk, mine, out_group, out_peers, ffn_scaling, cotangent, 256
     )
-    residual_own = residual[:token_count]
-    qkv_group = qkv_rows[:, :qkv_width]
-    hidden, gate_grad, up_grad, down_sum, qkv_peers = hidden_pass(
-        ffn_normed,
-        in_group,
-        cotangent,
-        (one_top, one_bottom, two_top, two_bottom),
-        down_group,
-        qkv_group,
-        256,
-    )
-    ffn_out_grad = lax.psum_scatter(down_sum, "blk", scatter_dimension=0, tiled=True)
-    in_sum, out_one, out_two, out_rest, grad_sum = feed_tail(
-        ffn_normed, gate_grad, up_grad, hidden, in_group, down_group
-    )
-    in_sum, ffn_out_grad = lax.optimization_barrier((in_sum, ffn_out_grad))
+    cot_near = (one_top, one_bottom, two_top, two_bottom)
+    hidden, gate_grad, up_grad, in_sum, cot_far, qkv_peers = hidden_pass(
+        ffn_normed, in_group, cotangent, cot_near, down_group, qkv_rows, qkv_width, 256
+    )
     in_part = lax.psum_scatter(
         in_sum.reshape(size, blk_size * depth, -1), "blk", scatter_dimension=1, tiled=True
     )
-    ffn_out_grad = wide(ffn_out_grad)
-    residual_grad, ffn_sum, out_sum, grads = residual_back(
+    down_sum, one_far, two_far, one_near, two_near, out_rest, grad_sum = feed_tail(
+        gate_grad, up_grad, hidden, in_group, down_group, (cotangent, *cot_near, cot_far)
+    )
+    through_top, through_bottom = permute(one_far, "heads", 1), permute(two_far, "heads", 2)
+    residual_grad, ffn_sum, grads, *out_slices = residual_back(
         grad_sum, residual, cotangent, ffn_scaling, attended_own, out_group, out_peers,
         min(128, half)
     )
-    out_one, out_two, grads = lax.optimization_barrier((out_one, out_two, grads))
-    out_top, out_bottom = permute(out_one, "heads", 1), permute(out_two, "heads", 2)
-    out_slices = jnp.split(out_sum.reshape(size, -1, width), size, axis=0)
-    out_slices = [piece[0] for piece in out_slices]
-    out_slices = [out_slices[0]] + [permute(out_slices[k], "heads", k) for k in range(1, size)]
-    query_grad, pair_sum = attend_back(
-        query_low, pair_all, first, low, grads, attended_blk, logs, group_size, query_rows, key_rows
-    )
-    returned = from_behind(pair_sum[:block_len].astype(jnp.bfloat16), "blk", -1)
-    out_top, out_bottom, returned = lax.optimization_barrier((out_top, out_bottom, returned))
-    top_send = (wide(out_rest[2 * half : 3 * half]) + wide(out_top[half:])).astype(jnp.bfloat16)
-    bottom_send = (wide(out_rest[3 * half :]) + wide(out_bottom[half:])).astype(jnp.bfloat16)
+    down_sum, in_part, grads, through_top, through_bottom = lax.optimization_barrier(
+        (down_sum, in_part, grads, through_top, through_bottom)
+    )
+    ffn_out_grad = wide(lax.psum_scatter(down_sum, "blk", scatter_dimension=0, tiled=True))
+    top_send = (wide(out_rest[:half]) + wide(through_top)).astype(jnp.bfloat16)
+    bottom_send = (wide(out_rest[half : 2 * half]) + wide(through_bottom)).astype(jnp.bfloat16)
     out_top_last = permute(top_send, "heads", 2)
     out_bottom_last = permute(bottom_send, "heads", 1)
-    layer_out = jnp.concatenate(
-        [
-            residual_own[:half] + wide(out_rest[:half]) + wide(out_top[:half]) + wide(out_top_last),
-            residual_own[half:]
-            + wide(out_rest[half : 2 * half])
-            + wide(out_bottom[:half])
-            + wide(out_bottom_last),
-        ],
-        axis=0,
-    ).astype(jnp.bfloat16)
-
+    out_slices = [piece.reshape(-1, width) for piece in out_slices]
+    out_slices = [out_slices[0]] + [permute(out_slices[k], "heads", k) for k in range(1, size)]
+    query_grad, pair_sum, behind = attend_back(
+        query_low, pair_all, first, low, grads, attended_blk, logs, group_size, query_rows, key_rows
+    )
+    pair_sum, out_top_last, out_bottom_last, *out_slices = lax.optimization_barrier(
+        (pair_sum, out_top_last, out_bottom_last, *out_slices)
+    )
     projected_grad, head_sum = project_back(
-        own, query_grad, pair_sum, returned, raw, head_gain, cosine, sine, size, 256
-    )
-    qkv_part = turned_product(normed, [projected_grad], 512)
-    input_grad, qkv_grad, gains, out_grad, ffn_in_grad = finish(
-        projected_grad, qkv_part, inputs, residual_grad, attn_scaling, ffn_sum, head_sum, qkv_group,
-        qkv_peers, out_slices, in_part, query_width, head_dim
+        query_grad, pair_sum, behind, raw, head_gain, cosine, sine, size, 256
+    )
+    out_top = permute(after(one_near, pair_sum), "heads", 1)
+    out_bottom = permute(after(two_near, pair_sum), "heads", 2)
+    qkv_part, got = qkv_terms(normed, projected_grad, 512)
+    input_grad, qkv_grad, gains, out_grad, ffn_in_grad, layer_out = finish(
+        projected_grad, got, qkv_part, inputs, residual_grad, attn_scaling, ffn_sum, head_sum,
+        qkv_rows, qkv_peers, out_slices, in_part, residual, out_rest,
+        (out_top, out_bottom, out_top_last, out_bottom_last), query_width, head_dim
     )
     return (
         layer_out,

time: 623 us -> 609 us (0.978)
  waiting for transfers between devices: 26.2 us -> 4.16 us
  Pallas kernels: 515 us -> 532 us
    pallas_call x4 -> x5, Pallas kernels: 186 us -> 208 us  [the longest x1 85.1 us: feed_tail(): pl.pallas_call(tail_kernel, grid=(16 + total // units,), in_specs=[pl.Blo...]
    reduce_scatter x1, waiting for transfers between devices: 17.2 us -> 0.02 us  [local(): lax.psum_scatter(in_sum.reshape(size, blk_size * depth, -1), 'blk', scatt...]
    pallas_call x1, Pallas kernels: 92.6 us -> 76.9 us  [begin(): pl.pallas_call(begin_kernel, out_shape=[jax.ShapeDtypeStruct((size * coun...]
    pallas_call x1, Pallas kernels: 27.5 us -> 35.7 us  [residual_back(): pl.pallas_call(residual_back_kernel, grid=(tiles + 1,), in_specs=[tile, t...]
    pallas_call x1, Pallas kernels: 60.2 us -> 68.1 us  [join(): pl.pallas_call(join_kernel, grid=(count // rows,), in_specs=[pl.BlockSpec...]
    unnamed x53 -> x73, local copies, waits for them, and re-layouts: 13.3 us -> 18.3 us
  transfers between devices with their start and end apart: 16 -> 17, of which waited for: 2 -> 2; matrix products, arithmetic and copies ran while one was open for 5% -> 2% of each run, Pallas kernels for 61% -> 76%
where the time goes in v5:
time: 609 us; the launch traced here: 600 us
  Pallas kernels  532 us (87%)
  local copies, waits for them, and re-layouts  24.3 us (4%)
  between operations  14.8 us (2%)
  starting transfers between devices  13.6 us (2%)
  other arithmetic  11.1 us (2%)
    pallas_call x1, Pallas kernels, feed_tail(): pl.pallas_call(tail_kernel, grid=(16 + total // units,), in_specs=[pl.Blo...  85.1 us
    pallas_call x1, Pallas kernels, begin(): pl.pallas_call(begin_kernel, out_shape=[jax.ShapeDtypeStruct((size * coun...  76.9 us
    pallas_call x1, Pallas kernels, hidden_pass(): pl.pallas_call(functools.partial(hidden_kernel, tiles), grid=(2 * tiles +...  74.5 us
    pallas_call x1, Pallas kernels, join(): pl.pallas_call(join_kernel, grid=(count // rows,), in_specs=[pl.BlockSpec...  68.1 us
    pallas_call x1, Pallas kernels, finish(): pl.pallas_call(functools.partial(finish_kernel, query_width, dim), out_sh...  63 us
    pallas_call x1, Pallas kernels, residual_back(): pl.pallas_call(residual_back_kernel, grid=(tiles + 1,), in_specs=[tile, t...  35.7 us
    pallas_call x1, Pallas kernels, attend_back(): pl.pallas_call(functools.partial(attend_back_kernel, heads, key_rows, (wi...  35 us
    pallas_call x1, Pallas kernels, project(): pl.pallas_call(functools.partial(project_kernel, dim), grid=(count // row...  29.2 us
  transfers between devices with their start and end apart: 17, of which 2 were waited for; matrix products, arithmetic and copies ran while one was open for 2% of the time, Pallas kernels for 76%

profile of v5, /device:TPU:0, one launch (start us, length us, event | category | flops | bytes accessed | tf_op | source)
XLA Modules:
  0.0 600.3 jit_solution(17345786440296419771)
XLA Ops:
  9.3 20.1 %trade.1 = bf16[4,64,2560]{2,1,0:T(8,128)(2,1)} custom-call(bf16[64,10240]{1,0:T(8,128)(2,1)S(1)} %copy-done.2), custom_call_target="tpu_custom_call" | custom-call | tf_op jit(solution)/shard_map/trade/pallas_call | solution.py:627
  30.9 76.9 %begin.1 = (bf16[2048,2048]{1,0:T(8,128)(2,1)}, bf16[4,512,512]{2,1,0:T(8,128)(2,1)}) custom-call(bf16[512,2048]{1,0:T(8,128)(2,1)} %refs_2_.1, bf16[4,64,512]{2,1,0:T(8,128)(2,1)} %bitcast.31), custom_call_target="tpu_custom_call" | custom-call | tf_op jit(solution)/shard_map/begin/pallas_call | solution.py:777
  107.9 3.7 fusion
  112.3 1.6 copy-done.6
  113.9 29.2 %project.1 = (bf16[2048,256]{1,0:T(8,128)(2,1)S(1)}, bf16[2048,128]{1,0:T(8,128)(2,1)S(1)}, f32[2048,384]{1,0:T(8,128)}, bf16[2048,2048]{1,0:T(8,128)(2,1)}, f32...) custom-call(bf16[2048,2048]{1,0:T(8,128)(2,1)} %get-tuple-element.80.x_ref, ...), custom_call_target="tpu_custom_call" | custom-call | flops 6442450944 | bytes 30000000 | tf_op jit(solution)/shard_map/project/pallas_call | solution.py:309
  148.4 3.1 fusion.1
  151.5 2.0 collective-permute-start.1
  154.9 16.3 %attend.1 = (bf16[2048,256]{1,0:T(8,128)(2,1)S(1)}, f32[4,1,2048]{2,1,0:T(1,128)S(1)}) custom-call(s32[5]{0:T(128)S(1)} %pad_add_fusion.first_ref, bf16[2048,256]{1,0:T(8,128)(2,1)S(1)} %copy-done.14, s32[1,2048]{1,0:T(1,128)S(1)} %bitcast.25, bf16[4096,128]{1,0:T(8,128)(2,1)S(1)} %pad_maximum_fusion.2.pair_ref), custom_call_target="tpu_custom_call" | custom-call | flops 20000000000 | bytes 8000000 | tf_op jit(solution)/shard_map/attend/pallas_call | solution.py:162
  172.4 68.1 %join.1 = (f32[2048,2048]{1,0:T(8,128)}, bf16[2048,2048]{1,0:T(8,128)(2,1)}, bf16[512,1024]{1,0:T(8,128)(2,1)}, bf16[256,2048]{1,0:T(8,128)(2,1)}, bf16[256,2048]{1,0:T(8,128)(2,1)}) custom-call(bf16[2048,2048]{1,0:T(8,128)(2,1)} %get-tuple-element.80.x_ref, bf16[256,2048]{1,0:T(8,128)(2,1)} %all-gather.4.cloned.1.call-done.side_ref.weight_ref, ...), custom_call_target="tpu_custom_call" | custom-call | flops 17179869184 | bytes 50000000 | tf_op jit(solution)/shard_map/join/pallas_call | solution.py:550
  240.5 74.5 %hidden_pass.1 = (bf16[2048,1280]{1,0:T(8,128)(2,1)}, bf16[2048,1280]{1,0:T(8,128)(2,1)}, bf16[2048,1280]{1,0:T(8,128)(2,1)}, bf16[2048,2560]{1,0:T(8,128)(2,1)}...) custom-call(bf16[2048,2048]{1,0:T(8,128)(2,1)} %get-tuple-element.91.normed_ref.turned_ref, ...), custom_call_target="tpu_custom_call" | custom-call | flops 53687091200 | bytes 70000000 | tf_op jit(solution)/shard_map/hidden_pass/pallas_call | solution.py:983
  315.3 85.1 %feed_tail.1 = (bf16[1280,2048]{1,0:T(8,128)(2,1)}, bf16[256,2048]{1,0:T(8,128)(2,1)}, bf16[256,2048]{1,0:T(8,128)(2,1)}, bf16[256,2048]{1,0:T(8,128)(2,1)}, bf1...) custom-call(bf16[2048,1280]{1,0:T(8,128)(2,1)} %get-tuple-element.97.gate_ref, ...), custom_call_target="tpu_custom_call" | custom-call | flops 42949672960 | bytes 70000000 | tf_op jit(solution)/shard_map/feed_tail/pallas_call | solution.py:1184
  402.5 35.7 %residual_back.1 = (f32[512,2048]{1,0:T(8,128)}, f32[1,2048]{1,0:T(1,128)}, bf16[4,512,256]{2,1,0:T(8,128)(2,1)}, bf16[4,32,2048]{2,1,0:T(8,128)(2,1)}, bf16[4,3...) custom-call(f32[512,2048]{1,0:T(8,128)} %get-tuple-element.103.grad_sum_ref, ...), custom_call_target="tpu_custom_call" | custom-call | flops 4294967296 | bytes 30000000 | tf_op jit(solution)/shard_map/residual_back/pallas_call | solution.py:1339
  440.3 1.5 collective-permute-start.9
  441.9 3.2 add_convert_fusion
  447.2 35.0 %attend_back.1 = (bf16[2048,256]{1,0:T(8,128)(2,1)S(1)}, f32[4096,128]{1,0:T(8,128)}, bf16[2048,128]{1,0:T(8,128)(2,1)S(1)}) custom-call(s32[5]{0:T(128)S(1)} %pad_add_fusion.first_ref, bf16[2048,256]{1,0:T(8,128)(2,1)S(1)} %copy-done.15, s32[1,2048]{1,0:T(1,128)S(1)} %bitcast.26, bf16[4096,128]{1,0:T(8,128)(2,1)S(1)} %pad_maximum_fusion.2.pair_ref, ...), custom_call_target="tpu_custom_call" | custom-call | flops 40000000000 | bytes 12000000 | tf_op jit(solution)/shard_map/attend_back/pallas_call | solution.py:192
  482.2 1.8 collective-permute-done.6.refs_11_
  484.0 1.9 collective-permute-start.10
  486.1 11.3 %project_back.1 = (bf16[2048,384]{1,0:T(8,128)(2,1)S(1)}, f32[1,320]{1,0:T(1,128)S(1)}) custom-call(bf16[2048,256]{1,0:T(8,128)(2,1)S(1)} %get-tuple-element.110.query_grad_ref, f32[4096,128]{1,0:T(8,128)} %get-tuple-element.119.pair_grad_ref, f32[2048,384]{1,0:T(8,128)} %get-tuple-element.120.raw_ref, f32[1,320]{1,0:T(1,128)S(1)} %copy-done.11, ...), custom_call_target="tpu_custom_call" | custom-call | flops 8000000000 | bytes 8000000 | tf_op jit(solution)/shard_map/project_back/pallas_call | solution.py:428
  497.5 17.2 %qkv_terms.1 = (bf16[2048,384]{1,0:T(8,128)(2,1)S(1)}, bf16[3,512,384]{2,1,0:T(8,128)(2,1)S(1)}) custom-call(bf16[2048,2048]{1,0:T(8,128)(2,1)} %get-tuple-element.82.normed_ref, bf16[2048,384]{1,0:T(8,128)(2,1)S(1)} %get-tuple-element.122.grad_ref.refs_4_), custom_call_target="tpu_custom_call" | custom-call | flops 6442450944 | bytes 20000000 | tf_op jit(solution)/shard_map/qkv_terms/pallas_call | solution.py:1422
  518.2 63.0 %finish.1 = (f32[512,2048]{1,0:T(8,128)}, f32[64,1536]{1,0:T(8,128)}, f32[8,128]{1,0:T(8,128)}, f32[32,2048]{1,0:T(8,128)}, f32[64,10240]{1,0:T(8,128)}, /*index=5*/bf16[512,2048]{1,0:T(8,128)(2,1)}) custom-call(bf16[3,512,384]{2,1,0:T(8,128)(2,1)} %copy-done.3, bf16[16,2,64,384]{3,2,1,0:T(8,128)(2,1)} %bitcast.24, f32[1,2048]{1,0:T(1,128)} %copy-done.7, ...), custom_call_target="tpu_custom_call" | custom-call | tf_op jit(solution)/shard_map/finish/pallas_call | solution.py:1726
  582.6 2.3 convert_element_type.42
  584.9 3.3 copy.36
  588.3 2.1 copy.37
  591.9 1.5 copy.40
  (128 shorter events, 25.0 us)
Async XLA Ops:
  7.2 22.3 %copy-start.33 = (bf16[64]{0:T(256)(128)(2,1)S(1)}, bf16[64]{0:T(256)(128)(2,1)}, u32[]{:S(2)}) copy-start(bf16[64]{0:T(256)(128)(2,1)} %param.15) | copy-start | bytes 388
  7.2 105.1 %all-gather.4.cloned.1.call-start = ((), (), s32[]{:S(2)}) async-start(), calls=%async_computation.2 | async-start | bytes 1179648 | tf_op jit(solution)/shard_map/all_gather | solution.py:1827
  7.9 164.4 %all-gather.6.cloned.1.call-start = ((), (), s32[]{:S(2)}) async-start(), calls=%async_computation.3 | async-start | bytes 11796480 | tf_op jit(solution)/shard_map/all_gather | solution.py:1829
  29.5 211.0 %all-gather.8.cloned.1.call-start = ((), (), s32[]{:S(2)}) async-start(), calls=%async_computation.4 | async-start | bytes 5898240 | tf_op jit(solution)/shard_map/all_gather | solution.py:1845
  29.6 78.3 %copy-start.31 = (bf16[64]{0:T(256)(128)(2,1)S(1)}, bf16[64]{0:T(256)(128)(2,1)}, u32[]{:S(2)}) copy-start(bf16[64]{0:T(256)(128)(2,1)} %param.16) | copy-start | bytes 388
  29.6 78.3 %copy-start.28 = (s32[2048]{0:T(1024)S(1)}, s32[2048]{0:T(1024)}, u32[]{:S(2)}) copy-start(s32[2048]{0:T(1024)} %param.12) | copy-start | bytes 24580
  112.3 30.8 %copy-start.4 = (f32[2048,64]{1,0:T(8,128)}, f32[2048,64]{1,0:T(8,128)S(1)}, u32[]{:S(2)}) copy-start(f32[2048,64]{1,0:T(8,128)S(1)} %get-tuple-element.167.cosine_ref) | copy-start | bytes 1572868
  145.3 2.8 collective-permute-start
  148.2 290.1 %reduce-scatter.3.cloned.1.call-start = ((), (), s32[]{:S(2)}) async-start(), calls=%async_computation.5 | async-start | bytes 11796480 | tf_op jit(solution)/shard_map/reduce_scatter | solution.py:1863
  151.5 88.9 %collective-permute-start.2 = (bf16[256,2048]{1,0:T(8,128)(2,1)}, bf16[256,2048]{1,0:T(8,128)(2,1)}, u32[]{:S(2)}, u32[]{:S(2)}) collective-permute-start(bf16[256,2048]{1,0:T(8,128)(2,1)} %get-tuple-element.150), channel_id=1, source_target_pairs={{0,16},{8,24},{16,0},{24,8},{1,17},{9,25},{17,1},{25,9},{2,18},{10... | collective-permute-start | bytes 3145736 | tf_op jit(solution)/shard_map/ppermute | solution.py:1775
  151.5 88.9 %collective-permute-start.1 = (bf16[256,2048]{1,0:T(8,128)(2,1)}, bf16[256,2048]{1,0:T(8,128)(2,1)}, u32[]{:S(2)}, u32[]{:S(2)}) collective-permute-start(bf16[256,2048]{1,0:T(8,128)(2,1)} %get-tuple-element.151), channel_id=1, source_target_pairs={{0,8},{8,0},{16,24},{24,16},{1,9},{9,1},{17,25},{25,17},{2,10},{10... | collective-permute-start | bytes 3145736 | tf_op jit(solution)/shard_map/ppermute | solution.py:1775
  315.0 267.6 %reduce-scatter.5.cloned.1.call-start = ((), (), s32[]{:S(2)}) async-start(), calls=%async_computation.6 | async-start | bytes 5898240 | tf_op jit(solution)/shard_map/reduce_scatter | solution.py:1877
  400.4 37.8 %collective-permute-start.3 = (bf16[256,2048]{1,0:T(8,128)(2,1)}, bf16[256,2048]{1,0:T(8,128)(2,1)}, u32[]{:S(2)}, u32[]{:S(2)}) collective-permute-start(bf16[256,2048]{1,0:T(8,128)(2,1)} %get-tuple-element.107), channel_id=1, source_target_pairs={{0,8},{8,0},{16,24},{24,16},{1,9},{9,1},{17,25},{25,17},{2,10},{10... | collective-permute-start | bytes 3145736 | tf_op jit(solution)/shard_map/ppermute | solution.py:1775
  401.7 36.6 %collective-permute-start.4 = (bf16[256,2048]{1,0:T(8,128)(2,1)}, bf16[256,2048]{1,0:T(8,128)(2,1)}, u32[]{:S(2)}, u32[]{:S(2)}) collective-permute-start(bf16[256,2048]{1,0:T(8,128)(2,1)} %get-tuple-element.108), channel_id=1, source_target_pairs={{0,16},{8,24},{16,0},{24,8},{1,17},{9,25},{17,1},{25,9},{2,18},{10... | collective-permute-start | bytes 3145736 | tf_op jit(solution)/shard_map/ppermute | solution.py:1775
  438.3 43.9 %collective-permute-start.7 = (bf16[128,2048]{1,0:T(8,128)(2,1)}, bf16[128,2048]{1,0:T(8,128)(2,1)S(1)}, u32[]{:S(2)}, u32[]{:S(2)}) collective-permute-start(bf16[128,2048]{1,0:T(8,128)(2,1)} %bitcast.41), channel_id=1, source_target_pairs={{0,8},{8,0},{16,24},{24,16},{1,9},{9,1},{17,25},{25,17},{2,10},{10... | collective-permute-start | bytes 1572872 | tf_op jit(solution)/shard_map/ppermute | solution.py:1775
  439.1 43.0 %collective-permute-start.8 = (bf16[128,2048]{1,0:T(8,128)(2,1)}, bf16[128,2048]{1,0:T(8,128)(2,1)S(1)}, u32[]{:S(2)}, u32[]{:S(2)}) collective-permute-start(bf16[128,2048]{1,0:T(8,128)(2,1)} %bitcast.40), channel_id=1, source_target_pairs={{0,16},{8,24},{16,0},{24,8},{1,17},{9,25},{17,1},{25,9},{2,18},{10... | collective-permute-start | bytes 1572872 | tf_op jit(solution)/shard_map/ppermute | solution.py:1775
  440.3 41.8 %collective-permute-start.9 = (bf16[128,2048]{1,0:T(8,128)(2,1)}, bf16[128,2048]{1,0:T(8,128)(2,1)S(1)}, u32[]{:S(2)}, u32[]{:S(2)}) collective-permute-start(bf16[128,2048]{1,0:T(8,128)(2,1)} %bitcast.39), channel_id=1, source_target_pairs={{0,24},{8,16},{16,8},{24,0},{1,25},{9,17},{17,9},{25,1},{2,26},{10... | collective-permute-start | bytes 1572872 | tf_op jit(solution)/shard_map/ppermute | solution.py:1775
  445.1 38.9 %collective-permute-start.6 = (bf16[256,2048]{1,0:T(8,128)(2,1)S(1)}, bf16[256,2048]{1,0:T(8,128)(2,1)S(1)}, u32[]{:S(2)}, u32[]{:S(2)}) collective-permute-start(bf16[256,2048]{1,0:T(8,128)(2,1)S(1)} %get-tuple-element.148), channel_id=1, source_target_pairs={{0,8},{8,0},{16,24},{24,16},{1,9},{9,1},{17,25},{25,17},{2,10},{10... | collective-permute-start | bytes 3145736 | tf_op jit(solution)/shard_map/ppermute | solution.py:1775
  445.9 38.1 %collective-permute-start.5 = (bf16[256,2048]{1,0:T(8,128)(2,1)S(1)}, bf16[256,2048]{1,0:T(8,128)(2,1)S(1)}, u32[]{:S(2)}, u32[]{:S(2)}) collective-permute-start(bf16[256,2048]{1,0:T(8,128)(2,1)S(1)} %get-tuple-element.149), channel_id=1, source_target_pairs={{0,16},{8,24},{16,0},{24,8},{1,17},{9,25},{17,1},{25,9},{2,18},{10... | collective-permute-start | bytes 3145736 | tf_op jit(solution)/shard_map/ppermute | solution.py:1775
  447.2 38.7 %copy-start.32 = (bf16[256,2048]{1,0:T(8,128)(2,1)S(1)}, bf16[256,2048]{1,0:T(8,128)(2,1)}, u32[]{:S(2)}) copy-start(bf16[256,2048]{1,0:T(8,128)(2,1)} %get-tuple-element.138) | copy-start | bytes 3145732
  447.2 38.9 %copy-start.5 = (f32[2048,64]{1,0:T(8,128)S(1)}, f32[2048,64]{1,0:T(8,128)}, u32[]{:S(2)}) copy-start(f32[2048,64]{1,0:T(8,128)} %copy-done.4) | copy-start | bytes 1572868
  447.2 38.9 %copy-start.11 = (f32[1,320]{1,0:T(1,128)S(1)}, f32[1,320]{1,0:T(1,128)}, u32[]{:S(2)}) copy-start(f32[1,320]{1,0:T(1,128)} %copy-done.10) | copy-start | bytes 3844
  484.0 32.8 %collective-permute-start.10 = (bf16[256,2048]{1,0:T(8,128)(2,1)}, bf16[256,2048]{1,0:T(8,128)(2,1)S(1)}, u32[]{:S(2)}, u32[]{:S(2)}) collective-permute-start(bf16[256,2048]{1,0:T(8,128)(2,1)} %get-tuple-element.136), channel_id=1, source_target_pairs={{0,8},{8,0},{16,24},{24,16},{1,9},{9,1},{17,25},{25,17},{2,10},{10... | collective-permute-start | bytes 3145736 | tf_op jit(solution)/shard_map/ppermute | solution.py:1775
  485.9 31.0 %collective-permute-start.11 = (bf16[256,2048]{1,0:T(8,128)(2,1)S(1)}, bf16[256,2048]{1,0:T(8,128)(2,1)S(1)}, u32[]{:S(2)}, u32[]{:S(2)}) collective-permute-start(bf16[256,2048]{1,0:T(8,128)(2,1)S(1)} %copy-done.32), channel_id=1, source_target_pairs={{0,16},{8,24},{16,0},{24,8},{1,17},{9,25},{17,1},{25,9},{2,18},{10... | collective-permute-start | bytes 3145736 | tf_op jit(solution)/shard_map/ppermute | solution.py:1775
  (28 other events, 226.9 us)
Sparse Core Ops, SparseCore 0:
  9.6 24.9 all-gather.3
  36.2 112.4 all-gather.5
  150.3 61.3 all-gather.7
  315.1 110.5 reduce-scatter.2
  438.4 64.5 reduce-scatter.4

commit v6 on v5

--- a/solution.py
+++ b/solution.py
@@ -16,12 +16,6 @@
 NEG = -1e30
 MESH = pl.DeviceIdType.MESH
 ROWS_IN_BOTH = (((1,), (1,)), ((), ()))
-
-
-def from_behind(block, axis, distance):
-    devices = range(lax.axis_size(axis))
-    route = [(i - distance, i) for i in devices if i - distance in devices]
-    return lax.ppermute(block, axis, route)
 
 
 def rotation(positions, head_dim):
@@ -256,13 +250,57 @@
 
 
 def project_kernel(
-    dim, x_ref, weight_ref, head_gain_ref, cosine_ref, sine_ref, side_ref, query_ref, pair_ref,
-    raw_ref, normed_ref, gain_ref, ffn_gain_ref, spread_ref, send_sem, recv_sem
+    dim, size, x_ref, weight_ref, head_gain_ref, cosine_ref, sine_ref, side_ref, query_ref, raw_ref,
+    normed_ref, gain_ref, ffn_gain_ref, spread_ref, pair_ref, pair_held, send_sem, recv_sem,
+    pair_sem, pair_send, pair_recv
 ):
     columns = raw_ref.shape[1]
     step, steps = pl.program_id(0), pl.num_programs(0)
     marks = (0, steps // 2, steps - 2)
-    end = spread_job(step, marks, side_ref, spread_ref, send_sem, recv_sem)
+    head, blk = lax.axis_index("heads"), lax.axis_index("blk")
+    last = lax.axis_size("blk") - 1
+    rows, block = x_ref.shape[0], pair_held.shape[0]
+    tiles = block // size // rows
+
+    @pl.when(step == 0)
+    def _():
+        barrier = pltpu.get_barrier_semaphore()
+        for place in ((head ^ 1, blk), (head ^ 2, blk), (head, blk ^ 1)):
+            pl.semaphore_signal(barrier, inc=1, device_id=place, device_id_type=MESH)
+
+        @pl.when(blk > 0)
+        def _():
+            pl.semaphore_signal(barrier, inc=1, device_id=(head, blk - 1), device_id_type=MESH)
+
+        @pl.when(blk < last)
+        def _():
+            pl.semaphore_wait(barrier, 4)
+
+        @pl.when(blk == last)
+        def _():
+            pl.semaphore_wait(barrier, 3)
+
+    end = spread_job(step, marks, side_ref, spread_ref, send_sem, recv_sem, False)
+
+    def chunk_rows(k, first):
+        return pl.ds(
+            pl.multiple_of(first + (head ^ k) * (block // size), block // size), block // size
+        )
+
+    def keep(k):
+        return pltpu.make_async_copy(
+            pair_held.at[chunk_rows(k, 0)], pair_ref.at[chunk_rows(k, block)], pair_sem.at[k]
+        )
+
+    def pass_on(k):
+        return pltpu.make_async_remote_copy(
+            src_ref=pair_held.at[chunk_rows(k, 0)],
+            dst_ref=pair_ref.at[chunk_rows(k, 0)],
+            send_sem=pair_send.at[k],
+            recv_sem=pair_recv.at[k],
+            device_id=(head, jnp.minimum(blk + 1, last)),
+            device_id_type=MESH,
+        )
 
     @pl.when(pl.program_id(0) == 0)
     def _():
@@ -276,16 +314,41 @@
     normed_ref[...] = normed
     raw = jnp.dot(normed, weight_ref[:, :columns], preferred_element_type=jnp.float32)
     raw_ref[...] = raw
-    turned_width = raw.shape[1] - pair_ref.shape[1] // 2
+    turned_width = raw.shape[1] - pair_held.shape[1] // 2
     heads = raw[:, :turned_width]
     heads = heads * lax.rsqrt(heads_apart(heads, dim) + EPS) * head_gain_ref[...]
     heads = turn(heads, cosine_ref[...], sine_ref[...], dim).astype(jnp.bfloat16)
     query_width = query_ref.shape[1]
     query_ref[...] = heads[:, :query_width]
-    pair_ref[...] = jnp.concatenate(
+    place = ((head ^ (step // tiles)) * tiles + lax.rem(step, tiles)) * rows
+    pair_held[pl.ds(pl.multiple_of(place, rows), rows)] = jnp.concatenate(
         [heads[:, query_width:], raw[:, turned_width:].astype(jnp.bfloat16)], axis=1
     )
-    pl.when(step == steps - 1)(end)
+    for k in range(size):
+
+        @pl.when(step == (k + 1) * tiles - 1)
+        def _(k=k):
+            keep(k).start()
+
+            @pl.when(blk < last)
+            def _():
+                pass_on(k).start()
+
+    @pl.when(step == steps - 1)
+    def _():
+        end()
+        for k in range(size):
+            keep(k).wait()
+
+        @pl.when(blk < last)
+        def _():
+            for k in range(size):
+                pass_on(k).wait_send()
+
+        @pl.when(blk > 0)
+        def _():
+            for k in range(size):
+                pass_on(k).wait_recv()
 
 
 def project(x, weight, head_gain, cosine, sine, side, size, query_width, rows):
@@ -307,7 +370,7 @@
     anywhere = pl.BlockSpec(memory_space=pl.ANY)
 
     return pl.pallas_call(
-        functools.partial(project_kernel, dim),
+        functools.partial(project_kernel, dim, size),
         grid=(count // rows,),
         in_specs=[
             pl.BlockSpec((rows, width), there),
@@ -319,23 +382,25 @@
         ],
         out_specs=[
             pl.BlockSpec((rows, query_width), apart),
-            pl.BlockSpec((rows, pair_width), apart),
             pl.BlockSpec((rows, out_width), apart),
             pl.BlockSpec((rows, width), there),
             pl.BlockSpec((1, width), whole),
             pl.BlockSpec((1, width), whole),
             anywhere,
+            anywhere,
         ],
         out_shape=[
             jax.ShapeDtypeStruct((count, query_width), jnp.bfloat16),
-            jax.ShapeDtypeStruct((count, pair_width), jnp.bfloat16),
             jax.ShapeDtypeStruct((count, out_width), jnp.float32),
             jax.ShapeDtypeStruct((count, width), jnp.bfloat16),
             jax.ShapeDtypeStruct((1, width), jnp.float32),
             jax.ShapeDtypeStruct((1, width), jnp.float32),
             jax.ShapeDtypeStruct((3, *side.shape), side.dtype),
-        ],
-        scratch_shapes=[pltpu.SemaphoreType.DMA((SPREAD_COUNT,))] * 2,
+            jax.ShapeDtypeStruct((2 * count, pair_width), jnp.bfloat16),
+        ],
+        scratch_shapes=[pltpu.VMEM((count, pair_width), jnp.bfloat16)]
+        + [pltpu.SemaphoreType.DMA((SPREAD_COUNT,))] * 2
+        + [pltpu.SemaphoreType.DMA((size,))] * 3,
         compiler_params=pltpu.CompilerParams(
             collective_id=5, has_side_effects=True, vmem_limit_bytes=48 << 20
         ),
@@ -1379,11 +1444,19 @@
     )(grad_sum, residual, cot, gain, attended, weight, weights)
 
 
-def qkv_terms_kernel(normed_ref, grad_ref, terms_ref, got_ref, send_sem, recv_sem):
+def qkv_terms_kernel(normed_ref, grad_ref, *refs):
+    size, blk_size = lax.axis_size("heads"), lax.axis_size("blk")
+    out_refs, refs = refs[:size], refs[size:]
+    (
+        terms_ref, got_ref, out_grad_ref, out_part_ref, out_got_ref, send_sem, recv_sem, o_send,
+        o_recv,
+    ) = refs
     step = pl.program_id(0)
-    size = lax.axis_size("heads")
+    pairs = blk_size // 2
     head, blk = lax.axis_index("heads"), lax.axis_index("blk")
+    core, pair = lax.rem(blk, 2), blk // 2
     count = got_ref.shape[1]
+    out_rows = out_grad_ref.shape[0]
     copies = [
         pltpu.make_async_remote_copy(
             src_ref=grad_ref.at[pl.ds(k * count, count)],
@@ -1396,14 +1469,51 @@
         for k in range(1, size)
     ]
 
+    def wide_of(block):
+        return block.astype(jnp.float32)
+
+    def out_copy(k, slot):
+        other = lax.rem(pair + k, pairs)
+        return pltpu.make_async_remote_copy(
+            src_ref=out_part_ref.at[other],
+            dst_ref=out_got_ref.at[slot],
+            send_sem=o_send.at[k],
+            recv_sem=o_recv.at[slot],
+            device_id=(head, other * 2 + core),
+            device_id_type=MESH,
+        )
+
     @pl.when(step == 0)
     def _():
         barrier = pltpu.get_barrier_semaphore()
         for k in range(1, size):
             pl.semaphore_signal(barrier, inc=1, device_id=(head ^ k, blk), device_id_type=MESH)
-        pl.semaphore_wait(barrier, size - 1)
+
+        def greet(k, carried):
+            place = (head, lax.rem(pair + k, pairs) * 2 + core)
+            pl.semaphore_signal(barrier, inc=1, device_id=place, device_id_type=MESH)
+            return carried
+
+        lax.fori_loop(1, pairs, greet, 0)
+        pl.semaphore_wait(barrier, size + pairs - 2)
         for copy in copies:
             copy.start()
+
+        def out_sum(index, carried):
+            here = pl.ds(pl.multiple_of(index * out_rows, out_rows), out_rows)
+            total = wide_of(out_refs[0][here])
+            for ref in out_refs[1:]:
+                total += wide_of(ref[here])
+            out_part_ref[index, :out_rows] = total.astype(jnp.bfloat16)
+            return carried
+
+        def start(k, carried):
+            out_copy(k, pair).start()
+            return carried
+
+        lax.fori_loop(0, pairs, out_sum, 0)
+        lax.fori_loop(1, pairs, start, 0)
+        out_got_ref[pair] = out_part_ref[pair]
 
     terms_ref[...] = lax.dot_general(
         normed_ref[...], grad_ref[...], (((0,), (0,)), ((), ())), preferred_element_type=jnp.float32
@@ -1414,27 +1524,55 @@
         for copy in copies:
             copy.wait()
 
-
-def qkv_terms(normed, grad, rows):
+        def finish(k, carried):
+            out_copy(k, lax.rem(pair + pairs - k, pairs)).wait()
+            return carried
+
+        lax.fori_loop(1, pairs, finish, 0)
+        total = wide_of(out_got_ref[0, :out_rows])
+        for b in range(1, pairs):
+            total += wide_of(out_got_ref[b, :out_rows])
+        out_grad_ref[...] = total
+
+
+def qkv_terms(normed, grad, outs, rows):
     count, height = normed.shape
     width = grad.shape[1]
-    size = lax.axis_size("heads")
+    size, blk_size = lax.axis_size("heads"), lax.axis_size("blk")
+    pairs = blk_size // 2
+    out_rows, out_width = outs[0].shape[0] // pairs, outs[0].shape[1]
+    held_rows = -(-out_rows // 16) * 16
+
+    def whole(i):
+        return (0, 0)
+
+    sems = pltpu.SemaphoreType.DMA
     return pl.pallas_call(
         qkv_terms_kernel,
         grid=(height // rows,),
         in_specs=[
             pl.BlockSpec((count, rows), lambda i: (0, i)),
-            pl.BlockSpec((count, width), lambda i: (0, 0)),
-        ],
+            pl.BlockSpec((count, width), whole),
+        ]
+        + [pl.BlockSpec(out.shape, whole) for out in outs],
         out_specs=[
             pl.BlockSpec((rows, width), lambda i: (i, 0)),
             pl.BlockSpec(memory_space=pl.ANY),
+            pl.BlockSpec((out_rows, out_width), whole),
         ],
         out_shape=[
             jax.ShapeDtypeStruct((height, width), jnp.bfloat16),
             jax.ShapeDtypeStruct((size - 1, count // size, width), jnp.bfloat16),
-        ],
-        scratch_shapes=[pltpu.SemaphoreType.DMA((size - 1,))] * 2,
+            jax.ShapeDtypeStruct((out_rows, out_width), jnp.float32),
+        ],
+        scratch_shapes=[
+            pltpu.VMEM((pairs, held_rows, out_width), jnp.bfloat16),
+            pltpu.VMEM((pairs, held_rows, out_width), jnp.bfloat16),
+            sems((size - 1,)),
+            sems((size - 1,)),
+            sems((pairs,)),
+            sems((pairs,)),
+        ],
         compiler_params=pltpu.CompilerParams(
             collective_id=7, has_side_effects=True, vmem_limit_bytes=48 << 20
         ),
@@ -1442,31 +1580,29 @@
             flops=4 * count * height * width, bytes_accessed=20_000_000, transcendentals=0
         ),
         name="qkv_terms",
-    )(normed, grad)
+    )(normed, grad, *outs)
 
 
 def finish_kernel(
-    query_width, dim, got_ref, qkv_ref, gain_ref, ffn_ref, head_ref, out_own_ref, out_one_ref, out_two_ref, out_three_ref, *refs
+    query_width, dim, got_ref, qkv_ref, gain_ref, ffn_ref, head_ref, *refs
 ):
     size, blk_size = lax.axis_size("heads"), lax.axis_size("blk")
-    out_refs = (out_own_ref, out_one_ref, out_two_ref, out_three_ref)
     sources, refs = refs[:12], refs[12:]
     (
-        grad_ref, qkv_grad_ref, gains_ref, out_grad_ref, in_grad_ref, layer_ref, *refs
+        grad_ref, qkv_grad_ref, gains_ref, in_grad_ref, layer_ref, *refs
     ) = refs
     held, refs = refs[:12], refs[12:]
     weight_ref, weights_ref, x_ref, residual_grad_ref, sent_ref, in_ref, residual_ref, rest_ref = held[:8]
     (
-        qkv_other_ref, qkv_sum_ref, qkv_got_ref, part_ref, gain_got_ref, out_part_ref,
-        out_got_ref, in_got_ref, load_sem, c_send, c_recv, q_send, q_recv, g_send,
-        g_recv, o_send, o_recv, i_send, i_recv,
+        qkv_other_ref, qkv_sum_ref, qkv_z_ref, qkv_mine_ref, qkv_got_ref, gain_mine_ref,
+        gain_away_ref, gain_other_ref, gain_sum_ref, gain_z_ref, gain_part_ref, gain_got_ref,
+        in_got_ref, load_sem, c_send, c_recv, z_send, z_recv, h_send,
+        h_recv, gc_send, gc_recv, gz_send, gz_recv, gh_send, gh_recv, i_send, i_recv,
     ) = refs
     devices = size * blk_size
     pairs = blk_size // 2
     head, blk = lax.axis_index("heads"), lax.axis_index("blk")
     core, pair = lax.rem(blk, 2), blk // 2
-    own = head * blk_size + blk
-    own_pair = head * pairs + pair
     count, width = x_ref.shape
     depth = width // devices
     barrier = pltpu.get_barrier_semaphore()
@@ -1485,17 +1621,19 @@
     for load in loads:
         load.start()
 
-    def place_of(index):
-        return (index // blk_size, lax.rem(index, blk_size))
+    def same_core(k):
+        return (head, lax.rem(pair + k, pairs) * 2 + core)
+
+    for k in range(1, size):
+        pl.semaphore_signal(barrier, inc=1, device_id=(head ^ k, blk), device_id_type=MESH)
+    pl.semaphore_signal(barrier, inc=1, device_id=(head, blk ^ 1), device_id_type=MESH)
 
     def greet(k, carried):
-        pl.semaphore_signal(
-            barrier, inc=1, device_id=place_of(lax.rem(own + k, devices)), device_id_type=MESH
-        )
+        pl.semaphore_signal(barrier, inc=1, device_id=same_core(k), device_id_type=MESH)
         return carried
 
-    lax.fori_loop(1, devices, greet, 0)
-    pl.semaphore_wait(barrier, devices - 1)
+    lax.fori_loop(1, pairs, greet, 0)
+    pl.semaphore_wait(barrier, size + pairs - 1)
 
     def copy(source, target, place, send, recv):
         return pltpu.make_async_remote_copy(
@@ -1507,6 +1645,19 @@
             device_id_type=MESH,
         )
 
+    in_sends = [
+        copy(
+            sources[5].at[head ^ k],
+            in_got_ref.at[k - 1],
+            (head ^ k, blk),
+            i_send.at[k - 1],
+            i_recv.at[k - 1],
+        )
+        for k in range(1, size)
+    ]
+    for sent in in_sends:
+        sent.start()
+
     across = copy(qkv_ref.at[:, 1 - core], qkv_other_ref, (head, blk ^ 1), c_send, c_recv)
     across.start()
     def wide_of(block):
@@ -1514,71 +1665,66 @@
 
     across.wait_recv()
 
-    def qkv_copy(k, slot):
-        other = lax.rem(own_pair + k, size * pairs)
+    def along(k, source_ref, target_ref, slot, send, recv):
         return copy(
-            qkv_sum_ref.at[other],
-            qkv_got_ref.at[slot],
-            (other // pairs, lax.rem(other, pairs) * 2 + core),
-            q_send.at[k],
-            q_recv.at[slot],
-        )
+            source_ref.at[:, lax.rem(pair + k, pairs)],
+            target_ref.at[slot],
+            same_core(k),
+            send.at[k],
+            recv.at[slot],
+        )
+
+    def around(source_ref, target_ref, slots, send, recv):
+        return [
+            copy(
+                source_ref.at[head ^ k],
+                target_ref.at[slots[k]],
+                (head ^ k, blk),
+                send.at[k - 1],
+                recv.at[slots[k]],
+            )
+            for k in range(1, size)
+        ]
+
+    def start_along(source_ref, target_ref, send, recv):
+        def start(k, carried):
+            along(k, source_ref, target_ref, pair, send, recv).start()
+            return carried
+
+        lax.fori_loop(1, pairs, start, 0)
+        target_ref[pair] = source_ref[:, pair]
+
+    def finish_along(source_ref, target_ref, send, recv):
+        def finish(k, carried):
+            slot = lax.rem(pair + pairs - k, pairs)
+            along(k, source_ref, target_ref, slot, send, recv).wait()
+            return carried
+
+        lax.fori_loop(1, pairs, finish, 0)
+        total = wide_of(target_ref[0])
+        for k in range(1, pairs):
+            total += wide_of(target_ref[k])
+        return total
+
+    here, there = [head] * size, [head ^ k for k in range(size)]
+
+    def start_around(source_ref, target_ref, send, recv):
+        for sent in around(source_ref, target_ref, here, send, recv):
+            sent.start()
+        target_ref[head] = source_ref[head]
+
+    def finish_around(source_ref, target_ref, send, recv):
+        for sent in around(source_ref, target_ref, there, send, recv):
+            sent.wait()
 
     def qkv_sum(index, carried):
-        qkv_sum_ref[index] = (
+        qkv_sum_ref[index // pairs, lax.rem(index, pairs)] = (
             wide_of(qkv_ref[index, core]) + wide_of(qkv_other_ref[index])
         ).astype(jnp.bfloat16)
         return carried
 
-    def start_qkv(k, carried):
-        qkv_copy(k, own_pair).start()
-        return carried
-
     lax.fori_loop(0, size * pairs, qkv_sum, 0)
-    lax.fori_loop(1, size * pairs, start_qkv, 0)
-    qkv_got_ref[own_pair] = qkv_sum_ref[own_pair]
-
-    def out_copy(k, slot):
-        other = lax.rem(pair + k, pairs)
-        return copy(
-            out_part_ref.at[other],
-            out_got_ref.at[slot],
-            (head, other * 2 + core),
-            o_send.at[k],
-            o_recv.at[slot],
-        )
-
-    out_rows = out_grad_ref.shape[0]
-
-    def out_sum(index, carried):
-        here = pl.ds(pl.multiple_of(index * out_rows, out_rows), out_rows)
-        total = wide_of(out_refs[0][here])
-        for ref in out_refs[1:]:
-            total += wide_of(ref[here])
-        out_part_ref[index, :out_rows] = total.astype(jnp.bfloat16)
-        return carried
-
-    def start_out(k, carried):
-        out_copy(k, pair).start()
-        return carried
-
-    lax.fori_loop(0, pairs, out_sum, 0)
-    lax.fori_loop(1, pairs, start_out, 0)
-    out_got_ref[pair] = out_part_ref[pair]
-
-    loads[5].wait()
-    in_sends = [
-        copy(
-            in_ref.at[head ^ k],
-            in_got_ref.at[k - 1],
-            (head ^ k, blk),
-            i_send.at[k - 1],
-            i_recv.at[k - 1],
-        )
-        for k in range(1, size)
-    ]
-    for sent in in_sends:
-        sent.start()
+    start_along(qkv_sum_ref, qkv_z_ref, z_send, z_recv)
 
     for load in loads[:5]:
         load.wait()
@@ -1609,13 +1755,13 @@
 
     attn_sum = lax.fori_loop(0, count // rows, tile, jnp.zeros((1, width), jnp.float32))
 
-    def by_device(row):
+    def by_device(row, which):
         lanes = jnp.concatenate(
-            [row[:, d * depth : (d + 1) * depth] for d in range(devices)], axis=0
+            [row[:, d * depth : (d + 1) * depth] for d in range(which, devices, 2)], axis=0
         )
         if depth < 64:
             lanes = jnp.concatenate(
-                [lanes, jnp.zeros((devices, 64 - depth), jnp.float32)], axis=1
+                [lanes, jnp.zeros((devices // 2, 64 - depth), jnp.float32)], axis=1
             )
         return lanes
 
@@ -1627,23 +1773,26 @@
     for c in range(query_width + dim, head_row.shape[1], dim):
         key_sum += head_row[:, c : c + dim]
     both = jnp.concatenate([query_sum, key_sum], axis=1)
-    part_ref[...] = jnp.zeros_like(part_ref)
-    part_ref[:, 0, :] = jnp.concatenate([by_device(attn_sum), by_device(ffn_ref[...])], axis=1)
-    part_ref[:, 1, :] = jnp.broadcast_to(both, (devices, 2 * dim))
-
-    def gain_copy(k, slot):
-        other = lax.rem(own + k, devices)
-        return copy(
-            part_ref.at[other], gain_got_ref.at[slot], place_of(other), g_send.at[k], g_recv.at[slot]
-        )
-
-    def start_gain(k, carried):
-        gain_copy(k, own).start()
-        return carried
-
-    lax.fori_loop(1, devices, start_gain, 0)
-    gain_got_ref[own] = part_ref[own]
-
+    gains = [
+        jnp.concatenate([by_device(attn_sum, c), by_device(ffn_ref[...], c)], axis=1)
+        for c in range(2)
+    ]
+    for ref, mine in ((gain_mine_ref, 0), (gain_away_ref, 1)):
+        ref[...] = jnp.zeros_like(ref)
+        ref[:, 0, :] = jnp.where(core == mine, gains[0], gains[1])
+        ref[:, 1, :] = jnp.broadcast_to(both, (devices // 2, 2 * dim))
+    gain_across = copy(gain_away_ref, gain_other_ref, (head, blk ^ 1), gc_send, gc_recv)
+    gain_across.start()
+    gain_across.wait()
+    gain_sum_ref[...] = (gain_mine_ref[...] + gain_other_ref[...]).reshape(gain_sum_ref.shape)
+    start_along(gain_sum_ref, gain_z_ref, gz_send, gz_recv)
+
+    qkv_mine_ref[...] = finish_along(qkv_sum_ref, qkv_z_ref, z_send, z_recv).astype(jnp.bfloat16)
+    start_around(qkv_mine_ref, qkv_got_ref, h_send, h_recv)
+    gain_part_ref[...] = finish_along(gain_sum_ref, gain_z_ref, gz_send, gz_recv)
+    start_around(gain_part_ref, gain_got_ref, gh_send, gh_recv)
+
+    loads[5].wait()
     units = in_ref.shape[2] // 2
     for k in range(size):
         if k:
@@ -1664,19 +1813,8 @@
             + wide_of(held[10 + part][...])
         ).astype(jnp.bfloat16)
 
-    def finish_qkv(k, carried):
-        qkv_copy(k, lax.rem(own_pair + size * pairs - k, size * pairs)).wait()
-        return carried
-
-    lax.fori_loop(1, size * pairs, finish_qkv, 0)
-
-    def group_sum(h):
-        total = wide_of(qkv_got_ref[h * pairs])
-        for b in range(1, pairs):
-            total += wide_of(qkv_got_ref[h * pairs + b])
-        return total
-
-    sums = [group_sum(h) for h in range(size)]
+    finish_around(qkv_mine_ref, qkv_got_ref, h_send, h_recv)
+    sums = [wide_of(qkv_got_ref[h]) for h in range(size)]
     key_end = query_width + (sums[0].shape[1] - query_width) // 2
     qkv_grad_ref[...] = jnp.concatenate(
         [total[:, :query_width] for total in sums]
@@ -1685,21 +1823,7 @@
         axis=1,
     )
 
-    def finish_out(k, carried):
-        out_copy(k, lax.rem(pair + pairs - k, pairs)).wait()
-        return carried
-
-    lax.fori_loop(1, pairs, finish_out, 0)
-    out_total = wide_of(out_got_ref[0, :out_rows])
-    for b in range(1, pairs):
-        out_total += wide_of(out_got_ref[b, :out_rows])
-    out_grad_ref[...] = out_total
-
-    def finish_gain(k, carried):
-        gain_copy(k, lax.rem(own + devices - k, devices)).wait()
-        return carried
-
-    lax.fori_loop(1, devices, finish_gain, 0)
+    finish_around(gain_part_ref, gain_got_ref, gh_send, gh_recv)
     gains_ref[...] = jnp.sum(gain_got_ref[...], axis=0)
     across.wait_send()
     for sent in in_sends:
@@ -1707,7 +1831,7 @@
 
 
 def finish(
-    sent, got, qkv_part, x, residual_grad, gain, ffn_sum, head_sum, weight, weights, outs, in_part,
+    sent, got, qkv_part, x, residual_grad, gain, ffn_sum, head_sum, weight, weights, in_part,
     residual, rest, terms, query_width, dim
 ):
     size, blk_size = lax.axis_size("heads"), lax.axis_size("blk")
@@ -1715,8 +1839,6 @@
     pairs = blk_size // 2
     count, width = x.shape
     depth, joined = width // devices, sent.shape[1]
-    out_rows = outs[0].shape[0] // pairs
-    held_rows = -(-out_rows // 16) * 16
     units = in_part.shape[2]
     vmem = pl.BlockSpec(memory_space=pltpu.VMEM)
     anywhere = pl.BlockSpec(memory_space=pl.ANY)
@@ -1729,12 +1851,11 @@
             jax.ShapeDtypeStruct((count, width), jnp.float32),
             jax.ShapeDtypeStruct((depth, size * joined), jnp.float32),
             jax.ShapeDtypeStruct((8, 128), jnp.float32),
-            jax.ShapeDtypeStruct((out_rows, width), jnp.float32),
             jax.ShapeDtypeStruct((depth, size * units), jnp.float32),
             jax.ShapeDtypeStruct((count, width), low),
         ],
-        in_specs=[vmem] * (5 + size) + [anywhere] * 12,
-        out_specs=[vmem] * 6,
+        in_specs=[vmem] * 5 + [anywhere] * 12,
+        out_specs=[vmem] * 5,
         scratch_shapes=[pltpu.VMEM((width, joined), low)]
         + [pltpu.VMEM(array.shape, array.dtype) for array in loaded]
         + [pltpu.VMEM((count, joined), low), pltpu.VMEM(in_part.shape, low)]
@@ -1742,23 +1863,32 @@
         + [pltpu.VMEM((count // 2, width), low)] * 4
         + [
             pltpu.VMEM((size * pairs, depth, joined), low),
-            pltpu.VMEM((size * pairs, depth, joined), low),
-            pltpu.VMEM((size * pairs, depth, joined), low),
-            pltpu.VMEM((devices, 8, 128), jnp.float32),
-            pltpu.VMEM((devices, 8, 128), jnp.float32),
-            pltpu.VMEM((pairs, held_rows, width), low),
-            pltpu.VMEM((pairs, held_rows, width), low),
+            pltpu.VMEM((size, pairs, depth, joined), low),
+            pltpu.VMEM((pairs, size, depth, joined), low),
+            pltpu.VMEM((size, depth, joined), low),
+            pltpu.VMEM((size, depth, joined), low),
+            pltpu.VMEM((devices // 2, 8, 128), jnp.float32),
+            pltpu.VMEM((devices // 2, 8, 128), jnp.float32),
+            pltpu.VMEM((devices // 2, 8, 128), jnp.float32),
+            pltpu.VMEM((size, pairs, 8, 128), jnp.float32),
+            pltpu.VMEM((pairs, size, 8, 128), jnp.float32),
+            pltpu.VMEM((size, 8, 128), jnp.float32),
+            pltpu.VMEM((size, 8, 128), jnp.float32),
             pltpu.VMEM((size - 1, depth, units), low),
             sems((12,)),
             sems,
             sems,
-            sems((size * pairs,)),
-            sems((size * pairs,)),
-            sems((devices,)),
-            sems((devices,)),
             sems((pairs,)),
             sems((pairs,)),
             sems((size - 1,)),
+            sems((size,)),
+            sems,
+            sems,
+            sems((pairs,)),
+            sems((pairs,)),
+            sems((size - 1,)),
+            sems((size,)),
+            sems((size - 1,)),
             sems((size - 1,)),
         ],
         compiler_params=pltpu.CompilerParams(
@@ -1766,7 +1896,7 @@
         ),
         name="finish",
     )(
-        got, qkv_part.reshape(size * pairs, 2, depth, joined), gain, ffn_sum, head_sum, *outs,
+        got, qkv_part.reshape(size * pairs, 2, depth, joined), gain, ffn_sum, head_sum,
         weight, *loaded, sent, in_part, residual, rest, *terms
     )
 
@@ -1836,11 +1966,9 @@
     head_gain = jnp.concatenate(
         [jnp.tile(q_gain, HEADS // size), jnp.tile(k_gain, KV_HEADS // size)]
     ).astype(jnp.float32)[None, :]
-    query_low, pair_blk, raw, normed, attn_scaling, ffn_scaling, out_peers = project(
+    query_low, raw, normed, attn_scaling, ffn_scaling, out_peers, pair_all = project(
         inputs_blk, qkv_rows, head_gain, cosine, sine, out_group, size, query_width, 256
     )
-    pair_behind = from_behind(pair_blk, "blk", 1)
-    pair_all = jnp.concatenate([pair_behind, pair_blk], axis=0)
     down_weight, pair_all = lax.optimization_barrier((ffn_out_weight, pair_all))
     down_group = lax.all_gather(down_weight, "blk", axis=0, tiled=True)
     query_rows, key_rows = token_count, 256
@@ -1892,10 +2020,10 @@
     )
     out_top = permute(after(one_near, pair_sum), "heads", 1)
     out_bottom = permute(after(two_near, pair_sum), "heads", 2)
-    qkv_part, got = qkv_terms(normed, projected_grad, 512)
-    input_grad, qkv_grad, gains, out_grad, ffn_in_grad, layer_out = finish(
+    qkv_part, got, out_grad = qkv_terms(normed, projected_grad, out_slices, 512)
+    input_grad, qkv_grad, gains, ffn_in_grad, layer_out = finish(
         projected_grad, got, qkv_part, inputs, residual_grad, attn_scaling, ffn_sum, head_sum,
-        qkv_rows, qkv_peers, out_slices, in_part, residual, out_rest,
+        qkv_rows, qkv_peers, in_part, residual, out_rest,
         (out_top, out_bottom, out_top_last, out_bottom_last), query_width, head_dim
     )
     return (

time: 609 us -> 589 us (0.967)
  Pallas kernels: 532 us -> 512 us
    pallas_call x1, Pallas kernels: 63 us -> 37.8 us  [finish(): pl.pallas_call(functools.partial(finish_kernel, query_width, dim), out_sh...]
    unnamed x73 -> x67, local copies, waits for them, and re-layouts: 18.3 us -> 21.5 us
  transfers between devices with their start and end apart: 17 -> 16, of which waited for: 2 -> 2; matrix products, arithmetic and copies ran while one was open for 2% -> 3% of each run, Pallas kernels for 76% -> 75%
where the time goes in v6:
time: 589 us; the launch traced here: 582 us
  Pallas kernels  512 us (87%)
  local copies, waits for them, and re-layouts  27.5 us (5%)
  between operations  14.4 us (2%)
  starting transfers between devices  11.8 us (2%)
  other arithmetic  11.5 us (2%)
    pallas_call x1, Pallas kernels, feed_tail(): pl.pallas_call(tail_kernel, grid=(16 + total // units,), in_specs=[pl.Blo...  85.6 us
    pallas_call x1, Pallas kernels, begin(): pl.pallas_call(begin_kernel, out_shape=[jax.ShapeDtypeStruct((size * coun...  76.9 us
    pallas_call x1, Pallas kernels, hidden_pass(): pl.pallas_call(functools.partial(hidden_kernel, tiles), grid=(2 * tiles +...  76.6 us
    pallas_call x1, Pallas kernels, join(): pl.pallas_call(join_kernel, grid=(count // rows,), in_specs=[pl.BlockSpec...  63 us
    pallas_call x1, Pallas kernels, finish(): pl.pallas_call(functools.partial(finish_kernel, query_width, dim), out_sh...  37.8 us
    pallas_call x1, Pallas kernels, residual_back(): pl.pallas_call(residual_back_kernel, grid=(tiles + 1,), in_specs=[tile, t...  36.3 us
    pallas_call x1, Pallas kernels, attend_back(): pl.pallas_call(functools.partial(attend_back_kernel, heads, key_rows, (wi...  34.8 us
    pallas_call x1, Pallas kernels, project(): pl.pallas_call(functools.partial(project_kernel, dim, size), grid=(count...  32 us
  transfers between devices with their start and end apart: 16, of which 2 were waited for; matrix products, arithmetic and copies ran while one was open for 3% of the time, Pallas kernels for 75%

profile of v6, /device:TPU:0, one launch (start us, length us, event | category | flops | bytes accessed | tf_op | source)
XLA Modules:
  0.0 581.7 jit_solution(14139755208556565134)
XLA Ops:
  9.3 20.1 %trade.1 = bf16[4,64,2560]{2,1,0:T(8,128)(2,1)} custom-call(bf16[64,10240]{1,0:T(8,128)(2,1)S(1)} %copy-done.2), custom_call_target="tpu_custom_call" | custom-call | tf_op jit(solution)/shard_map/trade/pallas_call | solution.py:692
  30.9 76.9 %begin.1 = (bf16[2048,2048]{1,0:T(8,128)(2,1)}, bf16[4,512,512]{2,1,0:T(8,128)(2,1)}) custom-call(bf16[512,2048]{1,0:T(8,128)(2,1)} %refs_2_.1, bf16[4,64,512]{2,1,0:T(8,128)(2,1)} %bitcast.32), custom_call_target="tpu_custom_call" | custom-call | tf_op jit(solution)/shard_map/begin/pallas_call | solution.py:842
  107.9 3.7 fusion
  113.6 32.0 %project.1 = (bf16[2048,256]{1,0:T(8,128)(2,1)S(1)}, f32[2048,384]{1,0:T(8,128)}, bf16[2048,2048]{1,0:T(8,128)(2,1)}, f32[1,2048]{1,0:T(1,128)S(1)}, f32[1,2048]...) custom-call(bf16[2048,2048]{1,0:T(8,128)(2,1)} %get-tuple-element.80.x_ref, ...), custom_call_target="tpu_custom_call" | custom-call | flops 6442450944 | bytes 30000000 | tf_op jit(solution)/shard_map/project/pallas_call | solution.py:372
  149.3 3.1 fusion.1
  152.6 1.8 collective-permute-start
  157.1 16.2 %attend.1 = (bf16[2048,256]{1,0:T(8,128)(2,1)S(1)}, f32[4,1,2048]{2,1,0:T(1,128)S(1)}) custom-call(s32[5]{0:T(128)S(1)} %pad_add_fusion.first_ref, bf16[2048,256]{1,0:T(8,128)(2,1)S(1)} %copy-done.13, s32[1,2048]{1,0:T(1,128)S(1)} %bitcast.25, bf16[4096,128]{1,0:T(8,128)(2,1)S(1)} %copy-done.16), custom_call_target="tpu_custom_call" | custom-call | flops 20000000000 | bytes 8000000 | tf_op jit(solution)/shard_map/attend/pallas_call | solution.py:156
  174.5 63.0 %join.1 = (f32[2048,2048]{1,0:T(8,128)}, bf16[2048,2048]{1,0:T(8,128)(2,1)}, bf16[512,1024]{1,0:T(8,128)(2,1)}, bf16[256,2048]{1,0:T(8,128)(2,1)}, bf16[256,2048]{1,0:T(8,128)(2,1)}) custom-call(bf16[2048,2048]{1,0:T(8,128)(2,1)} %get-tuple-element.80.x_ref, bf16[256,2048]{1,0:T(8,128)(2,1)} %all-gather.4.cloned.1.call-done.side_ref.weight_ref, ...), custom_call_target="tpu_custom_call" | custom-call | flops 17179869184 | bytes 50000000 | tf_op jit(solution)/shard_map/join/pallas_call | solution.py:615
  237.5 76.6 %hidden_pass.1 = (bf16[2048,1280]{1,0:T(8,128)(2,1)}, bf16[2048,1280]{1,0:T(8,128)(2,1)}, bf16[2048,1280]{1,0:T(8,128)(2,1)}, bf16[2048,2560]{1,0:T(8,128)(2,1)}...) custom-call(bf16[2048,2048]{1,0:T(8,128)(2,1)} %get-tuple-element.91.normed_ref.turned_ref, ...), custom_call_target="tpu_custom_call" | custom-call | flops 53687091200 | bytes 70000000 | tf_op jit(solution)/shard_map/hidden_pass/pallas_call | solution.py:1048
  314.3 85.6 %feed_tail.1 = (bf16[1280,2048]{1,0:T(8,128)(2,1)}, bf16[256,2048]{1,0:T(8,128)(2,1)}, bf16[256,2048]{1,0:T(8,128)(2,1)}, bf16[256,2048]{1,0:T(8,128)(2,1)}, bf1...) custom-call(bf16[2048,1280]{1,0:T(8,128)(2,1)} %get-tuple-element.97.gate_ref, ...), custom_call_target="tpu_custom_call" | custom-call | flops 42949672960 | bytes 70000000 | tf_op jit(solution)/shard_map/feed_tail/pallas_call | solution.py:1249
  402.0 36.3 %residual_back.1 = (f32[512,2048]{1,0:T(8,128)}, f32[1,2048]{1,0:T(1,128)}, bf16[4,512,256]{2,1,0:T(8,128)(2,1)}, bf16[4,32,2048]{2,1,0:T(8,128)(2,1)}, bf16[4,3...) custom-call(f32[512,2048]{1,0:T(8,128)} %get-tuple-element.103.grad_sum_ref, ...), custom_call_target="tpu_custom_call" | custom-call | flops 4294967296 | bytes 30000000 | tf_op jit(solution)/shard_map/residual_back/pallas_call | solution.py:1404
  438.4 1.4 collective-permute-start.6
  440.2 1.7 collective-permute-start.8
  442.0 3.7 add_convert_fusion
  447.1 34.8 %attend_back.1 = (bf16[2048,256]{1,0:T(8,128)(2,1)S(1)}, f32[4096,128]{1,0:T(8,128)}, bf16[2048,128]{1,0:T(8,128)(2,1)S(1)}) custom-call(s32[5]{0:T(128)S(1)} %pad_add_fusion.first_ref, bf16[2048,256]{1,0:T(8,128)(2,1)S(1)} %copy-done.14, s32[1,2048]{1,0:T(1,128)S(1)} %bitcast.26, bf16[4096,128]{1,0:T(8,128)(2,1)S(1)} %copy-done.17, ...), custom_call_target="tpu_custom_call" | custom-call | flops 40000000000 | bytes 12000000 | tf_op jit(solution)/shard_map/attend_back/pallas_call | solution.py:186
  481.9 2.4 collective-permute-done.5.refs_11_
  486.1 1.6 collective-permute-start.10
  487.8 11.3 %project_back.1 = (bf16[2048,384]{1,0:T(8,128)(2,1)S(1)}, f32[1,320]{1,0:T(1,128)S(1)}) custom-call(bf16[2048,256]{1,0:T(8,128)(2,1)S(1)} %get-tuple-element.110.query_grad_ref, f32[4096,128]{1,0:T(8,128)} %get-tuple-element.119.pair_grad_ref, f32[2048,384]{1,0:T(8,128)} %get-tuple-element.120.raw_ref, f32[1,320]{1,0:T(1,128)S(1)} %copy-done.9, ...), custom_call_target="tpu_custom_call" | custom-call | flops 8000000000 | bytes 8000000 | tf_op jit(solution)/shard_map/project_back/pallas_call | solution.py:493
  500.9 21.1 %qkv_terms.1 = (bf16[2048,384]{1,0:T(8,128)(2,1)S(1)}, bf16[3,512,384]{2,1,0:T(8,128)(2,1)S(1)}, f32[32,2048]{1,0:T(8,128)S(1)}) custom-call(bf16[2048,2048]{1,0:T(8,128)(2,1)} %get-tuple-element.82.normed_ref, bf16[2048,384]{1,0:T(8,128)(2,1)} %copy-done, bf16[128,2048]{1,0:T(8,128)(2,1)S(1)} %bitcast.27, ...), custom_call_target="tpu_custom_call" | custom-call | flops 6442450944 | bytes 20000000 | tf_op jit(solution)/shard_map/qkv_terms/pallas_call | solution.py:1550
  525.1 37.8 %finish.1 = (f32[512,2048]{1,0:T(8,128)}, f32[64,1536]{1,0:T(8,128)}, f32[8,128]{1,0:T(8,128)}, f32[64,10240]{1,0:T(8,128)}, bf16[512,2048]{1,0:T(8,128)(2,1)}) custom-call(bf16[3,512,384]{2,1,0:T(8,128)(2,1)} %copy-done.3, bf16[16,2,64,384]{3,2,1,0:T(8,128)(2,1)} %bitcast.24, f32[1,2048]{1,0:T(1,128)} %copy-done.5, f32[1,2048]{1,0:T(1,128)} %get-tuple-element.130.ffn_ref, ...), custom_call_target="tpu_custom_call" | custom-call | tf_op jit(solution)/shard_map/finish/pallas_call | solution.py:1848
  564.3 2.3 convert_element_type.42
  566.5 3.3 copy.36
  569.9 2.1 copy.37
  573.4 1.5 copy.40
  (119 shorter events, 26.7 us)
Async XLA Ops:
  7.2 22.3 %copy-start.30 = (bf16[64]{0:T(256)(128)(2,1)S(1)}, bf16[64]{0:T(256)(128)(2,1)}, u32[]{:S(2)}) copy-start(bf16[64]{0:T(256)(128)(2,1)} %param.15) | copy-start | bytes 388
  7.2 105.1 %all-gather.4.cloned.1.call-start = ((), (), s32[]{:S(2)}) async-start(), calls=%async_computation.2 | async-start | bytes 1179648 | tf_op jit(solution)/shard_map/all_gather | solution.py:1957
  7.9 166.5 %all-gather.6.cloned.1.call-start = ((), (), s32[]{:S(2)}) async-start(), calls=%async_computation.3 | async-start | bytes 11796480 | tf_op jit(solution)/shard_map/all_gather | solution.py:1959
  9.3 20.6 %slice-start = ((bf16[64,1536]{1,0:T(8,128)(2,1)}), bf16[64,1024]{1,0:T(8,128)(2,1)S(1)}, s32[]{:S(2)}) async-start(bf16[64,1536]{1,0:T(8,128)(2,1)} %param.14), calls=%async_computation.7 | async-start | bytes 262144 | tf_op jit(solution)/shard_map/slice | solution.py:1949
  9.3 20.6 %copy-start.26 = (bf16[64]{0:T(256)(128)(2,1)S(1)}, bf16[64]{0:T(256)(128)(2,1)}, u32[]{:S(2)}) copy-start(bf16[64]{0:T(256)(128)(2,1)} %param.13) | copy-start | bytes 388
  9.3 20.7 %copy-start.27 = (bf16[64]{0:T(256)(128)(2,1)S(1)}, bf16[64]{0:T(256)(128)(2,1)}, u32[]{:S(2)}) copy-start(bf16[64]{0:T(256)(128)(2,1)} %param.18) | copy-start | bytes 388
  29.4 208.1 %all-gather.8.cloned.1.call-start = ((), (), s32[]{:S(2)}) async-start(), calls=%async_computation.4 | async-start | bytes 5898240 | tf_op jit(solution)/shard_map/all_gather | solution.py:1973
  29.6 78.3 %copy-start.28 = (bf16[64]{0:T(256)(128)(2,1)S(1)}, bf16[64]{0:T(256)(128)(2,1)}, u32[]{:S(2)}) copy-start(bf16[64]{0:T(256)(128)(2,1)} %param.16) | copy-start | bytes 388
  29.6 78.3 %copy-start.25 = (s32[2048]{0:T(1024)S(1)}, s32[2048]{0:T(1024)}, u32[]{:S(2)}) copy-start(s32[2048]{0:T(1024)} %param.12) | copy-start | bytes 24580
  148.8 289.6 %reduce-scatter.3.cloned.1.call-start = ((), (), s32[]{:S(2)}) async-start(), calls=%async_computation.5 | async-start | bytes 11796480 | tf_op jit(solution)/shard_map/reduce_scatter | solution.py:1991
  152.4 85.0 %collective-permute-start.1 = (bf16[256,2048]{1,0:T(8,128)(2,1)}, bf16[256,2048]{1,0:T(8,128)(2,1)}, u32[]{:S(2)}, u32[]{:S(2)}) collective-permute-start(bf16[256,2048]{1,0:T(8,128)(2,1)} %get-tuple-element.150), channel_id=1, source_target_pairs={{0,16},{8,24},{16,0},{24,8},{1,17},{9,25},{17,1},{25,9},{2,18},{10... | collective-permute-start | bytes 3145736 | tf_op jit(solution)/shard_map/ppermute | solution.py:1905
  152.6 84.9 %collective-permute-start = (bf16[256,2048]{1,0:T(8,128)(2,1)}, bf16[256,2048]{1,0:T(8,128)(2,1)}, u32[]{:S(2)}, u32[]{:S(2)}) collective-permute-start(bf16[256,2048]{1,0:T(8,128)(2,1)} %get-tuple-element.151), channel_id=1, source_target_pairs={{0,8},{8,0},{16,24},{24,16},{1,9},{9,1},{17,25},{25,17},{2,10},{10... | collective-permute-start | bytes 3145736 | tf_op jit(solution)/shard_map/ppermute | solution.py:1905
  314.1 250.1 %reduce-scatter.5.cloned.1.call-start = ((), (), s32[]{:S(2)}) async-start(), calls=%async_computation.6 | async-start | bytes 5898240 | tf_op jit(solution)/shard_map/reduce_scatter | solution.py:2005
  400.0 38.4 %collective-permute-start.2 = (bf16[256,2048]{1,0:T(8,128)(2,1)}, bf16[256,2048]{1,0:T(8,128)(2,1)}, u32[]{:S(2)}, u32[]{:S(2)}) collective-permute-start(bf16[256,2048]{1,0:T(8,128)(2,1)} %get-tuple-element.107), channel_id=1, source_target_pairs={{0,8},{8,0},{16,24},{24,16},{1,9},{9,1},{17,25},{25,17},{2,10},{10... | collective-permute-start | bytes 3145736 | tf_op jit(solution)/shard_map/ppermute | solution.py:1905
  401.2 37.2 %collective-permute-start.3 = (bf16[256,2048]{1,0:T(8,128)(2,1)}, bf16[256,2048]{1,0:T(8,128)(2,1)}, u32[]{:S(2)}, u32[]{:S(2)}) collective-permute-start(bf16[256,2048]{1,0:T(8,128)(2,1)} %get-tuple-element.108), channel_id=1, source_target_pairs={{0,16},{8,24},{16,0},{24,8},{1,17},{9,25},{17,1},{25,9},{2,18},{10... | collective-permute-start | bytes 3145736 | tf_op jit(solution)/shard_map/ppermute | solution.py:1905
  438.4 43.5 %collective-permute-start.6 = (bf16[128,2048]{1,0:T(8,128)(2,1)}, bf16[128,2048]{1,0:T(8,128)(2,1)S(1)}, u32[]{:S(2)}, u32[]{:S(2)}) collective-permute-start(bf16[128,2048]{1,0:T(8,128)(2,1)} %bitcast.41), channel_id=1, source_target_pairs={{0,8},{8,0},{16,24},{24,16},{1,9},{9,1},{17,25},{25,17},{2,10},{10... | collective-permute-start | bytes 1572872 | tf_op jit(solution)/shard_map/ppermute | solution.py:1905
  439.9 42.0 %collective-permute-start.7 = (bf16[128,2048]{1,0:T(8,128)(2,1)}, bf16[128,2048]{1,0:T(8,128)(2,1)S(1)}, u32[]{:S(2)}, u32[]{:S(2)}) collective-permute-start(bf16[128,2048]{1,0:T(8,128)(2,1)} %bitcast.40), channel_id=1, source_target_pairs={{0,16},{8,24},{16,0},{24,8},{1,17},{9,25},{17,1},{25,9},{2,18},{10... | collective-permute-start | bytes 1572872 | tf_op jit(solution)/shard_map/ppermute | solution.py:1905
  440.2 41.7 %collective-permute-start.8 = (bf16[128,2048]{1,0:T(8,128)(2,1)}, bf16[128,2048]{1,0:T(8,128)(2,1)S(1)}, u32[]{:S(2)}, u32[]{:S(2)}) collective-permute-start(bf16[128,2048]{1,0:T(8,128)(2,1)} %bitcast.39), channel_id=1, source_target_pairs={{0,24},{8,16},{16,8},{24,0},{1,25},{9,17},{17,9},{25,1},{2,26},{10... | collective-permute-start | bytes 1572872 | tf_op jit(solution)/shard_map/ppermute | solution.py:1905
  445.7 38.6 %collective-permute-start.5 = (bf16[256,2048]{1,0:T(8,128)(2,1)S(1)}, bf16[256,2048]{1,0:T(8,128)(2,1)S(1)}, u32[]{:S(2)}, u32[]{:S(2)}) collective-permute-start(bf16[256,2048]{1,0:T(8,128)(2,1)S(1)} %get-tuple-element.148), channel_id=1, source_target_pairs={{0,8},{8,0},{16,24},{24,16},{1,9},{9,1},{17,25},{25,17},{2,10},{10... | collective-permute-start | bytes 3145736 | tf_op jit(solution)/shard_map/ppermute | solution.py:1905
  447.0 38.8 %collective-permute-start.4 = (bf16[256,2048]{1,0:T(8,128)(2,1)S(1)}, bf16[256,2048]{1,0:T(8,128)(2,1)S(1)}, u32[]{:S(2)}, u32[]{:S(2)}) collective-permute-start(bf16[256,2048]{1,0:T(8,128)(2,1)S(1)} %get-tuple-element.149), channel_id=1, source_target_pairs={{0,16},{8,24},{16,0},{24,8},{1,17},{9,25},{17,1},{25,9},{2,18},{10... | collective-permute-start | bytes 3145736 | tf_op jit(solution)/shard_map/ppermute | solution.py:1905
  447.1 39.1 %copy-start.29 = (bf16[256,2048]{1,0:T(8,128)(2,1)S(1)}, bf16[256,2048]{1,0:T(8,128)(2,1)}, u32[]{:S(2)}) copy-start(bf16[256,2048]{1,0:T(8,128)(2,1)} %get-tuple-element.138) | copy-start | bytes 3145732
  447.1 40.7 %copy-start.9 = (f32[1,320]{1,0:T(1,128)S(1)}, f32[1,320]{1,0:T(1,128)}, u32[]{:S(2)}) copy-start(f32[1,320]{1,0:T(1,128)} %copy-done.8) | copy-start | bytes 3844
  485.8 38.3 %collective-permute-start.9 = (bf16[256,2048]{1,0:T(8,128)(2,1)}, bf16[256,2048]{1,0:T(8,128)(2,1)S(1)}, u32[]{:S(2)}, u32[]{:S(2)}) collective-permute-start(bf16[256,2048]{1,0:T(8,128)(2,1)} %get-tuple-element.136), channel_id=1, source_target_pairs={{0,8},{8,0},{16,24},{24,16},{1,9},{9,1},{17,25},{25,17},{2,10},{10... | collective-permute-start | bytes 3145736 | tf_op jit(solution)/shard_map/ppermute | solution.py:1905
  486.1 37.9 %collective-permute-start.10 = (bf16[256,2048]{1,0:T(8,128)(2,1)S(1)}, bf16[256,2048]{1,0:T(8,128)(2,1)}, u32[]{:S(2)}, u32[]{:S(2)}) collective-permute-start(bf16[256,2048]{1,0:T(8,128)(2,1)S(1)} %copy-done.29), channel_id=1, source_target_pairs={{0,16},{8,24},{16,0},{24,8},{1,17},{9,25},{17,1},{25,9},{2,18},{10... | collective-permute-start | bytes 3145736 | tf_op jit(solution)/shard_map/ppermute | solution.py:1905
  (24 other events, 103.3 us)
Sparse Core Ops, SparseCore 0:
  9.6 24.9 all-gather.3
  36.2 112.4 all-gather.5
  150.3 59.6 all-gather.7
  314.2 109.2 reduce-scatter.2
  438.6 61.6 reduce-scatter.4

commit v7 on v6

--- a/solution.py
+++ b/solution.py
@@ -16,13 +16,6 @@
 NEG = -1e30
 MESH = pl.DeviceIdType.MESH
 ROWS_IN_BOTH = (((1,), (1,)), ((), ()))
-
-
-def rotation(positions, head_dim):
-    half_width = head_dim // 2
-    frequency = ROPE_BASE ** (-2.0 * jnp.arange(half_width, dtype=jnp.float32) / head_dim)
-    angles = positions.astype(jnp.float32)[:, None] * frequency[None, :]
-    return (jnp.cos(angles)[:, None, :], jnp.sin(angles)[:, None, :])
 
 
 def stack_heads(tile, heads, first):
@@ -170,7 +163,7 @@
             jax.ShapeDtypeStruct((count, width), jnp.bfloat16),
             jax.ShapeDtypeStruct((count // query_rows, 1, columns), jnp.float32),
         ],
-        compiler_params=pltpu.CompilerParams(vmem_limit_bytes=48 << 20),
+        compiler_params=pltpu.CompilerParams(vmem_limit_bytes=60 << 20),
         cost_estimate=pl.CostEstimate(
             flops=20_000_000_000, bytes_accessed=8_000_000, transcendentals=0
         ),
@@ -201,7 +194,7 @@
             jax.ShapeDtypeStruct(pair.shape, jnp.float32),
             jax.ShapeDtypeStruct(behind, jnp.bfloat16),
         ],
-        compiler_params=pltpu.CompilerParams(vmem_limit_bytes=48 << 20),
+        compiler_params=pltpu.CompilerParams(vmem_limit_bytes=60 << 20),
         cost_estimate=pl.CostEstimate(
             flops=40_000_000_000, bytes_accessed=12_000_000, transcendentals=0
         ),
@@ -402,7 +395,7 @@
         + [pltpu.SemaphoreType.DMA((SPREAD_COUNT,))] * 2
         + [pltpu.SemaphoreType.DMA((size,))] * 3,
         compiler_params=pltpu.CompilerParams(
-            collective_id=5, has_side_effects=True, vmem_limit_bytes=48 << 20
+            collective_id=5, has_side_effects=True, vmem_limit_bytes=60 << 20
         ),
         cost_estimate=pl.CostEstimate(
             flops=4 * count * width * out_width, bytes_accessed=30_000_000, transcendentals=0
@@ -516,7 +509,7 @@
             jax.ShapeDtypeStruct(head_gain.shape, jnp.float32),
         ],
         compiler_params=pltpu.CompilerParams(
-            collective_id=9, has_side_effects=True, vmem_limit_bytes=48 << 20
+            collective_id=9, has_side_effects=True, vmem_limit_bytes=60 << 20
         ),
         cost_estimate=pl.CostEstimate(
             flops=8_000_000_000, bytes_accessed=8_000_000, transcendentals=0
@@ -644,7 +637,7 @@
             sems((6,)),
         ],
         compiler_params=pltpu.CompilerParams(
-            collective_id=6, has_side_effects=True, vmem_limit_bytes=56 << 20
+            collective_id=6, has_side_effects=True, vmem_limit_bytes=60 << 20
         ),
         cost_estimate=pl.CostEstimate(
             flops=16 * count * width * columns, bytes_accessed=50_000_000, transcendentals=0
@@ -696,15 +689,16 @@
         out_specs=vmem,
         scratch_shapes=[pltpu.SemaphoreType.DMA((2 * size - 2,))] * 2,
         compiler_params=pltpu.CompilerParams(
-            collective_id=8, has_side_effects=True, vmem_limit_bytes=16 << 20
+            collective_id=8, has_side_effects=True, vmem_limit_bytes=60 << 20
         ),
         name="trade",
     )(weight)
 
 
 def begin_kernel(
-    x_ref, qkv_ref, x_out, qkv_out, local_sem, x_send, x_recv, q_send, q_recv, b_send, b_recv,
-    c_send, c_recv
+    x_ref, qkv_ref, cot_ref, position_ref, frequency_ref, x_out, qkv_out, cot_top, cot_bottom,
+    cosine_ref, sine_ref, held_ref, local_sem, x_send, x_recv, q_send, q_recv, b_send, b_recv, c_send,
+    c_recv
 ):
     head, blk = lax.axis_index("heads"), lax.axis_index("blk")
     size, blk_size = lax.axis_size("heads"), lax.axis_size("blk")
@@ -768,7 +762,13 @@
     ]
     own = [
         pltpu.make_async_copy(qkv_ref.at[head], qkv_out.at[head, rows], local_sem.at[0]),
-        pltpu.make_async_copy(x_ref, x_out.at[pl.ds(0, count)], local_sem.at[1]),
+        pltpu.make_async_copy(x_ref, held_ref.at[0], local_sem.at[1]),
+        pltpu.make_async_copy(cot_ref, held_ref.at[1], local_sem.at[2]),
+    ]
+    laid = [
+        pltpu.make_async_copy(held_ref.at[0], x_out.at[pl.ds(0, count)], local_sem.at[3]),
+        pltpu.make_async_copy(held_ref.at[1, pl.ds(0, half)], cot_top, local_sem.at[4]),
+        pltpu.make_async_copy(held_ref.at[1, pl.ds(half, half)], cot_bottom, local_sem.at[5]),
     ]
     for copy in qkv_copies + near + own:
         copy.start()
@@ -820,6 +820,22 @@
         copy.wait_recv()
     lax.fori_loop(1, pairs, start, 0)
     across(0, 0).start()
+    for copy in own[1:]:
+        copy.wait()
+    for copy in laid:
+        copy.start()
+
+    lanes = 512
+
+    def table(index, carried):
+        here = pl.ds(pl.multiple_of(index * lanes, lanes), lanes)
+        angle = frequency_ref[...] * position_ref[:, here].astype(jnp.float32)
+        cosine, sine = jnp.cos(angle).T, jnp.sin(angle).T
+        cosine_ref[here] = jnp.concatenate([cosine, cosine], axis=1)
+        sine_ref[here] = jnp.concatenate([-sine, sine], axis=1)
+        return carried
+
+    lax.fori_loop(0, position_ref.shape[1] // lanes, table, 0)
     lax.fori_loop(1, pairs, pass_on, 0)
     for first, second in zip(near, far):
         first.wait_recv()
@@ -828,27 +844,35 @@
         copy.wait_send()
     for copy in far:
         copy.wait()
-    own[1].wait()
+    for copy in laid:
+        copy.wait()
     lax.fori_loop(1, pairs, sent, 0)
     lax.fori_loop(0, pairs, finish, 0)
 
 
-def begin(x, qkv_parts):
+def begin(x, qkv_parts, cot, positions, frequency):
     size, blk_size = lax.axis_size("heads"), lax.axis_size("blk")
     count, width = x.shape
     depth, joined = qkv_parts.shape[1:]
     anywhere = pl.BlockSpec(memory_space=pl.ANY)
+    vmem = pl.BlockSpec(memory_space=pltpu.VMEM)
+    table = jax.ShapeDtypeStruct((positions.shape[1], 2 * frequency.shape[0]), jnp.float32)
     sems = pltpu.SemaphoreType.DMA
     return pl.pallas_call(
         begin_kernel,
         out_shape=[
             jax.ShapeDtypeStruct((size * count, width), x.dtype),
             jax.ShapeDtypeStruct((size, blk_size * depth, joined), x.dtype),
-        ],
-        in_specs=[anywhere] * 2,
-        out_specs=[anywhere] * 2,
+            jax.ShapeDtypeStruct((count // 2, width), x.dtype),
+            jax.ShapeDtypeStruct((count // 2, width), x.dtype),
+            table,
+            table,
+        ],
+        in_specs=[anywhere] * 3 + [vmem] * 2,
+        out_specs=[anywhere] * 4 + [vmem] * 2,
         scratch_shapes=[
-            sems((2,)),
+            pltpu.VMEM((2, count, width), x.dtype),
+            sems((6,)),
             sems((4,)),
             sems((4,)),
             sems((size - 1,)),
@@ -858,9 +882,11 @@
             sems((blk_size // 2,)),
             sems((blk_size // 2,)),
         ],
-        compiler_params=pltpu.CompilerParams(collective_id=1, has_side_effects=True),
+        compiler_params=pltpu.CompilerParams(
+            collective_id=1, has_side_effects=True, vmem_limit_bytes=60 << 20
+        ),
         name="begin",
-    )(x, qkv_parts)
+    )(x, qkv_parts, cot, positions, frequency)
 
 
 def spread_copies(source_ref, target_ref, send_sem, recv_sem):
@@ -1078,7 +1104,7 @@
             sems((SPREAD_COUNT,)),
         ],
         compiler_params=pltpu.CompilerParams(
-            collective_id=2, has_side_effects=True, vmem_limit_bytes=58 << 20
+            collective_id=2, has_side_effects=True, vmem_limit_bytes=60 << 20
         ),
         cost_estimate=pl.CostEstimate(
             flops=10 * count * width * total, bytes_accessed=70_000_000, transcendentals=0
@@ -1435,7 +1461,7 @@
             pltpu.SemaphoreType.DMA((size,)),
         ],
         compiler_params=pltpu.CompilerParams(
-            collective_id=4, has_side_effects=True, vmem_limit_bytes=56 << 20
+            collective_id=4, has_side_effects=True, vmem_limit_bytes=60 << 20
         ),
         cost_estimate=pl.CostEstimate(
             flops=4 * count * width * columns * size, bytes_accessed=30_000_000, transcendentals=0
@@ -1574,7 +1600,7 @@
             sems((pairs,)),
         ],
         compiler_params=pltpu.CompilerParams(
-            collective_id=7, has_side_effects=True, vmem_limit_bytes=48 << 20
+            collective_id=7, has_side_effects=True, vmem_limit_bytes=60 << 20
         ),
         cost_estimate=pl.CostEstimate(
             flops=4 * count * height * width, bytes_accessed=20_000_000, transcendentals=0
@@ -1958,11 +1984,12 @@
     in_rows = trade(ffn_in_weight)
     in_group = lax.all_gather(in_rows, "blk", axis=1, tiled=True).reshape(width, -1)
 
-    inputs_blk, qkv_rows = begin(after(inputs, in_rows), qkv_parts)
+    half_dim = jnp.arange(head_dim // 2, dtype=jnp.float32)
+    frequency = (ROPE_BASE ** (-2.0 * half_dim / head_dim))[:, None]
+    inputs_blk, qkv_rows, cot_top, cot_bottom, cosine, sine = begin(
+        after(inputs, in_rows), qkv_parts, cotangent, positions[None, :], frequency
+    )
     qkv_rows = qkv_rows.reshape(width, -1)
-    cosine, sine = rotation(positions, head_dim)
-    cosine = jnp.concatenate([cosine[:, 0], cosine[:, 0]], axis=-1)
-    sine = jnp.concatenate([-sine[:, 0], sine[:, 0]], axis=-1)
     head_gain = jnp.concatenate(
         [jnp.tile(q_gain, HEADS // size), jnp.tile(k_gain, KV_HEADS // size)]
     ).astype(jnp.float32)[None, :]
@@ -1978,8 +2005,7 @@
     attended_blk, logs = attend(query_low, pair_all, first, low, group_size, query_rows, key_rows)
 
     mine = jnp.concatenate([pick(attended_blk, k, "heads", 0) for k in range(size)], axis=0)
-    late = after(cotangent, inputs_blk)
-    one_top, two_bottom = permute(late[:half], "heads", 1), permute(late[half:], "heads", 2)
+    one_top, two_bottom = permute(cot_top, "heads", 1), permute(cot_bottom, "heads", 2)
     mine, in_group = lax.optimization_barrier((mine, in_group))
     residual, ffn_normed, attended_own, one_bottom, two_top = join(
         inputs_blk, mine, out_group, out_peers, ffn_scaling, cotangent, 256
@@ -1994,15 +2020,15 @@
     down_sum, one_far, two_far, one_near, two_near, out_rest, grad_sum = feed_tail(
         gate_grad, up_grad, hidden, in_group, down_group, (cotangent, *cot_near, cot_far)
     )
+    down_part = lax.psum_scatter(down_sum, "blk", scatter_dimension=0, tiled=True)
     through_top, through_bottom = permute(one_far, "heads", 1), permute(two_far, "heads", 2)
     residual_grad, ffn_sum, grads, *out_slices = residual_back(
         grad_sum, residual, cotangent, ffn_scaling, attended_own, out_group, out_peers,
         min(128, half)
     )
-    down_sum, in_part, grads, through_top, through_bottom = lax.optimization_barrier(
-        (down_sum, in_part, grads, through_top, through_bottom)
-    )
-    ffn_out_grad = wide(lax.psum_scatter(down_sum, "blk", scatter_dimension=0, tiled=True))
+    in_part, grads, through_top, through_bottom = lax.optimization_barrier(
+        (in_part, grads, through_top, through_bottom)
+    )
     top_send = (wide(out_rest[:half]) + wide(through_top)).astype(jnp.bfloat16)
     bottom_send = (wide(out_rest[half : 2 * half]) + wide(through_bottom)).astype(jnp.bfloat16)
     out_top_last = permute(top_send, "heads", 2)
@@ -2026,6 +2052,8 @@
         qkv_rows, qkv_peers, in_part, residual, out_rest,
         (out_top, out_bottom, out_top_last, out_bottom_last), query_width, head_dim
     )
+    down_part, gains = lax.optimization_barrier((down_part, gains))
+    ffn_out_grad = wide(down_part)
     return (
         layer_out,
         input_grad,

time: 589 us -> 580 us (0.985); the launches traced: 582 us -> 579 us
  Pallas kernels: 512 us -> 527 us
  local copies, waits for them, and re-layouts: 27.5 us -> 14.8 us
    unnamed x67 -> x39, local copies, waits for them, and re-layouts: 21.5 us -> 10.7 us
  transfers between devices with their start and end apart: 16 -> 16, of which waited for: 2 -> 0; matrix products, arithmetic and copies ran while one was open for 3% -> 2% of each run, Pallas kernels for 75% -> 78%
where the time goes in v7:
time: 580 us; the launch traced here: 579 us
  Pallas kernels  527 us (91%)
  local copies, waits for them, and re-layouts  14.8 us (3%)
  between operations  14.2 us (2%)
  starting transfers between devices  13.6 us (2%)
  other arithmetic  8.42 us (1%)
    pallas_call x1, Pallas kernels, feed_tail(): pl.pallas_call(tail_kernel, grid=(16 + total // units,), in_specs=[pl.Blo...  84.6 us
    pallas_call x1, Pallas kernels, begin(): pl.pallas_call(begin_kernel, out_shape=[jax.ShapeDtypeStruct((size * coun...  78.9 us
    pallas_call x1, Pallas kernels, hidden_pass(): pl.pallas_call(functools.partial(hidden_kernel, tiles), grid=(2 * tiles +...  74.5 us
    pallas_call x1, Pallas kernels, join(): pl.pallas_call(join_kernel, grid=(count // rows,), in_specs=[pl.BlockSpec...  63.2 us
    pallas_call x1, Pallas kernels, finish(): pl.pallas_call(functools.partial(finish_kernel, query_width, dim), out_sh...  41.5 us
    pallas_call x1, Pallas kernels, attend_back(): pl.pallas_call(functools.partial(attend_back_kernel, heads, key_rows, (wi...  37.2 us
    pallas_call x1, Pallas kernels, residual_back(): pl.pallas_call(residual_back_kernel, grid=(tiles + 1,), in_specs=[tile, t...  35.5 us
    pallas_call x1, Pallas kernels, project(): pl.pallas_call(functools.partial(project_kernel, dim, size), grid=(count...  31.9 us
  transfers between devices with their start and end apart: 16, of which 0 were waited for; matrix products, arithmetic and copies ran while one was open for 2% of the time, Pallas kernels for 78%

profile of v7, /device:TPU:0, one launch (start us, length us, event | category | flops | bytes accessed | tf_op | source)
XLA Modules:
  0.0 578.7 jit_solution(868570336971936429)
XLA Ops:
  8.0 21.5 %trade.1 = bf16[4,64,2560]{2,1,0:T(8,128)(2,1)} custom-call(bf16[64,10240]{1,0:T(8,128)(2,1)} %in_ref.1), custom_call_target="tpu_custom_call" | custom-call | tf_op jit(solution)/shard_map/trade/pallas_call | solution.py:685
  31.7 78.9 %begin.1 = (bf16[2048,2048]{1,0:T(8,128)(2,1)}, bf16[4,512,512]{2,1,0:T(8,128)(2,1)}, bf16[256,2048]{1,0:T(8,128)(2,1)}, bf16[256,2048]{1,0:T(8,128)(2,1)}, f32[2048,64]{1,0:T(8,128)}, /*index=5*/f32[2048,64]{1,0:T(8,128)}) custom-call(bf16[512,2048]{1,0:T(8,128)(2,1)} %refs_2_.1, bf16[4,64,512]{2,1,0:T(8,128)(2,1)} %bitcast.30, bf16[512,2048]{1,0:T(8,128)(2,1)} %cot_ref.9, ...), custom_call_target="tpu_custom_call" | custom-call | tf_op jit(solution)/shard_map/begin/pallas_call | solution.py:861
  111.1 31.9 %project.1 = (bf16[2048,256]{1,0:T(8,128)(2,1)}, f32[2048,384]{1,0:T(8,128)}, bf16[2048,2048]{1,0:T(8,128)(2,1)}, f32[1,2048]{1,0:T(1,128)}, f32[1,2048]{1,0:T(1...) custom-call(bf16[2048,2048]{1,0:T(8,128)(2,1)} %get-tuple-element.84.x_ref, bf16[2048,512]{1,0:T(8,128)(2,1)} %bitcast.26, ...), custom_call_target="tpu_custom_call" | custom-call | flops 6442450944 | bytes 30000000 | tf_op jit(solution)/shard_map/project/pallas_call | solution.py:365
  143.1 2.2 collective-permute-start
  146.2 18.3 %attend.1 = (bf16[2048,256]{1,0:T(8,128)(2,1)}, f32[4,1,2048]{2,1,0:T(1,128)}) custom-call(s32[5]{0:T(128)} %pad_add_fusion.first_ref, bf16[2048,256]{1,0:T(8,128)(2,1)} %get-tuple-element.89.query_ref, s32[1,2048]{1,0:T(1,128)} %bitcast.34, bf16[4096,128]{1,0:T(8,128)(2,1)} %get-tuple-element.91.pair_ref), custom_call_target="tpu_custom_call" | custom-call | flops 20000000000 | bytes 8000000 | tf_op jit(solution)/shard_map/attend/pallas_call | solution.py:149
  166.8 63.2 %join.1 = (f32[2048,2048]{1,0:T(8,128)}, bf16[2048,2048]{1,0:T(8,128)(2,1)}, bf16[512,1024]{1,0:T(8,128)(2,1)}, bf16[256,2048]{1,0:T(8,128)(2,1)}, bf16[256,2048]{1,0:T(8,128)(2,1)}) custom-call(bf16[2048,2048]{1,0:T(8,128)(2,1)} %get-tuple-element.84.x_ref, bf16[256,2048]{1,0:T(8,128)(2,1)} %all-gather.4.cloned.1.call-done.side_ref.weight_ref, ...), custom_call_target="tpu_custom_call" | custom-call | flops 17179869184 | bytes 50000000 | tf_op jit(solution)/shard_map/join/pallas_call | solution.py:608
  231.3 74.5 %hidden_pass.1 = (bf16[2048,1280]{1,0:T(8,128)(2,1)}, bf16[2048,1280]{1,0:T(8,128)(2,1)}, bf16[2048,1280]{1,0:T(8,128)(2,1)}, bf16[2048,2560]{1,0:T(8,128)(2,1)}...) custom-call(bf16[2048,2048]{1,0:T(8,128)(2,1)} %get-tuple-element.97.normed_ref.turned_ref, ...), custom_call_target="tpu_custom_call" | custom-call | flops 53687091200 | bytes 70000000 | tf_op jit(solution)/shard_map/hidden_pass/pallas_call | solution.py:1074
  306.1 84.6 %feed_tail.1 = (bf16[1280,2048]{1,0:T(8,128)(2,1)}, bf16[256,2048]{1,0:T(8,128)(2,1)}, bf16[256,2048]{1,0:T(8,128)(2,1)}, bf16[256,2048]{1,0:T(8,128)(2,1)}, bf1...) custom-call(bf16[2048,1280]{1,0:T(8,128)(2,1)} %get-tuple-element.105.gate_ref, ...), custom_call_target="tpu_custom_call" | custom-call | flops 42949672960 | bytes 70000000 | tf_op jit(solution)/shard_map/feed_tail/pallas_call | solution.py:1275
  390.6 2.1 collective-permute-start.2
  393.8 35.5 %residual_back.1 = (f32[512,2048]{1,0:T(8,128)}, f32[1,2048]{1,0:T(1,128)}, bf16[4,512,256]{2,1,0:T(8,128)(2,1)}, bf16[4,32,2048]{2,1,0:T(8,128)(2,1)}, bf16[4,3...) custom-call(f32[512,2048]{1,0:T(8,128)} %get-tuple-element.109.grad_sum_ref, ...), custom_call_target="tpu_custom_call" | custom-call | flops 4294967296 | bytes 30000000 | tf_op jit(solution)/shard_map/residual_back/pallas_call | solution.py:1430
  429.4 1.5 collective-permute-start.6
  431.4 1.5 collective-permute-start.8
  432.9 3.3 add_convert_fusion
  436.2 1.4 collective-permute-start.4
  438.2 37.2 %attend_back.1 = (bf16[2048,256]{1,0:T(8,128)(2,1)}, f32[4096,128]{1,0:T(8,128)}, bf16[2048,128]{1,0:T(8,128)(2,1)}) custom-call(s32[5]{0:T(128)} %pad_add_fusion.first_ref, bf16[2048,256]{1,0:T(8,128)(2,1)} %get-tuple-element.89.query_ref, s32[1,2048]{1,0:T(1,128)} %bitcast.35, bf16[4096,128]{1,0:T(8,128)(2,1)} %get-tuple-element.91.pair_ref, ...), custom_call_target="tpu_custom_call" | custom-call | flops 40000000000 | bytes 12000000 | tf_op jit(solution)/shard_map/attend_back/pallas_call | solution.py:179
  475.5 1.5 collective-permute-start.9
  477.7 12.8 %project_back.1 = (bf16[2048,384]{1,0:T(8,128)(2,1)}, f32[1,320]{1,0:T(1,128)}) custom-call(bf16[2048,256]{1,0:T(8,128)(2,1)} %get-tuple-element.116.query_grad_ref, f32[4096,128]{1,0:T(8,128)} %get-tuple-element.125.pair_grad_ref, f32[2048,384]{1,0:T(8,128)} %get-tuple-element.126.raw_ref, f32[1,320]{1,0:T(1,128)} %maximum_convert_fusion.head_gain_ref, ...), custom_call_target="tpu_custom_call" | custom-call | flops 8000000000 | bytes 8000000 | tf_op jit(solution)/shard_map/project_back/pallas_call | solution.py:486
  490.5 26.9 %qkv_terms.1 = (bf16[2048,384]{1,0:T(8,128)(2,1)}, bf16[3,512,384]{2,1,0:T(8,128)(2,1)}, f32[32,2048]{1,0:T(8,128)}) custom-call(bf16[2048,2048]{1,0:T(8,128)(2,1)} %get-tuple-element.88.normed_ref, bf16[2048,384]{1,0:T(8,128)(2,1)} %get-tuple-element.128.grad_ref.refs_4_, bf16[128,2048]{1,0:T(8,128)(2,1)} %bitcast.40, ...), custom_call_target="tpu_custom_call" | custom-call | flops 6442450944 | bytes 20000000 | tf_op jit(solution)/shard_map/qkv_terms/pallas_call | solution.py:1576
  518.4 41.5 %finish.1 = (f32[512,2048]{1,0:T(8,128)}, f32[64,1536]{1,0:T(8,128)}, f32[8,128]{1,0:T(8,128)}, f32[64,10240]{1,0:T(8,128)}, bf16[512,2048]{1,0:T(8,128)(2,1)}) custom-call(bf16[3,512,384]{2,1,0:T(8,128)(2,1)} %get-tuple-element.133.got_ref, bf16[16,2,64,384]{3,2,1,0:T(8,128)(2,1)} %bitcast.29, f32[1,2048]{1,0:T(1,128)} %get-tuple-element.135.gain_ref, ...), custom_call_target="tpu_custom_call" | custom-call | tf_op jit(solution)/shard_map/finish/pallas_call | solution.py:1874
  560.0 1.4 slice_bitcast_fusion
  561.4 2.3 convert_element_type.38
  563.7 3.3 copy.32
  567.0 2.1 copy.33
  570.6 1.5 copy.36
  (88 shorter events, 13.4 us)
Async XLA Ops:
  7.2 104.0 %all-gather.4.cloned.1.call-start = ((), (), s32[]{:S(2)}) async-start(), calls=%async_computation.2 | async-start | bytes 1179648 | tf_op jit(solution)/shard_map/all_gather | solution.py:1983
  7.9 21.7 %slice-start = ((bf16[64,1536]{1,0:T(8,128)(2,1)}), bf16[64,1024]{1,0:T(8,128)(2,1)S(1)}, s32[]{:S(2)}) async-start(bf16[64,1536]{1,0:T(8,128)(2,1)} %param.14), calls=%async_computation.7 | async-start | bytes 262144 | tf_op jit(solution)/shard_map/slice | solution.py:1975
  7.9 21.7 %copy-start.5 = (bf16[64,1536]{1,0:T(8,128)(2,1)S(1)}, bf16[64,1536]{1,0:T(8,128)(2,1)}, u32[]{:S(2)}) copy-start(bf16[64,1536]{1,0:T(8,128)(2,1)} %param.14) | copy-start | bytes 589828
  7.9 22.0 %copy-start.16 = (bf16[64]{0:T(256)(128)(2,1)S(1)}, bf16[64]{0:T(256)(128)(2,1)}, u32[]{:S(2)}) copy-start(bf16[64]{0:T(256)(128)(2,1)} %param.15) | copy-start | bytes 388
  7.9 22.1 %copy-start.10 = (bf16[64]{0:T(256)(128)(2,1)S(1)}, bf16[64]{0:T(256)(128)(2,1)}, u32[]{:S(2)}) copy-start(bf16[64]{0:T(256)(128)(2,1)} %param.13) | copy-start | bytes 388
  8.0 22.2 %copy-start.11 = (bf16[64]{0:T(256)(128)(2,1)S(1)}, bf16[64]{0:T(256)(128)(2,1)}, u32[]{:S(2)}) copy-start(bf16[64]{0:T(256)(128)(2,1)} %param.18) | copy-start | bytes 388
  8.0 158.8 %all-gather.6.cloned.1.call-start = ((), (), s32[]{:S(2)}) async-start(), calls=%async_computation.3 | async-start | bytes 11796480 | tf_op jit(solution)/shard_map/all_gather | solution.py:1985
  29.6 200.5 %all-gather.8.cloned.1.call-start = ((), (), s32[]{:S(2)}) async-start(), calls=%async_computation.4 | async-start | bytes 5898240 | tf_op jit(solution)/shard_map/all_gather | solution.py:2000
  31.7 78.9 %copy-start.12 = (bf16[64]{0:T(256)(128)(2,1)S(1)}, bf16[64]{0:T(256)(128)(2,1)}, u32[]{:S(2)}) copy-start(bf16[64]{0:T(256)(128)(2,1)} %param.16) | copy-start | bytes 388
  111.1 34.3 %copy-start.8 = (s32[2048]{0:T(1024)S(1)}, s32[2048]{0:T(1024)}, u32[]{:S(2)}) copy-start(s32[2048]{0:T(1024)} %param.12) | copy-start | bytes 24580
  143.1 289.8 %reduce-scatter.3.cloned.1.call-start = ((), (), s32[]{:S(2)}) async-start(), calls=%async_computation.5 | async-start | bytes 11796480 | tf_op jit(solution)/shard_map/reduce_scatter | solution.py:2017
  143.1 86.9 %collective-permute-start = (bf16[256,2048]{1,0:T(8,128)(2,1)}, bf16[256,2048]{1,0:T(8,128)(2,1)S(1)}, u32[]{:S(2)}, u32[]{:S(2)}) collective-permute-start(bf16[256,2048]{1,0:T(8,128)(2,1)} %get-tuple-element.100), channel_id=1, source_target_pairs={{0,8},{8,0},{16,24},{24,16},{1,9},{9,1},{17,25},{25,17},{2,10},{10... | collective-permute-start | bytes 3145736 | tf_op jit(solution)/shard_map/ppermute | solution.py:1931
  145.4 84.6 %collective-permute-start.1 = (bf16[256,2048]{1,0:T(8,128)(2,1)}, bf16[256,2048]{1,0:T(8,128)(2,1)S(1)}, u32[]{:S(2)}, u32[]{:S(2)}) collective-permute-start(bf16[256,2048]{1,0:T(8,128)(2,1)} %get-tuple-element.103), channel_id=1, source_target_pairs={{0,16},{8,24},{16,0},{24,8},{1,17},{9,25},{17,1},{25,9},{2,18},{10... | collective-permute-start | bytes 3145736 | tf_op jit(solution)/shard_map/ppermute | solution.py:1931
  305.8 254.2 %reduce-scatter.5.cloned.1.call-start = ((), (), s32[]{:S(2)}) async-start(), calls=%async_computation.6 | async-start | bytes 5898240 | tf_op jit(solution)/shard_map/reduce_scatter | solution.py:2023
  390.6 42.3 %collective-permute-start.2 = (bf16[256,2048]{1,0:T(8,128)(2,1)}, bf16[256,2048]{1,0:T(8,128)(2,1)S(1)}, u32[]{:S(2)}, u32[]{:S(2)}) collective-permute-start(bf16[256,2048]{1,0:T(8,128)(2,1)} %get-tuple-element.113), channel_id=1, source_target_pairs={{0,8},{8,0},{16,24},{24,16},{1,9},{9,1},{17,25},{25,17},{2,10},{10... | collective-permute-start | bytes 3145736 | tf_op jit(solution)/shard_map/ppermute | solution.py:1931
  392.7 40.2 %collective-permute-start.3 = (bf16[256,2048]{1,0:T(8,128)(2,1)S(1)}, bf16[256,2048]{1,0:T(8,128)(2,1)S(1)}, u32[]{:S(2)}, u32[]{:S(2)}) collective-permute-start(bf16[256,2048]{1,0:T(8,128)(2,1)S(1)} %copy-done.15), channel_id=1, source_target_pairs={{0,16},{8,24},{16,0},{24,8},{1,17},{9,25},{17,1},{25,9},{2,18},{10... | collective-permute-start | bytes 3145736 | tf_op jit(solution)/shard_map/ppermute | solution.py:1931
  429.4 46.1 %collective-permute-start.6 = (bf16[128,2048]{1,0:T(8,128)(2,1)}, bf16[128,2048]{1,0:T(8,128)(2,1)}, u32[]{:S(2)}, u32[]{:S(2)}) collective-permute-start(bf16[128,2048]{1,0:T(8,128)(2,1)} %bitcast.43), channel_id=1, source_target_pairs={{0,8},{8,0},{16,24},{24,16},{1,9},{9,1},{17,25},{25,17},{2,10},{10... | collective-permute-start | bytes 1572872 | tf_op jit(solution)/shard_map/ppermute | solution.py:1931
  430.9 44.6 %collective-permute-start.7 = (bf16[128,2048]{1,0:T(8,128)(2,1)}, bf16[128,2048]{1,0:T(8,128)(2,1)}, u32[]{:S(2)}, u32[]{:S(2)}) collective-permute-start(bf16[128,2048]{1,0:T(8,128)(2,1)} %bitcast.42), channel_id=1, source_target_pairs={{0,16},{8,24},{16,0},{24,8},{1,17},{9,25},{17,1},{25,9},{2,18},{10... | collective-permute-start | bytes 1572872 | tf_op jit(solution)/shard_map/ppermute | solution.py:1931
  431.4 44.1 %collective-permute-start.8 = (bf16[128,2048]{1,0:T(8,128)(2,1)}, bf16[128,2048]{1,0:T(8,128)(2,1)}, u32[]{:S(2)}, u32[]{:S(2)}) collective-permute-start(bf16[128,2048]{1,0:T(8,128)(2,1)} %bitcast.41), channel_id=1, source_target_pairs={{0,24},{8,16},{16,8},{24,0},{1,25},{9,17},{17,9},{25,1},{2,26},{10... | collective-permute-start | bytes 1572872 | tf_op jit(solution)/shard_map/ppermute | solution.py:1931
  436.2 39.3 %collective-permute-start.4 = (bf16[256,2048]{1,0:T(8,128)(2,1)}, bf16[256,2048]{1,0:T(8,128)(2,1)S(1)}, u32[]{:S(2)}, u32[]{:S(2)}) collective-permute-start(bf16[256,2048]{1,0:T(8,128)(2,1)} %get-tuple-element.157), channel_id=1, source_target_pairs={{0,16},{8,24},{16,0},{24,8},{1,17},{9,25},{17,1},{25,9},{2,18},{10... | collective-permute-start | bytes 3145736 | tf_op jit(solution)/shard_map/ppermute | solution.py:1931
  437.6 37.9 %collective-permute-start.5 = (bf16[256,2048]{1,0:T(8,128)(2,1)S(1)}, bf16[256,2048]{1,0:T(8,128)(2,1)S(1)}, u32[]{:S(2)}, u32[]{:S(2)}) collective-permute-start(bf16[256,2048]{1,0:T(8,128)(2,1)S(1)} %get-tuple-element.156), channel_id=1, source_target_pairs={{0,8},{8,0},{16,24},{24,16},{1,9},{9,1},{17,25},{25,17},{2,10},{10... | collective-permute-start | bytes 3145736 | tf_op jit(solution)/shard_map/ppermute | solution.py:1931
  475.5 15.0 %copy-start.2 = (bf16[256,2048]{1,0:T(8,128)(2,1)}, bf16[256,2048]{1,0:T(8,128)(2,1)S(1)}, u32[]{:S(2)}) copy-start(bf16[256,2048]{1,0:T(8,128)(2,1)S(1)} %collective-permute-done.4.refs_10_) | copy-start | bytes 3145732
  475.5 41.9 %collective-permute-start.9 = (bf16[256,2048]{1,0:T(8,128)(2,1)}, bf16[256,2048]{1,0:T(8,128)(2,1)S(1)}, u32[]{:S(2)}, u32[]{:S(2)}) collective-permute-start(bf16[256,2048]{1,0:T(8,128)(2,1)} %get-tuple-element.142), channel_id=1, source_target_pairs={{0,8},{8,0},{16,24},{24,16},{1,9},{9,1},{17,25},{25,17},{2,10},{10... | collective-permute-start | bytes 3145736 | tf_op jit(solution)/shard_map/ppermute | solution.py:1931
  477.0 40.4 %collective-permute-start.10 = (bf16[256,2048]{1,0:T(8,128)(2,1)}, bf16[256,2048]{1,0:T(8,128)(2,1)}, u32[]{:S(2)}, u32[]{:S(2)}) collective-permute-start(bf16[256,2048]{1,0:T(8,128)(2,1)} %get-tuple-element.144), channel_id=1, source_target_pairs={{0,16},{8,24},{16,0},{24,8},{1,17},{9,25},{17,1},{25,9},{2,18},{10... | collective-permute-start | bytes 3145736 | tf_op jit(solution)/shard_map/ppermute | solution.py:1931
  (10 other events, 33.0 us)
Sparse Core Ops, SparseCore 0:
  9.6 24.9 all-gather.3
  36.2 113.9 all-gather.5
  151.8 59.6 all-gather.7
  305.9 113.2 reduce-scatter.2
  421.4 58.2 reduce-scatter.4

commit v8 on v7

--- a/solution.py
+++ b/solution.py
@@ -404,88 +404,232 @@
     )(x, weight, head_gain, cosine, sine, side)
 
 
-def project_back_kernel(
-    dim, size, query_grad_ref, pair_grad_ref, raw_ref, head_gain_ref, cosine_ref, sine_ref,
-    behind_ref, grad_ref, gain_grad_ref, returned_ref, send_sem, recv_sem
+def far_first(index):
+    return jnp.where(index == 0, 3, jnp.where(index == 3, 0, index))
+
+
+def back_terms_kernel(
+    dim, query_grad_ref, pair_grad_ref, raw_ref, head_gain_ref, cosine_ref, sine_ref, normed_ref,
+    behind_ref, one_ref, two_ref, *refs
 ):
+    size, blk_size = lax.axis_size("heads"), lax.axis_size("blk")
+    out_refs, refs = refs[:size], refs[size:]
+    (
+        own_grad_ref, gain_grad_ref, terms_ref, got_ref, out_grad_ref, early_ref, returned_ref, grads_ref,
+        out_part_ref, out_got_ref, b_send, b_recv, s_send, s_recv, o_send, o_recv, n_send,
+        n_recv,
+    ) = refs
     step = pl.program_id(0)
+    pairs, last = blk_size // 2, blk_size - 1
     head, blk = lax.axis_index("heads"), lax.axis_index("blk")
-    last = lax.axis_size("blk") - 1
+    core, pair = lax.rem(blk, 2), blk // 2
     rows = raw_ref.shape[0]
-    tiles = returned_ref.shape[0] // size // rows
-    back = pltpu.make_async_remote_copy(
-        src_ref=behind_ref,
-        dst_ref=returned_ref,
-        send_sem=send_sem,
-        recv_sem=recv_sem,
-        device_id=(head, jnp.maximum(blk - 1, 0)),
-        device_id_type=MESH,
-    )
+    block = returned_ref.shape[0]
+    count = block // size
+    tiles = count // rows
+    out_rows = out_grad_ref.shape[0]
+    chunk = far_first(jnp.minimum(step // tiles, size - 1))
+
+    def copy(source, target, place, send, recv):
+        return pltpu.make_async_remote_copy(
+            src_ref=source,
+            dst_ref=target,
+            send_sem=send,
+            recv_sem=recv,
+            device_id=place,
+            device_id_type=MESH,
+        )
+
+    def back(k):
+        here = pl.ds(pl.multiple_of((head ^ k) * count, count), count)
+        place = (head, jnp.maximum(blk - 1, 0))
+        return copy(behind_ref.at[here], returned_ref.at[here], place, b_send.at[k], b_recv.at[k])
+
+    def share(k):
+        return copy(
+            grads_ref.at[pl.ds(k * count, count)],
+            got_ref.at[k - 1],
+            (head ^ k, blk),
+            s_send.at[k - 1],
+            s_recv.at[k - 1],
+        )
+
+    near = [
+        copy(
+            ref.at[pl.ds(0, early_ref.shape[1])],
+            early_ref.at[part],
+            (head ^ (1 + part), blk),
+            n_send.at[part],
+            n_recv.at[part],
+        )
+        for part, ref in enumerate((one_ref, two_ref))
+    ]
+
+    def wide_of(value):
+        return value.astype(jnp.float32)
+
+    def out_copy(k, slot):
+        other = lax.rem(pair + k, pairs)
+        return copy(
+            out_part_ref.at[other],
+            out_got_ref.at[slot],
+            (head, other * 2 + core),
+            o_send.at[k],
+            o_recv.at[slot],
+        )
 
     @pl.when(step == 0)
     def _():
+        gain_grad_ref[...] = jnp.zeros_like(gain_grad_ref)
         barrier = pltpu.get_barrier_semaphore()
+        for k in range(1, size):
+            pl.semaphore_signal(barrier, inc=1, device_id=(head ^ k, blk), device_id_type=MESH)
+
+        def greet(k, carried):
+            place = (head, lax.rem(pair + k, pairs) * 2 + core)
+            pl.semaphore_signal(barrier, inc=1, device_id=place, device_id_type=MESH)
+            return carried
+
+        lax.fori_loop(1, pairs, greet, 0)
 
         @pl.when(blk < last)
         def _():
-            pl.semaphore_signal(
-                barrier, inc=1, device_id=(head, blk + 1), device_id_type=MESH
-            )
+            pl.semaphore_signal(barrier, inc=1, device_id=(head, blk + 1), device_id_type=MESH)
+
+        @pl.when(blk == 0)
+        def _():
+            pl.semaphore_wait(barrier, size + pairs - 2)
 
         @pl.when(blk > 0)
         def _():
-            pl.semaphore_wait(barrier, 1)
-            back.start()
+            pl.semaphore_wait(barrier, size + pairs - 1)
+            for k in (3, 1, 2, 0):
+                back(k).start()
 
         @pl.when(blk == last)
         def _():
             returned_ref[...] = jnp.zeros_like(returned_ref)
 
-        @pl.when(blk < last)
+        for sent in near:
+            sent.start()
+
+    for index, k in enumerate((3, 1, 2, 0)):
+
+        @pl.when((step == index * tiles) & (blk < last))
+        def _(k=k):
+            back(k).wait_recv()
+
+    @pl.when(step < size * tiles)
+    def _():
+        place = ((head ^ chunk) * tiles + lax.rem(step, tiles)) * rows
+        returned = returned_ref[pl.ds(pl.multiple_of(place, rows), rows)]
+        pair_grad = (pair_grad_ref[...] + wide_of(returned)).astype(jnp.bfloat16)
+        half = pair_grad.shape[1] // 2
+        grads = wide_of(jnp.concatenate([query_grad_ref[...], pair_grad[:, :half]], axis=1))
+        grads = turn(grads, cosine_ref[...], -sine_ref[...], dim)
+        values = raw_ref[:, : grads.shape[1]]
+        inverse = lax.rsqrt(heads_apart(values, dim) + EPS)
+        gain_grad_ref[...] += jnp.sum(grads * values * inverse, axis=0, keepdims=True)
+        scaled = grads * head_gain_ref[...]
+        moment = spread_mean(scaled * values, dim)
+        values_grad = inverse * scaled - values * inverse * inverse * inverse * moment
+        value = jnp.concatenate([values_grad.astype(jnp.bfloat16), pair_grad[:, half:]], axis=1)
+        held = (chunk * tiles + lax.rem(step, tiles)) * rows
+        grads_ref[pl.ds(pl.multiple_of(held, rows), rows)] = value
+
+        @pl.when(chunk == 0)
         def _():
-            back.wait_recv()
-
-        gain_grad_ref[...] = jnp.zeros_like(gain_grad_ref)
-
-    place = ((head ^ (step // tiles)) * tiles + lax.rem(step, tiles)) * rows
-    returned = returned_ref[pl.ds(pl.multiple_of(place, rows), rows)]
-    pair_grad = pair_grad_ref[...] + returned.astype(jnp.float32)
-    pair_grad = pair_grad.astype(jnp.bfloat16)
-    half = pair_grad.shape[1] // 2
-    grads = jnp.concatenate([query_grad_ref[...], pair_grad[:, :half]], axis=1).astype(jnp.float32)
-    grads = turn(grads, cosine_ref[...], -sine_ref[...], dim)
-    values = raw_ref[:, : grads.shape[1]]
-    inverse = lax.rsqrt(heads_apart(values, dim) + EPS)
-    gain_grad_ref[...] += jnp.sum(grads * values * inverse, axis=0, keepdims=True)
-    scaled = grads * head_gain_ref[...]
-    moment = spread_mean(scaled * values, dim)
-    values_grad = inverse * scaled - values * inverse * inverse * inverse * moment
-    grad_ref[...] = jnp.concatenate([values_grad.astype(jnp.bfloat16), pair_grad[:, half:]], axis=1)
-
-    @pl.when((step == pl.num_programs(0) - 1) & (blk > 0))
-    def _():
-        back.wait_send()
-
-
-def project_back(query_grad, pair_sum, behind, raw, head_gain, cosine, sine, size, rows):
+            own_grad_ref[...] = value
+
+    for index, k in enumerate((3, 1, 2)):
+
+        @pl.when(step == (index + 1) * tiles - 1)
+        def _(k=k):
+            share(k).start()
+
+    @pl.when(step == size * tiles)
+    def _():
+        def out_sum(index, carried):
+            here = pl.ds(pl.multiple_of(index * out_rows, out_rows), out_rows)
+            total = wide_of(out_refs[0][here])
+            for ref in out_refs[1:]:
+                total += wide_of(ref[here])
+            out_part_ref[index, :out_rows] = total.astype(jnp.bfloat16)
+            return carried
+
+        def start(k, carried):
+            out_copy(k, pair).start()
+            return carried
+
+        lax.fori_loop(0, pairs, out_sum, 0)
+        lax.fori_loop(1, pairs, start, 0)
+        out_got_ref[pair] = out_part_ref[pair]
+
+    @pl.when(step >= size * tiles)
+    def _():
+        terms_ref[...] = lax.dot_general(
+            normed_ref[...],
+            grads_ref[...],
+            (((0,), (0,)), ((), ())),
+            preferred_element_type=jnp.float32,
+        ).astype(terms_ref.dtype)
+
+    @pl.when(step == pl.num_programs(0) - 1)
+    def _():
+        def finish(k, carried):
+            out_copy(k, lax.rem(pair + pairs - k, pairs)).wait()
+            return carried
+
+        lax.fori_loop(1, pairs, finish, 0)
+        total = wide_of(out_got_ref[0, :out_rows])
+        for b in range(1, pairs):
+            total += wide_of(out_got_ref[b, :out_rows])
+        out_grad_ref[...] = total
+        for k in range(1, size):
+            share(k).wait()
+        for sent in near:
+            sent.wait()
+
+        @pl.when(blk > 0)
+        def _():
+            for k in range(size):
+                back(k).wait_send()
+
+
+def back_terms(
+    query_grad, pair_sum, behind, raw, head_gain, cosine, sine, normed, near, outs, rows, columns
+):
     count, query_width = query_grad.shape
     pair_width = pair_sum.shape[1]
     out_width = raw.shape[1]
+    height = normed.shape[1]
     dim = cosine.shape[1]
-    tiles = count // size // rows
+    size, blk_size = lax.axis_size("heads"), lax.axis_size("blk")
+    pairs = blk_size // 2
+    tokens = count // size
+    tiles = tokens // rows
+    first = size * tiles
+    out_rows, out_columns = outs[0].shape[0] // pairs, outs[0].shape[1]
+    held_rows = -(-out_rows // 16) * 16
 
     def apart(i):
-        return ((lax.axis_index("heads") ^ (i // tiles)) * tiles + i % tiles, 0)
+        i = jnp.minimum(i, first - 1)
+        return ((lax.axis_index("heads") ^ far_first(i // tiles)) * tiles + i % tiles, 0)
 
     def after_behind(i):
         return (apart(i)[0] + count // rows, 0)
 
+    def later(i):
+        return jnp.maximum(i - first, 0)
+
     def whole(i):
         return (0, 0)
 
+    sems = pltpu.SemaphoreType.DMA
+    low = jnp.bfloat16
     return pl.pallas_call(
-        functools.partial(project_back_kernel, dim, size),
-        grid=(count // rows,),
+        functools.partial(back_terms_kernel, dim),
+        grid=(first + height // columns,),
         in_specs=[
             pl.BlockSpec((rows, query_width), apart),
             pl.BlockSpec((rows, pair_width), after_behind),
@@ -493,29 +637,52 @@
             pl.BlockSpec(head_gain.shape, whole),
             pl.BlockSpec((rows, dim), apart),
             pl.BlockSpec((rows, dim), apart),
+            pl.BlockSpec((count, columns), lambda i: (0, later(i))),
             pl.BlockSpec(memory_space=pl.ANY),
-        ],
+            pl.BlockSpec(memory_space=pl.ANY),
+            pl.BlockSpec(memory_space=pl.ANY),
+        ]
+        + [pl.BlockSpec(out.shape, whole) for out in outs],
         out_specs=[
-            pl.BlockSpec((rows, out_width), lambda i: (i, 0)),
+            pl.BlockSpec(
+                (rows, out_width), lambda i: (jnp.clip(i - (size - 1) * tiles, 0, tiles - 1), 0)
+            ),
             pl.BlockSpec(head_gain.shape, whole),
+            pl.BlockSpec((columns, out_width), lambda i: (later(i), 0)),
+            pl.BlockSpec(memory_space=pl.ANY),
+            pl.BlockSpec((out_rows, out_columns), whole),
+            pl.BlockSpec(memory_space=pl.ANY),
+        ],
+        out_shape=[
+            jax.ShapeDtypeStruct((tokens, out_width), low),
+            jax.ShapeDtypeStruct(head_gain.shape, jnp.float32),
+            jax.ShapeDtypeStruct((height, out_width), low),
+            jax.ShapeDtypeStruct((size - 1, tokens, out_width), low),
+            jax.ShapeDtypeStruct((out_rows, out_columns), jnp.float32),
+            jax.ShapeDtypeStruct((2, near[0].shape[0] // 2, near[0].shape[1]), low),
         ],
         scratch_shapes=[
-            pltpu.VMEM(behind.shape, behind.dtype),
-            pltpu.SemaphoreType.DMA,
-            pltpu.SemaphoreType.DMA,
-        ],
-        out_shape=[
-            jax.ShapeDtypeStruct((count, out_width), jnp.bfloat16),
-            jax.ShapeDtypeStruct(head_gain.shape, jnp.float32),
+            pltpu.VMEM(behind.shape, low),
+            pltpu.VMEM((count, out_width), low),
+            pltpu.VMEM((pairs, held_rows, out_columns), low),
+            pltpu.VMEM((pairs, held_rows, out_columns), low),
+            sems((size,)),
+            sems((size,)),
+            sems((size - 1,)),
+            sems((size - 1,)),
+            sems((pairs,)),
+            sems((pairs,)),
+            sems((2,)),
+            sems((2,)),
         ],
         compiler_params=pltpu.CompilerParams(
             collective_id=9, has_side_effects=True, vmem_limit_bytes=60 << 20
         ),
         cost_estimate=pl.CostEstimate(
-            flops=8_000_000_000, bytes_accessed=8_000_000, transcendentals=0
+            flops=20_000_000_000, bytes_accessed=20_000_000, transcendentals=0
         ),
-        name="project_back",
-    )(query_grad, pair_sum, raw, head_gain, cosine, sine, behind)
+        name="back_terms",
+    )(query_grad, pair_sum, raw, head_gain, cosine, sine, normed, behind, *near, *outs)
 
 
 def join_kernel(
@@ -1007,11 +1174,13 @@
         greet_near(True)
         for copy in far:
             copy.start()
-        for load in loads:
+        for load in loads[:3]:
             load.wait()
 
     @pl.when(step == tiles)
     def _():
+        for load in loads[3:]:
+            load.wait()
         for copy in far:
             copy.wait()
         keep.start()
@@ -1470,150 +1639,11 @@
     )(grad_sum, residual, cot, gain, attended, weight, weights)
 
 
-def qkv_terms_kernel(normed_ref, grad_ref, *refs):
-    size, blk_size = lax.axis_size("heads"), lax.axis_size("blk")
-    out_refs, refs = refs[:size], refs[size:]
-    (
-        terms_ref, got_ref, out_grad_ref, out_part_ref, out_got_ref, send_sem, recv_sem, o_send,
-        o_recv,
-    ) = refs
-    step = pl.program_id(0)
-    pairs = blk_size // 2
-    head, blk = lax.axis_index("heads"), lax.axis_index("blk")
-    core, pair = lax.rem(blk, 2), blk // 2
-    count = got_ref.shape[1]
-    out_rows = out_grad_ref.shape[0]
-    copies = [
-        pltpu.make_async_remote_copy(
-            src_ref=grad_ref.at[pl.ds(k * count, count)],
-            dst_ref=got_ref.at[k - 1],
-            send_sem=send_sem.at[k - 1],
-            recv_sem=recv_sem.at[k - 1],
-            device_id=(head ^ k, blk),
-            device_id_type=MESH,
-        )
-        for k in range(1, size)
-    ]
-
-    def wide_of(block):
-        return block.astype(jnp.float32)
-
-    def out_copy(k, slot):
-        other = lax.rem(pair + k, pairs)
-        return pltpu.make_async_remote_copy(
-            src_ref=out_part_ref.at[other],
-            dst_ref=out_got_ref.at[slot],
-            send_sem=o_send.at[k],
-            recv_sem=o_recv.at[slot],
-            device_id=(head, other * 2 + core),
-            device_id_type=MESH,
-        )
-
-    @pl.when(step == 0)
-    def _():
-        barrier = pltpu.get_barrier_semaphore()
-        for k in range(1, size):
-            pl.semaphore_signal(barrier, inc=1, device_id=(head ^ k, blk), device_id_type=MESH)
-
-        def greet(k, carried):
-            place = (head, lax.rem(pair + k, pairs) * 2 + core)
-            pl.semaphore_signal(barrier, inc=1, device_id=place, device_id_type=MESH)
-            return carried
-
-        lax.fori_loop(1, pairs, greet, 0)
-        pl.semaphore_wait(barrier, size + pairs - 2)
-        for copy in copies:
-            copy.start()
-
-        def out_sum(index, carried):
-            here = pl.ds(pl.multiple_of(index * out_rows, out_rows), out_rows)
-            total = wide_of(out_refs[0][here])
-            for ref in out_refs[1:]:
-                total += wide_of(ref[here])
-            out_part_ref[index, :out_rows] = total.astype(jnp.bfloat16)
-            return carried
-
-        def start(k, carried):
-            out_copy(k, pair).start()
-            return carried
-
-        lax.fori_loop(0, pairs, out_sum, 0)
-        lax.fori_loop(1, pairs, start, 0)
-        out_got_ref[pair] = out_part_ref[pair]
-
-    terms_ref[...] = lax.dot_general(
-        normed_ref[...], grad_ref[...], (((0,), (0,)), ((), ())), preferred_element_type=jnp.float32
-    ).astype(terms_ref.dtype)
-
-    @pl.when(step == pl.num_programs(0) - 1)
-    def _():
-        for copy in copies:
-            copy.wait()
-
-        def finish(k, carried):
-            out_copy(k, lax.rem(pair + pairs - k, pairs)).wait()
-            return carried
-
-        lax.fori_loop(1, pairs, finish, 0)
-        total = wide_of(out_got_ref[0, :out_rows])
-        for b in range(1, pairs):
-            total += wide_of(out_got_ref[b, :out_rows])
-        out_grad_ref[...] = total
-
-
-def qkv_terms(normed, grad, outs, rows):
-    count, height = normed.shape
-    width = grad.shape[1]
-    size, blk_size = lax.axis_size("heads"), lax.axis_size("blk")
-    pairs = blk_size // 2
-    out_rows, out_width = outs[0].shape[0] // pairs, outs[0].shape[1]
-    held_rows = -(-out_rows // 16) * 16
-
-    def whole(i):
-        return (0, 0)
-
-    sems = pltpu.SemaphoreType.DMA
-    return pl.pallas_call(
-        qkv_terms_kernel,
-        grid=(height // rows,),
-        in_specs=[
-            pl.BlockSpec((count, rows), lambda i: (0, i)),
-            pl.BlockSpec((count, width), whole),
-        ]
-        + [pl.BlockSpec(out.shape, whole) for out in outs],
-        out_specs=[
-            pl.BlockSpec((rows, width), lambda i: (i, 0)),
-            pl.BlockSpec(memory_space=pl.ANY),
-            pl.BlockSpec((out_rows, out_width), whole),
-        ],
-        out_shape=[
-            jax.ShapeDtypeStruct((height, width), jnp.bfloat16),
-            jax.ShapeDtypeStruct((size - 1, count // size, width), jnp.bfloat16),
-            jax.ShapeDtypeStruct((out_rows, out_width), jnp.float32),
-        ],
-        scratch_shapes=[
-            pltpu.VMEM((pairs, held_rows, out_width), jnp.bfloat16),
-            pltpu.VMEM((pairs, held_rows, out_width), jnp.bfloat16),
-            sems((size - 1,)),
-            sems((size - 1,)),
-            sems((pairs,)),
-            sems((pairs,)),
-        ],
-        compiler_params=pltpu.CompilerParams(
-            collective_id=7, has_side_effects=True, vmem_limit_bytes=60 << 20
-        ),
-        cost_estimate=pl.CostEstimate(
-            flops=4 * count * height * width, bytes_accessed=20_000_000, transcendentals=0
-        ),
-        name="qkv_terms",
-    )(normed, grad, *outs)
-
-
 def finish_kernel(
     query_width, dim, got_ref, qkv_ref, gain_ref, ffn_ref, head_ref, *refs
 ):
     size, blk_size = lax.axis_size("heads"), lax.axis_size("blk")
-    sources, refs = refs[:12], refs[12:]
+    sources, early_ref, refs = refs[:12], refs[12], refs[13:]
     (
         grad_ref, qkv_grad_ref, gains_ref, in_grad_ref, layer_ref, *refs
     ) = refs
@@ -1623,7 +1653,7 @@
         qkv_other_ref, qkv_sum_ref, qkv_z_ref, qkv_mine_ref, qkv_got_ref, gain_mine_ref,
         gain_away_ref, gain_other_ref, gain_sum_ref, gain_z_ref, gain_part_ref, gain_got_ref,
         in_got_ref, load_sem, c_send, c_recv, z_send, z_recv, h_send,
-        h_recv, gc_send, gc_recv, gz_send, gz_recv, gh_send, gh_recv, i_send, i_recv,
+        h_recv, gc_send, gc_recv, gz_send, gz_recv, gh_send, gh_recv, i_send, i_recv, n_send, n_recv,
     ) = refs
     devices = size * blk_size
     pairs = blk_size // 2
@@ -1643,6 +1673,14 @@
             load_sem.at[index],
         )
         for index, (source, target) in enumerate(zip(sources, held))
+        if index not in (8, 9)
+    ]
+    early = early_ref.shape[1]
+    loads += [
+        pltpu.make_async_copy(
+            early_ref.at[part], held[8 + part].at[pl.ds(0, early)], load_sem.at[8 + part]
+        )
+        for part in range(2)
     ]
     for load in loads:
         load.start()
@@ -1681,7 +1719,17 @@
         )
         for k in range(1, size)
     ]
-    for sent in in_sends:
+    near_sends = [
+        copy(
+            sources[8 + part].at[pl.ds(early, count // 2 - early)],
+            held[8 + part].at[pl.ds(early, count // 2 - early)],
+            (head ^ (1 + part), blk),
+            n_send.at[part],
+            n_recv.at[part],
+        )
+        for part in range(2)
+    ]
+    for sent in in_sends + near_sends:
         sent.start()
 
     across = copy(qkv_ref.at[:, 1 - core], qkv_other_ref, (head, blk ^ 1), c_send, c_recv)
@@ -1831,6 +1879,8 @@
 
     for load in loads[6:]:
         load.wait()
+    for sent in near_sends:
+        sent.wait_recv()
     half = count // 2
     for part in range(2):
         here = slice(part * half, (part + 1) * half)
@@ -1852,13 +1902,13 @@
     finish_around(gain_part_ref, gain_got_ref, gh_send, gh_recv)
     gains_ref[...] = jnp.sum(gain_got_ref[...], axis=0)
     across.wait_send()
-    for sent in in_sends:
+    for sent in in_sends + near_sends:
         sent.wait_send()
 
 
 def finish(
     sent, got, qkv_part, x, residual_grad, gain, ffn_sum, head_sum, weight, weights, in_part,
-    residual, rest, terms, query_width, dim
+    residual, rest, terms, early, query_width, dim
 ):
     size, blk_size = lax.axis_size("heads"), lax.axis_size("blk")
     devices = size * blk_size
@@ -1880,7 +1930,7 @@
             jax.ShapeDtypeStruct((depth, size * units), jnp.float32),
             jax.ShapeDtypeStruct((count, width), low),
         ],
-        in_specs=[vmem] * 5 + [anywhere] * 12,
+        in_specs=[vmem] * 5 + [anywhere] * 13,
         out_specs=[vmem] * 5,
         scratch_shapes=[pltpu.VMEM((width, joined), low)]
         + [pltpu.VMEM(array.shape, array.dtype) for array in loaded]
@@ -1916,6 +1966,8 @@
             sems((size,)),
             sems((size - 1,)),
             sems((size - 1,)),
+            sems((2,)),
+            sems((2,)),
         ],
         compiler_params=pltpu.CompilerParams(
             collective_id=0, has_side_effects=True, vmem_limit_bytes=60 << 20
@@ -1923,7 +1975,7 @@
         name="finish",
     )(
         got, qkv_part.reshape(size * pairs, 2, depth, joined), gain, ffn_sum, head_sum,
-        weight, *loaded, sent, in_part, residual, rest, *terms
+        weight, *loaded, sent, in_part, residual, rest, *terms, early
     )
 
 
@@ -2041,16 +2093,14 @@
     pair_sum, out_top_last, out_bottom_last, *out_slices = lax.optimization_barrier(
         (pair_sum, out_top_last, out_bottom_last, *out_slices)
     )
-    projected_grad, head_sum = project_back(
-        query_grad, pair_sum, behind, raw, head_gain, cosine, sine, size, 256
-    )
-    out_top = permute(after(one_near, pair_sum), "heads", 1)
-    out_bottom = permute(after(two_near, pair_sum), "heads", 2)
-    qkv_part, got, out_grad = qkv_terms(normed, projected_grad, out_slices, 512)
+    projected_grad, head_sum, qkv_part, got, out_grad, early = back_terms(
+        query_grad, pair_sum, behind, raw, head_gain, cosine, sine, normed, (one_near, two_near),
+        out_slices, 256, 512
+    )
     input_grad, qkv_grad, gains, ffn_in_grad, layer_out = finish(
         projected_grad, got, qkv_part, inputs, residual_grad, attn_scaling, ffn_sum, head_sum,
         qkv_rows, qkv_peers, in_part, residual, out_rest,
-        (out_top, out_bottom, out_top_last, out_bottom_last), query_width, head_dim
+        (one_near, two_near, out_top_last, out_bottom_last), early, query_width, head_dim
     )
     down_part, gains = lax.optimization_barrier((down_part, gains))
     ffn_out_grad = wide(down_part)

time: 580 us -> 576 us (level)
    pallas_call x2 -> x1, Pallas kernels: 39.7 us -> 35.9 us  [back_terms(): pl.pallas_call(functools.partial(back_terms_kernel, dim), grid=(first + h...]
    ppermute x11 -> x9, starting transfers between devices: 13.2 us -> 10.8 us  [permute(): lax.ppermute(block, axis, [(i, i ^ k) for i in range(lax.axis_size(axis))])]
  transfers between devices with their start and end apart: 16 -> 14, of which waited for: 0 -> 1; matrix products, arithmetic and copies ran while one was open for 2% -> 2% of each run, Pallas kernels for 78% -> 79%
where the time goes in v8:
time: 576 us
  Pallas kernels  528 us (92%)
  between operations  14.1 us (2%)
  local copies, waits for them, and re-layouts  13.8 us (2%)
  starting transfers between devices  11.2 us (2%)
  other arithmetic  8.45 us (1%)
    pallas_call x1, Pallas kernels, feed_tail(): pl.pallas_call(tail_kernel, grid=(16 + total // units,), in_specs=[pl.Blo...  86.3 us
    pallas_call x1, Pallas kernels, begin(): pl.pallas_call(begin_kernel, out_shape=[jax.ShapeDtypeStruct((size * coun...  78.9 us
    pallas_call x1, Pallas kernels, hidden_pass(): pl.pallas_call(functools.partial(hidden_kernel, tiles), grid=(2 * tiles +...  75.2 us
    pallas_call x1, Pallas kernels, join(): pl.pallas_call(join_kernel, grid=(count // rows,), in_specs=[pl.BlockSpec...  68.7 us
    pallas_call x1, Pallas kernels, finish(): pl.pallas_call(functools.partial(finish_kernel, query_width, dim), out_sh...  37.5 us
    pallas_call x1, Pallas kernels, attend_back(): pl.pallas_call(functools.partial(attend_back_kernel, heads, key_rows, (wi...  37.3 us
    pallas_call x1, Pallas kernels, residual_back(): pl.pallas_call(residual_back_kernel, grid=(tiles + 1,), in_specs=[tile, t...  36.2 us
    pallas_call x1, Pallas kernels, back_terms(): pl.pallas_call(functools.partial(back_terms_kernel, dim), grid=(first + h...  35.9 us
  transfers between devices with their start and end apart: 14, of which 1 were waited for; matrix products, arithmetic and copies ran while one was open for 2% of the time, Pallas kernels for 79%

profile of v8, /device:TPU:0, one launch (start us, length us, event | category | flops | bytes accessed | tf_op | source)
XLA Modules:
  0.0 576.3 jit_solution(12194122348114979177)
XLA Ops:
  8.0 21.5 %trade.1 = bf16[4,64,2560]{2,1,0:T(8,128)(2,1)} custom-call(bf16[64,10240]{1,0:T(8,128)(2,1)} %in_ref.1), custom_call_target="tpu_custom_call" | custom-call | tf_op jit(solution)/shard_map/trade/pallas_call | solution.py:852
  31.7 78.9 %begin.1 = (bf16[2048,2048]{1,0:T(8,128)(2,1)}, bf16[4,512,512]{2,1,0:T(8,128)(2,1)}, bf16[256,2048]{1,0:T(8,128)(2,1)}, bf16[256,2048]{1,0:T(8,128)(2,1)}, f32[2048,64]{1,0:T(8,128)}, /*index=5*/f32[2048,64]{1,0:T(8,128)}) custom-call(bf16[512,2048]{1,0:T(8,128)(2,1)} %refs_2_.1, bf16[4,64,512]{2,1,0:T(8,128)(2,1)} %bitcast.30, bf16[512,2048]{1,0:T(8,128)(2,1)} %cot_ref.9, ...), custom_call_target="tpu_custom_call" | custom-call | tf_op jit(solution)/shard_map/begin/pallas_call | solution.py:1028
  111.2 32.0 %project.1 = (bf16[2048,256]{1,0:T(8,128)(2,1)}, f32[2048,384]{1,0:T(8,128)}, bf16[2048,2048]{1,0:T(8,128)(2,1)}, f32[1,2048]{1,0:T(1,128)}, f32[1,2048]{1,0:T(1...) custom-call(bf16[2048,2048]{1,0:T(8,128)(2,1)} %get-tuple-element.83.x_ref, bf16[2048,512]{1,0:T(8,128)(2,1)} %bitcast.26, ...), custom_call_target="tpu_custom_call" | custom-call | flops 6442450944 | bytes 30000000 | tf_op jit(solution)/shard_map/project/pallas_call | solution.py:365
  143.2 2.2 collective-permute-start
  146.2 18.3 %attend.1 = (bf16[2048,256]{1,0:T(8,128)(2,1)}, f32[4,1,2048]{2,1,0:T(1,128)}) custom-call(s32[5]{0:T(128)} %pad_add_fusion.first_ref, bf16[2048,256]{1,0:T(8,128)(2,1)} %get-tuple-element.87.query_ref, s32[1,2048]{1,0:T(1,128)} %bitcast.34, bf16[4096,128]{1,0:T(8,128)(2,1)} %get-tuple-element.89.pair_ref), custom_call_target="tpu_custom_call" | custom-call | flops 20000000000 | bytes 8000000 | tf_op jit(solution)/shard_map/attend/pallas_call | solution.py:149
  164.5 1.3 constant_dynamic-slice_fusion.3
  166.8 68.7 %join.1 = (f32[2048,2048]{1,0:T(8,128)}, bf16[2048,2048]{1,0:T(8,128)(2,1)}, bf16[512,1024]{1,0:T(8,128)(2,1)}, bf16[256,2048]{1,0:T(8,128)(2,1)}, bf16[256,2048]{1,0:T(8,128)(2,1)}) custom-call(bf16[2048,2048]{1,0:T(8,128)(2,1)} %get-tuple-element.83.x_ref, bf16[256,2048]{1,0:T(8,128)(2,1)} %all-gather.4.cloned.1.call-done.side_ref.weight_ref, ...), custom_call_target="tpu_custom_call" | custom-call | flops 17179869184 | bytes 50000000 | tf_op jit(solution)/shard_map/join/pallas_call | solution.py:775
  236.9 75.2 %hidden_pass.1 = (bf16[2048,1280]{1,0:T(8,128)(2,1)}, bf16[2048,1280]{1,0:T(8,128)(2,1)}, bf16[2048,1280]{1,0:T(8,128)(2,1)}, bf16[2048,2560]{1,0:T(8,128)(2,1)}...) custom-call(bf16[2048,2048]{1,0:T(8,128)(2,1)} %get-tuple-element.95.normed_ref.turned_ref, ...), custom_call_target="tpu_custom_call" | custom-call | flops 53687091200 | bytes 70000000 | tf_op jit(solution)/shard_map/hidden_pass/pallas_call | solution.py:1243
  312.3 86.3 %feed_tail.1 = (bf16[1280,2048]{1,0:T(8,128)(2,1)}, bf16[256,2048]{1,0:T(8,128)(2,1)}, bf16[256,2048]{1,0:T(8,128)(2,1)}, bf16[256,2048]{1,0:T(8,128)(2,1)}, bf1...) custom-call(bf16[2048,1280]{1,0:T(8,128)(2,1)} %get-tuple-element.103.gate_ref, ...), custom_call_target="tpu_custom_call" | custom-call | flops 42949672960 | bytes 70000000 | tf_op jit(solution)/shard_map/feed_tail/pallas_call | solution.py:1444
  398.7 1.9 collective-permute-start.2
  400.5 1.1 collective-permute-start.3
  401.7 36.2 %residual_back.1 = (f32[512,2048]{1,0:T(8,128)}, f32[1,2048]{1,0:T(1,128)}, bf16[4,512,256]{2,1,0:T(8,128)(2,1)}, bf16[4,32,2048]{2,1,0:T(8,128)(2,1)}, bf16[4,3...) custom-call(f32[512,2048]{1,0:T(8,128)} %get-tuple-element.107.grad_sum_ref, ...), custom_call_target="tpu_custom_call" | custom-call | flops 4294967296 | bytes 30000000 | tf_op jit(solution)/shard_map/residual_back/pallas_call | solution.py:1599
  437.8 1.5 collective-permute-start.6
  439.9 1.5 collective-permute-start.8
  441.4 3.3 add_convert_fusion
  444.7 1.4 collective-permute-start.4
  446.7 37.3 %attend_back.1 = (bf16[2048,256]{1,0:T(8,128)(2,1)}, f32[4096,128]{1,0:T(8,128)}, bf16[2048,128]{1,0:T(8,128)(2,1)}) custom-call(s32[5]{0:T(128)} %pad_add_fusion.first_ref, bf16[2048,256]{1,0:T(8,128)(2,1)} %get-tuple-element.87.query_ref, s32[1,2048]{1,0:T(1,128)} %bitcast.35, bf16[4096,128]{1,0:T(8,128)(2,1)} %get-tuple-element.89.pair_ref, ...), custom_call_target="tpu_custom_call" | custom-call | flops 40000000000 | bytes 12000000 | tf_op jit(solution)/shard_map/attend_back/pallas_call | solution.py:179
  484.2 35.9 %back_terms.1 = (bf16[512,384]{1,0:T(8,128)(2,1)}, f32[1,320]{1,0:T(1,128)}, bf16[2048,384]{1,0:T(8,128)(2,1)}, bf16[3,512,384]{2,1,0:T(8,128)(2,1)}, f32[32,2048]{1,0:T(8,128)}, /*index=5*/bf16[2,128,2048]{2,1,0:T(8,128)(2,1)}) custom-call(bf16[2048,256]{1,0:T(8,128)(2,1)} %get-tuple-element.114.query_grad_ref, ...), custom_call_target="tpu_custom_call" | custom-call | flops 20000000000 | bytes 20000000 | tf_op jit(solution)/shard_map/back_terms/pallas_call | solution.py:630
  520.1 37.5 %finish.1 = (f32[512,2048]{1,0:T(8,128)}, f32[64,1536]{1,0:T(8,128)}, f32[8,128]{1,0:T(8,128)}, f32[64,10240]{1,0:T(8,128)}, bf16[512,2048]{1,0:T(8,128)(2,1)}) custom-call(bf16[3,512,384]{2,1,0:T(8,128)(2,1)} %get-tuple-element.133.got_ref, bf16[16,2,64,384]{3,2,1,0:T(8,128)(2,1)} %bitcast.29, f32[1,2048]{1,0:T(1,128)} %get-tuple-element.135.gain_ref, ...), custom_call_target="tpu_custom_call" | custom-call | tf_op jit(solution)/shard_map/finish/pallas_call | solution.py:1924
  557.6 1.4 slice_bitcast_fusion
  559.0 2.3 convert_element_type.38
  561.3 3.3 copy.32
  564.7 2.1 copy.33
  568.3 1.5 copy.36
  (81 shorter events, 9.7 us)
Async XLA Ops:
  7.2 104.0 %all-gather.4.cloned.1.call-start = ((), (), s32[]{:S(2)}) async-start(), calls=%async_computation.2 | async-start | bytes 1179648 | tf_op jit(solution)/shard_map/all_gather | solution.py:2035
  7.9 21.7 %slice-start = ((bf16[64,1536]{1,0:T(8,128)(2,1)}), bf16[64,1024]{1,0:T(8,128)(2,1)S(1)}, s32[]{:S(2)}) async-start(bf16[64,1536]{1,0:T(8,128)(2,1)} %param.14), calls=%async_computation.7 | async-start | bytes 262144 | tf_op jit(solution)/shard_map/slice | solution.py:2027
  7.9 21.7 %copy-start.4 = (bf16[64,1536]{1,0:T(8,128)(2,1)S(1)}, bf16[64,1536]{1,0:T(8,128)(2,1)}, u32[]{:S(2)}) copy-start(bf16[64,1536]{1,0:T(8,128)(2,1)} %param.14) | copy-start | bytes 589828
  7.9 22.0 %copy-start.15 = (bf16[64]{0:T(256)(128)(2,1)S(1)}, bf16[64]{0:T(256)(128)(2,1)}, u32[]{:S(2)}) copy-start(bf16[64]{0:T(256)(128)(2,1)} %param.15) | copy-start | bytes 388
  7.9 22.1 %copy-start.9 = (bf16[64]{0:T(256)(128)(2,1)S(1)}, bf16[64]{0:T(256)(128)(2,1)}, u32[]{:S(2)}) copy-start(bf16[64]{0:T(256)(128)(2,1)} %param.13) | copy-start | bytes 388
  8.0 22.2 %copy-start.10 = (bf16[64]{0:T(256)(128)(2,1)S(1)}, bf16[64]{0:T(256)(128)(2,1)}, u32[]{:S(2)}) copy-start(bf16[64]{0:T(256)(128)(2,1)} %param.18) | copy-start | bytes 388
  8.0 158.9 %all-gather.6.cloned.1.call-start = ((), (), s32[]{:S(2)}) async-start(), calls=%async_computation.3 | async-start | bytes 11796480 | tf_op jit(solution)/shard_map/all_gather | solution.py:2037
  29.6 206.0 %all-gather.8.cloned.1.call-start = ((), (), s32[]{:S(2)}) async-start(), calls=%async_computation.4 | async-start | bytes 5898240 | tf_op jit(solution)/shard_map/all_gather | solution.py:2052
  31.7 78.9 %copy-start.11 = (bf16[64]{0:T(256)(128)(2,1)S(1)}, bf16[64]{0:T(256)(128)(2,1)}, u32[]{:S(2)}) copy-start(bf16[64]{0:T(256)(128)(2,1)} %param.16) | copy-start | bytes 388
  111.2 34.3 %copy-start.7 = (s32[2048]{0:T(1024)S(1)}, s32[2048]{0:T(1024)}, u32[]{:S(2)}) copy-start(s32[2048]{0:T(1024)} %param.12) | copy-start | bytes 24580
  143.2 298.2 %reduce-scatter.3.cloned.1.call-start = ((), (), s32[]{:S(2)}) async-start(), calls=%async_computation.5 | async-start | bytes 11796480 | tf_op jit(solution)/shard_map/reduce_scatter | solution.py:2069
  143.2 92.3 %collective-permute-start = (bf16[256,2048]{1,0:T(8,128)(2,1)}, bf16[256,2048]{1,0:T(8,128)(2,1)S(1)}, u32[]{:S(2)}, u32[]{:S(2)}) collective-permute-start(bf16[256,2048]{1,0:T(8,128)(2,1)} %get-tuple-element.98), channel_id=1, source_target_pairs={{0,8},{8,0},{16,24},{24,16},{1,9},{9,1},{17,25},{25,17},{2,10},{10... | collective-permute-start | bytes 3145736 | tf_op jit(solution)/shard_map/ppermute | solution.py:1983
  145.4 90.2 %collective-permute-start.1 = (bf16[256,2048]{1,0:T(8,128)(2,1)}, bf16[256,2048]{1,0:T(8,128)(2,1)S(1)}, u32[]{:S(2)}, u32[]{:S(2)}) collective-permute-start(bf16[256,2048]{1,0:T(8,128)(2,1)} %get-tuple-element.101), channel_id=1, source_target_pairs={{0,16},{8,24},{16,0},{24,8},{1,17},{9,25},{17,1},{25,9},{2,18},{10... | collective-permute-start | bytes 3145736 | tf_op jit(solution)/shard_map/ppermute | solution.py:1983
  312.1 245.5 %reduce-scatter.5.cloned.1.call-start = ((), (), s32[]{:S(2)}) async-start(), calls=%async_computation.6 | async-start | bytes 5898240 | tf_op jit(solution)/shard_map/reduce_scatter | solution.py:2075
  398.7 42.7 %collective-permute-start.2 = (bf16[256,2048]{1,0:T(8,128)(2,1)}, bf16[256,2048]{1,0:T(8,128)(2,1)S(1)}, u32[]{:S(2)}, u32[]{:S(2)}) collective-permute-start(bf16[256,2048]{1,0:T(8,128)(2,1)} %get-tuple-element.111), channel_id=1, source_target_pairs={{0,8},{8,0},{16,24},{24,16},{1,9},{9,1},{17,25},{25,17},{2,10},{10... | collective-permute-start | bytes 3145736 | tf_op jit(solution)/shard_map/ppermute | solution.py:1983
  400.5 40.9 %collective-permute-start.3 = (bf16[256,2048]{1,0:T(8,128)(2,1)S(1)}, bf16[256,2048]{1,0:T(8,128)(2,1)S(1)}, u32[]{:S(2)}, u32[]{:S(2)}) collective-permute-start(bf16[256,2048]{1,0:T(8,128)(2,1)S(1)} %copy-done.14), channel_id=1, source_target_pairs={{0,16},{8,24},{16,0},{24,8},{1,17},{9,25},{17,1},{25,9},{2,18},{10... | collective-permute-start | bytes 3145736 | tf_op jit(solution)/shard_map/ppermute | solution.py:1983
  437.8 46.1 %collective-permute-start.6 = (bf16[128,2048]{1,0:T(8,128)(2,1)}, bf16[128,2048]{1,0:T(8,128)(2,1)}, u32[]{:S(2)}, u32[]{:S(2)}) collective-permute-start(bf16[128,2048]{1,0:T(8,128)(2,1)} %bitcast.43), channel_id=1, source_target_pairs={{0,8},{8,0},{16,24},{24,16},{1,9},{9,1},{17,25},{25,17},{2,10},{10... | collective-permute-start | bytes 1572872 | tf_op jit(solution)/shard_map/ppermute | solution.py:1983
  439.3 44.7 %collective-permute-start.7 = (bf16[128,2048]{1,0:T(8,128)(2,1)}, bf16[128,2048]{1,0:T(8,128)(2,1)}, u32[]{:S(2)}, u32[]{:S(2)}) collective-permute-start(bf16[128,2048]{1,0:T(8,128)(2,1)} %bitcast.42), channel_id=1, source_target_pairs={{0,16},{8,24},{16,0},{24,8},{1,17},{9,25},{17,1},{25,9},{2,18},{10... | collective-permute-start | bytes 1572872 | tf_op jit(solution)/shard_map/ppermute | solution.py:1983
  439.9 44.1 %collective-permute-start.8 = (bf16[128,2048]{1,0:T(8,128)(2,1)}, bf16[128,2048]{1,0:T(8,128)(2,1)}, u32[]{:S(2)}, u32[]{:S(2)}) collective-permute-start(bf16[128,2048]{1,0:T(8,128)(2,1)} %bitcast.41), channel_id=1, source_target_pairs={{0,24},{8,16},{16,8},{24,0},{1,25},{9,17},{17,9},{25,1},{2,26},{10... | collective-permute-start | bytes 1572872 | tf_op jit(solution)/shard_map/ppermute | solution.py:1983
  444.7 39.4 %collective-permute-start.4 = (bf16[256,2048]{1,0:T(8,128)(2,1)}, bf16[256,2048]{1,0:T(8,128)(2,1)S(1)}, u32[]{:S(2)}, u32[]{:S(2)}) collective-permute-start(bf16[256,2048]{1,0:T(8,128)(2,1)} %get-tuple-element.155), channel_id=1, source_target_pairs={{0,16},{8,24},{16,0},{24,8},{1,17},{9,25},{17,1},{25,9},{2,18},{10... | collective-permute-start | bytes 3145736 | tf_op jit(solution)/shard_map/ppermute | solution.py:1983
  446.1 38.1 %collective-permute-start.5 = (bf16[256,2048]{1,0:T(8,128)(2,1)S(1)}, bf16[256,2048]{1,0:T(8,128)(2,1)S(1)}, u32[]{:S(2)}, u32[]{:S(2)}) collective-permute-start(bf16[256,2048]{1,0:T(8,128)(2,1)S(1)} %get-tuple-element.154), channel_id=1, source_target_pairs={{0,8},{8,0},{16,24},{24,16},{1,9},{9,1},{17,25},{25,17},{2,10},{10... | collective-permute-start | bytes 3145736 | tf_op jit(solution)/shard_map/ppermute | solution.py:1983
  484.1 35.9 %copy-start.2 = (bf16[256,2048]{1,0:T(8,128)(2,1)}, bf16[256,2048]{1,0:T(8,128)(2,1)S(1)}, u32[]{:S(2)}) copy-start(bf16[256,2048]{1,0:T(8,128)(2,1)S(1)} %collective-permute-done.4.refs_10_) | copy-start | bytes 3145732
  484.1 36.0 %copy-start.3 = (bf16[256,2048]{1,0:T(8,128)(2,1)}, bf16[256,2048]{1,0:T(8,128)(2,1)S(1)}, u32[]{:S(2)}) copy-start(bf16[256,2048]{1,0:T(8,128)(2,1)S(1)} %collective-permute-done.5.refs_11_) | copy-start | bytes 3145732
  564.7 3.6 copy-start.1
  (7 other events, 13.2 us)
Sparse Core Ops, SparseCore 0:
  9.6 24.9 all-gather.3
  36.2 113.9 all-gather.5
  151.8 59.6 all-gather.7
  312.2 106.6 reduce-scatter.2
  421.0 58.2 reduce-scatter.4

commit v9 on v8

--- a/solution.py
+++ b/solution.py
@@ -1643,11 +1643,11 @@
     query_width, dim, got_ref, qkv_ref, gain_ref, ffn_ref, head_ref, *refs
 ):
     size, blk_size = lax.axis_size("heads"), lax.axis_size("blk")
-    sources, early_ref, refs = refs[:12], refs[12], refs[13:]
+    sources, early_ref, down_ref, refs = refs[:12], refs[12], refs[13], refs[14:]
     (
-        grad_ref, qkv_grad_ref, gains_ref, in_grad_ref, layer_ref, *refs
+        grad_ref, qkv_grad_ref, gains_ref, in_grad_ref, layer_ref, down_grad_ref, *refs
     ) = refs
-    held, refs = refs[:12], refs[12:]
+    held, down_held, refs = refs[:12], refs[12], refs[13:]
     weight_ref, weights_ref, x_ref, residual_grad_ref, sent_ref, in_ref, residual_ref, rest_ref = held[:8]
     (
         qkv_other_ref, qkv_sum_ref, qkv_z_ref, qkv_mine_ref, qkv_got_ref, gain_mine_ref,
@@ -1682,6 +1682,7 @@
         )
         for part in range(2)
     ]
+    loads.append(pltpu.make_async_copy(down_ref, down_held, load_sem.at[12]))
     for load in loads:
         load.start()
 
@@ -1879,6 +1880,7 @@
 
     for load in loads[6:]:
         load.wait()
+    down_grad_ref[...] = wide_of(down_held[...])
     for sent in near_sends:
         sent.wait_recv()
     half = count // 2
@@ -1908,7 +1910,7 @@
 
 def finish(
     sent, got, qkv_part, x, residual_grad, gain, ffn_sum, head_sum, weight, weights, in_part,
-    residual, rest, terms, early, query_width, dim
+    residual, rest, terms, early, down_part, query_width, dim
 ):
     size, blk_size = lax.axis_size("heads"), lax.axis_size("blk")
     devices = size * blk_size
@@ -1929,14 +1931,16 @@
             jax.ShapeDtypeStruct((8, 128), jnp.float32),
             jax.ShapeDtypeStruct((depth, size * units), jnp.float32),
             jax.ShapeDtypeStruct((count, width), low),
-        ],
-        in_specs=[vmem] * 5 + [anywhere] * 13,
-        out_specs=[vmem] * 5,
+            jax.ShapeDtypeStruct(down_part.shape, jnp.float32),
+        ],
+        in_specs=[vmem] * 5 + [anywhere] * 14,
+        out_specs=[vmem] * 6,
         scratch_shapes=[pltpu.VMEM((width, joined), low)]
         + [pltpu.VMEM(array.shape, array.dtype) for array in loaded]
         + [pltpu.VMEM((count, joined), low), pltpu.VMEM(in_part.shape, low)]
         + [pltpu.VMEM((count, width), jnp.float32), pltpu.VMEM((count, width), low)]
         + [pltpu.VMEM((count // 2, width), low)] * 4
+        + [pltpu.VMEM(down_part.shape, low)]
         + [
             pltpu.VMEM((size * pairs, depth, joined), low),
             pltpu.VMEM((size, pairs, depth, joined), low),
@@ -1951,7 +1955,7 @@
             pltpu.VMEM((size, 8, 128), jnp.float32),
             pltpu.VMEM((size, 8, 128), jnp.float32),
             pltpu.VMEM((size - 1, depth, units), low),
-            sems((12,)),
+            sems((13,)),
             sems,
             sems,
             sems((pairs,)),
@@ -1975,7 +1979,7 @@
         name="finish",
     )(
         got, qkv_part.reshape(size * pairs, 2, depth, joined), gain, ffn_sum, head_sum,
-        weight, *loaded, sent, in_part, residual, rest, *terms, early
+        weight, *loaded, sent, in_part, residual, rest, *terms, early, down_part
     )
 
 
@@ -2097,13 +2101,11 @@
         query_grad, pair_sum, behind, raw, head_gain, cosine, sine, normed, (one_near, two_near),
         out_slices, 256, 512
     )
-    input_grad, qkv_grad, gains, ffn_in_grad, layer_out = finish(
+    input_grad, qkv_grad, gains, ffn_in_grad, layer_out, ffn_out_grad = finish(
         projected_grad, got, qkv_part, inputs, residual_grad, attn_scaling, ffn_sum, head_sum,
         qkv_rows, qkv_peers, in_part, residual, out_rest,
-        (one_near, two_near, out_top_last, out_bottom_last), early, query_width, head_dim
-    )
-    down_part, gains = lax.optimization_barrier((down_part, gains))
-    ffn_out_grad = wide(down_part)
+        (one_near, two_near, out_top_last, out_bottom_last), early, down_part, query_width, head_dim
+    )
     return (
         layer_out,
         input_grad,

time: 576 us -> 580 us (level)
    unnamed x37 -> x40, local copies, waits for them, and re-layouts: 9.71 us -> 12.6 us
  transfers between devices with their start and end apart: 14 -> 14, of which waited for: 1 -> 1; matrix products, arithmetic and copies ran while one was open for 2% -> 2% of each run, Pallas kernels for 79% -> 72%
where the time goes in v9:
time: 580 us; the launch traced here: 578 us
  Pallas kernels  531 us (92%)
  local copies, waits for them, and re-layouts  16.6 us (3%)
  between operations  14.1 us (2%)
  starting transfers between devices  9.21 us (2%)
  other arithmetic  6.15 us (1%)
    pallas_call x1, Pallas kernels, feed_tail(): pl.pallas_call(tail_kernel, grid=(16 + total // units,), in_specs=[pl.Blo...  86.5 us
    pallas_call x1, Pallas kernels, begin(): pl.pallas_call(begin_kernel, out_shape=[jax.ShapeDtypeStruct((size * coun...  78.9 us
    pallas_call x1, Pallas kernels, hidden_pass(): pl.pallas_call(functools.partial(hidden_kernel, tiles), grid=(2 * tiles +...  74.2 us
    pallas_call x1, Pallas kernels, join(): pl.pallas_call(join_kernel, grid=(count // rows,), in_specs=[pl.BlockSpec...  67.6 us
    pallas_call x1, Pallas kernels, back_terms(): pl.pallas_call(functools.partial(back_terms_kernel, dim), grid=(first + h...  39.8 us
    pallas_call x1, Pallas kernels, finish(): pl.pallas_call(functools.partial(finish_kernel, query_width, dim), out_sh...  38.3 us
    pallas_call x1, Pallas kernels, attend_back(): pl.pallas_call(functools.partial(attend_back_kernel, heads, key_rows, (wi...  37.2 us
    pallas_call x1, Pallas kernels, residual_back(): pl.pallas_call(residual_back_kernel, grid=(tiles + 1,), in_specs=[tile, t...  36.4 us
  transfers between devices with their start and end apart: 14, of which 1 were waited for; matrix products, arithmetic and copies ran while one was open for 2% of the time, Pallas kernels for 72%

profile of v9, /device:TPU:0, one launch (start us, length us, event | category | flops | bytes accessed | tf_op | source)
XLA Modules:
  0.0 577.9 jit_solution(994000237951533848)
XLA Ops:
  8.0 21.5 %trade.1 = bf16[4,64,2560]{2,1,0:T(8,128)(2,1)} custom-call(bf16[64,10240]{1,0:T(8,128)(2,1)} %in_ref.1), custom_call_target="tpu_custom_call" | custom-call | tf_op jit(solution)/shard_map/trade/pallas_call | solution.py:852
  31.7 78.9 %begin.1 = (bf16[2048,2048]{1,0:T(8,128)(2,1)}, bf16[4,512,512]{2,1,0:T(8,128)(2,1)}, bf16[256,2048]{1,0:T(8,128)(2,1)}, bf16[256,2048]{1,0:T(8,128)(2,1)}, f32[2048,64]{1,0:T(8,128)}, /*index=5*/f32[2048,64]{1,0:T(8,128)}) custom-call(bf16[512,2048]{1,0:T(8,128)(2,1)} %refs_2_.1, bf16[4,64,512]{2,1,0:T(8,128)(2,1)} %bitcast.30, bf16[512,2048]{1,0:T(8,128)(2,1)} %cot_ref.9, ...), custom_call_target="tpu_custom_call" | custom-call | tf_op jit(solution)/shard_map/begin/pallas_call | solution.py:1028
  111.2 32.0 %project.1 = (bf16[2048,256]{1,0:T(8,128)(2,1)}, f32[2048,384]{1,0:T(8,128)}, bf16[2048,2048]{1,0:T(8,128)(2,1)}, f32[1,2048]{1,0:T(1,128)}, f32[1,2048]{1,0:T(1...) custom-call(bf16[2048,2048]{1,0:T(8,128)(2,1)} %get-tuple-element.82.x_ref, bf16[2048,512]{1,0:T(8,128)(2,1)} %bitcast.26, ...), custom_call_target="tpu_custom_call" | custom-call | flops 6442450944 | bytes 30000000 | tf_op jit(solution)/shard_map/project/pallas_call | solution.py:365
  143.3 2.1 collective-permute-start
  146.2 18.3 %attend.1 = (bf16[2048,256]{1,0:T(8,128)(2,1)}, f32[4,1,2048]{2,1,0:T(1,128)}) custom-call(s32[5]{0:T(128)} %pad_add_fusion.first_ref, bf16[2048,256]{1,0:T(8,128)(2,1)} %get-tuple-element.86.query_ref, s32[1,2048]{1,0:T(1,128)} %bitcast.34, bf16[4096,128]{1,0:T(8,128)(2,1)} %get-tuple-element.88.pair_ref), custom_call_target="tpu_custom_call" | custom-call | flops 20000000000 | bytes 8000000 | tf_op jit(solution)/shard_map/attend/pallas_call | solution.py:149
  164.5 1.3 constant_dynamic-slice_fusion.3
  165.8 1.0 pad_maximum_fusion.mine_ref
  166.8 67.6 %join.1 = (f32[2048,2048]{1,0:T(8,128)}, bf16[2048,2048]{1,0:T(8,128)(2,1)}, bf16[512,1024]{1,0:T(8,128)(2,1)}, bf16[256,2048]{1,0:T(8,128)(2,1)}, bf16[256,2048]{1,0:T(8,128)(2,1)}) custom-call(bf16[2048,2048]{1,0:T(8,128)(2,1)} %get-tuple-element.82.x_ref, bf16[256,2048]{1,0:T(8,128)(2,1)} %all-gather.4.cloned.1.call-done.side_ref.weight_ref, ...), custom_call_target="tpu_custom_call" | custom-call | flops 17179869184 | bytes 50000000 | tf_op jit(solution)/shard_map/join/pallas_call | solution.py:775
  235.7 74.2 %hidden_pass.1 = (bf16[2048,1280]{1,0:T(8,128)(2,1)}, bf16[2048,1280]{1,0:T(8,128)(2,1)}, bf16[2048,1280]{1,0:T(8,128)(2,1)}, bf16[2048,2560]{1,0:T(8,128)(2,1)}...) custom-call(bf16[2048,2048]{1,0:T(8,128)(2,1)} %get-tuple-element.94.normed_ref.turned_ref, ...), custom_call_target="tpu_custom_call" | custom-call | flops 53687091200 | bytes 70000000 | tf_op jit(solution)/shard_map/hidden_pass/pallas_call | solution.py:1243
  310.2 86.5 %feed_tail.1 = (bf16[1280,2048]{1,0:T(8,128)(2,1)}, bf16[256,2048]{1,0:T(8,128)(2,1)}, bf16[256,2048]{1,0:T(8,128)(2,1)}, bf16[256,2048]{1,0:T(8,128)(2,1)}, bf1...) custom-call(bf16[2048,1280]{1,0:T(8,128)(2,1)} %get-tuple-element.102.gate_ref, ...), custom_call_target="tpu_custom_call" | custom-call | flops 42949672960 | bytes 70000000 | tf_op jit(solution)/shard_map/feed_tail/pallas_call | solution.py:1444
  397.0 1.0 copy-done.15
  398.9 36.4 %residual_back.1 = (f32[512,2048]{1,0:T(8,128)}, f32[1,2048]{1,0:T(1,128)}, bf16[4,512,256]{2,1,0:T(8,128)(2,1)}, bf16[4,32,2048]{2,1,0:T(8,128)(2,1)}, bf16[4,3...) custom-call(f32[512,2048]{1,0:T(8,128)} %get-tuple-element.106.grad_sum_ref, ...), custom_call_target="tpu_custom_call" | custom-call | flops 4294967296 | bytes 30000000 | tf_op jit(solution)/shard_map/residual_back/pallas_call | solution.py:1599
  436.0 1.4 collective-permute-start.7
  437.3 1.5 collective-permute-start.8
  438.9 3.3 add_convert_fusion
  442.7 1.4 collective-permute-start.5
  444.1 37.2 %attend_back.1 = (bf16[2048,256]{1,0:T(8,128)(2,1)}, f32[4096,128]{1,0:T(8,128)}, bf16[2048,128]{1,0:T(8,128)(2,1)}) custom-call(s32[5]{0:T(128)} %pad_add_fusion.first_ref, bf16[2048,256]{1,0:T(8,128)(2,1)} %get-tuple-element.86.query_ref, s32[1,2048]{1,0:T(1,128)} %bitcast.35, bf16[4096,128]{1,0:T(8,128)(2,1)} %get-tuple-element.88.pair_ref, ...), custom_call_target="tpu_custom_call" | custom-call | flops 40000000000 | bytes 12000000 | tf_op jit(solution)/shard_map/attend_back/pallas_call | solution.py:179
  481.5 39.8 %back_terms.1 = (bf16[512,384]{1,0:T(8,128)(2,1)}, f32[1,320]{1,0:T(1,128)}, bf16[2048,384]{1,0:T(8,128)(2,1)}, bf16[3,512,384]{2,1,0:T(8,128)(2,1)}, f32[32,2048]{1,0:T(8,128)}, /*index=5*/bf16[2,128,2048]{2,1,0:T(8,128)(2,1)}) custom-call(bf16[2048,256]{1,0:T(8,128)(2,1)} %get-tuple-element.113.query_grad_ref, ...), custom_call_target="tpu_custom_call" | custom-call | flops 20000000000 | bytes 20000000 | tf_op jit(solution)/shard_map/back_terms/pallas_call | solution.py:630
  521.4 38.3 %finish.1 = (f32[512,2048]{1,0:T(8,128)}, f32[64,1536]{1,0:T(8,128)}, f32[8,128]{1,0:T(8,128)}, f32[64,10240]{1,0:T(8,128)}, bf16[512,2048]{1,0:T(8,128)(2,1)}, /*index=5*/f32[160,2048]{1,0:T(8,128)}) custom-call(bf16[3,512,384]{2,1,0:T(8,128)(2,1)} %get-tuple-element.132.got_ref, bf16[16,2,64,384]{3,2,1,0:T(8,128)(2,1)} %bitcast.29, ...), custom_call_target="tpu_custom_call" | custom-call | tf_op jit(solution)/shard_map/finish/pallas_call | solution.py:1926
  559.7 1.4 slice_bitcast_fusion
  561.1 3.3 copy.33
  564.4 2.1 copy.34
  568.0 1.5 copy.37
  570.3 1.1 copy.38
  (83 shorter events, 10.4 us)
Async XLA Ops:
  7.2 104.0 %all-gather.4.cloned.1.call-start = ((), (), s32[]{:S(2)}) async-start(), calls=%async_computation.2 | async-start | bytes 1179648 | tf_op jit(solution)/shard_map/all_gather | solution.py:2039
  7.9 21.7 %slice-start = ((bf16[64,1536]{1,0:T(8,128)(2,1)}), bf16[64,1024]{1,0:T(8,128)(2,1)S(1)}, s32[]{:S(2)}) async-start(bf16[64,1536]{1,0:T(8,128)(2,1)} %param.14), calls=%async_computation.7 | async-start | bytes 262144 | tf_op jit(solution)/shard_map/slice | solution.py:2031
  7.9 21.7 %copy-start.5 = (bf16[64,1536]{1,0:T(8,128)(2,1)S(1)}, bf16[64,1536]{1,0:T(8,128)(2,1)}, u32[]{:S(2)}) copy-start(bf16[64,1536]{1,0:T(8,128)(2,1)} %param.14) | copy-start | bytes 589828
  7.9 22.0 %copy-start.16 = (bf16[64]{0:T(256)(128)(2,1)S(1)}, bf16[64]{0:T(256)(128)(2,1)}, u32[]{:S(2)}) copy-start(bf16[64]{0:T(256)(128)(2,1)} %param.15) | copy-start | bytes 388
  7.9 22.1 %copy-start.10 = (bf16[64]{0:T(256)(128)(2,1)S(1)}, bf16[64]{0:T(256)(128)(2,1)}, u32[]{:S(2)}) copy-start(bf16[64]{0:T(256)(128)(2,1)} %param.13) | copy-start | bytes 388
  8.0 22.2 %copy-start.11 = (bf16[64]{0:T(256)(128)(2,1)S(1)}, bf16[64]{0:T(256)(128)(2,1)}, u32[]{:S(2)}) copy-start(bf16[64]{0:T(256)(128)(2,1)} %param.18) | copy-start | bytes 388
  8.0 158.9 %all-gather.6.cloned.1.call-start = ((), (), s32[]{:S(2)}) async-start(), calls=%async_computation.3 | async-start | bytes 11796480 | tf_op jit(solution)/shard_map/all_gather | solution.py:2041
  29.6 204.9 %all-gather.8.cloned.1.call-start = ((), (), s32[]{:S(2)}) async-start(), calls=%async_computation.4 | async-start | bytes 5898240 | tf_op jit(solution)/shard_map/all_gather | solution.py:2056
  31.7 78.9 %copy-start.12 = (bf16[64]{0:T(256)(128)(2,1)S(1)}, bf16[64]{0:T(256)(128)(2,1)}, u32[]{:S(2)}) copy-start(bf16[64]{0:T(256)(128)(2,1)} %param.16) | copy-start | bytes 388
  111.2 34.3 %copy-start.8 = (s32[2048]{0:T(1024)S(1)}, s32[2048]{0:T(1024)}, u32[]{:S(2)}) copy-start(s32[2048]{0:T(1024)} %param.12) | copy-start | bytes 24580
  143.2 295.7 %reduce-scatter.3.cloned.1.call-start = ((), (), s32[]{:S(2)}) async-start(), calls=%async_computation.5 | async-start | bytes 11796480 | tf_op jit(solution)/shard_map/reduce_scatter | solution.py:2073
  143.3 91.1 %collective-permute-start = (bf16[256,2048]{1,0:T(8,128)(2,1)}, bf16[256,2048]{1,0:T(8,128)(2,1)S(1)}, u32[]{:S(2)}, u32[]{:S(2)}) collective-permute-start(bf16[256,2048]{1,0:T(8,128)(2,1)} %get-tuple-element.97), channel_id=1, source_target_pairs={{0,8},{8,0},{16,24},{24,16},{1,9},{9,1},{17,25},{25,17},{2,10},{10... | collective-permute-start | bytes 3145736 | tf_op jit(solution)/shard_map/ppermute | solution.py:1987
  145.4 89.0 %collective-permute-start.1 = (bf16[256,2048]{1,0:T(8,128)(2,1)}, bf16[256,2048]{1,0:T(8,128)(2,1)S(1)}, u32[]{:S(2)}, u32[]{:S(2)}) collective-permute-start(bf16[256,2048]{1,0:T(8,128)(2,1)} %get-tuple-element.100), channel_id=1, source_target_pairs={{0,16},{8,24},{16,0},{24,8},{1,17},{9,25},{17,1},{25,9},{2,18},{10... | collective-permute-start | bytes 3145736 | tf_op jit(solution)/shard_map/ppermute | solution.py:1987
  310.0 211.4 %reduce-scatter.5.cloned.1.call-start = ((), (), s32[]{:S(2)}) async-start(), calls=%async_computation.6 | async-start | bytes 5898240 | tf_op jit(solution)/shard_map/reduce_scatter | solution.py:2079
  396.8 42.1 %collective-permute-start.2 = (bf16[256,2048]{1,0:T(8,128)(2,1)}, bf16[256,2048]{1,0:T(8,128)(2,1)S(1)}, u32[]{:S(2)}, u32[]{:S(2)}) collective-permute-start(bf16[256,2048]{1,0:T(8,128)(2,1)} %get-tuple-element.110), channel_id=1, source_target_pairs={{0,8},{8,0},{16,24},{24,16},{1,9},{9,1},{17,25},{25,17},{2,10},{10... | collective-permute-start | bytes 3145736 | tf_op jit(solution)/shard_map/ppermute | solution.py:1987
  398.0 40.8 %collective-permute-start.3 = (bf16[256,2048]{1,0:T(8,128)(2,1)S(1)}, bf16[256,2048]{1,0:T(8,128)(2,1)S(1)}, u32[]{:S(2)}, u32[]{:S(2)}) collective-permute-start(bf16[256,2048]{1,0:T(8,128)(2,1)S(1)} %copy-done.15), channel_id=1, source_target_pairs={{0,16},{8,24},{16,0},{24,8},{1,17},{9,25},{17,1},{25,9},{2,18},{10... | collective-permute-start | bytes 3145736 | tf_op jit(solution)/shard_map/ppermute | solution.py:1987
  435.3 46.1 %collective-permute-start.6 = (bf16[128,2048]{1,0:T(8,128)(2,1)}, bf16[128,2048]{1,0:T(8,128)(2,1)}, u32[]{:S(2)}, u32[]{:S(2)}) collective-permute-start(bf16[128,2048]{1,0:T(8,128)(2,1)} %bitcast.43), channel_id=1, source_target_pairs={{0,8},{8,0},{16,24},{24,16},{1,9},{9,1},{17,25},{25,17},{2,10},{10... | collective-permute-start | bytes 1572872 | tf_op jit(solution)/shard_map/ppermute | solution.py:1987
  436.0 45.4 %collective-permute-start.7 = (bf16[128,2048]{1,0:T(8,128)(2,1)}, bf16[128,2048]{1,0:T(8,128)(2,1)}, u32[]{:S(2)}, u32[]{:S(2)}) collective-permute-start(bf16[128,2048]{1,0:T(8,128)(2,1)} %bitcast.42), channel_id=1, source_target_pairs={{0,16},{8,24},{16,0},{24,8},{1,17},{9,25},{17,1},{25,9},{2,18},{10... | collective-permute-start | bytes 1572872 | tf_op jit(solution)/shard_map/ppermute | solution.py:1987
  437.3 44.1 %collective-permute-start.8 = (bf16[128,2048]{1,0:T(8,128)(2,1)}, bf16[128,2048]{1,0:T(8,128)(2,1)}, u32[]{:S(2)}, u32[]{:S(2)}) collective-permute-start(bf16[128,2048]{1,0:T(8,128)(2,1)} %bitcast.41), channel_id=1, source_target_pairs={{0,24},{8,16},{16,8},{24,0},{1,25},{9,17},{17,9},{25,1},{2,26},{10... | collective-permute-start | bytes 1572872 | tf_op jit(solution)/shard_map/ppermute | solution.py:1987
  442.2 39.3 %collective-permute-start.4 = (bf16[256,2048]{1,0:T(8,128)(2,1)}, bf16[256,2048]{1,0:T(8,128)(2,1)S(1)}, u32[]{:S(2)}, u32[]{:S(2)}) collective-permute-start(bf16[256,2048]{1,0:T(8,128)(2,1)} %get-tuple-element.153), channel_id=1, source_target_pairs={{0,16},{8,24},{16,0},{24,8},{1,17},{9,25},{17,1},{25,9},{2,18},{10... | collective-permute-start | bytes 3145736 | tf_op jit(solution)/shard_map/ppermute | solution.py:1987
  442.7 38.8 %collective-permute-start.5 = (bf16[256,2048]{1,0:T(8,128)(2,1)S(1)}, bf16[256,2048]{1,0:T(8,128)(2,1)S(1)}, u32[]{:S(2)}, u32[]{:S(2)}) collective-permute-start(bf16[256,2048]{1,0:T(8,128)(2,1)S(1)} %get-tuple-element.152), channel_id=1, source_target_pairs={{0,8},{8,0},{16,24},{24,16},{1,9},{9,1},{17,25},{25,17},{2,10},{10... | collective-permute-start | bytes 3145736 | tf_op jit(solution)/shard_map/ppermute | solution.py:1987
  481.5 39.9 %copy-start.3 = (bf16[256,2048]{1,0:T(8,128)(2,1)}, bf16[256,2048]{1,0:T(8,128)(2,1)S(1)}, u32[]{:S(2)}) copy-start(bf16[256,2048]{1,0:T(8,128)(2,1)S(1)} %collective-permute-done.4.refs_10_) | copy-start | bytes 3145732
  481.5 39.9 %copy-start.4 = (bf16[256,2048]{1,0:T(8,128)(2,1)}, bf16[256,2048]{1,0:T(8,128)(2,1)S(1)}, u32[]{:S(2)}) copy-start(bf16[256,2048]{1,0:T(8,128)(2,1)S(1)} %collective-permute-done.5.refs_11_) | copy-start | bytes 3145732
  564.4 3.6 copy-start.1
  (8 other events, 14.9 us)
Sparse Core Ops, SparseCore 0:
  9.6 24.9 all-gather.3
  36.2 113.9 all-gather.5
  151.8 59.6 all-gather.7
  310.1 108.1 reduce-scatter.2
  420.5 58.2 reduce-scatter.4
